TPU v7x, 32 devices: a whole 2x2x4 slice. The times are simulated.
32 devices in a mesh: seq: 16 (over z, x, core), req: 2 (over y).
Axes of the slice: x: 2, y: 2, z: 4, core: 2. Of those that a mesh axis runs over, the one named last changes fastest.
Arguments:
- tokens: bfloat16 [2048, 2048], P('seq'), may hold values from -6 to 6
- norm_gain: float32 [2048], replicated, may hold values from 0.5 to 1.5
- w_query: bfloat16 [2048, 1024], P(None, 'req'), as said below
- key_projection: bfloat16 [2048, 512], P(None, 'req')
- value_projection: bfloat16 [2048, 512], P(None, 'req'), may hold values from -0.125 to 0.125
- w_out: bfloat16 [1024, 2048], P('req'), may hold values from -0.1875 to 0.1875
- lengths: int32 [4], replicated, may hold values from 1 to 1365, 2048 in all
- block_split: int32 [16], replicated, may hold values from 0 to 15, each once
- page_slot: int32 [64], replicated, may hold values from 0 to 127, as said below
Outputs:
- hidden: bfloat16 [2048, 2048], P(('seq', 'req'))
- key_value_cache: bfloat16 [128, 2, 32, 512], P('seq', None, None, 'req')
Inputs may be any that keep to these rules, and one draw needn't show every extreme that they name: block_split is a permutation; index i of seq holds block block_split[i] and its mirror. `page_slot`: distinct slots; slot s lies on index s // 8 of seq. `w_query`: a projection scaled like 2 / sqrt(2048).
All inputs are finite; a program needn't handle non-finite values.
Results may differ from a plain program's by a relative error of at most 0.014.
The roundings to bfloat16 on the way count: a program that leaves them out, or rounds other values in their place, can miss the bound.
Values may be sent and summed in bfloat16 or wider, within the bound.
No kernel may reach another device: no remote copies, remote signals or barrier semaphores. Data moves between devices by JAX's collectives and lax.ppermute only.
A program may use at most 128 MiB of HBM per device.

v0:
```python
import math

import jax
import jax.numpy as jnp
from jax import lax
from jax.sharding import PartitionSpec as P

HEAD_SIZE = 128
PAGE_TOKENS = 32


theta_base = 1000000.0
norm_eps = 1e-05
far_below = -1e30


def rotary_rows(heads, offset_list):
    half_width = heads.shape[-1] // 2
    exponent = jnp.arange(half_width, dtype=jnp.float32) * (2.0 / heads.shape[-1])
    inv_freq = jnp.power(theta_base, -exponent)
    angle = offset_list.astype(jnp.float32)[:, None] * inv_freq[None, :]
    cosine = jnp.concatenate([jnp.cos(angle), jnp.cos(angle)], -1)[:, None, :]
    sine = jnp.concatenate([jnp.sin(angle), jnp.sin(angle)], -1)[:, None, :]
    rolled = jnp.concatenate([-heads[..., half_width:], heads[..., :half_width]], -1)
    return heads * cosine + rolled * sine


def slot_positions(block_split, lengths, total_rows, shard_rows):
    row_ids = jnp.arange(total_rows, dtype=jnp.int32)
    half_rows = shard_rows // 2
    cycle_size = block_split.shape[0]
    owner_dev = row_ids // shard_rows
    device_ids = jnp.arange(cycle_size, dtype=jnp.int32)
    first_block = jnp.sum(
        jnp.where(owner_dev[:, None] == device_ids[None, :], block_split[None, :], 0), 1
    )
    block_ids = jnp.where(
        row_ids % shard_rows < half_rows, first_block, 2 * cycle_size - 1 - first_block
    )
    position = block_ids * half_rows + row_ids % half_rows
    request_ends = jnp.cumsum(lengths)
    request_begins = request_ends - lengths
    request = jnp.sum((position[:, None] >= request_ends[None, :]).astype(jnp.int32), 1)
    prompt_ids = jnp.arange(lengths.shape[0], dtype=jnp.int32)
    begins = jnp.sum(
        jnp.where(request[:, None] == prompt_ids[None, :], request_begins[None, :], 0), 1
    )
    return (position, request, position - begins)


def on_device(
    tokens,
    norm_gain,
    w_query,
    key_projection,
    value_projection,
    w_out,
    lengths,
    block_split,
    page_slot,
):
    shard_rows = tokens.shape[0]
    half_rows = shard_rows // 2
    cycle_size = lax.axis_size("seq")
    device = lax.axis_index("seq")
    first_row = device * shard_rows
    position, request, offset_list = slot_positions(
        block_split, lengths, shard_rows * cycle_size, shard_rows
    )
    q_pos = lax.dynamic_slice_in_dim(position, first_row, shard_rows, 0)
    q_req = lax.dynamic_slice_in_dim(request, first_row, shard_rows, 0)
    q_off = lax.dynamic_slice_in_dim(offset_list, first_row, shard_rows, 0)
    cache_rows = 2 * shard_rows
    slot_count = cache_rows // PAGE_TOKENS
    slot_ids = page_slot[position // PAGE_TOKENS]
    holder = slot_ids // slot_count
    target_rows = jnp.where(
        holder == device, slot_ids % slot_count * PAGE_TOKENS + position % PAGE_TOKENS, -1
    )
    heads_local = w_query.shape[1] // HEAD_SIZE
    kv_local = key_projection.shape[1] // HEAD_SIZE
    group_width = heads_local // kv_local
    scale_factor = 1.0 / math.sqrt(HEAD_SIZE)
    widened = tokens.astype(jnp.float32)
    normalized_input = (
        widened * lax.rsqrt(jnp.mean(widened * widened, -1, keepdims=True) + norm_eps) * norm_gain
    ).astype(jnp.bfloat16)
    queries = rotary_rows(
        jnp.dot(normalized_input, w_query, preferred_element_type=jnp.float32).reshape(
            shard_rows, heads_local, HEAD_SIZE
        ),
        q_off,
    )
    queries = queries.astype(jnp.bfloat16).reshape(shard_rows, kv_local, group_width, HEAD_SIZE)
    key_matrix_rows = rotary_rows(
        jnp.dot(normalized_input, key_projection, preferred_element_type=jnp.float32).reshape(
            shard_rows, kv_local, HEAD_SIZE
        ),
        q_off,
    )
    key_matrix_rows = key_matrix_rows.astype(jnp.bfloat16).reshape(shard_rows, kv_local * HEAD_SIZE)
    value_matrix_rows = jnp.dot(
        normalized_input, value_projection, preferred_element_type=jnp.float32
    ).astype(jnp.bfloat16)

    def attend(moments, key_block, value_block, visible):
        run_max, run_sum, run_acc = moments
        width = key_block.shape[0]
        key_heads = key_block.reshape(width, kv_local, HEAD_SIZE)
        value_heads = value_block.reshape(width, kv_local, HEAD_SIZE)
        scores = (
            jnp.einsum("qhgd,khd->hgqk", queries, key_heads, preferred_element_type=jnp.float32)
            * scale_factor
        )
        masked = jnp.where(visible[None, None], scores, far_below)
        new_max = jnp.maximum(run_max, jnp.max(masked, -1))
        weights = jnp.where(visible[None, None], jnp.exp(masked - new_max[..., None]), 0.0)
        factor = jnp.exp(run_max - new_max)
        new_sum = run_sum * factor + jnp.sum(weights, -1)
        added = jnp.einsum(
            "hgqk,khd->hgqd",
            weights.astype(jnp.bfloat16),
            value_heads,
            preferred_element_type=jnp.float32,
        )
        return (new_max, new_sum, run_acc * factor[..., None] + added)

    def store(parts, key_block, value_block, key_target):
        cache_grid = jnp.arange(cache_rows, dtype=jnp.int32)
        placer = (cache_grid[:, None] == key_target[None, :]).astype(jnp.bfloat16)
        return (
            parts[0] + jnp.dot(placer, key_block, preferred_element_type=jnp.float32),
            parts[1] + jnp.dot(placer, value_block, preferred_element_type=jnp.float32),
        )

    start_max = jnp.full((kv_local, group_width, shard_rows), far_below, jnp.float32)
    start_sum = jnp.zeros((kv_local, group_width, shard_rows), jnp.float32)
    start_acc = jnp.zeros((kv_local, group_width, shard_rows, HEAD_SIZE), jnp.float32)
    start_keys = jnp.zeros((cache_rows, kv_local * HEAD_SIZE), jnp.float32)
    start_values = jnp.zeros((cache_rows, kv_local * HEAD_SIZE), jnp.float32)
    state = (start_max, start_sum, start_acc, start_keys, start_values)
    absorb_state = state
    key_piece = lax.all_gather(key_matrix_rows, "seq", axis=0, tiled=True)
    value_piece = lax.all_gather(value_matrix_rows, "seq", axis=0, tiled=True)
    length = key_piece.shape[0]
    sub_width = math.gcd(length, 1024)

    def sub_step(carried, sub_index):
        offset = sub_index * sub_width
        key_block = lax.dynamic_slice_in_dim(key_piece, offset, sub_width, 0)
        value_block = lax.dynamic_slice_in_dim(value_piece, offset, sub_width, 0)
        key_pos = lax.dynamic_slice_in_dim(position, offset, sub_width, 0)
        key_req = lax.dynamic_slice_in_dim(request, offset, sub_width, 0)
        key_target = lax.dynamic_slice_in_dim(target_rows, offset, sub_width, 0)
        visible = (key_req[None, :] == q_req[:, None]) & (key_pos[None, :] <= q_pos[:, None])
        moments = carried[:3]
        cache_parts = carried[3:]
        moments = attend(moments, key_block, value_block, visible)
        cache_parts = lax.cond(
            jnp.any(key_target >= 0),
            store,
            lambda parts, key_block, value_block, key_target: parts,
            cache_parts,
            key_block,
            value_block,
            key_target,
        )
        return (moments + cache_parts, None)

    absorb_state, _ = lax.scan(
        sub_step, absorb_state, jnp.arange(length // sub_width, dtype=jnp.int32)
    )
    state = absorb_state
    run_max, run_sum, run_acc, cache_keys, cache_values = state
    normalised = run_acc / run_sum[..., None]
    context = (
        jnp.transpose(normalised, (2, 0, 1, 3))
        .reshape(shard_rows, heads_local * HEAD_SIZE)
        .astype(jnp.bfloat16)
    )
    summed = lax.psum_scatter(
        jnp.dot(context, w_out, preferred_element_type=jnp.float32).astype(jnp.bfloat16),
        "req",
        scatter_dimension=0,
        tiled=True,
    ).astype(jnp.float32)
    residual = lax.dynamic_slice_in_dim(tokens, lax.axis_index("req") * half_rows, half_rows, 0)
    hidden = (summed + residual.astype(jnp.float32)).astype(jnp.bfloat16)
    key_value_cache = jnp.stack(
        [
            cache_keys.reshape(slot_count, PAGE_TOKENS, kv_local * HEAD_SIZE),
            cache_values.reshape(slot_count, PAGE_TOKENS, kv_local * HEAD_SIZE),
        ],
        1,
    ).astype(jnp.bfloat16)
    return (hidden, key_value_cache)


def solution(mesh):
    in_specs = (
        P("seq", None),
        P(),
        P(None, "req"),
        P(None, "req"),
        P(None, "req"),
        P("req", None),
        P(),
        P(),
        P(),
    )
    out_specs = (P(("seq", "req"), None), P("seq", None, None, "req"))
    return jax.shard_map(
        on_device, mesh=mesh, in_specs=in_specs, out_specs=out_specs, check_vma=False
    )
```

profile of v0, /device:TPU:0, one launch (start us, length us, event | category | flops | bytes accessed | tf_op | source)
XLA Modules:
  0.0 149.8 jit_solution(6020855363518437872)
XLA Ops:
  7.3 1.4 fusion.15
  8.7 2.4 %convolution_convert_fusion.1 = bf16[128,256]{1,0:T(8,128)(2,1)} fusion(bf16[2048,256]{1,0:T(8,128)(2,1)} %param.17, bf16[128,2048]{1,0:T(8,128)(2,1)} %param.13, f32[2048]{0:T(1024)} %param.14, f32[128]{0:T(128)S(1)} %add_rsqrt_fusion), kind=kOutput, calls=%fused_computation.31 | convolution fusion | flops 135299072 | bytes 1647104 | tf_op jit(solution)/shard_map/dot_general | solution.py:102
  11.1 1.6 %fusion.44 = f32[128,256]{1,0:T(8,128)S(1)} fusion(bf16[2048,256]{1,0:T(8,128)(2,1)} %param.16, bf16[128,2048]{1,0:T(8,128)(2,1)S(1)} %copy-done.4, f32[2048]{0:T(1024)S(1)} %copy-done.11, f32[128]{0:T(128)S(1)} %add_rsqrt_fusion), kind=kOutput, calls=%fused_computation.171 | convolution fusion | flops 135266304 | bytes 1712640 | tf_op jit(solution)/shard_map/dot_general | solution.py:96
  16.9 1.3 dynamic_slice.31
  18.2 2.1 %fusion.42 = f32[128,512]{1,0:T(8,128)S(1)} fusion(bf16[2048,512]{1,0:T(8,128)(2,1)} %param.15, bf16[128,2048]{1,0:T(8,128)(2,1)S(1)} %copy-done.4, f32[2048]{0:T(1024)S(1)} %copy-done.11, f32[128]{0:T(128)S(1)} %add_rsqrt_fusion), kind=kOutput, calls=%fused_computation.170 | convolution fusion | flops 269484032 | bytes 2892288 | tf_op jit(solution)/shard_map/dot_general | solution.py:89
  23.7 4.2 %compare_select_fusion.1 = (s32[2048,1]{0,1:T(1,128)S(1)}, s32[2048,1]{0,1:T(1,128)S(1)}) fusion(s32[]{:T(128)} %bitcast.63, s32[]{:T(128)} %bitcast.64, s32[]{:T(128)} %bitcast.65, s32[]{:T(128)} %bitcast.66, s32[]{:T(128)} %bitcast.67, s32[]{:T(128)} %bitcast.69, s32[]{:T(128)} %bitcast.68, s32[2048,1]{0,1:T(1,128)S(1)} %bitcast.147), kind=kLoop, calls=%fused_computation.115 | loop fusion | flops 96256 | bytes 24604 | tf_op jit(solution)/shard_map/gather | solution.py:75
  28.0 1.4 compare_reduce_fusion.57
  29.4 36.5 %fusion.29 = s32[2048]{0:T(1024)} fusion(pred[2048]{0:T(1024)(128)(4,1)S(1)} %get-tuple-element.273, pred[2048]{0:T(1024)(128)(4,1)S(1)} %get-tuple-element.272, pred[2048]{0:T(1024)(128)(4,1)S(1)} %get-tuple-element.271, pred[2048]{0:T(1024)(128)(4,1)S(1)} %get-tuple-element.270, pred[2048]{0:T(1024)(128)(4,1)S(1)} %get-tuple-element.269, ...), kind=kLoop, calls=%fused_computation.150 | loop fusion | flops 221184 | bytes 141544 | tf_op jit(solution)/shard_map/jit(_where)/select_n | solution.py:77
  66.7 24.9 %all-gather.3.cloned.1.call-done = bf16[2048,256]{1,0:T(8,128)(2,1)} async-done(((bf16[128,256]{1,0:T(8,128)(2,1)}), bf16[2048,256]{1,0:T(8,128)(2,1)}) %all-gather.3.cloned.1.call-update) | async-done | bytes 1048592 | tf_op jit(solution)/shard_map/all_gather | solution.py:143
  92.8 32.0 %while.19 = (s32[]{:T(128)}, f32[2,2,128]{2,1,0:T(2,128)S(1)}, f32[2,2,128]{2,1,0:T(2,128)}, f32[2,2,128,128]{3,2,1,0:T(8,128)}, f32[256,256]{1,0:T(8,128)}, /*i...) while((s32[]{:T(128)}, f32[2,2,128]{2,1,0:T(2,128)S(1)}, ...), condition=%wide.region_11.12_spmd.clone, body=%wide.region_5.11_spmd.clone.sunk | while | flops 544936448 | bytes 19621384 | solution.py:170
  95.3 1.3 compare_reduce_fusion.59
  98.2 2.1 %constant_dynamic-slice_fusion.3 = (bf16[1024,256]{1,0:T(8,128)(2,1)S(1)}, bf16[1024,256]{1,0:T(8,128)(2,1)}) fusion(bf16[2048,256]{1,0:T(8,128)(2,1)} %get-tuple-element.554, s32[]{:T(128)S(6)} %select_n.231, bf16[2048,256]{1,0:T(8,128)(2,1)} %get-tuple-element.552), kind=kLoop, calls=%fused_computation.23.clone.1 | loop fusion | bytes 2097156 | tf_op jit(solution)/shard_map/while/body/eval_jaxpr/dynamic_slice | solution.py:151
  102.5 3.5 %conditional.3 = ((f32[256,256]{1,0:T(8,128)}, f32[256,256]{1,0:T(8,128)S(1)})) conditional(s32[]{:T(128)} %convert_element_type.99, (f32[256,256]{1,0:T(8,128)}, f32[256,256]{1,0:T(8,128)S(1)}) %tuple.177, (s32[1024]{0:T(1024)S(1)}, bf16[1024,256]{0,1:T(8,128)(2,1)S(1)}, f32[256,256]{1,0:T(8,128)}, bf16[1024,256]{0,1:T(8,128)(2,1)}, ...), branch_computations={%region_9.9_spmd, %region_10.10_spmd} | conditional | flops 269090816 | bytes 2105368 | solution.py:159
  102.5 1.5 convolution_add_fusion
  104.0 2.0 %convolution_add_fusion.1 = f32[256,256]{1,0:T(8,128)} fusion(f32[256,256]{1,0:T(8,128)} %get-tuple-element.74, bf16[1024,256]{0,1:T(8,128)(2,1)S(1)} %get-tuple-element.198, s32[1024]{0:T(1024)S(1)} %get-tuple-element.75), kind=kOutput, calls=%fused_computation.1 | convolution fusion | flops 134545408 | bytes 1052672 | tf_op jit(solution)/shard_map/while/body/eval_jaxpr/cond/branch_1_fun/dot_general | solution.py:132
  111.3 1.3 compare_reduce_fusion.59
  114.2 2.1 %constant_dynamic-slice_fusion.3 = (bf16[1024,256]{1,0:T(8,128)(2,1)S(1)}, bf16[1024,256]{1,0:T(8,128)(2,1)}) fusion(bf16[2048,256]{1,0:T(8,128)(2,1)} %get-tuple-element.554, s32[]{:T(128)S(6)} %select_n.231, bf16[2048,256]{1,0:T(8,128)(2,1)} %get-tuple-element.552), kind=kLoop, calls=%fused_computation.23.clone.1 | loop fusion | bytes 2097156 | tf_op jit(solution)/shard_map/while/body/eval_jaxpr/dynamic_slice | solution.py:151
  116.3 1.2 copy.69
  118.5 3.5 %conditional.3 = ((f32[256,256]{1,0:T(8,128)}, f32[256,256]{1,0:T(8,128)S(1)})) conditional(s32[]{:T(128)} %convert_element_type.99, (f32[256,256]{1,0:T(8,128)}, f32[256,256]{1,0:T(8,128)S(1)}) %tuple.177, (s32[1024]{0:T(1024)S(1)}, bf16[1024,256]{0,1:T(8,128)(2,1)S(1)}, f32[256,256]{1,0:T(8,128)}, bf16[1024,256]{0,1:T(8,128)(2,1)}, ...), branch_computations={%region_9.9_spmd, %region_10.10_spmd} | conditional | flops 269090816 | bytes 2105368 | solution.py:159
  118.5 1.5 convolution_add_fusion
  120.0 2.0 %convolution_add_fusion.1 = f32[256,256]{1,0:T(8,128)} fusion(f32[256,256]{1,0:T(8,128)} %get-tuple-element.74, bf16[1024,256]{0,1:T(8,128)(2,1)S(1)} %get-tuple-element.198, s32[1024]{0:T(1024)S(1)} %get-tuple-element.75), kind=kOutput, calls=%fused_computation.1 | convolution fusion | flops 134545408 | bytes 1052672 | tf_op jit(solution)/shard_map/while/body/eval_jaxpr/cond/branch_1_fun/dot_general | solution.py:132
  126.7 1.3 convolution_convert_fusion
  128.7 12.8 %reduce-scatter.2.cloned.1.call-done = bf16[64,2048]{1,0:T(8,128)(2,1)} async-done(((bf16[128,2048]{1,0:T(8,128)(2,1)}), bf16[64,2048]{1,0:T(8,128)(2,1)}) %reduce-scatter.2.cloned.1.call-update) | async-done | bytes 262160 | tf_op jit(solution)/shard_map/reduce_scatter | solution.py:181
  141.6 1.7 %add_convert_fusion = bf16[64,2048]{1,0:T(8,128)(2,1)} fusion(bf16[64,2048]{1,0:T(8,128)(2,1)} %reduce-scatter.2.cloned.1.call-done, bf16[128,2048]{1,0:T(8,128)(2,1)S(1)} %copy-done.5, s32[]{:T(128)S(6)} %select_n.140), kind=kLoop, calls=%fused_computation.35 | loop fusion | flops 524288 | bytes 786436 | tf_op jit(solution)/shard_map/convert_element_type | solution.py:188
  (108 shorter events, 26.5 us)
Async XLA Ops:
  7.2 119.5 %copy-start = (bf16[512,2048]{1,0:T(8,128)(2,1)S(1)}, bf16[512,2048]{1,0:T(8,128)(2,1)}, u32[]{:S(2)}) copy-start(bf16[512,2048]{1,0:T(8,128)(2,1)} %param.18) | copy-start | bytes 6291460
  7.2 3.9 %copy-start.4 = (bf16[128,2048]{1,0:T(8,128)(2,1)S(1)}, bf16[128,2048]{1,0:T(8,128)(2,1)}, u32[]{:S(2)}) copy-start(bf16[128,2048]{1,0:T(8,128)(2,1)} %param.13) | copy-start | bytes 1572868
  7.2 3.9 %copy-start.11 = (f32[2048]{0:T(1024)S(1)}, f32[2048]{0:T(1024)}, u32[]{:S(2)}) copy-start(f32[2048]{0:T(1024)} %param.14) | copy-start | bytes 24580
  7.2 5.5 %copy-start.13 = (s32[4]{0:T(128)S(1)}, s32[4]{0:T(128)}, u32[]{:S(2)}) copy-start(s32[4]{0:T(128)} %param.19) | copy-start | bytes 52
  7.2 59.5 %all-gather.5.cloned.1.call-start = ((), (), s32[]{:S(2)}) async-start(), calls=%async_computation.2 | async-start | bytes 1114112 | tf_op jit(solution)/shard_map/all_gather | solution.py:144
  8.6 4.4 %copy-start.12 = (s32[16]{0:T(128)S(1)}, s32[16]{0:T(128)}, u32[]{:S(2)}) copy-start(s32[16]{0:T(128)} %param.20) | copy-start | bytes 196
  11.1 80.5 %all-gather.3.cloned.1.call-start = ((), (), s32[]{:S(2)}) async-start(), calls=%async_computation.1 | async-start | bytes 1114112 | tf_op jit(solution)/shard_map/all_gather | solution.py:143
  16.8 124.8 %reduce-scatter.2.cloned.1.call-start = ((), (), s32[]{:S(2)}) async-start(), calls=%async_computation.3 | async-start | bytes 786432 | tf_op jit(solution)/shard_map/reduce_scatter | solution.py:181
  18.2 2.7 %copy-start.6 = (s32[64]{0:T(128)S(1)}, s32[64]{0:T(128)}, u32[]{:S(2)}) copy-start(s32[64]{0:T(128)} %param.21) | copy-start | bytes 772
  102.5 3.5 %copy-start.3 = (bf16[128,2,2,128]{3,0,2,1:T(8,128)(2,1)S(1)}, bf16[128,2,2,128]{3,0,2,1:T(8,128)(2,1)}, u32[]{:S(2)}) copy-start(bf16[128,2,2,128]{3,0,2,1:T(8,128)(2,1)} %get-tuple-element.553) | copy-start | bytes 393220 | tf_op jit(solution)/shard_map/while
  106.0 1.1 copy-start.9
  106.0 1.1 copy-start.1
  106.0 1.1 copy-start.7
  107.1 0.9 copy-start.10
  108.1 0.7 copy-start.8
  118.5 3.5 %copy-start.3 = (bf16[128,2,2,128]{3,0,2,1:T(8,128)(2,1)S(1)}, bf16[128,2,2,128]{3,0,2,1:T(8,128)(2,1)}, u32[]{:S(2)}) copy-start(bf16[128,2,2,128]{3,0,2,1:T(8,128)(2,1)} %get-tuple-element.553) | copy-start | bytes 393220 | tf_op jit(solution)/shard_map/while
  122.0 1.1 copy-start.9
  122.0 1.1 copy-start.1
  122.0 1.1 copy-start.7
  123.1 0.9 copy-start.10
  124.1 0.7 copy-start.8
  124.8 3.2 %copy-start.2 = (f32[256,256]{1,0:T(8,128)S(1)}, f32[256,256]{1,0:T(8,128)}, u32[]{:S(2)}) copy-start(f32[256,256]{1,0:T(8,128)} %get-tuple-element.105) | copy-start | bytes 786436
  126.6 14.9 %copy-start.5 = (bf16[128,2048]{1,0:T(8,128)(2,1)S(1)}, bf16[128,2048]{1,0:T(8,128)(2,1)}, u32[]{:S(2)}) copy-start(bf16[128,2048]{1,0:T(8,128)(2,1)} %param.13) | copy-start | bytes 1572868
Sparse Core Ops, SparseCore 0:
  11.2 40.7 all-gather.4
  54.7 36.8 all-gather.2
  128.1 13.4 reduce-scatter.1
where the time goes:
time: 151 us; the launch traced here: 150 us
  other arithmetic  57.1 us (38%)
  waiting for transfers between devices  37.7 us (25%)
  local copies, waits for them, and re-layouts  21 us (14%)
  matrix products  17.1 us (11%)
  between operations  14 us (9%)
  loops' own time  2.72 us (2%)
    select_n x1, other arithmetic, on_device(): jnp.where(holder == device, slot_ids % slot_count * PAGE_TOKENS + positio...  36.5 us
    all_gather x1, waiting for transfers between devices, on_device(): key_piece = lax.all_gather(key_matrix_rows, 'seq', axis=0, tiled=True)  24.9 us
    reduce_scatter x1, waiting for transfers between devices, on_device(): lax.psum_scatter(jnp.dot(context, w_out, preferred_element_type=jnp.float...  12.8 us
    dynamic_slice x4, local copies, waits for them, and re-layouts, sub_step(): value_block = lax.dynamic_slice_in_dim(value_piece, offset, sub_width, 0)  6.16 us
    gather x2, other arithmetic, on_device(): slot_ids = page_slot[position // PAGE_TOKENS]  5.68 us
    dot_general x2, matrix products, store(): jnp.dot(placer, key_block, preferred_element_type=jnp.float32)  4.02 us
  transfers between devices with their start and end apart: 3, of which 2 were waited for; matrix products, arithmetic and copies ran while one was open for 37% of the time, Pallas kernels for 0%

commit v1 on v0

v1 whole, which is shorter than its diff:
```python
import functools
import math

import jax
import jax.numpy as jnp
import numpy as np
from jax import lax
from jax.experimental import pallas as pl
from jax.experimental.pallas import tpu as pltpu
from jax.sharding import PartitionSpec as P

HEAD = 128
PAGE = 32
THETA = 1000000.0
EPS = 1e-05
MASKED = -1e30
FLOOR = -1e29
WEIGHT_STEPS = 4
VMEM_BYTES = 48 * 1024 * 1024

f32 = jnp.float32
bf16 = jnp.bfloat16


def whole_vmem():
    return pl.BlockSpec(memory_space=pltpu.VMEM)


def whole_smem():
    return pl.BlockSpec(memory_space=pltpu.SMEM)


def anywhere():
    return pl.BlockSpec(memory_space=pl.ANY)


def inverse_frequencies():
    exponent = np.arange(HEAD // 2, dtype=np.float64) * (2.0 / HEAD)
    freq = (THETA**-exponent).astype(np.float32)
    return jnp.asarray(np.concatenate([freq, freq])[None, :])


def first_block(block_ref, shard):
    blocks = block_ref.shape[0]
    first = block_ref[shard]
    return first, 2 * blocks - 1 - first


def prompt_begin(position, len_ref):
    begin = jnp.zeros_like(position)
    start = jnp.int32(0)
    for r in range(len_ref.shape[0] - 1):
        start = start + len_ref[r]
        begin = jnp.where(position >= start, start, begin)
    return begin


def rotary_tables(shard, block_ref, len_ref, freq, rows):
    half = rows // 2
    row = lax.broadcasted_iota(jnp.int32, (rows, HEAD), 0)
    lane = lax.broadcasted_iota(jnp.int32, (rows, HEAD), 1)
    first, second = first_block(block_ref, shard)
    position = jnp.where(row < half, first * half + row, second * half + row - half)
    rel = (position - prompt_begin(position, len_ref)).astype(f32)
    angle = rel * freq
    sine = jnp.sin(angle)
    return jnp.cos(angle), jnp.where(lane < HEAD // 2, -sine, sine)


def rotate(u, cosine, signed_sine):
    return u * cosine + pltpu.roll(u, HEAD // 2, 1) * signed_sine


def weight_copies(refs, scratch, sems):
    copies = []
    depth = scratch.shape[0] // WEIGHT_STEPS
    for step in range(WEIGHT_STEPS):
        group, column = [], 0
        for i, ref in enumerate(refs):
            rows, cols = pl.ds(step * depth, depth), pl.ds(column, ref.shape[1])
            group.append(
                pltpu.make_async_copy(ref.at[rows, :], scratch.at[rows, cols], sems.at[step, i])
            )
            column += ref.shape[1]
        copies.append(group)
    return copies


def stepped_dot(left, copies, scratch):
    depth = scratch.shape[0] // WEIGHT_STEPS
    total = None
    for step in range(WEIGHT_STEPS):
        for copy in copies[step]:
            copy.wait()
        rows = pl.ds(step * depth, depth)
        part = jnp.dot(left[:, step * depth : (step + 1) * depth], scratch[rows, :], preferred_element_type=f32)
        total = part if total is None else total + part
    return total


def key_value_kernel(
    block_ref, len_ref, freq_ref, tok_ref, gain_ref, wk_ref, wv_ref,
    normed_ref, kv_ref, cos_ref, sin_ref, weights, sems,
):
    copies = weight_copies((wk_ref, wv_ref), weights, sems)
    for group in copies:
        for copy in group:
            copy.start()
    rows = tok_ref.shape[0]
    cosine, sine = rotary_tables(lax.axis_index("seq"), block_ref, len_ref, freq_ref[...], rows)
    cos_ref[...] = cosine
    sin_ref[...] = sine
    wide = tok_ref[...].astype(f32)
    scale = lax.rsqrt(jnp.mean(wide * wide, -1, keepdims=True) + EPS)
    normed = (wide * scale * gain_ref[...]).astype(bf16)
    normed_ref[...] = normed
    product = stepped_dot(normed, copies, weights)
    key_width = wk_ref.shape[1]
    for h in range(key_width // HEAD):
        cols = slice(h * HEAD, (h + 1) * HEAD)
        kv_ref[:, cols] = rotate(product[:, cols], cosine, sine).astype(bf16)
    kv_ref[:, key_width:] = product[:, key_width:].astype(bf16)


def query_kernel(normed_ref, cos_ref, sin_ref, wq_ref, q_ref, weights, sems):
    copies = weight_copies((wq_ref,), weights, sems)
    for group in copies:
        for copy in group:
            copy.start()
    cosine, sine = cos_ref[...], sin_ref[...]
    product = stepped_dot(normed_ref[...], copies, weights)
    for h in range(wq_ref.shape[1] // HEAD):
        cols = slice(h * HEAD, (h + 1) * HEAD)
        q_ref[:, cols] = rotate(product[:, cols], cosine, sine).astype(bf16)


def attend_kernel(
    n, chunk, sources, block_ref, len_ref, slot_ref, q_ref, tok_ref, wo_ref, *rest,
):
    counts = [count for count, _ in sources]
    pieces, rest = rest[: len(counts)], rest[len(counts) :]
    send_ref, keep_ref, cache_ref, kv, wo, context, page_of, kv_sem, wo_sem = rest
    shard = lax.axis_index("seq")
    part = lax.axis_index("req")
    rows, q_width = q_ref.shape
    half = rows // 2
    key_width = kv.shape[1] // 2
    kv_heads = key_width // HEAD
    group = q_width // key_width

    for ref, (count, source_of) in zip(pieces, sources):
        for i in range(count):
            for block, at in zip(first_block(block_ref, source_of(shard, i)), (0, half)):
                pltpu.make_async_copy(
                    ref.at[pl.ds(i * rows + at, half), :],
                    kv.at[pl.ds(pl.multiple_of(block * half, half), half), :],
                    kv_sem,
                ).start()
    out_copy = pltpu.make_async_copy(wo_ref, wo, wo_sem)
    out_copy.start()

    slots = cache_ref.shape[0]
    for t in range(slots):
        page_of[t] = -1

    def note_page(p, carry):
        slot = slot_ref[p] - shard * slots

        @pl.when((slot >= 0) & (slot < slots))
        def _():
            page_of[slot] = p

        return carry

    lax.fori_loop(0, slot_ref.shape[0], note_page, 0)
    pltpu.make_async_copy(kv, kv, kv_sem).wait()

    for t in range(slots):
        page = page_of[t]

        @pl.when(page >= 0)
        def _():
            held = kv[pl.ds(pl.multiple_of(page * PAGE, PAGE), PAGE), :]
            cache_ref[t, 0] = held[:, :key_width]
            cache_ref[t, 1] = held[:, key_width:]

        @pl.when(page < 0)
        def _():
            cache_ref[t] = jnp.zeros(cache_ref.shape[1:], bf16)

    scale = math.log2(math.e) / math.sqrt(HEAD)
    for at, block in zip((0, half), first_block(block_ref, shard)):
        row_position = block * half + lax.broadcasted_iota(jnp.int32, (half, 1), 0)
        row_begin = prompt_begin(row_position, len_ref)
        lane = lax.broadcasted_iota(jnp.int32, (group * half, chunk), 1)
        ends = jnp.concatenate([row_position] * group, 0)
        begins = jnp.concatenate([row_begin] * group, 0)
        start = jnp.int32(0)
        lowest = jnp.int32(0)
        for r in range(len_ref.shape[0] - 1):
            start = start + len_ref[r]
            lowest = jnp.where(block * half >= start, start, lowest)
        queries = [
            jnp.concatenate(
                [
                    q_ref[at : at + half, (g * group + j) * HEAD : (g * group + j + 1) * HEAD]
                    for j in range(group)
                ],
                0,
            )
            for g in range(kv_heads)
        ]

        def absorb(c, state):
            offset = pl.multiple_of(c * chunk, chunk)
            visible = (lane >= begins - offset) & (lane <= ends - offset)
            out = []
            for g in range(kv_heads):
                top, total, acc = state[g]
                keys = kv[pl.ds(offset, chunk), g * HEAD : (g + 1) * HEAD]
                values = kv[pl.ds(offset, chunk), key_width + g * HEAD : key_width + (g + 1) * HEAD]
                scores = lax.dot_general(
                    queries[g], keys, (((1,), (1,)), ((), ())), preferred_element_type=f32
                )
                scores = jnp.where(visible, scores * scale, MASKED)
                new_top = jnp.maximum(top, jnp.max(scores, -1, keepdims=True))
                weights = jnp.exp2(scores - new_top)
                factor = jnp.exp2(top - new_top)
                total = total * factor + jnp.sum(weights, -1, keepdims=True)
                acc = acc * factor + jnp.dot(weights.astype(bf16), values, preferred_element_type=f32)
                out.append((new_top, total, acc))
            return tuple(out)

        zero = (
            jnp.full((group * half, 1), FLOOR, f32),
            jnp.zeros((group * half, 1), f32),
            jnp.zeros((group * half, HEAD), f32),
        )
        low = lowest // chunk
        high = (block * half + half + chunk - 1) // chunk
        state = lax.fori_loop(low, high, absorb, (zero,) * kv_heads)
        for g in range(kv_heads):
            _, total, acc = state[g]
            result = (acc / total).astype(bf16)
            for j in range(group):
                h = g * group + j
                context[at : at + half, h * HEAD : (h + 1) * HEAD] = result[j * half : (j + 1) * half]

    out_copy.wait()
    product = jnp.dot(context[...], wo[...], preferred_element_type=f32)
    near, far = product[:half], product[half:]
    tok = tok_ref[pl.ds(pl.multiple_of(part * half, half), half), :].astype(f32)
    mine = jnp.where(part == 0, near, far)
    theirs = jnp.where(part == 0, far, near)
    send_ref[...] = theirs.astype(bf16)
    keep_ref[...] = mine + tok


def gather_shards(kv, n):
    rows = kv.shape[0]
    if n % 4 or n > 16:
        everyone = lax.all_gather(kv, "seq", axis=0, tiled=True)
        return [everyone], [(n, lambda shard, i: i)]
    outer = n // 4

    def moved(shift, flip):
        def source_of(shard, i):
            plane, inner = shard // 4, shard % 4
            if flip & 2:
                inner = jnp.where(inner >= 2, inner - 2, inner + 2)
            if flip & 1:
                inner = inner + 1 - 2 * (inner % 2)
            plane = lax.rem(plane + outer - shift, outer)
            return plane * 4 + inner

        return source_of

    def swap(x, bit):
        return lax.ppermute(x, "seq", [(i, i ^ bit) for i in range(n)])

    arrays, sources = [kv], [(1, moved(0, 0))]
    for shift in range(1, outer):
        perm = [(i, (i + 4 * shift) % n) for i in range(n)]
        arrays.append(lax.ppermute(kv, "seq", perm))
        sources.append((1, moved(shift, 0)))
    for flip in (2, 1):
        held = list(zip(arrays, sources))
        for k, (x, _) in enumerate(held):
            arrays.append(swap(x, flip))
            if flip == 2:
                sources.append((1, moved(k, 2)))
            else:
                sources.append((1, moved(k % outer, 1 + 2 * (k // outer))))
    return arrays, sources


def on_device(
    n, parts, tokens, norm_gain, w_query, key_projection, value_projection, w_out, lengths, block_split, page_slot,
):
    rows, width = tokens.shape
    half = rows // 2
    q_width = w_query.shape[1]
    kv_width = key_projection.shape[1] + value_projection.shape[1]
    params = pltpu.CompilerParams(vmem_limit_bytes=VMEM_BYTES)
    struct = jax.ShapeDtypeStruct
    normed, kv, cosine, sine = pl.pallas_call(
        key_value_kernel,
        out_shape=(
            struct((rows, width), bf16),
            struct((rows, kv_width), bf16),
            struct((rows, HEAD), f32),
            struct((rows, HEAD), f32),
        ),
        in_specs=[whole_smem()] * 2 + [whole_vmem()] * 3 + [anywhere()] * 2,
        out_specs=(whole_vmem(),) * 4,
        scratch_shapes=[
            pltpu.VMEM((width, kv_width), bf16),
            pltpu.SemaphoreType.DMA((WEIGHT_STEPS, 2)),
        ],
        compiler_params=params,
        cost_estimate=pl.CostEstimate(
            flops=2 * rows * width * kv_width, bytes_accessed=2 * width * kv_width, transcendentals=0
        ),
        name="key_value",
    )(
        block_split, lengths, inverse_frequencies(), tokens, norm_gain.reshape(1, width),
        key_projection, value_projection,
    )
    queries = pl.pallas_call(
        query_kernel,
        out_shape=struct((rows, q_width), bf16),
        in_specs=[whole_vmem()] * 3 + [anywhere()],
        out_specs=whole_vmem(),
        scratch_shapes=[
            pltpu.VMEM((width, q_width), bf16),
            pltpu.SemaphoreType.DMA((WEIGHT_STEPS, 1)),
        ],
        compiler_params=params,
        cost_estimate=pl.CostEstimate(
            flops=2 * rows * width * q_width, bytes_accessed=2 * width * q_width, transcendentals=0
        ),
        name="query",
    )(normed, cosine, sine, w_query)
    arrays, sources = gather_shards(kv, n)
    total_rows = n * rows
    chunk = math.gcd(total_rows, 512)
    slots = 2 * rows // PAGE
    sent, kept, cache = pl.pallas_call(
        functools.partial(attend_kernel, n, chunk, sources),
        out_shape=(
            struct((half, width), bf16),
            struct((half, width), f32),
            struct((slots, 2, PAGE, kv_width // 2), bf16),
        ),
        in_specs=[whole_smem()] * 3 + [whole_vmem()] * 2 + [anywhere()] * (1 + len(arrays)),
        out_specs=(whole_vmem(),) * 3,
        scratch_shapes=[
            pltpu.VMEM((total_rows, kv_width), bf16),
            pltpu.VMEM(w_out.shape, bf16),
            pltpu.VMEM((rows, q_width), bf16),
            pltpu.SMEM((slots,), jnp.int32),
            pltpu.SemaphoreType.DMA,
            pltpu.SemaphoreType.DMA,
        ],
        compiler_params=params,
        cost_estimate=pl.CostEstimate(
            flops=4 * rows * total_rows * q_width, bytes_accessed=2 * total_rows * kv_width, transcendentals=0
        ),
        name="attend",
    )(block_split, lengths, page_slot, queries, tokens, w_out, *arrays)
    received = lax.ppermute(sent, "req", [(i, (i + 1) % parts) for i in range(parts)])
    hidden = (kept + received.astype(f32)).astype(bf16)
    return hidden, cache


def solution(mesh):
    in_specs = (
        P("seq", None),
        P(),
        P(None, "req"),
        P(None, "req"),
        P(None, "req"),
        P("req", None),
        P(),
        P(),
        P(),
    )
    out_specs = (P(("seq", "req"), None), P("seq", None, None, "req"))
    body = functools.partial(on_device, mesh.shape["seq"], mesh.shape["req"])
    return jax.shard_map(body, mesh=mesh, in_specs=in_specs, out_specs=out_specs, check_vma=False)
```

time: 151 us -> 53.7 us (0.36)
  other arithmetic: 57.1 us -> 0.75 us
  matrix products: 17.1 us -> 0 us
  waiting for transfers between devices: 37.7 us -> 21.8 us
  local copies, waits for them, and re-layouts: 21 us -> 6.32 us
  between operations: 14 us -> 0.76 us
  starting transfers between devices: 0.12 us -> 12.4 us
  Pallas kernels: 0 us -> 11.3 us
  loops' own time: 2.72 us -> 0 us
    select_n x2 -> x0, other arithmetic: 36.5 us -> none  [the longest x1 36.5 us: on_device(): jnp.where(holder == device, slot_ids % slot_count * PAGE_TOKENS + positio...]
    all_gather x2 -> x0, waiting for transfers between devices: 24.9 us -> none  [the longest x1 24.9 us: on_device(): key_piece = lax.all_gather(key_matrix_rows, 'seq', axis=0, tiled=True)]
    ppermute x0 -> x16, waiting for transfers between devices: none -> 21.8 us  [the longest x3 9.82 us: gather_shards(): arrays.append(lax.ppermute(kv, 'seq', perm))]
    dot_general x12 -> x0, matrix products: 17.1 us -> none  [the longest x2 4.02 us: store(): jnp.dot(placer, key_block, preferred_element_type=jnp.float32)]
    dynamic_slice x13 -> x0, local copies, waits for them, and re-layouts: 13.7 us -> none  [the longest x4 6.16 us: sub_step(): value_block = lax.dynamic_slice_in_dim(value_piece, offset, sub_width, 0)]
    reduce_scatter x1 -> x0, waiting for transfers between devices: 12.8 us -> none  [on_device(): lax.psum_scatter(jnp.dot(context, w_out, preferred_element_type=jnp.float...]
    ppermute x0 -> x16, starting transfers between devices: none -> 12.4 us  [the longest x12 6.16 us: swap(): return lax.ppermute(x, 'seq', [(i, i ^ bit) for i in range(n)])]
    pallas_call x0 -> x3, Pallas kernels: none -> 11.3 us  [the longest x1 8.4 us: on_device(): pl.pallas_call(functools.partial(attend_kernel, n, chunk, sources), out_s...]
  transfers between devices with their start and end apart: 3 -> 16, of which waited for: 2 -> 6; matrix products, arithmetic and copies ran while one was open for 37% -> 0% of each run, Pallas kernels for 0% -> 2%
where the time goes in v1:
time: 53.7 us; the launch traced here: 53.4 us
  waiting for transfers between devices  21.8 us (41%)
  starting transfers between devices  12.4 us (23%)
  Pallas kernels  11.3 us (21%)
  local copies, waits for them, and re-layouts  6.32 us (12%)
  between operations  0.76 us (1%)
  other arithmetic  0.75 us (1%)
    ppermute x3, waiting for transfers between devices, gather_shards(): arrays.append(lax.ppermute(kv, 'seq', perm))  9.82 us
    pallas_call x1, Pallas kernels, on_device(): pl.pallas_call(functools.partial(attend_kernel, n, chunk, sources), out_s...  8.4 us
    unnamed x22, local copies, waits for them, and re-layouts  6.32 us
    ppermute x12, starting transfers between devices, swap(): return lax.ppermute(x, 'seq', [(i, i ^ bit) for i in range(n)])  6.16 us
    ppermute x1, waiting for transfers between devices, on_device(): lax.ppermute(sent, 'req', [(i, (i + 1) % parts) for i in range(parts)])  6.13 us
    ppermute x12, waiting for transfers between devices, swap(): return lax.ppermute(x, 'seq', [(i, i ^ bit) for i in range(n)])  5.87 us
    ppermute x3, starting transfers between devices, gather_shards(): arrays.append(lax.ppermute(kv, 'seq', perm))  4.62 us
    pallas_call x1, Pallas kernels, on_device(): pl.pallas_call(key_value_kernel, out_shape=(struct((rows, width), bf16),...  2.03 us
  transfers between devices with their start and end apart: 16, of which 6 were waited for; matrix products, arithmetic and copies ran while one was open for 0% of the time, Pallas kernels for 2%

profile of v1, /device:TPU:0, one launch (start us, length us, event | category | flops | bytes accessed | tf_op | source)
XLA Modules:
  0.0 53.4 jit_solution(10400454528473628496)
XLA Ops:
  0.7 1.2 %copy-done.2 = bf16[128,2048]{1,0:T(8,128)(2,1)S(1)} copy-done((bf16[128,2048]{1,0:T(8,128)(2,1)S(1)}, bf16[128,2048]{1,0:T(8,128)(2,1)}, u32[]{:S(2)}) %copy-start.2) | copy-done | bytes 524312
  1.8 1.2 %copy-done.4 = bf16[2048,256]{1,0:T(8,128)(2,1)S(1)} copy-done((bf16[2048,256]{1,0:T(8,128)(2,1)S(1)}, bf16[2048,256]{1,0:T(8,128)(2,1)}, u32[]{:S(2)}) %copy-start.4) | copy-done | bytes 1048600
  3.1 1.2 %copy-done.5 = bf16[2048,256]{1,0:T(8,128)(2,1)S(1)} copy-done((bf16[2048,256]{1,0:T(8,128)(2,1)S(1)}, bf16[2048,256]{1,0:T(8,128)(2,1)}, u32[]{:S(2)}) %copy-start.5) | copy-done | bytes 1048600
  4.3 0.7 %copy-done.6 = f32[2048]{0:T(1024)S(1)} copy-done((f32[2048]{0:T(1024)S(1)}, f32[2048]{0:T(1024)}, u32[]{:S(2)}) %copy-start.6) | copy-done | bytes 8216
  5.0 0.7 %copy-done.7 = s32[16]{0:T(128)S(1)} copy-done((s32[16]{0:T(128)S(1)}, s32[16]{0:T(128)}, u32[]{:S(2)}) %copy-start.7) | copy-done | bytes 88
  5.6 0.7 %copy-done.8 = s32[4]{0:T(128)S(1)} copy-done((s32[4]{0:T(128)S(1)}, s32[4]{0:T(128)}, u32[]{:S(2)}) %copy-start.8) | copy-done | bytes 40
  6.3 0.7 %copy-done.10 = f32[1,128]{1,0:T(1,128)S(1)} copy-done((f32[1,128]{1,0:T(1,128)S(1)}, f32[1,128]{1,0:T(1,128)}, u32[]{:S(2)}) %copy-start.10) | copy-done | bytes 536
  7.0 2.0 %key_value.1 = (bf16[128,2048]{1,0:T(8,128)(2,1)S(1)}, bf16[128,512]{1,0:T(8,128)(2,1)S(1)}, f32[128,128]{1,0:T(8,128)S(1)}, f32[128,128]{1,0:T(8,128)S(1)}) custom-call(s32[16]{0:T(128)S(1)} %copy-done.7, s32[4]{0:T(128)S(1)} %copy-done.8, f32[1,128]{1,0:T(1,128)S(1)} %copy-done.10, bf16[128,2048]{1,0:T(8,128)(2,1)S(1)} %copy-done.2, ...), custom_call_target="tpu_custom_call" | custom-call | flops 268435456 | bytes 2097152 | tf_op jit(solution)/shard_map/key_value/pallas_call | solution.py:306
  9.0 3.0 %collective-permute-start.3 = (bf16[128,512]{1,0:T(8,128)(2,1)S(1)}, bf16[128,512]{1,0:T(8,128)(2,1)S(1)}, u32[]{:S(2)}, u32[]{:S(2)}) collective-permute-start(bf16[128,512]{1,0:T(8,128)(2,1)S(1)} %get-tuple-element.12.rest_0_), channel_id=1, source_target_pairs={{0,4},{2,6},{4,0},{6,2},{8,12},{10,14},{12,8},{14,10},{16,20},{18,... | collective-permute-start | bytes 393224 | tf_op jit(solution)/shard_map/ppermute | solution.py:279
  12.0 3.6 %collective-permute-start.2 = (bf16[128,512]{1,0:T(8,128)(2,1)S(1)}, bf16[128,512]{1,0:T(8,128)(2,1)S(1)}, u32[]{:S(2)}, u32[]{:S(2)}) collective-permute-start(bf16[128,512]{1,0:T(8,128)(2,1)S(1)} %get-tuple-element.12.rest_0_), channel_id=1, source_target_pairs={{0,24},{2,26},{4,28},{6,30},{8,0},{10,2},{12,4},{14,6},{16,8},{18,... | collective-permute-start | bytes 393224 | tf_op jit(solution)/shard_map/ppermute | solution.py:284
  15.6 1.0 %collective-permute-start = (bf16[128,512]{1,0:T(8,128)(2,1)S(1)}, bf16[128,512]{1,0:T(8,128)(2,1)S(1)}, u32[]{:S(2)}, u32[]{:S(2)}) collective-permute-start(bf16[128,512]{1,0:T(8,128)(2,1)S(1)} %get-tuple-element.12.rest_0_), channel_id=1, source_target_pairs={{0,8},{2,10},{4,12},{6,14},{8,16},{10,18},{12,20},{14,22},{16,24},... | collective-permute-start | bytes 393224 | tf_op jit(solution)/shard_map/ppermute | solution.py:284
  16.7 3.0 %collective-permute-done.2.rest_3_ = bf16[128,512]{1,0:T(8,128)(2,1)S(1)} collective-permute-done((bf16[128,512]{1,0:T(8,128)(2,1)S(1)}, bf16[128,512]{1,0:T(8,128)(2,1)S(1)}, u32[]{:S(2)}, u32[]{:S(2)}) %collective-permute-start.2) | collective-permute-done | bytes 131104 | tf_op jit(solution)/shard_map/ppermute | solution.py:284
  19.6 0.5 %collective-permute-start.6 = (bf16[128,512]{1,0:T(8,128)(2,1)S(1)}, bf16[128,512]{1,0:T(8,128)(2,1)S(1)}, u32[]{:S(2)}, u32[]{:S(2)}) collective-permute-start(bf16[128,512]{1,0:T(8,128)(2,1)S(1)} %collective-permute-done.2.rest_3_), channel_id=1, source_target_pairs={{0,4},{2,6},{4,0},{6,2},{8,12},{10,14},{12,8},{14,10},{16,20},{18,... | collective-permute-start | bytes 393224 | tf_op jit(solution)/shard_map/ppermute | solution.py:279
  20.2 6.9 %collective-permute-done.1.rest_2_ = bf16[128,512]{1,0:T(8,128)(2,1)S(1)} collective-permute-done((bf16[128,512]{1,0:T(8,128)(2,1)S(1)}, bf16[128,512]{1,0:T(8,128)(2,1)S(1)}, u32[]{:S(2)}, u32[]{:S(2)}) %collective-permute-start.1) | collective-permute-done | bytes 131104 | tf_op jit(solution)/shard_map/ppermute | solution.py:284
  27.0 0.5 %collective-permute-start.5 = (bf16[128,512]{1,0:T(8,128)(2,1)S(1)}, bf16[128,512]{1,0:T(8,128)(2,1)S(1)}, u32[]{:S(2)}, u32[]{:S(2)}) collective-permute-start(bf16[128,512]{1,0:T(8,128)(2,1)S(1)} %collective-permute-done.1.rest_2_), channel_id=1, source_target_pairs={{0,4},{2,6},{4,0},{6,2},{8,12},{10,14},{12,8},{14,10},{16,20},{18,... | collective-permute-start | bytes 393224 | tf_op jit(solution)/shard_map/ppermute | solution.py:279
  27.6 1.5 %collective-permute-start.4 = (bf16[128,512]{1,0:T(8,128)(2,1)S(1)}, bf16[128,512]{1,0:T(8,128)(2,1)S(1)}, u32[]{:S(2)}, u32[]{:S(2)}) collective-permute-start(bf16[128,512]{1,0:T(8,128)(2,1)S(1)} %collective-permute-done.rest_1_), channel_id=1, source_target_pairs={{0,4},{2,6},{4,0},{6,2},{8,12},{10,14},{12,8},{14,10},{16,20},{18,... | collective-permute-start | bytes 393224 | tf_op jit(solution)/shard_map/ppermute | solution.py:279
  29.1 0.5 collective-permute-start.8
  29.6 3.8 %collective-permute-done.5.rest_6_ = bf16[128,512]{1,0:T(8,128)(2,1)S(1)} collective-permute-done((bf16[128,512]{1,0:T(8,128)(2,1)S(1)}, bf16[128,512]{1,0:T(8,128)(2,1)S(1)}, u32[]{:S(2)}, u32[]{:S(2)}) %collective-permute-start.5) | collective-permute-done | bytes 131104 | tf_op jit(solution)/shard_map/ppermute | solution.py:279
  33.4 1.7 %collective-permute-done.4.rest_5_ = bf16[128,512]{1,0:T(8,128)(2,1)S(1)} collective-permute-done((bf16[128,512]{1,0:T(8,128)(2,1)S(1)}, bf16[128,512]{1,0:T(8,128)(2,1)S(1)}, u32[]{:S(2)}, u32[]{:S(2)}) %collective-permute-start.4) | collective-permute-done | bytes 131104 | tf_op jit(solution)/shard_map/ppermute | solution.py:279
  35.1 0.9 %query.1.q_ref = bf16[128,512]{1,0:T(8,128)(2,1)S(1)} custom-call(bf16[128,2048]{1,0:T(8,128)(2,1)S(1)} %get-tuple-element.9.normed_ref, f32[128,128]{1,0:T(8,128)S(1)} %get-tuple-element.10.cos_ref, f32[128,128]{1,0:T(8,128)S(1)} %get-tuple-element.11.sin_ref, bf16[2048,512]{1,0:T(8,128)(2,1)S(1)} %copy-done), custom_call_target="tpu_custom_call" | custom-call | flops 268435456 | bytes 2097152 | tf_op jit(solution)/shard_map/query/pallas_call | solution.py:329
  36.5 8.4 %attend.1 = (bf16[64,2048]{1,0:T(8,128)(2,1)S(1)}, f32[64,2048]{1,0:T(8,128)S(1)}, bf16[8,2,32,256]{3,2,1,0:T(8,128)(2,1)}) custom-call(s32[16]{0:T(128)S(1)} %copy-done.7, s32[4]{0:T(128)S(1)} %copy-done.8, s32[64]{0:T(128)S(1)} %copy-done.9, bf16[128,512]{1,0:T(8,128)(2,1)S(1)} %query.1.q_ref, bf16[128,2048]{1,0:T(8,128)(2,1)S(1)} %copy-done.3, ...), custom_call_target="tpu_custom_call" | custom-call | flops 536870912 | bytes 2097152 | tf_op jit(solution)/shard_map/attend/pallas_call | solution.py:348
  44.9 1.6 %collective-permute-start.15 = (bf16[64,2048]{1,0:T(8,128)(2,1)S(1)}, bf16[64,2048]{1,0:T(8,128)(2,1)S(1)}, u32[]{:S(2)}, u32[]{:S(2)}) collective-permute-start(bf16[64,2048]{1,0:T(8,128)(2,1)S(1)} %get-tuple-element.14), channel_id=1, source_target_pairs={{0,1},{1,0},{2,3},{3,2},{4,5},{5,4},{6,7},{7,6},{8,9},{9,8},{10,11... | collective-permute-start | bytes 786440 | tf_op jit(solution)/shard_map/ppermute | solution.py:371
  46.5 6.1 %collective-permute-done.15 = bf16[64,2048]{1,0:T(8,128)(2,1)S(1)} collective-permute-done((bf16[64,2048]{1,0:T(8,128)(2,1)S(1)}, bf16[64,2048]{1,0:T(8,128)(2,1)S(1)}, u32[]{:S(2)}, u32[]{:S(2)}) %collective-permute-start.15) | collective-permute-done | bytes 262176 | tf_op jit(solution)/shard_map/ppermute | solution.py:371
  52.6 0.8 %add_convert_fusion = bf16[64,2048]{1,0:T(8,128)(2,1)} fusion(f32[64,2048]{1,0:T(8,128)S(1)} %get-tuple-element.13, bf16[64,2048]{1,0:T(8,128)(2,1)S(1)} %collective-permute-done.15), kind=kLoop, calls=%fused_computation | loop fusion | flops 393216 | bytes 1048576 | tf_op jit(solution)/shard_map/convert_element_type | solution.py:372
  (34 shorter events, 0.5 us)
Async XLA Ops:
  0.6 34.5 %copy-start = (bf16[2048,512]{1,0:T(8,128)(2,1)S(1)}, bf16[2048,512]{1,0:T(8,128)(2,1)}, u32[]{:S(2)}) copy-start(bf16[2048,512]{1,0:T(8,128)(2,1)} %wq_ref.1) | copy-start | bytes 6291460
  0.6 1.2 %copy-start.2 = (bf16[128,2048]{1,0:T(8,128)(2,1)S(1)}, bf16[128,2048]{1,0:T(8,128)(2,1)}, u32[]{:S(2)}) copy-start(bf16[128,2048]{1,0:T(8,128)(2,1)} %tok_ref.3) | copy-start | bytes 1572868
  1.8 1.2 %copy-start.4 = (bf16[2048,256]{1,0:T(8,128)(2,1)S(1)}, bf16[2048,256]{1,0:T(8,128)(2,1)}, u32[]{:S(2)}) copy-start(bf16[2048,256]{1,0:T(8,128)(2,1)} %wk_ref.1) | copy-start | bytes 3145732
  3.1 1.2 %copy-start.5 = (bf16[2048,256]{1,0:T(8,128)(2,1)S(1)}, bf16[2048,256]{1,0:T(8,128)(2,1)}, u32[]{:S(2)}) copy-start(bf16[2048,256]{1,0:T(8,128)(2,1)} %wv_ref.1) | copy-start | bytes 3145732
  4.3 0.7 %copy-start.6 = (f32[2048]{0:T(1024)S(1)}, f32[2048]{0:T(1024)}, u32[]{:S(2)}) copy-start(f32[2048]{0:T(1024)} %param.11) | copy-start | bytes 24580
  9.0 27.5 %copy-start.1 = (bf16[512,2048]{1,0:T(8,128)(2,1)S(1)}, bf16[512,2048]{1,0:T(8,128)(2,1)}, u32[]{:S(2)}) copy-start(bf16[512,2048]{1,0:T(8,128)(2,1)} %wo_ref.1) | copy-start | bytes 6291460
  9.0 27.5 %copy-start.3 = (bf16[128,2048]{1,0:T(8,128)(2,1)S(1)}, bf16[128,2048]{1,0:T(8,128)(2,1)}, u32[]{:S(2)}) copy-start(bf16[128,2048]{1,0:T(8,128)(2,1)} %tok_ref.3) | copy-start | bytes 1572868
  9.0 27.5 %copy-start.9 = (s32[64]{0:T(128)S(1)}, s32[64]{0:T(128)}, u32[]{:S(2)}) copy-start(s32[64]{0:T(128)} %slot_ref.1) | copy-start | bytes 772
  9.0 7.6 %collective-permute-start.3 = (bf16[128,512]{1,0:T(8,128)(2,1)S(1)}, bf16[128,512]{1,0:T(8,128)(2,1)S(1)}, u32[]{:S(2)}, u32[]{:S(2)}) collective-permute-start(bf16[128,512]{1,0:T(8,128)(2,1)S(1)} %get-tuple-element.12.rest_0_), channel_id=1, source_target_pairs={{0,4},{2,6},{4,0},{6,2},{8,12},{10,14},{12,8},{14,10},{16,20},{18,... | collective-permute-start | bytes 393224 | tf_op jit(solution)/shard_map/ppermute | solution.py:279
  12.0 7.6 %collective-permute-start.2 = (bf16[128,512]{1,0:T(8,128)(2,1)S(1)}, bf16[128,512]{1,0:T(8,128)(2,1)S(1)}, u32[]{:S(2)}, u32[]{:S(2)}) collective-permute-start(bf16[128,512]{1,0:T(8,128)(2,1)S(1)} %get-tuple-element.12.rest_0_), channel_id=1, source_target_pairs={{0,24},{2,26},{4,28},{6,30},{8,0},{10,2},{12,4},{14,6},{16,8},{18,... | collective-permute-start | bytes 393224 | tf_op jit(solution)/shard_map/ppermute | solution.py:284
  15.6 4.0 %collective-permute-start.7 = (bf16[128,512]{1,0:T(8,128)(2,1)S(1)}, bf16[128,512]{1,0:T(8,128)(2,1)S(1)}, u32[]{:S(2)}, u32[]{:S(2)}) collective-permute-start(bf16[128,512]{1,0:T(8,128)(2,1)S(1)} %get-tuple-element.12.rest_0_), channel_id=1, source_target_pairs={{0,2},{2,0},{4,6},{6,4},{8,10},{10,8},{12,14},{14,12},{16,18},{18,... | collective-permute-start | bytes 393224 | tf_op jit(solution)/shard_map/ppermute | solution.py:279
  15.6 11.4 %collective-permute-start.1 = (bf16[128,512]{1,0:T(8,128)(2,1)S(1)}, bf16[128,512]{1,0:T(8,128)(2,1)S(1)}, u32[]{:S(2)}, u32[]{:S(2)}) collective-permute-start(bf16[128,512]{1,0:T(8,128)(2,1)S(1)} %get-tuple-element.12.rest_0_), channel_id=1, source_target_pairs={{0,16},{2,18},{4,20},{6,22},{8,24},{10,26},{12,28},{14,30},{16,0},... | collective-permute-start | bytes 393224 | tf_op jit(solution)/shard_map/ppermute | solution.py:284
  15.6 11.9 %collective-permute-start = (bf16[128,512]{1,0:T(8,128)(2,1)S(1)}, bf16[128,512]{1,0:T(8,128)(2,1)S(1)}, u32[]{:S(2)}, u32[]{:S(2)}) collective-permute-start(bf16[128,512]{1,0:T(8,128)(2,1)S(1)} %get-tuple-element.12.rest_0_), channel_id=1, source_target_pairs={{0,8},{2,10},{4,12},{6,14},{8,16},{10,18},{12,20},{14,22},{16,24},... | collective-permute-start | bytes 393224 | tf_op jit(solution)/shard_map/ppermute | solution.py:284
  16.7 12.4 %collective-permute-start.11 = (bf16[128,512]{1,0:T(8,128)(2,1)S(1)}, bf16[128,512]{1,0:T(8,128)(2,1)S(1)}, u32[]{:S(2)}, u32[]{:S(2)}) collective-permute-start(bf16[128,512]{1,0:T(8,128)(2,1)S(1)} %collective-permute-done.3.rest_4_), channel_id=1, source_target_pairs={{0,2},{2,0},{4,6},{6,4},{8,10},{10,8},{12,14},{14,12},{16,18},{18,... | collective-permute-start | bytes 393224 | tf_op jit(solution)/shard_map/ppermute | solution.py:279
  19.6 9.4 %collective-permute-start.10 = (bf16[128,512]{1,0:T(8,128)(2,1)S(1)}, bf16[128,512]{1,0:T(8,128)(2,1)S(1)}, u32[]{:S(2)}, u32[]{:S(2)}) collective-permute-start(bf16[128,512]{1,0:T(8,128)(2,1)S(1)} %collective-permute-done.2.rest_3_), channel_id=1, source_target_pairs={{0,2},{2,0},{4,6},{6,4},{8,10},{10,8},{12,14},{14,12},{16,18},{18,... | collective-permute-start | bytes 393224 | tf_op jit(solution)/shard_map/ppermute | solution.py:279
  19.6 9.9 %collective-permute-start.6 = (bf16[128,512]{1,0:T(8,128)(2,1)S(1)}, bf16[128,512]{1,0:T(8,128)(2,1)S(1)}, u32[]{:S(2)}, u32[]{:S(2)}) collective-permute-start(bf16[128,512]{1,0:T(8,128)(2,1)S(1)} %collective-permute-done.2.rest_3_), channel_id=1, source_target_pairs={{0,4},{2,6},{4,0},{6,2},{8,12},{10,14},{12,8},{14,10},{16,20},{18,... | collective-permute-start | bytes 393224 | tf_op jit(solution)/shard_map/ppermute | solution.py:279
  27.0 6.4 %collective-permute-start.5 = (bf16[128,512]{1,0:T(8,128)(2,1)S(1)}, bf16[128,512]{1,0:T(8,128)(2,1)S(1)}, u32[]{:S(2)}, u32[]{:S(2)}) collective-permute-start(bf16[128,512]{1,0:T(8,128)(2,1)S(1)} %collective-permute-done.1.rest_2_), channel_id=1, source_target_pairs={{0,4},{2,6},{4,0},{6,2},{8,12},{10,14},{12,8},{14,10},{16,20},{18,... | collective-permute-start | bytes 393224 | tf_op jit(solution)/shard_map/ppermute | solution.py:279
  27.6 7.6 %collective-permute-start.4 = (bf16[128,512]{1,0:T(8,128)(2,1)S(1)}, bf16[128,512]{1,0:T(8,128)(2,1)S(1)}, u32[]{:S(2)}, u32[]{:S(2)}) collective-permute-start(bf16[128,512]{1,0:T(8,128)(2,1)S(1)} %collective-permute-done.rest_1_), channel_id=1, source_target_pairs={{0,4},{2,6},{4,0},{6,2},{8,12},{10,14},{12,8},{14,10},{16,20},{18,... | collective-permute-start | bytes 393224 | tf_op jit(solution)/shard_map/ppermute | solution.py:279
  29.1 7.0 %collective-permute-start.9 = (bf16[128,512]{1,0:T(8,128)(2,1)S(1)}, bf16[128,512]{1,0:T(8,128)(2,1)S(1)}, u32[]{:S(2)}, u32[]{:S(2)}) collective-permute-start(bf16[128,512]{1,0:T(8,128)(2,1)S(1)} %collective-permute-done.1.rest_2_), channel_id=1, source_target_pairs={{0,2},{2,0},{4,6},{6,4},{8,10},{10,8},{12,14},{14,12},{16,18},{18,... | collective-permute-start | bytes 393224 | tf_op jit(solution)/shard_map/ppermute | solution.py:279
  29.1 7.0 %collective-permute-start.8 = (bf16[128,512]{1,0:T(8,128)(2,1)S(1)}, bf16[128,512]{1,0:T(8,128)(2,1)S(1)}, u32[]{:S(2)}, u32[]{:S(2)}) collective-permute-start(bf16[128,512]{1,0:T(8,128)(2,1)S(1)} %collective-permute-done.rest_1_), channel_id=1, source_target_pairs={{0,2},{2,0},{4,6},{6,4},{8,10},{10,8},{12,14},{14,12},{16,18},{18,... | collective-permute-start | bytes 393224 | tf_op jit(solution)/shard_map/ppermute | solution.py:279
  29.6 6.5 %collective-permute-start.14 = (bf16[128,512]{1,0:T(8,128)(2,1)S(1)}, bf16[128,512]{1,0:T(8,128)(2,1)S(1)}, u32[]{:S(2)}, u32[]{:S(2)}) collective-permute-start(bf16[128,512]{1,0:T(8,128)(2,1)S(1)} %collective-permute-done.6.rest_7_), channel_id=1, source_target_pairs={{0,2},{2,0},{4,6},{6,4},{8,10},{10,8},{12,14},{14,12},{16,18},{18,... | collective-permute-start | bytes 393224 | tf_op jit(solution)/shard_map/ppermute | solution.py:279
  33.4 2.7 %collective-permute-start.13 = (bf16[128,512]{1,0:T(8,128)(2,1)S(1)}, bf16[128,512]{1,0:T(8,128)(2,1)S(1)}, u32[]{:S(2)}, u32[]{:S(2)}) collective-permute-start(bf16[128,512]{1,0:T(8,128)(2,1)S(1)} %collective-permute-done.5.rest_6_), channel_id=1, source_target_pairs={{0,2},{2,0},{4,6},{6,4},{8,10},{10,8},{12,14},{14,12},{16,18},{18,... | collective-permute-start | bytes 393224 | tf_op jit(solution)/shard_map/ppermute | solution.py:279
  35.1 1.3 %collective-permute-start.12 = (bf16[128,512]{1,0:T(8,128)(2,1)S(1)}, bf16[128,512]{1,0:T(8,128)(2,1)S(1)}, u32[]{:S(2)}, u32[]{:S(2)}) collective-permute-start(bf16[128,512]{1,0:T(8,128)(2,1)S(1)} %collective-permute-done.4.rest_5_), channel_id=1, source_target_pairs={{0,2},{2,0},{4,6},{6,4},{8,10},{10,8},{12,14},{14,12},{16,18},{18,... | collective-permute-start | bytes 393224 | tf_op jit(solution)/shard_map/ppermute | solution.py:279
  44.9 7.7 %collective-permute-start.15 = (bf16[64,2048]{1,0:T(8,128)(2,1)S(1)}, bf16[64,2048]{1,0:T(8,128)(2,1)S(1)}, u32[]{:S(2)}, u32[]{:S(2)}) collective-permute-start(bf16[64,2048]{1,0:T(8,128)(2,1)S(1)} %get-tuple-element.14), channel_id=1, source_target_pairs={{0,1},{1,0},{2,3},{3,2},{4,5},{5,4},{6,7},{7,6},{8,9},{9,8},{10,11... | collective-permute-start | bytes 786440 | tf_op jit(solution)/shard_map/ppermute | solution.py:371
  (3 other events, 2.0 us)

commit v2 on v1

v2 whole, which is shorter than its diff:
```python
import functools
import math

import jax
import jax.numpy as jnp
import numpy as np
from jax import lax
from jax.experimental import pallas as pl
from jax.experimental.pallas import tpu as pltpu
from jax.sharding import PartitionSpec as P

HEAD = 128
PAGE = 32
THETA = 1000000.0
EPS = 1e-05
MASKED = -1e30
FLOOR = -1e29
WEIGHT_STEPS = 4
MIB = 1024 * 1024
SCALE = math.log2(math.e) / math.sqrt(HEAD)

f32 = jnp.float32
bf16 = jnp.bfloat16
struct = jax.ShapeDtypeStruct


def in_vmem(count):
    return [pl.BlockSpec(memory_space=pltpu.VMEM)] * count


def in_smem(count):
    return [pl.BlockSpec(memory_space=pltpu.SMEM)] * count


def in_hbm(count):
    return [pl.BlockSpec(memory_space=pltpu.HBM)] * count


def kernel_params(mib):
    return pltpu.CompilerParams(vmem_limit_bytes=mib * MIB)


def cost(flops, moved):
    return pl.CostEstimate(flops=flops, bytes_accessed=moved, transcendentals=0)


def inverse_frequencies():
    exponent = np.arange(HEAD // 2, dtype=np.float64) * (2.0 / HEAD)
    freq = (THETA**-exponent).astype(np.float32)
    return jnp.asarray(np.concatenate([freq, freq])[None, :])


def blocks_of(block_ref, shard):
    first = block_ref[shard]
    return first, 2 * block_ref.shape[0] - 1 - first


def prompt_begin(position, len_ref):
    begin = jnp.zeros_like(position)
    start = jnp.int32(0)
    for r in range(len_ref.shape[0] - 1):
        start = start + len_ref[r]
        begin = jnp.where(position >= start, start, begin)
    return begin


def positions(block_ref, shards, rows, dim, shape):
    half = rows // 2
    index = lax.broadcasted_iota(jnp.int32, shape, dim)
    blocks = [block for shard in shards for block in blocks_of(block_ref, shard)]
    offset = blocks[0] * half
    for i, block in enumerate(blocks[1:], 1):
        offset = jnp.where(index >= i * half, (block - i) * half, offset)
    return index + offset


def rotate(u, cosine, signed_sine):
    return u * cosine + pltpu.roll(u, HEAD // 2, 1) * signed_sine


def weight_copies(refs, scratch, sems):
    copies = []
    depth = scratch.shape[0] // WEIGHT_STEPS
    for step in range(WEIGHT_STEPS):
        group, column = [], 0
        for i, ref in enumerate(refs):
            rows, cols = pl.ds(step * depth, depth), pl.ds(column, ref.shape[1])
            group.append(
                pltpu.make_async_copy(ref.at[rows, :], scratch.at[rows, cols], sems.at[step, i])
            )
            column += ref.shape[1]
        copies.append(group)
    return copies


def start_all(copies):
    for group in copies:
        for copy in group:
            copy.start()


def stepped_dot(left, copies, scratch):
    depth = scratch.shape[0] // WEIGHT_STEPS
    total = None
    for step in range(WEIGHT_STEPS):
        for copy in copies[step]:
            copy.wait()
        rows = slice(step * depth, (step + 1) * depth)
        part = jnp.dot(left[:, rows], scratch[rows, :], preferred_element_type=f32)
        total = part if total is None else total + part
    return total


def key_value_kernel(
    block_hbm, len_hbm, freq_hbm, tok_hbm, gain_hbm, wk_ref, wv_ref,
    normed_ref, kv_ref, cos_ref, sin_ref,
    block_ref, len_ref, freq_ref, tok_ref, gain_ref, weights, small_sems, sems,
):
    small = [
        pltpu.make_async_copy(source, target, small_sems.at[i])
        for i, (source, target) in enumerate(
            (
                (block_hbm, block_ref),
                (len_hbm, len_ref),
                (freq_hbm, freq_ref),
                (tok_hbm, tok_ref),
                (gain_hbm, gain_ref),
            )
        )
    ]
    copies = weight_copies((wk_ref, wv_ref), weights, sems)
    for copy in small:
        copy.start()
    start_all(copies)
    rows = tok_ref.shape[0]
    for copy in small[:3]:
        copy.wait()
    position = positions(block_ref, [lax.axis_index("seq")], rows, 0, (rows, HEAD))
    angle = (position - prompt_begin(position, len_ref)).astype(f32) * freq_ref[...]
    cosine, sine = jnp.cos(angle), jnp.sin(angle)
    lane = lax.broadcasted_iota(jnp.int32, (rows, HEAD), 1)
    sine = jnp.where(lane < HEAD // 2, -sine, sine)
    cos_ref[...] = cosine
    sin_ref[...] = sine
    for copy in small[3:]:
        copy.wait()
    wide = tok_ref[...].astype(f32)
    scale = lax.rsqrt(jnp.mean(wide * wide, -1, keepdims=True) + EPS)
    normed = (wide * scale * gain_ref[...]).astype(bf16)
    normed_ref[...] = normed
    product = stepped_dot(normed, copies, weights)
    key_width = wk_ref.shape[1]
    for h in range(key_width // HEAD):
        cols = slice(h * HEAD, (h + 1) * HEAD)
        kv_ref[:, cols] = rotate(product[:, cols], cosine, sine).astype(bf16)
    kv_ref[:, key_width:] = product[:, key_width:].astype(bf16)


def query_kernel(normed_ref, cos_ref, sin_ref, wq_ref, q_ref, weights, sems):
    copies = weight_copies((wq_ref,), weights, sems)
    start_all(copies)
    cosine, sine = cos_ref[...], sin_ref[...]
    product = stepped_dot(normed_ref[...], copies, weights)
    for h in range(wq_ref.shape[1] // HEAD):
        cols = slice(h * HEAD, (h + 1) * HEAD)
        q_ref[:, cols] = rotate(product[:, cols], cosine, sine).astype(bf16)


def attend_kernel(sources, first, last, block_ref, len_ref, q_ref, far_ref, *refs):
    pieces, refs = refs[: len(sources)], refs[len(sources) :]
    shard = lax.axis_index("seq")
    rows, q_width = q_ref.shape
    key_width = pieces[0].shape[1] // 2
    kv_heads = key_width // HEAD
    group = q_width // key_width
    both = 2 * rows
    q_pos = positions(block_ref, [shard, shard ^ 1], rows, 0, (both, 1))
    q_begin = prompt_begin(q_pos, len_ref)
    queries = [
        jnp.concatenate(
            [
                ref[:, h * HEAD : (h + 1) * HEAD]
                for h in range(g * group, (g + 1) * group)
                for ref in (q_ref, far_ref)
            ],
            0,
        )
        for g in range(kv_heads)
    ]

    def absorb(state, blocks, shards):
        width = rows * len(blocks)
        key_pos = positions(block_ref, shards, rows, 1, (1, width))
        bias = jnp.where((key_pos >= q_begin) & (key_pos <= q_pos), 0.0, MASKED)
        bias = jnp.concatenate([bias] * group, 0)
        out = []
        for g in range(kv_heads):
            top, total, acc = state[g]
            keys = jnp.concatenate([b[:, g * HEAD : (g + 1) * HEAD] for b in blocks], 0)
            values = jnp.concatenate(
                [b[:, key_width + g * HEAD : key_width + (g + 1) * HEAD] for b in blocks], 0
            )
            scores = lax.dot_general(
                queries[g], keys, (((1,), (1,)), ((), ())), preferred_element_type=f32
            )
            scores = scores * SCALE + bias
            new_top = jnp.maximum(top, jnp.max(scores, -1, keepdims=True))
            weights = jnp.exp2(scores - new_top)
            factor = jnp.exp2(top - new_top)
            total = total * factor + jnp.sum(weights, -1, keepdims=True)
            acc = acc * factor + jnp.dot(weights.astype(bf16), values, preferred_element_type=f32)
            out.append((new_top, total, acc))
        return tuple(out)

    if first:
        state = (
            (
                jnp.full((group * both, 1), FLOOR, f32),
                jnp.zeros((group * both, 1), f32),
                jnp.zeros((group * both, HEAD), f32),
            ),
        ) * kv_heads
    else:
        (top_ref, total_ref, acc_ref), refs = refs[:3], refs[3:]
        state = tuple(
            (top_ref[g][:, :1], total_ref[g][:, :1], acc_ref[g]) for g in range(kv_heads)
        )
    if all(count == 1 for count, _ in sources):
        for i in range(0, len(sources), 2):
            span = range(i, min(i + 2, len(sources)))
            state = absorb(
                state, [pieces[k][...] for k in span], [sources[k][1](shard, 0) for k in span]
            )
    else:
        for ref, (count, source_of) in zip(pieces, sources):

            def step(i, carried):
                at = pl.multiple_of(i * rows, rows)
                return absorb(carried, [ref[pl.ds(at, rows), :]], [source_of(shard, i)])

            state = lax.fori_loop(0, count, step, state)

    if not last:
        top_ref, total_ref, acc_ref = refs
        for g in range(kv_heads):
            top, total, acc = state[g]
            top_ref[g] = jnp.broadcast_to(top, acc.shape)
            total_ref[g] = jnp.broadcast_to(total, acc.shape)
            acc_ref[g] = acc
        return
    mine_ref, log_ref, packed_ref = refs
    lane = lax.broadcasted_iota(jnp.int32, (rows, HEAD), 1)
    logs = jnp.zeros((rows, HEAD), f32)
    parts = jnp.zeros((rows, HEAD), f32)
    for g in range(kv_heads):
        top, total, acc = state[g]
        some = total > 0.0
        safe = jnp.where(some, total, 1.0)
        result = acc / safe
        log_sum = jnp.where(some, top + jnp.log(safe) * math.log2(math.e), FLOOR)
        for j in range(group):
            h = g * group + j
            cols = slice(h * HEAD, (h + 1) * HEAD)
            near = slice(j * both, j * both + rows)
            far = slice(j * both + rows, (j + 1) * both)
            mine_ref[:, cols] = result[near]
            packed_ref[:, cols] = result[far].astype(bf16)
            logs = jnp.where(lane == h, log_sum[near], logs)
            left = log_sum[far]
            for t in range(3):
                part = left.astype(bf16).astype(f32)
                parts = jnp.where(lane == 3 * h + t, part, parts)
                left = left - part
    log_ref[...] = logs
    packed_ref[:, q_width:] = parts.astype(bf16)


def merge_kernel(mine_ref, log_ref, packed_ref, wo_ref, sent_ref, kept_ref):
    rows, q_width = mine_ref.shape
    half = rows // 2
    logs = log_ref[...]
    parts = packed_ref[:, q_width:].astype(f32)
    heads = []
    for h in range(q_width // HEAD):
        cols = slice(h * HEAD, (h + 1) * HEAD)
        near = logs[:, h : h + 1]
        far = parts[:, 3 * h : 3 * h + 1] + parts[:, 3 * h + 1 : 3 * h + 2] + parts[:, 3 * h + 2 : 3 * h + 3]
        top = jnp.maximum(near, far)
        near, far = jnp.exp2(near - top), jnp.exp2(far - top)
        joined = mine_ref[:, cols] * near + packed_ref[:, cols].astype(f32) * far
        heads.append((joined / (near + far)).astype(bf16))
    context = jnp.concatenate(heads, 1)
    upper = lax.axis_index("req") == 0
    kept_ref[...] = jnp.where(upper, context[:half], context[half:])
    leaving = jnp.where(upper, context[half:], context[:half])
    sent_ref[...] = jnp.dot(leaving, wo_ref[...], preferred_element_type=f32).astype(bf16)


def keep_kernel(context_ref, wo_ref, tok_ref, out_ref):
    half = context_ref.shape[0]
    first = pl.multiple_of(lax.axis_index("req") * half, half)
    residual = tok_ref[pl.ds(first, half), :].astype(f32)
    out_ref[...] = jnp.dot(context_ref[...], wo_ref[...], preferred_element_type=f32) + residual


def cache_kernel(sources, block_ref, slot_ref, *refs):
    pieces, (mine_ref, other_ref) = refs[: len(sources)], refs[len(sources) :]
    shard = lax.axis_index("seq")
    slots = mine_ref.shape[0]
    key_width = mine_ref.shape[3]
    rows = slots * PAGE // 2
    pages = rows // 2 // PAGE
    mine_ref[...] = jnp.zeros_like(mine_ref)
    other_ref[...] = jnp.zeros_like(other_ref)

    def place(ref, at, source):
        for k, block in enumerate(blocks_of(block_ref, source)):
            for j in range(pages):
                slot = slot_ref[block * pages + j]
                holder = slot // slots
                local = slot - holder * slots
                offset = at + (k * pages + j) * PAGE
                if not isinstance(offset, int):
                    offset = pl.multiple_of(offset, PAGE)
                for target, owner in ((mine_ref, shard), (other_ref, shard ^ 1)):

                    @pl.when(holder == owner)
                    def _():
                        target[local, 0] = ref[pl.ds(offset, PAGE), :key_width]
                        target[local, 1] = ref[pl.ds(offset, PAGE), key_width:]

    for ref, (count, source_of) in zip(pieces, sources):
        if count == 1:
            place(ref, 0, source_of(shard, 0))
        else:

            def step(i, carry):
                place(ref, i * rows, source_of(shard, i))
                return carry

            lax.fori_loop(0, count, step, 0)


def swap(x, n, bit):
    return lax.ppermute(x, "seq", [(i, i ^ bit) for i in range(n)])


def gather_shards(kv, n):
    if n % 4 or n > 16:
        same = [list(range(c, n, 2)) for c in range(2)]
        everyone = lax.all_gather(kv, "seq", axis=0, tiled=True, axis_index_groups=same)
        return [([everyone], [(n // 2, lambda shard, i: 2 * i + shard % 2)])]
    outer = n // 4

    def moved(shift, flip):
        def source_of(shard, i):
            plane = lax.rem(shard // 4 + outer - shift, outer)
            return plane * 4 + ((shard % 4) ^ flip)

        return 1, source_of

    early, late = [(kv, moved(0, 0)), (swap(kv, n, 2), moved(0, 2))], []
    for k, shift in enumerate(range(outer - 1, 0, -1)):
        turned = lax.ppermute(kv, "seq", [(i, (i + 4 * shift) % n) for i in range(n)])
        (early if k < 2 else late).append((turned, moved(shift, 0)))
        late.append((swap(turned, n, 2), moved(shift, 2)))
    return [tuple(zip(*group)) for group in (early, late) if group]


def on_device(
    n, parts, tokens, norm_gain, w_query, key_projection, value_projection, w_out, lengths, block_split, page_slot,
):
    rows, width = tokens.shape
    half = rows // 2
    q_width = w_query.shape[1]
    kv_width = key_projection.shape[1] + value_projection.shape[1]
    kv_heads = key_projection.shape[1] // HEAD
    stacked = 2 * rows * q_width // (kv_heads * HEAD)
    normed, kv, cosine, sine = pl.pallas_call(
        key_value_kernel,
        out_shape=(
            struct((rows, width), bf16),
            struct((rows, kv_width), bf16),
            struct((rows, HEAD), f32),
            struct((rows, HEAD), f32),
        ),
        in_specs=in_hbm(7),
        out_specs=tuple(in_vmem(4)),
        scratch_shapes=[
            pltpu.SMEM(block_split.shape, jnp.int32),
            pltpu.SMEM(lengths.shape, jnp.int32),
            pltpu.VMEM((1, HEAD), f32),
            pltpu.VMEM((rows, width), bf16),
            pltpu.VMEM((1, width), f32),
            pltpu.VMEM((width, kv_width), bf16),
            pltpu.SemaphoreType.DMA((5,)),
            pltpu.SemaphoreType.DMA((WEIGHT_STEPS, 2)),
        ],
        compiler_params=kernel_params(62),
        cost_estimate=cost(2 * rows * width * kv_width, 2 * width * kv_width),
        name="key_value",
    )(
        block_split, lengths, inverse_frequencies(), tokens, norm_gain.reshape(1, width),
        key_projection, value_projection,
    )
    queries = pl.pallas_call(
        query_kernel,
        out_shape=struct((rows, q_width), bf16),
        in_specs=in_vmem(3) + in_hbm(1),
        out_specs=in_vmem(1)[0],
        scratch_shapes=[
            pltpu.VMEM((width, q_width), bf16),
            pltpu.SemaphoreType.DMA((WEIGHT_STEPS, 1)),
        ],
        compiler_params=kernel_params(24),
        cost_estimate=cost(2 * rows * width * q_width, 2 * width * q_width),
        name="query",
    )(normed, cosine, sine, w_query)
    groups = gather_shards(kv, n)
    far_queries = swap(queries, n, 1)

    state = ()
    for i, (arrays, sources) in enumerate(groups):
        first, last = i == 0, i == len(groups) - 1
        if last:
            shapes = (
                struct((rows, q_width), f32),
                struct((rows, HEAD), f32),
                struct((rows, q_width + HEAD), bf16),
            )
        else:
            shapes = (struct((kv_heads, stacked, HEAD), f32),) * 3
        keys = sum(count for count, _ in sources) * rows
        state = pl.pallas_call(
            functools.partial(attend_kernel, sources, first, last),
            out_shape=shapes,
            in_specs=in_smem(2) + in_vmem(2 + len(arrays) + len(state)),
            out_specs=tuple(in_vmem(len(shapes))),
            compiler_params=kernel_params(32),
            cost_estimate=cost(8 * rows * keys * q_width, 2 * keys * kv_width),
            name="attend",
        )(block_split, lengths, queries, far_queries, *arrays, *state)
    mine, logs, packed = state
    packed = swap(packed, n, 1)
    sent, kept = pl.pallas_call(
        merge_kernel,
        out_shape=(struct((half, width), bf16), struct((half, q_width), bf16)),
        in_specs=in_vmem(4),
        out_specs=tuple(in_vmem(2)),
        compiler_params=kernel_params(24),
        cost_estimate=cost(rows * width * q_width, 2 * width * q_width),
        name="merge",
    )(mine, logs, packed, w_out)
    received = lax.ppermute(sent, "req", [(i, (i + 1) % parts) for i in range(parts)])
    kept = pl.pallas_call(
        keep_kernel,
        out_shape=struct((half, width), f32),
        in_specs=in_vmem(3),
        out_specs=in_vmem(1)[0],
        compiler_params=kernel_params(24),
        cost_estimate=cost(rows * width * q_width, 2 * width * q_width),
        name="keep",
    )(kept, w_out, tokens)

    arrays = [x for held, _ in groups for x in held]
    sources = [s for _, where in groups for s in where]
    arrays, _ = lax.optimization_barrier((arrays, sent))
    shape = (2 * rows // PAGE, 2, PAGE, kv_width // 2)
    cache, other = pl.pallas_call(
        functools.partial(cache_kernel, sources),
        out_shape=(struct(shape, bf16),) * 2,
        in_specs=in_smem(2) + in_vmem(len(arrays)),
        out_specs=tuple(in_vmem(2)),
        compiler_params=kernel_params(32),
        cost_estimate=cost(0, 4 * rows * kv_width),
        name="cache",
    )(block_split, page_slot, *arrays)
    cache = cache + swap(other, n, 1)
    hidden = (kept + received.astype(f32)).astype(bf16)
    return hidden, cache


def solution(mesh):
    in_specs = (
        P("seq", None),
        P(),
        P(None, "req"),
        P(None, "req"),
        P(None, "req"),
        P("req", None),
        P(),
        P(),
        P(),
    )
    out_specs = (P(("seq", "req"), None), P("seq", None, None, "req"))
    body = functools.partial(on_device, mesh.shape["seq"], mesh.shape["req"])
    return jax.shard_map(body, mesh=mesh, in_specs=in_specs, out_specs=out_specs, check_vma=False)
```

time: 53.7 us -> 47.9 us (0.89)
  waiting for transfers between devices: 21.8 us -> 15.7 us
  local copies, waits for them, and re-layouts: 6.32 us -> 4.34 us
  Pallas kernels: 11.3 us -> 12.2 us
  other arithmetic: 0.75 us -> 1.54 us
  starting transfers between devices: 12.4 us -> 13 us
    ppermute x3, waiting for transfers between devices: 9.82 us -> 0.08 us  [gather_shards(): lax.ppermute(kv, 'seq', [(i, (i + 4 * shift) % n) for i in range(n)])]
    ppermute x12 -> x7, waiting for transfers between devices: 5.87 us -> 9.87 us  [swap(): return lax.ppermute(x, 'seq', [(i, i ^ bit) for i in range(n)])]
    ppermute x3, starting transfers between devices: 4.62 us -> 7.01 us  [gather_shards(): lax.ppermute(kv, 'seq', [(i, (i + 4 * shift) % n) for i in range(n)])]
    unnamed x22 -> x20, local copies, waits for them, and re-layouts: 6.32 us -> 4.34 us
    ppermute x12 -> x7, starting transfers between devices: 6.16 us -> 4.47 us  [swap(): return lax.ppermute(x, 'seq', [(i, i ^ bit) for i in range(n)])]
    pallas_call x1, Pallas kernels: 2.03 us -> 3.23 us  [on_device(): pl.pallas_call(key_value_kernel, out_shape=(struct((rows, width), bf16),...]
    add x0 -> x1, other arithmetic: none -> 0.79 us  [on_device(): cache = cache + swap(other, n, 1)]
    pallas_call x1 -> x5, Pallas kernels: 8.4 us -> 8.05 us  [the longest x2 5.36 us: on_device(): pl.pallas_call(functools.partial(attend_kernel, sources, first, last), ou...]
  transfers between devices with their start and end apart: 16 -> 11, of which waited for: 6 -> 7; matrix products, arithmetic and copies ran while one was open for 0% -> 2% of each run, Pallas kernels for 2% -> 6%
where the time goes in v2:
time: 47.9 us; the launch traced here: 47.6 us
  waiting for transfers between devices  15.7 us (33%)
  starting transfers between devices  13 us (27%)
  Pallas kernels  12.2 us (25%)
  local copies, waits for them, and re-layouts  4.34 us (9%)
  other arithmetic  1.54 us (3%)
  between operations  0.77 us (2%)
    ppermute x7, waiting for transfers between devices, swap(): return lax.ppermute(x, 'seq', [(i, i ^ bit) for i in range(n)])  9.87 us
    ppermute x3, starting transfers between devices, gather_shards(): lax.ppermute(kv, 'seq', [(i, (i + 4 * shift) % n) for i in range(n)])  7.01 us
    ppermute x1, waiting for transfers between devices, on_device(): lax.ppermute(sent, 'req', [(i, (i + 1) % parts) for i in range(parts)])  5.75 us
    pallas_call x2, Pallas kernels, on_device(): pl.pallas_call(functools.partial(attend_kernel, sources, first, last), ou...  5.36 us
    ppermute x7, starting transfers between devices, swap(): return lax.ppermute(x, 'seq', [(i, i ^ bit) for i in range(n)])  4.47 us
    unnamed x20, local copies, waits for them, and re-layouts  4.34 us
    pallas_call x1, Pallas kernels, on_device(): pl.pallas_call(key_value_kernel, out_shape=(struct((rows, width), bf16),...  3.23 us
    ppermute x1, starting transfers between devices, on_device(): lax.ppermute(sent, 'req', [(i, (i + 1) % parts) for i in range(parts)])  1.54 us
  transfers between devices with their start and end apart: 11, of which 7 were waited for; matrix products, arithmetic and copies ran while one was open for 2% of the time, Pallas kernels for 6%

profile of v2, /device:TPU:0, one launch (start us, length us, event | category | flops | bytes accessed | tf_op | source)
XLA Modules:
  0.0 47.6 jit_solution(13043005094246491465)
XLA Ops:
  0.6 3.2 %key_value.1 = (bf16[128,2048]{1,0:T(8,128)(2,1)}, bf16[128,512]{1,0:T(8,128)(2,1)}, f32[128,128]{1,0:T(8,128)}, f32[128,128]{1,0:T(8,128)}) custom-call(s32[16]{0:T(128)} %block_ref.5, s32[4]{0:T(128)} %len_ref.3, f32[1,128]{1,0:T(1,128)} %constant.2.clone.freq_hbm, bf16[128,2048]{1,0:T(8,128)(2,1)} %tok_ref.1, f32[1,2048]{1,0:T(1,128)} %bitcast.1, ...), custom_call_target="tpu_custom_call" | custom-call | flops 268435456 | bytes 2097152 | tf_op jit(solution)/shard_map/key_value/pallas_call | solution.py:379
  3.9 3.1 %collective-permute-start.5 = (bf16[128,512]{1,0:T(8,128)(2,1)}, bf16[128,512]{1,0:T(8,128)(2,1)S(1)}, u32[]{:S(2)}, u32[]{:S(2)}) collective-permute-start(bf16[128,512]{1,0:T(8,128)(2,1)} %get-tuple-element.36.refs_0_), channel_id=1, source_target_pairs={{0,8},{2,10},{4,12},{6,14},{8,16},{10,18},{12,20},{14,22},{16,24},... | collective-permute-start | bytes 393224 | tf_op jit(solution)/shard_map/ppermute | solution.py:364
  7.0 2.6 %collective-permute-start.3 = (bf16[128,512]{1,0:T(8,128)(2,1)}, bf16[128,512]{1,0:T(8,128)(2,1)S(1)}, u32[]{:S(2)}, u32[]{:S(2)}) collective-permute-start(bf16[128,512]{1,0:T(8,128)(2,1)} %get-tuple-element.36.refs_0_), channel_id=1, source_target_pairs={{0,16},{2,18},{4,20},{6,22},{8,24},{10,26},{12,28},{14,30},{16,0},... | collective-permute-start | bytes 393224 | tf_op jit(solution)/shard_map/ppermute | solution.py:364
  9.6 1.3 %collective-permute-start.1 = (bf16[128,512]{1,0:T(8,128)(2,1)}, bf16[128,512]{1,0:T(8,128)(2,1)S(1)}, u32[]{:S(2)}, u32[]{:S(2)}) collective-permute-start(bf16[128,512]{1,0:T(8,128)(2,1)} %get-tuple-element.36.refs_0_), channel_id=1, source_target_pairs={{0,24},{2,26},{4,28},{6,30},{8,0},{10,2},{12,4},{14,6},{16,8},{18,... | collective-permute-start | bytes 393224 | tf_op jit(solution)/shard_map/ppermute | solution.py:364
  10.9 1.6 %copy-done.1 = bf16[2048,512]{1,0:T(8,128)(2,1)S(1)} copy-done((bf16[2048,512]{1,0:T(8,128)(2,1)S(1)}, bf16[2048,512]{1,0:T(8,128)(2,1)}, u32[]{:S(2)}) %copy-start.1) | copy-done | bytes 2097176
  12.5 1.0 %copy-done.3 = bf16[128,2048]{1,0:T(8,128)(2,1)S(1)} copy-done((bf16[128,2048]{1,0:T(8,128)(2,1)S(1)}, bf16[128,2048]{1,0:T(8,128)(2,1)}, u32[]{:S(2)}) %copy-start.3) | copy-done | bytes 524312
  13.5 0.8 %copy-done.5 = f32[128,128]{1,0:T(8,128)S(1)} copy-done((f32[128,128]{1,0:T(8,128)S(1)}, f32[128,128]{1,0:T(8,128)}, u32[]{:S(2)}) %copy-start.5) | copy-done | bytes 65560
  14.4 0.8 %copy-done.6 = f32[128,128]{1,0:T(8,128)S(1)} copy-done((f32[128,128]{1,0:T(8,128)S(1)}, f32[128,128]{1,0:T(8,128)}, u32[]{:S(2)}) %copy-start.6) | copy-done | bytes 65560
  15.2 0.9 %query.1.q_ref = bf16[128,512]{1,0:T(8,128)(2,1)S(1)} custom-call(bf16[128,2048]{1,0:T(8,128)(2,1)S(1)} %copy-done.3, f32[128,128]{1,0:T(8,128)S(1)} %copy-done.5, f32[128,128]{1,0:T(8,128)S(1)} %copy-done.6, bf16[2048,512]{1,0:T(8,128)(2,1)S(1)} %copy-done.1), custom_call_target="tpu_custom_call" | custom-call | flops 268435456 | bytes 2097152 | tf_op jit(solution)/shard_map/query/pallas_call | solution.py:406
  16.2 1.6 %collective-permute-start.7 = (bf16[128,512]{1,0:T(8,128)(2,1)S(1)}, bf16[128,512]{1,0:T(8,128)(2,1)S(1)}, u32[]{:S(2)}, u32[]{:S(2)}) collective-permute-start(bf16[128,512]{1,0:T(8,128)(2,1)S(1)} %copy-done.4), channel_id=1, source_target_pairs={{0,4},{2,6},{4,0},{6,2},{8,12},{10,14},{12,8},{14,10},{16,20},{18,... | collective-permute-start | bytes 393224 | tf_op jit(solution)/shard_map/ppermute | solution.py:345
  18.4 1.5 %collective-permute-start.4 = (bf16[128,512]{1,0:T(8,128)(2,1)S(1)}, bf16[128,512]{1,0:T(8,128)(2,1)S(1)}, u32[]{:S(2)}, u32[]{:S(2)}) collective-permute-start(bf16[128,512]{1,0:T(8,128)(2,1)S(1)} %collective-permute-done.3.refs_3_), channel_id=1, source_target_pairs={{0,4},{2,6},{4,0},{6,2},{8,12},{10,14},{12,8},{14,10},{16,20},{18,... | collective-permute-start | bytes 393224 | tf_op jit(solution)/shard_map/ppermute | solution.py:345
  20.4 2.2 %collective-permute-done.7.refs_1_ = bf16[128,512]{1,0:T(8,128)(2,1)S(1)} collective-permute-done((bf16[128,512]{1,0:T(8,128)(2,1)S(1)}, bf16[128,512]{1,0:T(8,128)(2,1)S(1)}, u32[]{:S(2)}, u32[]{:S(2)}) %collective-permute-start.7) | collective-permute-done | bytes 131104 | tf_op jit(solution)/shard_map/ppermute | solution.py:345
  22.6 1.6 %attend.2 = (f32[2,512,128]{2,1,0:T(8,128)S(1)}, f32[2,512,128]{2,1,0:T(8,128)S(1)}, f32[2,512,128]{2,1,0:T(8,128)S(1)}) custom-call(s32[16]{0:T(128)S(1)} %copy-done.7, s32[4]{0:T(128)S(1)} %copy-done.8, bf16[128,512]{1,0:T(8,128)(2,1)S(1)} %query.1.q_ref, bf16[128,512]{1,0:T(8,128)(2,1)S(1)} %collective-permute-done.far_ref, ...), custom_call_target="tpu_custom_call" | custom-call | flops 268435456 | bytes 524288 | tf_op jit(solution)/shard_map/attend/pallas_call | solution.py:434
  24.3 1.2 %collective-permute-done.6.refs_3_.refs_7_ = bf16[128,512]{1,0:T(8,128)(2,1)S(1)} collective-permute-done((bf16[128,512]{1,0:T(8,128)(2,1)S(1)}, bf16[128,512]{1,0:T(8,128)(2,1)S(1)}, u32[]{:S(2)}, u32[]{:S(2)}) %collective-permute-start.6) | collective-permute-done | bytes 131104 | tf_op jit(solution)/shard_map/ppermute | solution.py:345
  25.4 2.8 %collective-permute-done.4.refs_1_.refs_5_ = bf16[128,512]{1,0:T(8,128)(2,1)S(1)} collective-permute-done((bf16[128,512]{1,0:T(8,128)(2,1)S(1)}, bf16[128,512]{1,0:T(8,128)(2,1)S(1)}, u32[]{:S(2)}, u32[]{:S(2)}) %collective-permute-start.4) | collective-permute-done | bytes 131104 | tf_op jit(solution)/shard_map/ppermute | solution.py:345
  28.2 2.3 %collective-permute-done.2.refs_0_.refs_4_ = bf16[128,512]{1,0:T(8,128)(2,1)S(1)} collective-permute-done((bf16[128,512]{1,0:T(8,128)(2,1)S(1)}, bf16[128,512]{1,0:T(8,128)(2,1)S(1)}, u32[]{:S(2)}, u32[]{:S(2)}) %collective-permute-start.2) | collective-permute-done | bytes 131104 | tf_op jit(solution)/shard_map/ppermute | solution.py:345
  30.6 3.7 %attend.3 = (f32[128,512]{1,0:T(8,128)S(1)}, f32[128,128]{1,0:T(8,128)S(1)}, bf16[128,640]{1,0:T(8,128)(2,1)S(1)}) custom-call(s32[16]{0:T(128)S(1)} %copy-done.7, s32[4]{0:T(128)S(1)} %copy-done.8, bf16[128,512]{1,0:T(8,128)(2,1)S(1)} %query.1.q_ref, bf16[128,512]{1,0:T(8,128)(2,1)S(1)} %collective-permute-done.far_ref, ...), custom_call_target="tpu_custom_call" | custom-call | flops 268435456 | bytes 524288 | tf_op jit(solution)/shard_map/attend/pallas_call | solution.py:434
  34.4 1.4 %collective-permute-done.8.packed_ref = bf16[128,640]{1,0:T(8,128)(2,1)S(1)} collective-permute-done((bf16[128,640]{1,0:T(8,128)(2,1)S(1)}, bf16[128,640]{1,0:T(8,128)(2,1)S(1)}, u32[]{:S(2)}, u32[]{:S(2)}) %collective-permute-start.8) | collective-permute-done | bytes 163872 | tf_op jit(solution)/shard_map/ppermute | solution.py:345
  35.8 1.0 %merge.1 = (bf16[64,2048]{1,0:T(8,128)(2,1)S(1)}, bf16[64,512]{1,0:T(8,128)(2,1)S(1)}) custom-call(f32[128,512]{1,0:T(8,128)S(1)} %get-tuple-element.31.mine_ref, f32[128,128]{1,0:T(8,128)S(1)} %get-tuple-element.32.log_ref, bf16[128,640]{1,0:T(8,128)(2,1)S(1)} %collective-permute-done.8.packed_ref, bf16[512,2048]{1,0:T(8,128)(2,1)S(1)} %copy-done), custom_call_target="tpu_custom_call" | custom-call | flops 134217728 | bytes 2097152 | tf_op jit(solution)/shard_map/merge/pallas_call | solution.py:445
  36.8 1.2 %cache.1 = (bf16[8,2,32,256]{3,2,1,0:T(8,128)(2,1)S(1)}, bf16[8,2,32,256]{3,2,1,0:T(8,128)(2,1)S(1)}) custom-call(s32[16]{0:T(128)S(1)} %copy-done.7, s32[64]{0:T(128)S(1)} %copy-done.9, bf16[128,512]{1,0:T(8,128)(2,1)S(1)} %copy-done.4, bf16[128,512]{1,0:T(8,128)(2,1)S(1)} %collective-permute-done.7.refs_1_, ...), custom_call_target="tpu_custom_call" | custom-call | bytes 262144 | tf_op jit(solution)/shard_map/cache/pallas_call | solution.py:469
  38.2 1.5 %collective-permute-start.9 = (bf16[64,2048]{1,0:T(8,128)(2,1)S(1)}, bf16[64,2048]{1,0:T(8,128)(2,1)S(1)}, u32[]{:S(2)}, u32[]{:S(2)}) collective-permute-start(bf16[64,2048]{1,0:T(8,128)(2,1)S(1)} %get-tuple-element.35), channel_id=1, source_target_pairs={{0,1},{1,0},{2,3},{3,2},{4,5},{5,4},{6,7},{7,6},{8,9},{9,8},{10,11... | collective-permute-start | bytes 786440 | tf_op jit(solution)/shard_map/ppermute | solution.py:454
  40.3 0.8 %add.7 = bf16[8,2,32,256]{3,2,1,0:T(8,128)(2,1)} add(bf16[8,2,32,256]{3,2,1,0:T(8,128)(2,1)S(1)} %get-tuple-element.44, bf16[8,2,32,256]{3,2,1,0:T(8,128)(2,1)S(1)} %collective-permute-done.10) | non-fusion elementwise | flops 131072 | bytes 786432 | tf_op jit(solution)/shard_map/add | solution.py:478
  41.1 5.8 %collective-permute-done.9 = bf16[64,2048]{1,0:T(8,128)(2,1)S(1)} collective-permute-done((bf16[64,2048]{1,0:T(8,128)(2,1)S(1)}, bf16[64,2048]{1,0:T(8,128)(2,1)S(1)}, u32[]{:S(2)}, u32[]{:S(2)}) %collective-permute-start.9) | collective-permute-done | bytes 262176 | tf_op jit(solution)/shard_map/ppermute | solution.py:454
  46.8 0.8 %add_convert_fusion = bf16[64,2048]{1,0:T(8,128)(2,1)} fusion(f32[64,2048]{1,0:T(8,128)S(1)} %keep.1, bf16[64,2048]{1,0:T(8,128)(2,1)S(1)} %collective-permute-done.9), kind=kLoop, calls=%fused_computation | loop fusion | flops 393216 | bytes 1048576 | tf_op jit(solution)/shard_map/convert_element_type | solution.py:479
  (27 shorter events, 2.0 us)
Async XLA Ops:
  3.9 18.7 %copy-start.7 = (s32[16]{0:T(128)S(1)}, s32[16]{0:T(128)}, u32[]{:S(2)}) copy-start(s32[16]{0:T(128)} %block_ref.5) | copy-start | bytes 196
  3.9 18.7 %copy-start.8 = (s32[4]{0:T(128)S(1)}, s32[4]{0:T(128)}, u32[]{:S(2)}) copy-start(s32[4]{0:T(128)} %len_ref.3) | copy-start | bytes 52
  3.9 13.9 %collective-permute-start.5 = (bf16[128,512]{1,0:T(8,128)(2,1)}, bf16[128,512]{1,0:T(8,128)(2,1)S(1)}, u32[]{:S(2)}, u32[]{:S(2)}) collective-permute-start(bf16[128,512]{1,0:T(8,128)(2,1)} %get-tuple-element.36.refs_0_), channel_id=1, source_target_pairs={{0,8},{2,10},{4,12},{6,14},{8,16},{10,18},{12,20},{14,22},{16,24},... | collective-permute-start | bytes 393224 | tf_op jit(solution)/shard_map/ppermute | solution.py:364
  7.0 11.4 %collective-permute-start.3 = (bf16[128,512]{1,0:T(8,128)(2,1)}, bf16[128,512]{1,0:T(8,128)(2,1)S(1)}, u32[]{:S(2)}, u32[]{:S(2)}) collective-permute-start(bf16[128,512]{1,0:T(8,128)(2,1)} %get-tuple-element.36.refs_0_), channel_id=1, source_target_pairs={{0,16},{2,18},{4,20},{6,22},{8,24},{10,26},{12,28},{14,30},{16,0},... | collective-permute-start | bytes 393224 | tf_op jit(solution)/shard_map/ppermute | solution.py:364
  9.6 10.3 %collective-permute-start.1 = (bf16[128,512]{1,0:T(8,128)(2,1)}, bf16[128,512]{1,0:T(8,128)(2,1)S(1)}, u32[]{:S(2)}, u32[]{:S(2)}) collective-permute-start(bf16[128,512]{1,0:T(8,128)(2,1)} %get-tuple-element.36.refs_0_), channel_id=1, source_target_pairs={{0,24},{2,26},{4,28},{6,30},{8,0},{10,2},{12,4},{14,6},{16,8},{18,... | collective-permute-start | bytes 393224 | tf_op jit(solution)/shard_map/ppermute | solution.py:364
  10.9 1.6 %copy-start.1 = (bf16[2048,512]{1,0:T(8,128)(2,1)S(1)}, bf16[2048,512]{1,0:T(8,128)(2,1)}, u32[]{:S(2)}) copy-start(bf16[2048,512]{1,0:T(8,128)(2,1)} %wq_ref.1) | copy-start | bytes 6291460
  12.5 1.0 %copy-start.3 = (bf16[128,2048]{1,0:T(8,128)(2,1)S(1)}, bf16[128,2048]{1,0:T(8,128)(2,1)}, u32[]{:S(2)}) copy-start(bf16[128,2048]{1,0:T(8,128)(2,1)} %get-tuple-element.24.normed_ref) | copy-start | bytes 1572868
  13.5 0.8 %copy-start.5 = (f32[128,128]{1,0:T(8,128)S(1)}, f32[128,128]{1,0:T(8,128)}, u32[]{:S(2)}) copy-start(f32[128,128]{1,0:T(8,128)} %get-tuple-element.25.cos_ref) | copy-start | bytes 196612
  14.4 0.8 %copy-start.6 = (f32[128,128]{1,0:T(8,128)S(1)}, f32[128,128]{1,0:T(8,128)}, u32[]{:S(2)}) copy-start(f32[128,128]{1,0:T(8,128)} %get-tuple-element.26.sin_ref) | copy-start | bytes 196612
  15.2 1.0 %copy-start.4 = (bf16[128,512]{1,0:T(8,128)(2,1)S(1)}, bf16[128,512]{1,0:T(8,128)(2,1)}, u32[]{:S(2)}) copy-start(bf16[128,512]{1,0:T(8,128)(2,1)} %get-tuple-element.36.refs_0_) | copy-start | bytes 393220
  16.1 19.6 %copy-start = (bf16[512,2048]{1,0:T(8,128)(2,1)S(1)}, bf16[512,2048]{1,0:T(8,128)(2,1)}, u32[]{:S(2)}) copy-start(bf16[512,2048]{1,0:T(8,128)(2,1)} %wo_ref.3) | copy-start | bytes 6291460
  16.2 4.3 %collective-permute-start = (bf16[128,512]{1,0:T(8,128)(2,1)S(1)}, bf16[128,512]{1,0:T(8,128)(2,1)S(1)}, u32[]{:S(2)}, u32[]{:S(2)}) collective-permute-start(bf16[128,512]{1,0:T(8,128)(2,1)S(1)} %query.1.q_ref), channel_id=1, source_target_pairs={{0,2},{2,0},{4,6},{6,4},{8,10},{10,8},{12,14},{14,12},{16,18},{18,... | collective-permute-start | bytes 393224 | tf_op jit(solution)/shard_map/ppermute | solution.py:345
  16.2 6.4 %collective-permute-start.7 = (bf16[128,512]{1,0:T(8,128)(2,1)S(1)}, bf16[128,512]{1,0:T(8,128)(2,1)S(1)}, u32[]{:S(2)}, u32[]{:S(2)}) collective-permute-start(bf16[128,512]{1,0:T(8,128)(2,1)S(1)} %copy-done.4), channel_id=1, source_target_pairs={{0,4},{2,6},{4,0},{6,2},{8,12},{10,14},{12,8},{14,10},{16,20},{18,... | collective-permute-start | bytes 393224 | tf_op jit(solution)/shard_map/ppermute | solution.py:345
  17.8 7.6 %collective-permute-start.6 = (bf16[128,512]{1,0:T(8,128)(2,1)S(1)}, bf16[128,512]{1,0:T(8,128)(2,1)S(1)}, u32[]{:S(2)}, u32[]{:S(2)}) collective-permute-start(bf16[128,512]{1,0:T(8,128)(2,1)S(1)} %collective-permute-done.5.refs_2_.refs_6_), channel_id=1, source_target_pairs={{0,4},{2,6},{4,0},{6,2},{8,12},{10,14},{12,8},{14,10},{16,20},{18,... | collective-permute-start | bytes 393224 | tf_op jit(solution)/shard_map/ppermute | solution.py:345
  18.4 9.8 %collective-permute-start.4 = (bf16[128,512]{1,0:T(8,128)(2,1)S(1)}, bf16[128,512]{1,0:T(8,128)(2,1)S(1)}, u32[]{:S(2)}, u32[]{:S(2)}) collective-permute-start(bf16[128,512]{1,0:T(8,128)(2,1)S(1)} %collective-permute-done.3.refs_3_), channel_id=1, source_target_pairs={{0,4},{2,6},{4,0},{6,2},{8,12},{10,14},{12,8},{14,10},{16,20},{18,... | collective-permute-start | bytes 393224 | tf_op jit(solution)/shard_map/ppermute | solution.py:345
  19.9 10.7 %collective-permute-start.2 = (bf16[128,512]{1,0:T(8,128)(2,1)S(1)}, bf16[128,512]{1,0:T(8,128)(2,1)S(1)}, u32[]{:S(2)}, u32[]{:S(2)}) collective-permute-start(bf16[128,512]{1,0:T(8,128)(2,1)S(1)} %collective-permute-done.1.refs_2_), channel_id=1, source_target_pairs={{0,4},{2,6},{4,0},{6,2},{8,12},{10,14},{12,8},{14,10},{16,20},{18,... | collective-permute-start | bytes 393224 | tf_op jit(solution)/shard_map/ppermute | solution.py:345
  30.6 6.2 %copy-start.9 = (s32[64]{0:T(128)S(1)}, s32[64]{0:T(128)}, u32[]{:S(2)}) copy-start(s32[64]{0:T(128)} %slot_ref.1) | copy-start | bytes 772
  34.3 5.5 %copy-start.2 = (bf16[128,2048]{1,0:T(8,128)(2,1)S(1)}, bf16[128,2048]{1,0:T(8,128)(2,1)}, u32[]{:S(2)}) copy-start(bf16[128,2048]{1,0:T(8,128)(2,1)} %tok_ref.1) | copy-start | bytes 1572868
  34.3 1.5 %collective-permute-start.8 = (bf16[128,640]{1,0:T(8,128)(2,1)S(1)}, bf16[128,640]{1,0:T(8,128)(2,1)S(1)}, u32[]{:S(2)}, u32[]{:S(2)}) collective-permute-start(bf16[128,640]{1,0:T(8,128)(2,1)S(1)} %get-tuple-element.33), channel_id=1, source_target_pairs={{0,2},{2,0},{4,6},{6,4},{8,10},{10,8},{12,14},{14,12},{16,18},{18,... | collective-permute-start | bytes 491528 | tf_op jit(solution)/shard_map/ppermute | solution.py:345
  38.0 2.2 %collective-permute-start.10 = (bf16[8,2,32,256]{3,2,1,0:T(8,128)(2,1)S(1)}, bf16[8,2,32,256]{3,2,1,0:T(8,128)(2,1)S(1)}, u32[]{:S(2)}, u32[]{:S(2)}) collective-permute-start(bf16[8,2,32,256]{3,2,1,0:T(8,128)(2,1)S(1)} %get-tuple-element.45), channel_id=1, source_target_pairs={{0,2},{2,0},{4,6},{6,4},{8,10},{10,8},{12,14},{14,12},{16,18},{18,... | collective-permute-start | bytes 786440 | tf_op jit(solution)/shard_map/ppermute | solution.py:345
  38.2 8.6 %collective-permute-start.9 = (bf16[64,2048]{1,0:T(8,128)(2,1)S(1)}, bf16[64,2048]{1,0:T(8,128)(2,1)S(1)}, u32[]{:S(2)}, u32[]{:S(2)}) collective-permute-start(bf16[64,2048]{1,0:T(8,128)(2,1)S(1)} %get-tuple-element.35), channel_id=1, source_target_pairs={{0,1},{1,0},{2,3},{3,2},{4,5},{5,4},{6,7},{7,6},{8,9},{9,8},{10,11... | collective-permute-start | bytes 786440 | tf_op jit(solution)/shard_map/ppermute | solution.py:454

commit v3 on v2

--- a/solution.py
+++ b/solution.py
@@ -156,9 +156,21 @@
     kv_ref[:, key_width:] = product[:, key_width:].astype(bf16)
 
 
-def query_kernel(normed_ref, cos_ref, sin_ref, wq_ref, q_ref, weights, sems):
+def query_kernel(
+    normed_hbm, cos_hbm, sin_hbm, wq_ref, q_ref, normed_ref, cos_ref, sin_ref, weights, small_sems, sems,
+):
+    small = [
+        pltpu.make_async_copy(source, target, small_sems.at[i])
+        for i, (source, target) in enumerate(
+            ((normed_hbm, normed_ref), (cos_hbm, cos_ref), (sin_hbm, sin_ref))
+        )
+    ]
     copies = weight_copies((wq_ref,), weights, sems)
+    for copy in small:
+        copy.start()
     start_all(copies)
+    for copy in small:
+        copy.wait()
     cosine, sine = cos_ref[...], sin_ref[...]
     product = stepped_dot(normed_ref[...], copies, weights)
     for h in range(wq_ref.shape[1] // HEAD):
@@ -248,48 +260,53 @@
             total_ref[g] = jnp.broadcast_to(total, acc.shape)
             acc_ref[g] = acc
         return
-    mine_ref, log_ref, packed_ref = refs
+    mine_ref, stat_ref, packed_ref = refs
+    heads = q_width // HEAD
     lane = lax.broadcasted_iota(jnp.int32, (rows, HEAD), 1)
-    logs = jnp.zeros((rows, HEAD), f32)
-    parts = jnp.zeros((rows, HEAD), f32)
+    mine = jnp.zeros((rows, HEAD), f32)
+    theirs = jnp.zeros((rows, HEAD), f32)
     for g in range(kv_heads):
         top, total, acc = state[g]
-        some = total > 0.0
-        safe = jnp.where(some, total, 1.0)
-        result = acc / safe
-        log_sum = jnp.where(some, top + jnp.log(safe) * math.log2(math.e), FLOOR)
         for j in range(group):
             h = g * group + j
             cols = slice(h * HEAD, (h + 1) * HEAD)
             near = slice(j * both, j * both + rows)
             far = slice(j * both + rows, (j + 1) * both)
-            mine_ref[:, cols] = result[near]
-            packed_ref[:, cols] = result[far].astype(bf16)
-            logs = jnp.where(lane == h, log_sum[near], logs)
-            left = log_sum[far]
-            for t in range(3):
-                part = left.astype(bf16).astype(f32)
-                parts = jnp.where(lane == 3 * h + t, part, parts)
-                left = left - part
-    log_ref[...] = logs
+            mine_ref[:, cols] = acc[near]
+            packed_ref[:, cols] = acc[far].astype(bf16)
+            for value, at in ((top, h), (total, heads + h)):
+                mine = jnp.where(lane == at, value[near], mine)
+                theirs = jnp.where(lane % (2 * heads) == at, value[far], theirs)
+    stat_ref[...] = mine
+    high = theirs.astype(bf16).astype(f32)
+    middle = (theirs - high).astype(bf16).astype(f32)
+    low = theirs - high - middle
+    third = lane // (2 * heads)
+    parts = jnp.where(third == 0, high, jnp.where(third == 1, middle, low))
     packed_ref[:, q_width:] = parts.astype(bf16)
 
 
-def merge_kernel(mine_ref, log_ref, packed_ref, wo_ref, sent_ref, kept_ref):
+def merge_kernel(mine_ref, stat_ref, packed_ref, wo_ref, sent_ref, kept_ref):
     rows, q_width = mine_ref.shape
+    heads = q_width // HEAD
     half = rows // 2
-    logs = log_ref[...]
+    near = stat_ref[...]
     parts = packed_ref[:, q_width:].astype(f32)
-    heads = []
-    for h in range(q_width // HEAD):
+    far = parts
+    for t in (1, 2):
+        far = far + pltpu.roll(parts, HEAD - 2 * heads * t, 1)
+    top = jnp.maximum(near, far)
+    near_part, far_part = jnp.exp2(near - top), jnp.exp2(far - top)
+    near_total, far_total = pltpu.roll(near, HEAD - heads, 1), pltpu.roll(far, HEAD - heads, 1)
+    total = near_total * near_part + far_total * far_part
+    near_part, far_part = near_part / total, far_part / total
+    joined = []
+    for h in range(heads):
         cols = slice(h * HEAD, (h + 1) * HEAD)
-        near = logs[:, h : h + 1]
-        far = parts[:, 3 * h : 3 * h + 1] + parts[:, 3 * h + 1 : 3 * h + 2] + parts[:, 3 * h + 2 : 3 * h + 3]
-        top = jnp.maximum(near, far)
-        near, far = jnp.exp2(near - top), jnp.exp2(far - top)
-        joined = mine_ref[:, cols] * near + packed_ref[:, cols].astype(f32) * far
-        heads.append((joined / (near + far)).astype(bf16))
-    context = jnp.concatenate(heads, 1)
+        ours = mine_ref[:, cols] * near_part[:, h : h + 1]
+        theirs = packed_ref[:, cols].astype(f32) * far_part[:, h : h + 1]
+        joined.append((ours + theirs).astype(bf16))
+    context = jnp.concatenate(joined, 1)
     upper = lax.axis_index("req") == 0
     kept_ref[...] = jnp.where(upper, context[:half], context[half:])
     leaving = jnp.where(upper, context[half:], context[:half])
@@ -359,12 +376,15 @@
 
         return 1, source_of
 
-    early, late = [(kv, moved(0, 0)), (swap(kv, n, 2), moved(0, 2))], []
-    for k, shift in enumerate(range(outer - 1, 0, -1)):
+    own, beside = (kv, moved(0, 0)), (swap(kv, n, 2), moved(0, 2))
+    shifts = sorted(range(1, outer), key=lambda s: (min(s, outer - s), -s))
+    along, across = [], []
+    for shift in shifts:
         turned = lax.ppermute(kv, "seq", [(i, (i + 4 * shift) % n) for i in range(n)])
-        (early if k < 2 else late).append((turned, moved(shift, 0)))
-        late.append((swap(turned, n, 2), moved(shift, 2)))
-    return [tuple(zip(*group)) for group in (early, late) if group]
+        along.append((turned, moved(shift, 0)))
+        across.append((swap(turned, n, 2), moved(shift, 2)))
+    groups = [[own, beside] + along[:2], along[2:] + across[:-2], across[-2:]]
+    return [tuple(zip(*group)) for group in groups if group]
 
 
 def on_device(
@@ -403,20 +423,28 @@
         block_split, lengths, inverse_frequencies(), tokens, norm_gain.reshape(1, width),
         key_projection, value_projection,
     )
+    groups = gather_shards(kv, n)
+    if len(groups[0][0]) > 1:
+        (own, beside, *others), sources = groups[0]
+        normed, beside = lax.optimization_barrier((normed, beside))
+        groups[0] = ((own, beside, *others), sources)
     queries = pl.pallas_call(
         query_kernel,
         out_shape=struct((rows, q_width), bf16),
-        in_specs=in_vmem(3) + in_hbm(1),
+        in_specs=in_hbm(4),
         out_specs=in_vmem(1)[0],
         scratch_shapes=[
+            pltpu.VMEM((rows, width), bf16),
+            pltpu.VMEM((rows, HEAD), f32),
+            pltpu.VMEM((rows, HEAD), f32),
             pltpu.VMEM((width, q_width), bf16),
+            pltpu.SemaphoreType.DMA((3,)),
             pltpu.SemaphoreType.DMA((WEIGHT_STEPS, 1)),
         ],
-        compiler_params=kernel_params(24),
+        compiler_params=kernel_params(62),
         cost_estimate=cost(2 * rows * width * q_width, 2 * width * q_width),
         name="query",
     )(normed, cosine, sine, w_query)
-    groups = gather_shards(kv, n)
     far_queries = swap(queries, n, 1)
 
     state = ()
@@ -440,8 +468,22 @@
             cost_estimate=cost(8 * rows * keys * q_width, 2 * keys * kv_width),
             name="attend",
         )(block_split, lengths, queries, far_queries, *arrays, *state)
-    mine, logs, packed = state
+    mine, stats, packed = state
     packed = swap(packed, n, 1)
+    arrays = [x for held, _ in groups for x in held]
+    sources = [s for _, where in groups for s in where]
+    arrays, mine = lax.optimization_barrier((arrays, mine))
+    shape = (2 * rows // PAGE, 2, PAGE, kv_width // 2)
+    cache, other = pl.pallas_call(
+        functools.partial(cache_kernel, sources),
+        out_shape=(struct(shape, bf16),) * 2,
+        in_specs=in_smem(2) + in_vmem(len(arrays)),
+        out_specs=tuple(in_vmem(2)),
+        compiler_params=kernel_params(32),
+        cost_estimate=cost(0, 4 * rows * kv_width),
+        name="cache",
+    )(block_split, page_slot, *arrays)
+    mine, cache, other = lax.optimization_barrier((mine, cache, other))
     sent, kept = pl.pallas_call(
         merge_kernel,
         out_shape=(struct((half, width), bf16), struct((half, q_width), bf16)),
@@ -450,7 +492,7 @@
         compiler_params=kernel_params(24),
         cost_estimate=cost(rows * width * q_width, 2 * width * q_width),
         name="merge",
-    )(mine, logs, packed, w_out)
+    )(mine, stats, packed, w_out)
     received = lax.ppermute(sent, "req", [(i, (i + 1) % parts) for i in range(parts)])
     kept = pl.pallas_call(
         keep_kernel,
@@ -462,19 +504,6 @@
         name="keep",
     )(kept, w_out, tokens)
 
-    arrays = [x for held, _ in groups for x in held]
-    sources = [s for _, where in groups for s in where]
-    arrays, _ = lax.optimization_barrier((arrays, sent))
-    shape = (2 * rows // PAGE, 2, PAGE, kv_width // 2)
-    cache, other = pl.pallas_call(
-        functools.partial(cache_kernel, sources),
-        out_shape=(struct(shape, bf16),) * 2,
-        in_specs=in_smem(2) + in_vmem(len(arrays)),
-        out_specs=tuple(in_vmem(2)),
-        compiler_params=kernel_params(32),
-        cost_estimate=cost(0, 4 * rows * kv_width),
-        name="cache",
-    )(block_split, page_slot, *arrays)
     cache = cache + swap(other, n, 1)
     hidden = (kept + received.astype(f32)).astype(bf16)
     return hidden, cache

time: 47.9 us -> 43.8 us (0.914)
  waiting for transfers between devices: 15.7 us -> 11.5 us
  Pallas kernels: 12.2 us -> 16.2 us
  local copies, waits for them, and re-layouts: 4.34 us -> 1.84 us
  starting transfers between devices: 13 us -> 11.7 us
    ppermute x7, waiting for transfers between devices: 9.87 us -> 0.02 us  [swap(): return lax.ppermute(x, 'seq', [(i, i ^ bit) for i in range(n)])]
    ppermute x3, waiting for transfers between devices: 0.08 us -> 6.03 us  [gather_shards(): lax.ppermute(kv, 'seq', [(i, (i + 4 * shift) % n) for i in range(n)])]
    unnamed x20 -> x18, local copies, waits for them, and re-layouts: 4.34 us -> 1.84 us
    ppermute x3, starting transfers between devices: 7.01 us -> 4.62 us  [gather_shards(): lax.ppermute(kv, 'seq', [(i, (i + 4 * shift) % n) for i in range(n)])]
    pallas_call x2 -> x3, Pallas kernels: 5.36 us -> 7.48 us  [on_device(): pl.pallas_call(functools.partial(attend_kernel, sources, first, last), ou...]
    pallas_call x1, Pallas kernels: 0.91 us -> 3 us  [on_device(): pl.pallas_call(query_kernel, out_shape=struct((rows, q_width), bf16), in_...]
    ppermute x7, starting transfers between devices: 4.47 us -> 5.51 us  [swap(): return lax.ppermute(x, 'seq', [(i, i ^ bit) for i in range(n)])]
  transfers between devices with their start and end apart: 11 -> 11, of which waited for: 7 -> 4; matrix products, arithmetic and copies ran while one was open for 2% -> 2% of each run, Pallas kernels for 6% -> 23%
where the time goes in v3:
time: 43.8 us; the launch traced here: 43.6 us
  Pallas kernels  16.2 us (37%)
  starting transfers between devices  11.7 us (27%)
  waiting for transfers between devices  11.5 us (26%)
  local copies, waits for them, and re-layouts  1.84 us (4%)
  other arithmetic  1.54 us (4%)
  between operations  0.83 us (2%)
    pallas_call x3, Pallas kernels, on_device(): pl.pallas_call(functools.partial(attend_kernel, sources, first, last), ou...  7.48 us
    ppermute x3, waiting for transfers between devices, gather_shards(): lax.ppermute(kv, 'seq', [(i, (i + 4 * shift) % n) for i in range(n)])  6.03 us
    ppermute x7, starting transfers between devices, swap(): return lax.ppermute(x, 'seq', [(i, i ^ bit) for i in range(n)])  5.51 us
    ppermute x1, waiting for transfers between devices, on_device(): lax.ppermute(sent, 'req', [(i, (i + 1) % parts) for i in range(parts)])  5.44 us
    ppermute x3, starting transfers between devices, gather_shards(): lax.ppermute(kv, 'seq', [(i, (i + 4 * shift) % n) for i in range(n)])  4.62 us
    pallas_call x1, Pallas kernels, on_device(): pl.pallas_call(key_value_kernel, out_shape=(struct((rows, width), bf16),...  3.24 us
    pallas_call x1, Pallas kernels, on_device(): pl.pallas_call(query_kernel, out_shape=struct((rows, q_width), bf16), in_...  3 us
    unnamed x18, local copies, waits for them, and re-layouts  1.84 us
  transfers between devices with their start and end apart: 11, of which 4 were waited for; matrix products, arithmetic and copies ran while one was open for 2% of the time, Pallas kernels for 23%

profile of v3, /device:TPU:0, one launch (start us, length us, event | category | flops | bytes accessed | tf_op | source)
XLA Modules:
  0.0 43.6 jit_solution(18294913356221223280)
XLA Ops:
  0.6 3.2 %key_value.1 = (bf16[128,2048]{1,0:T(8,128)(2,1)}, bf16[128,512]{1,0:T(8,128)(2,1)}, f32[128,128]{1,0:T(8,128)}, f32[128,128]{1,0:T(8,128)}) custom-call(s32[16]{0:T(128)} %block_ref.7, s32[4]{0:T(128)} %len_ref.5, f32[1,128]{1,0:T(1,128)} %constant.2.clone.freq_hbm, bf16[128,2048]{1,0:T(8,128)(2,1)} %tok_ref.1, f32[1,2048]{1,0:T(1,128)} %bitcast.1, ...), custom_call_target="tpu_custom_call" | custom-call | flops 268435456 | bytes 2097152 | tf_op jit(solution)/shard_map/key_value/pallas_call | solution.py:399
  3.9 3.0 %collective-permute-start = (bf16[128,512]{1,0:T(8,128)(2,1)}, bf16[128,512]{1,0:T(8,128)(2,1)S(1)}, u32[]{:S(2)}, u32[]{:S(2)}) collective-permute-start(bf16[128,512]{1,0:T(8,128)(2,1)} %get-tuple-element.47.refs_0_), channel_id=1, source_target_pairs={{0,4},{2,6},{4,0},{6,2},{8,12},{10,14},{12,8},{14,10},{16,20},{18,... | collective-permute-start | bytes 393224 | tf_op jit(solution)/shard_map/ppermute | solution.py:362
  6.9 3.6 %collective-permute-start.1 = (bf16[128,512]{1,0:T(8,128)(2,1)}, bf16[128,512]{1,0:T(8,128)(2,1)S(1)}, u32[]{:S(2)}, u32[]{:S(2)}) collective-permute-start(bf16[128,512]{1,0:T(8,128)(2,1)} %get-tuple-element.47.refs_0_), channel_id=1, source_target_pairs={{0,24},{2,26},{4,28},{6,30},{8,0},{10,2},{12,4},{14,6},{16,8},{18,... | collective-permute-start | bytes 393224 | tf_op jit(solution)/shard_map/ppermute | solution.py:383
  10.5 1.0 %collective-permute-start.3 = (bf16[128,512]{1,0:T(8,128)(2,1)}, bf16[128,512]{1,0:T(8,128)(2,1)S(1)}, u32[]{:S(2)}, u32[]{:S(2)}) collective-permute-start(bf16[128,512]{1,0:T(8,128)(2,1)} %get-tuple-element.47.refs_0_), channel_id=1, source_target_pairs={{0,16},{2,18},{4,20},{6,22},{8,24},{10,26},{12,28},{14,30},{16,0},... | collective-permute-start | bytes 393224 | tf_op jit(solution)/shard_map/ppermute | solution.py:383
  11.5 3.0 %query.1.q_ref = bf16[128,512]{1,0:T(8,128)(2,1)} custom-call(bf16[128,2048]{1,0:T(8,128)(2,1)} %get-tuple-element.36.normed_hbm, f32[128,128]{1,0:T(8,128)} %get-tuple-element.37.cos_hbm, f32[128,128]{1,0:T(8,128)} %get-tuple-element.38.sin_hbm, bf16[2048,512]{1,0:T(8,128)(2,1)} %wq_ref.1), custom_call_target="tpu_custom_call" | custom-call | flops 268435456 | bytes 2097152 | tf_op jit(solution)/shard_map/query/pallas_call | solution.py:431
  14.6 0.2 collective-permute-done.1.refs_2_
  14.8 0.7 %collective-permute-start.4 = (bf16[128,512]{1,0:T(8,128)(2,1)S(1)}, bf16[128,512]{1,0:T(8,128)(2,1)S(1)}, u32[]{:S(2)}, u32[]{:S(2)}) collective-permute-start(bf16[128,512]{1,0:T(8,128)(2,1)S(1)} %collective-permute-done.1.refs_2_), channel_id=1, source_target_pairs={{0,4},{2,6},{4,0},{6,2},{8,12},{10,14},{12,8},{14,10},{16,20},{18,... | collective-permute-start | bytes 393224 | tf_op jit(solution)/shard_map/ppermute | solution.py:362
  15.5 3.2 %collective-permute-done.2.refs_3_ = bf16[128,512]{1,0:T(8,128)(2,1)S(1)} collective-permute-done((bf16[128,512]{1,0:T(8,128)(2,1)}, bf16[128,512]{1,0:T(8,128)(2,1)S(1)}, u32[]{:S(2)}, u32[]{:S(2)}) %collective-permute-start.2) | collective-permute-done | bytes 131104 | tf_op jit(solution)/shard_map/ppermute | solution.py:383
  18.7 0.5 %collective-permute-start.5 = (bf16[128,512]{1,0:T(8,128)(2,1)S(1)}, bf16[128,512]{1,0:T(8,128)(2,1)S(1)}, u32[]{:S(2)}, u32[]{:S(2)}) collective-permute-start(bf16[128,512]{1,0:T(8,128)(2,1)S(1)} %collective-permute-done.2.refs_3_), channel_id=1, source_target_pairs={{0,4},{2,6},{4,0},{6,2},{8,12},{10,14},{12,8},{14,10},{16,20},{18,... | collective-permute-start | bytes 393224 | tf_op jit(solution)/shard_map/ppermute | solution.py:362
  19.2 2.7 %collective-permute-done.3.refs_0_.refs_4_ = bf16[128,512]{1,0:T(8,128)(2,1)S(1)} collective-permute-done((bf16[128,512]{1,0:T(8,128)(2,1)}, bf16[128,512]{1,0:T(8,128)(2,1)S(1)}, u32[]{:S(2)}, u32[]{:S(2)}) %collective-permute-start.3) | collective-permute-done | bytes 131104 | tf_op jit(solution)/shard_map/ppermute | solution.py:383
  21.9 0.5 %collective-permute-start.6 = (bf16[128,512]{1,0:T(8,128)(2,1)S(1)}, bf16[128,512]{1,0:T(8,128)(2,1)S(1)}, u32[]{:S(2)}, u32[]{:S(2)}) collective-permute-start(bf16[128,512]{1,0:T(8,128)(2,1)S(1)} %collective-permute-done.3.refs_0_.refs_4_), channel_id=1, source_target_pairs={{0,4},{2,6},{4,0},{6,2},{8,12},{10,14},{12,8},{14,10},{16,20},{18,... | collective-permute-start | bytes 393224 | tf_op jit(solution)/shard_map/ppermute | solution.py:362
  22.5 0.9 %copy-done.2 = bf16[128,512]{1,0:T(8,128)(2,1)S(1)} copy-done((bf16[128,512]{1,0:T(8,128)(2,1)S(1)}, bf16[128,512]{1,0:T(8,128)(2,1)}, u32[]{:S(2)}) %copy-start.2) | copy-done | bytes 131096
  23.4 1.6 %attend.3 = (f32[2,512,128]{2,1,0:T(8,128)S(1)}, f32[2,512,128]{2,1,0:T(8,128)S(1)}, f32[2,512,128]{2,1,0:T(8,128)S(1)}) custom-call(s32[16]{0:T(128)S(1)} %copy-done.6, s32[4]{0:T(128)S(1)} %copy-done.7, bf16[128,512]{1,0:T(8,128)(2,1)S(1)} %copy-done.2, bf16[128,512]{1,0:T(8,128)(2,1)S(1)} %collective-permute-done.7.far_ref, ...), custom_call_target="tpu_custom_call" | custom-call | flops 268435456 | bytes 524288 | tf_op jit(solution)/shard_map/attend/pallas_call | solution.py:462
  25.0 0.9 %copy-done.3 = bf16[128,512]{1,0:T(8,128)(2,1)S(1)} copy-done((bf16[128,512]{1,0:T(8,128)(2,1)S(1)}, bf16[128,512]{1,0:T(8,128)(2,1)}, u32[]{:S(2)}) %copy-start.3) | copy-done | bytes 131096
  25.9 2.9 %attend.4 = (f32[2,512,128]{2,1,0:T(8,128)S(1)}, f32[2,512,128]{2,1,0:T(8,128)S(1)}, f32[2,512,128]{2,1,0:T(8,128)S(1)}) custom-call(s32[16]{0:T(128)S(1)} %copy-done.6, s32[4]{0:T(128)S(1)} %copy-done.7, bf16[128,512]{1,0:T(8,128)(2,1)S(1)} %copy-done.3, bf16[128,512]{1,0:T(8,128)(2,1)S(1)} %collective-permute-done.7.far_ref, ...), custom_call_target="tpu_custom_call" | custom-call | flops 134217728 | bytes 262144 | tf_op jit(solution)/shard_map/attend/pallas_call | solution.py:462
  28.9 2.9 %attend.5 = (f32[128,512]{1,0:T(8,128)S(1)}, f32[128,128]{1,0:T(8,128)S(1)}, bf16[128,640]{1,0:T(8,128)(2,1)S(1)}) custom-call(s32[16]{0:T(128)S(1)} %copy-done.6, s32[4]{0:T(128)S(1)} %copy-done.7, bf16[128,512]{1,0:T(8,128)(2,1)S(1)} %copy-done.4, bf16[128,512]{1,0:T(8,128)(2,1)S(1)} %collective-permute-done.7.far_ref, ...), custom_call_target="tpu_custom_call" | custom-call | flops 134217728 | bytes 262144 | tf_op jit(solution)/shard_map/attend/pallas_call | solution.py:462
  32.0 1.2 %cache.1 = (bf16[8,2,32,256]{3,2,1,0:T(8,128)(2,1)S(1)}, bf16[8,2,32,256]{3,2,1,0:T(8,128)(2,1)S(1)}) custom-call(s32[16]{0:T(128)S(1)} %copy-done.6, s32[64]{0:T(128)S(1)} %copy-done.8, bf16[128,512]{1,0:T(8,128)(2,1)S(1)} %copy-done.5, bf16[128,512]{1,0:T(8,128)(2,1)S(1)} %collective-permute-done.refs_1_, ...), custom_call_target="tpu_custom_call" | custom-call | bytes 262144 | tf_op jit(solution)/shard_map/cache/pallas_call | solution.py:477
  33.2 0.6 %collective-permute-start.10 = (bf16[8,2,32,256]{3,2,1,0:T(8,128)(2,1)S(1)}, bf16[8,2,32,256]{3,2,1,0:T(8,128)(2,1)S(1)}, u32[]{:S(2)}, u32[]{:S(2)}) collective-permute-start(bf16[8,2,32,256]{3,2,1,0:T(8,128)(2,1)S(1)} %get-tuple-element.63), channel_id=1, source_target_pairs={{0,2},{2,0},{4,6},{6,4},{8,10},{10,8},{12,14},{14,12},{16,18},{18,... | collective-permute-start | bytes 786440 | tf_op jit(solution)/shard_map/ppermute | solution.py:362
  33.8 0.7 %merge.1 = (bf16[64,2048]{1,0:T(8,128)(2,1)S(1)}, bf16[64,512]{1,0:T(8,128)(2,1)S(1)}) custom-call(f32[128,512]{1,0:T(8,128)S(1)} %get-tuple-element.57.mine_ref, f32[128,128]{1,0:T(8,128)S(1)} %get-tuple-element.58.stat_ref, bf16[128,640]{1,0:T(8,128)(2,1)S(1)} %collective-permute-done.8.packed_ref, bf16[512,2048]{1,0:T(8,128)(2,1)S(1)} %copy-done), custom_call_target="tpu_custom_call" | custom-call | flops 134217728 | bytes 2097152 | tf_op jit(solution)/shard_map/merge/pallas_call | solution.py:487
  34.5 1.6 %collective-permute-start.9 = (bf16[64,2048]{1,0:T(8,128)(2,1)S(1)}, bf16[64,2048]{1,0:T(8,128)(2,1)S(1)}, u32[]{:S(2)}, u32[]{:S(2)}) collective-permute-start(bf16[64,2048]{1,0:T(8,128)(2,1)S(1)} %get-tuple-element.61), channel_id=1, source_target_pairs={{0,1},{1,0},{2,3},{3,2},{4,5},{5,4},{6,7},{7,6},{8,9},{9,8},{10,11... | collective-permute-start | bytes 786440 | tf_op jit(solution)/shard_map/ppermute | solution.py:496
  36.1 0.5 %keep.1 = f32[64,2048]{1,0:T(8,128)S(1)} custom-call(bf16[64,512]{1,0:T(8,128)(2,1)S(1)} %get-tuple-element.60.context_ref, bf16[512,2048]{1,0:T(8,128)(2,1)S(1)} %copy-done, bf16[128,2048]{1,0:T(8,128)(2,1)S(1)} %copy-done.1), custom_call_target="tpu_custom_call" | custom-call | flops 134217728 | bytes 2097152 | tf_op jit(solution)/shard_map/keep/pallas_call | solution.py:497
  36.6 0.8 %add.7 = bf16[8,2,32,256]{3,2,1,0:T(8,128)(2,1)} add(bf16[8,2,32,256]{3,2,1,0:T(8,128)(2,1)S(1)} %get-tuple-element.62, bf16[8,2,32,256]{3,2,1,0:T(8,128)(2,1)S(1)} %collective-permute-done.10) | non-fusion elementwise | flops 131072 | bytes 786432 | tf_op jit(solution)/shard_map/add | solution.py:507
  37.4 5.4 %collective-permute-done.9 = bf16[64,2048]{1,0:T(8,128)(2,1)S(1)} collective-permute-done((bf16[64,2048]{1,0:T(8,128)(2,1)S(1)}, bf16[64,2048]{1,0:T(8,128)(2,1)S(1)}, u32[]{:S(2)}, u32[]{:S(2)}) %collective-permute-start.9) | collective-permute-done | bytes 262176 | tf_op jit(solution)/shard_map/ppermute | solution.py:496
  42.8 0.8 %add_convert_fusion = bf16[64,2048]{1,0:T(8,128)(2,1)} fusion(f32[64,2048]{1,0:T(8,128)S(1)} %keep.1, bf16[64,2048]{1,0:T(8,128)(2,1)S(1)} %collective-permute-done.9), kind=kLoop, calls=%fused_computation | loop fusion | flops 393216 | bytes 1048576 | tf_op jit(solution)/shard_map/convert_element_type | solution.py:508
  (26 shorter events, 0.2 us)
Async XLA Ops:
  3.9 18.6 %copy-start.5 = (bf16[128,512]{1,0:T(8,128)(2,1)S(1)}, bf16[128,512]{1,0:T(8,128)(2,1)}, u32[]{:S(2)}) copy-start(bf16[128,512]{1,0:T(8,128)(2,1)} %get-tuple-element.47.refs_0_) | copy-start | bytes 393220
  3.9 18.6 %copy-start.6 = (s32[16]{0:T(128)S(1)}, s32[16]{0:T(128)}, u32[]{:S(2)}) copy-start(s32[16]{0:T(128)} %block_ref.7) | copy-start | bytes 196
  3.9 18.6 %copy-start.7 = (s32[4]{0:T(128)S(1)}, s32[4]{0:T(128)}, u32[]{:S(2)}) copy-start(s32[4]{0:T(128)} %len_ref.5) | copy-start | bytes 52
  3.9 7.6 %collective-permute-start = (bf16[128,512]{1,0:T(8,128)(2,1)}, bf16[128,512]{1,0:T(8,128)(2,1)S(1)}, u32[]{:S(2)}, u32[]{:S(2)}) collective-permute-start(bf16[128,512]{1,0:T(8,128)(2,1)} %get-tuple-element.47.refs_0_), channel_id=1, source_target_pairs={{0,4},{2,6},{4,0},{6,2},{8,12},{10,14},{12,8},{14,10},{16,20},{18,... | collective-permute-start | bytes 393224 | tf_op jit(solution)/shard_map/ppermute | solution.py:362
  6.9 7.9 %collective-permute-start.1 = (bf16[128,512]{1,0:T(8,128)(2,1)}, bf16[128,512]{1,0:T(8,128)(2,1)S(1)}, u32[]{:S(2)}, u32[]{:S(2)}) collective-permute-start(bf16[128,512]{1,0:T(8,128)(2,1)} %get-tuple-element.47.refs_0_), channel_id=1, source_target_pairs={{0,24},{2,26},{4,28},{6,30},{8,0},{10,2},{12,4},{14,6},{16,8},{18,... | collective-permute-start | bytes 393224 | tf_op jit(solution)/shard_map/ppermute | solution.py:383
  10.5 8.2 %collective-permute-start.2 = (bf16[128,512]{1,0:T(8,128)(2,1)}, bf16[128,512]{1,0:T(8,128)(2,1)S(1)}, u32[]{:S(2)}, u32[]{:S(2)}) collective-permute-start(bf16[128,512]{1,0:T(8,128)(2,1)} %get-tuple-element.47.refs_0_), channel_id=1, source_target_pairs={{0,8},{2,10},{4,12},{6,14},{8,16},{10,18},{12,20},{14,22},{16,24},... | collective-permute-start | bytes 393224 | tf_op jit(solution)/shard_map/ppermute | solution.py:383
  10.5 11.4 %collective-permute-start.3 = (bf16[128,512]{1,0:T(8,128)(2,1)}, bf16[128,512]{1,0:T(8,128)(2,1)S(1)}, u32[]{:S(2)}, u32[]{:S(2)}) collective-permute-start(bf16[128,512]{1,0:T(8,128)(2,1)} %get-tuple-element.47.refs_0_), channel_id=1, source_target_pairs={{0,16},{2,18},{4,20},{6,22},{8,24},{10,26},{12,28},{14,30},{16,0},... | collective-permute-start | bytes 393224 | tf_op jit(solution)/shard_map/ppermute | solution.py:383
  14.5 7.9 %collective-permute-start.7 = (bf16[128,512]{1,0:T(8,128)(2,1)}, bf16[128,512]{1,0:T(8,128)(2,1)S(1)}, u32[]{:S(2)}, u32[]{:S(2)}) collective-permute-start(bf16[128,512]{1,0:T(8,128)(2,1)} %query.1.q_ref), channel_id=1, source_target_pairs={{0,2},{2,0},{4,6},{6,4},{8,10},{10,8},{12,14},{14,12},{16,18},{18,... | collective-permute-start | bytes 393224 | tf_op jit(solution)/shard_map/ppermute | solution.py:362
  14.8 10.2 %collective-permute-start.4 = (bf16[128,512]{1,0:T(8,128)(2,1)S(1)}, bf16[128,512]{1,0:T(8,128)(2,1)S(1)}, u32[]{:S(2)}, u32[]{:S(2)}) collective-permute-start(bf16[128,512]{1,0:T(8,128)(2,1)S(1)} %collective-permute-done.1.refs_2_), channel_id=1, source_target_pairs={{0,4},{2,6},{4,0},{6,2},{8,12},{10,14},{12,8},{14,10},{16,20},{18,... | collective-permute-start | bytes 393224 | tf_op jit(solution)/shard_map/ppermute | solution.py:362
  18.7 10.2 %collective-permute-start.5 = (bf16[128,512]{1,0:T(8,128)(2,1)S(1)}, bf16[128,512]{1,0:T(8,128)(2,1)S(1)}, u32[]{:S(2)}, u32[]{:S(2)}) collective-permute-start(bf16[128,512]{1,0:T(8,128)(2,1)S(1)} %collective-permute-done.2.refs_3_), channel_id=1, source_target_pairs={{0,4},{2,6},{4,0},{6,2},{8,12},{10,14},{12,8},{14,10},{16,20},{18,... | collective-permute-start | bytes 393224 | tf_op jit(solution)/shard_map/ppermute | solution.py:362
  21.9 7.0 %collective-permute-start.6 = (bf16[128,512]{1,0:T(8,128)(2,1)S(1)}, bf16[128,512]{1,0:T(8,128)(2,1)S(1)}, u32[]{:S(2)}, u32[]{:S(2)}) collective-permute-start(bf16[128,512]{1,0:T(8,128)(2,1)S(1)} %collective-permute-done.3.refs_0_.refs_4_), channel_id=1, source_target_pairs={{0,4},{2,6},{4,0},{6,2},{8,12},{10,14},{12,8},{14,10},{16,20},{18,... | collective-permute-start | bytes 393224 | tf_op jit(solution)/shard_map/ppermute | solution.py:362
  22.5 0.9 %copy-start.2 = (bf16[128,512]{1,0:T(8,128)(2,1)S(1)}, bf16[128,512]{1,0:T(8,128)(2,1)}, u32[]{:S(2)}) copy-start(bf16[128,512]{1,0:T(8,128)(2,1)} %query.1.q_ref) | copy-start | bytes 393220
  23.4 5.5 %copy-start.4 = (bf16[128,512]{1,0:T(8,128)(2,1)S(1)}, bf16[128,512]{1,0:T(8,128)(2,1)}, u32[]{:S(2)}) copy-start(bf16[128,512]{1,0:T(8,128)(2,1)} %query.1.q_ref) | copy-start | bytes 393220
  25.0 0.9 %copy-start.3 = (bf16[128,512]{1,0:T(8,128)(2,1)S(1)}, bf16[128,512]{1,0:T(8,128)(2,1)}, u32[]{:S(2)}) copy-start(bf16[128,512]{1,0:T(8,128)(2,1)} %query.1.q_ref) | copy-start | bytes 393220
  25.9 6.0 %copy-start.8 = (s32[64]{0:T(128)S(1)}, s32[64]{0:T(128)}, u32[]{:S(2)}) copy-start(s32[64]{0:T(128)} %slot_ref.1) | copy-start | bytes 772
  28.9 4.9 %copy-start = (bf16[512,2048]{1,0:T(8,128)(2,1)S(1)}, bf16[512,2048]{1,0:T(8,128)(2,1)}, u32[]{:S(2)}) copy-start(bf16[512,2048]{1,0:T(8,128)(2,1)} %wo_ref.3) | copy-start | bytes 6291460
  31.9 4.2 %copy-start.1 = (bf16[128,2048]{1,0:T(8,128)(2,1)S(1)}, bf16[128,2048]{1,0:T(8,128)(2,1)}, u32[]{:S(2)}) copy-start(bf16[128,2048]{1,0:T(8,128)(2,1)} %tok_ref.1) | copy-start | bytes 1572868
  31.9 1.9 %collective-permute-start.8 = (bf16[128,640]{1,0:T(8,128)(2,1)S(1)}, bf16[128,640]{1,0:T(8,128)(2,1)S(1)}, u32[]{:S(2)}, u32[]{:S(2)}) collective-permute-start(bf16[128,640]{1,0:T(8,128)(2,1)S(1)} %get-tuple-element.59), channel_id=1, source_target_pairs={{0,2},{2,0},{4,6},{6,4},{8,10},{10,8},{12,14},{14,12},{16,18},{18,... | collective-permute-start | bytes 491528 | tf_op jit(solution)/shard_map/ppermute | solution.py:362
  33.2 3.4 %collective-permute-start.10 = (bf16[8,2,32,256]{3,2,1,0:T(8,128)(2,1)S(1)}, bf16[8,2,32,256]{3,2,1,0:T(8,128)(2,1)S(1)}, u32[]{:S(2)}, u32[]{:S(2)}) collective-permute-start(bf16[8,2,32,256]{3,2,1,0:T(8,128)(2,1)S(1)} %get-tuple-element.63), channel_id=1, source_target_pairs={{0,2},{2,0},{4,6},{6,4},{8,10},{10,8},{12,14},{14,12},{16,18},{18,... | collective-permute-start | bytes 786440 | tf_op jit(solution)/shard_map/ppermute | solution.py:362
  34.5 8.3 %collective-permute-start.9 = (bf16[64,2048]{1,0:T(8,128)(2,1)S(1)}, bf16[64,2048]{1,0:T(8,128)(2,1)S(1)}, u32[]{:S(2)}, u32[]{:S(2)}) collective-permute-start(bf16[64,2048]{1,0:T(8,128)(2,1)S(1)} %get-tuple-element.61), channel_id=1, source_target_pairs={{0,1},{1,0},{2,3},{3,2},{4,5},{5,4},{6,7},{7,6},{8,9},{9,8},{10,11... | collective-permute-start | bytes 786440 | tf_op jit(solution)/shard_map/ppermute | solution.py:496

commit v4 on v3

--- a/solution.py
+++ b/solution.py
@@ -111,10 +111,10 @@
     return total
 
 
-def key_value_kernel(
-    block_hbm, len_hbm, freq_hbm, tok_hbm, gain_hbm, wk_ref, wv_ref,
-    normed_ref, kv_ref, cos_ref, sin_ref,
-    block_ref, len_ref, freq_ref, tok_ref, gain_ref, weights, small_sems, sems,
+def project_kernel(
+    block_hbm, len_hbm, freq_hbm, tok_hbm, gain_hbm, wk_hbm, wv_hbm, wq_hbm,
+    kv_ref, q_ref,
+    block_ref, len_ref, freq_ref, tok_ref, gain_ref, kv_weights, q_weights, small_sems, kv_sems, q_sems,
 ):
     small = [
         pltpu.make_async_copy(source, target, small_sems.at[i])
@@ -128,10 +128,12 @@
             )
         )
     ]
-    copies = weight_copies((wk_ref, wv_ref), weights, sems)
+    kv_copies = weight_copies((wk_hbm, wv_hbm), kv_weights, kv_sems)
+    q_copies = weight_copies((wq_hbm,), q_weights, q_sems)
     for copy in small:
         copy.start()
-    start_all(copies)
+    start_all(kv_copies)
+    start_all(q_copies)
     rows = tok_ref.shape[0]
     for copy in small[:3]:
         copy.wait()
@@ -140,45 +142,24 @@
     cosine, sine = jnp.cos(angle), jnp.sin(angle)
     lane = lax.broadcasted_iota(jnp.int32, (rows, HEAD), 1)
     sine = jnp.where(lane < HEAD // 2, -sine, sine)
-    cos_ref[...] = cosine
-    sin_ref[...] = sine
     for copy in small[3:]:
         copy.wait()
     wide = tok_ref[...].astype(f32)
     scale = lax.rsqrt(jnp.mean(wide * wide, -1, keepdims=True) + EPS)
     normed = (wide * scale * gain_ref[...]).astype(bf16)
-    normed_ref[...] = normed
-    product = stepped_dot(normed, copies, weights)
-    key_width = wk_ref.shape[1]
+    product = stepped_dot(normed, kv_copies, kv_weights)
+    key_width = wk_hbm.shape[1]
     for h in range(key_width // HEAD):
         cols = slice(h * HEAD, (h + 1) * HEAD)
         kv_ref[:, cols] = rotate(product[:, cols], cosine, sine).astype(bf16)
     kv_ref[:, key_width:] = product[:, key_width:].astype(bf16)
-
-
-def query_kernel(
-    normed_hbm, cos_hbm, sin_hbm, wq_ref, q_ref, normed_ref, cos_ref, sin_ref, weights, small_sems, sems,
-):
-    small = [
-        pltpu.make_async_copy(source, target, small_sems.at[i])
-        for i, (source, target) in enumerate(
-            ((normed_hbm, normed_ref), (cos_hbm, cos_ref), (sin_hbm, sin_ref))
-        )
-    ]
-    copies = weight_copies((wq_ref,), weights, sems)
-    for copy in small:
-        copy.start()
-    start_all(copies)
-    for copy in small:
-        copy.wait()
-    cosine, sine = cos_ref[...], sin_ref[...]
-    product = stepped_dot(normed_ref[...], copies, weights)
-    for h in range(wq_ref.shape[1] // HEAD):
+    product = stepped_dot(normed, q_copies, q_weights)
+    for h in range(wq_hbm.shape[1] // HEAD):
         cols = slice(h * HEAD, (h + 1) * HEAD)
         q_ref[:, cols] = rotate(product[:, cols], cosine, sine).astype(bf16)
 
 
-def attend_kernel(sources, first, last, block_ref, len_ref, q_ref, far_ref, *refs):
+def attend_kernel(sources, block_ref, len_ref, q_ref, far_ref, *refs):
     pieces, refs = refs[: len(sources)], refs[len(sources) :]
     shard = lax.axis_index("seq")
     rows, q_width = q_ref.shape
@@ -224,19 +205,13 @@
             out.append((new_top, total, acc))
         return tuple(out)
 
-    if first:
-        state = (
-            (
-                jnp.full((group * both, 1), FLOOR, f32),
-                jnp.zeros((group * both, 1), f32),
-                jnp.zeros((group * both, HEAD), f32),
-            ),
-        ) * kv_heads
-    else:
-        (top_ref, total_ref, acc_ref), refs = refs[:3], refs[3:]
-        state = tuple(
-            (top_ref[g][:, :1], total_ref[g][:, :1], acc_ref[g]) for g in range(kv_heads)
-        )
+    state = (
+        (
+            jnp.full((group * both, 1), FLOOR, f32),
+            jnp.zeros((group * both, 1), f32),
+            jnp.zeros((group * both, HEAD), f32),
+        ),
+    ) * kv_heads
     if all(count == 1 for count, _ in sources):
         for i in range(0, len(sources), 2):
             span = range(i, min(i + 2, len(sources)))
@@ -252,14 +227,6 @@
 
             state = lax.fori_loop(0, count, step, state)
 
-    if not last:
-        top_ref, total_ref, acc_ref = refs
-        for g in range(kv_heads):
-            top, total, acc = state[g]
-            top_ref[g] = jnp.broadcast_to(top, acc.shape)
-            total_ref[g] = jnp.broadcast_to(total, acc.shape)
-            acc_ref[g] = acc
-        return
     mine_ref, stat_ref, packed_ref = refs
     heads = q_width // HEAD
     lane = lax.broadcasted_iota(jnp.int32, (rows, HEAD), 1)
@@ -286,26 +253,33 @@
     packed_ref[:, q_width:] = parts.astype(bf16)
 
 
-def merge_kernel(mine_ref, stat_ref, packed_ref, wo_ref, sent_ref, kept_ref):
-    rows, q_width = mine_ref.shape
+def merge_kernel(wo_ref, *refs):
+    partials, (sent_ref, kept_ref) = refs[:-2], refs[-2:]
+    rows, q_width = partials[0].shape
     heads = q_width // HEAD
     half = rows // 2
-    near = stat_ref[...]
-    parts = packed_ref[:, q_width:].astype(f32)
-    far = parts
-    for t in (1, 2):
-        far = far + pltpu.roll(parts, HEAD - 2 * heads * t, 1)
-    top = jnp.maximum(near, far)
-    near_part, far_part = jnp.exp2(near - top), jnp.exp2(far - top)
-    near_total, far_total = pltpu.roll(near, HEAD - heads, 1), pltpu.roll(far, HEAD - heads, 1)
-    total = near_total * near_part + far_total * far_part
-    near_part, far_part = near_part / total, far_part / total
+    held = []
+    for mine_ref, stat_ref, packed_ref in zip(partials[::3], partials[1::3], partials[2::3]):
+        parts = packed_ref[:, q_width:].astype(f32)
+        stats = parts
+        for t in (1, 2):
+            stats = stats + pltpu.roll(parts, HEAD - 2 * heads * t, 1)
+        held += [(mine_ref, stat_ref[...]), (packed_ref, stats)]
+    top = functools.reduce(jnp.maximum, [stats for _, stats in held])
+    shares = [jnp.exp2(stats - top) for _, stats in held]
+    total = sum(
+        share * pltpu.roll(stats, HEAD - heads, 1) for share, (_, stats) in zip(shares, held)
+    )
+    shares = [share / total for share in shares]
     joined = []
     for h in range(heads):
         cols = slice(h * HEAD, (h + 1) * HEAD)
-        ours = mine_ref[:, cols] * near_part[:, h : h + 1]
-        theirs = packed_ref[:, cols].astype(f32) * far_part[:, h : h + 1]
-        joined.append((ours + theirs).astype(bf16))
+        joined.append(
+            sum(
+                ref[:, cols].astype(f32) * share[:, h : h + 1]
+                for (ref, _), share in zip(held, shares)
+            ).astype(bf16)
+        )
     context = jnp.concatenate(joined, 1)
     upper = lax.axis_index("req") == 0
     kept_ref[...] = jnp.where(upper, context[:half], context[half:])
@@ -383,7 +357,7 @@
         turned = lax.ppermute(kv, "seq", [(i, (i + 4 * shift) % n) for i in range(n)])
         along.append((turned, moved(shift, 0)))
         across.append((swap(turned, n, 2), moved(shift, 2)))
-    groups = [[own, beside] + along[:2], along[2:] + across[:-2], across[-2:]]
+    groups = [[own, beside] + along[::2], along[1::2] + across[:1], across[1:]]
     return [tuple(zip(*group)) for group in groups if group]
 
 
@@ -394,18 +368,11 @@
     half = rows // 2
     q_width = w_query.shape[1]
     kv_width = key_projection.shape[1] + value_projection.shape[1]
-    kv_heads = key_projection.shape[1] // HEAD
-    stacked = 2 * rows * q_width // (kv_heads * HEAD)
-    normed, kv, cosine, sine = pl.pallas_call(
-        key_value_kernel,
-        out_shape=(
-            struct((rows, width), bf16),
-            struct((rows, kv_width), bf16),
-            struct((rows, HEAD), f32),
-            struct((rows, HEAD), f32),
-        ),
-        in_specs=in_hbm(7),
-        out_specs=tuple(in_vmem(4)),
+    kv, queries = pl.pallas_call(
+        project_kernel,
+        out_shape=(struct((rows, kv_width), bf16), struct((rows, q_width), bf16)),
+        in_specs=in_hbm(8),
+        out_specs=tuple(in_vmem(2)),
         scratch_shapes=[
             pltpu.SMEM(block_split.shape, jnp.int32),
             pltpu.SMEM(lengths.shape, jnp.int32),
@@ -413,63 +380,39 @@
             pltpu.VMEM((rows, width), bf16),
             pltpu.VMEM((1, width), f32),
             pltpu.VMEM((width, kv_width), bf16),
+            pltpu.VMEM((width, q_width), bf16),
             pltpu.SemaphoreType.DMA((5,)),
             pltpu.SemaphoreType.DMA((WEIGHT_STEPS, 2)),
-        ],
-        compiler_params=kernel_params(62),
-        cost_estimate=cost(2 * rows * width * kv_width, 2 * width * kv_width),
-        name="key_value",
-    )(
-        block_split, lengths, inverse_frequencies(), tokens, norm_gain.reshape(1, width),
-        key_projection, value_projection,
-    )
-    groups = gather_shards(kv, n)
-    if len(groups[0][0]) > 1:
-        (own, beside, *others), sources = groups[0]
-        normed, beside = lax.optimization_barrier((normed, beside))
-        groups[0] = ((own, beside, *others), sources)
-    queries = pl.pallas_call(
-        query_kernel,
-        out_shape=struct((rows, q_width), bf16),
-        in_specs=in_hbm(4),
-        out_specs=in_vmem(1)[0],
-        scratch_shapes=[
-            pltpu.VMEM((rows, width), bf16),
-            pltpu.VMEM((rows, HEAD), f32),
-            pltpu.VMEM((rows, HEAD), f32),
-            pltpu.VMEM((width, q_width), bf16),
-            pltpu.SemaphoreType.DMA((3,)),
             pltpu.SemaphoreType.DMA((WEIGHT_STEPS, 1)),
         ],
         compiler_params=kernel_params(62),
-        cost_estimate=cost(2 * rows * width * q_width, 2 * width * q_width),
-        name="query",
-    )(normed, cosine, sine, w_query)
+        cost_estimate=cost(2 * rows * width * (kv_width + q_width), 2 * width * (kv_width + q_width)),
+        name="project",
+    )(
+        block_split, lengths, inverse_frequencies(), tokens, norm_gain.reshape(1, width),
+        key_projection, value_projection, w_query,
+    )
+    groups = gather_shards(kv, n)
     far_queries = swap(queries, n, 1)
 
-    state = ()
-    for i, (arrays, sources) in enumerate(groups):
-        first, last = i == 0, i == len(groups) - 1
-        if last:
-            shapes = (
+    partials = []
+    for arrays, sources in groups:
+        keys = sum(count for count, _ in sources) * rows
+        mine, stats, packed = pl.pallas_call(
+            functools.partial(attend_kernel, sources),
+            out_shape=(
                 struct((rows, q_width), f32),
                 struct((rows, HEAD), f32),
                 struct((rows, q_width + HEAD), bf16),
-            )
-        else:
-            shapes = (struct((kv_heads, stacked, HEAD), f32),) * 3
-        keys = sum(count for count, _ in sources) * rows
-        state = pl.pallas_call(
-            functools.partial(attend_kernel, sources, first, last),
-            out_shape=shapes,
-            in_specs=in_smem(2) + in_vmem(2 + len(arrays) + len(state)),
-            out_specs=tuple(in_vmem(len(shapes))),
+            ),
+            in_specs=in_smem(2) + in_vmem(2 + len(arrays)),
+            out_specs=tuple(in_vmem(3)),
             compiler_params=kernel_params(32),
             cost_estimate=cost(8 * rows * keys * q_width, 2 * keys * kv_width),
             name="attend",
-        )(block_split, lengths, queries, far_queries, *arrays, *state)
-    mine, stats, packed = state
-    packed = swap(packed, n, 1)
+        )(block_split, lengths, queries, far_queries, *arrays)
+        partials += [mine, stats, swap(packed, n, 1)]
+        queries, partials[-2] = lax.optimization_barrier((queries, stats))
     arrays = [x for held, _ in groups for x in held]
     sources = [s for _, where in groups for s in where]
     arrays, mine = lax.optimization_barrier((arrays, mine))
@@ -483,16 +426,16 @@
         cost_estimate=cost(0, 4 * rows * kv_width),
         name="cache",
     )(block_split, page_slot, *arrays)
-    mine, cache, other = lax.optimization_barrier((mine, cache, other))
+    partials[-3], cache, other = lax.optimization_barrier((mine, cache, other))
     sent, kept = pl.pallas_call(
         merge_kernel,
         out_shape=(struct((half, width), bf16), struct((half, q_width), bf16)),
-        in_specs=in_vmem(4),
+        in_specs=in_vmem(1 + len(partials)),
         out_specs=tuple(in_vmem(2)),
         compiler_params=kernel_params(24),
         cost_estimate=cost(rows * width * q_width, 2 * width * q_width),
         name="merge",
-    )(mine, stats, packed, w_out)
+    )(w_out, *partials)
     received = lax.ppermute(sent, "req", [(i, (i + 1) % parts) for i in range(parts)])
     kept = pl.pallas_call(
         keep_kernel,

time: 43.8 us -> 44 us (level)
  Pallas kernels: 16.2 us -> 11.3 us
  starting transfers between devices: 11.7 us -> 14.9 us
  local copies, waits for them, and re-layouts: 1.84 us -> 3.63 us
    pallas_call x5 -> x4, Pallas kernels: 13.7 us -> 8.34 us  [the longest x1 4.32 us: on_device(): pl.pallas_call(project_kernel, out_shape=(struct((rows, kv_width), bf16),...]
    unnamed x18, local copies, waits for them, and re-layouts: 1.84 us -> 3.63 us
    ppermute x7 -> x9, starting transfers between devices: 5.51 us -> 7.24 us  [swap(): return lax.ppermute(x, 'seq', [(i, i ^ bit) for i in range(n)])]
    ppermute x3, starting transfers between devices: 4.62 us -> 6.11 us  [gather_shards(): lax.ppermute(kv, 'seq', [(i, (i + 4 * shift) % n) for i in range(n)])]
    pallas_call x1, Pallas kernels: 0.74 us -> 1.2 us  [on_device(): pl.pallas_call(merge_kernel, out_shape=(struct((half, width), bf16), stru...]
  transfers between devices with their start and end apart: 11 -> 13, of which waited for: 4 -> 4; matrix products, arithmetic and copies ran while one was open for 2% -> 2% of each run, Pallas kernels for 23% -> 16%
where the time goes in v4:
time: 44 us; the launch traced here: 43.8 us
  starting transfers between devices  14.9 us (34%)
  waiting for transfers between devices  11.6 us (26%)
  Pallas kernels  11.3 us (26%)
  local copies, waits for them, and re-layouts  3.63 us (8%)
  other arithmetic  1.54 us (4%)
  between operations  0.8 us (2%)
    ppermute x9, starting transfers between devices, swap(): return lax.ppermute(x, 'seq', [(i, i ^ bit) for i in range(n)])  7.24 us
    ppermute x3, waiting for transfers between devices, gather_shards(): lax.ppermute(kv, 'seq', [(i, (i + 4 * shift) % n) for i in range(n)])  6.18 us
    ppermute x3, starting transfers between devices, gather_shards(): lax.ppermute(kv, 'seq', [(i, (i + 4 * shift) % n) for i in range(n)])  6.11 us
    ppermute x1, waiting for transfers between devices, on_device(): lax.ppermute(sent, 'req', [(i, (i + 1) % parts) for i in range(parts)])  5.42 us
    pallas_call x1, Pallas kernels, on_device(): pl.pallas_call(project_kernel, out_shape=(struct((rows, kv_width), bf16),...  4.32 us
    pallas_call x3, Pallas kernels, on_device(): pl.pallas_call(functools.partial(attend_kernel, sources), out_shape=(stru...  4.02 us
    unnamed x18, local copies, waits for them, and re-layouts  3.63 us
    ppermute x1, starting transfers between devices, on_device(): lax.ppermute(sent, 'req', [(i, (i + 1) % parts) for i in range(parts)])  1.59 us
  transfers between devices with their start and end apart: 13, of which 4 were waited for; matrix products, arithmetic and copies ran while one was open for 2% of the time, Pallas kernels for 16%

profile of v4, /device:TPU:0, one launch (start us, length us, event | category | flops | bytes accessed | tf_op | source)
XLA Modules:
  0.0 43.8 jit_solution(3269951577433089566)
XLA Ops:
  0.7 4.3 %project.1 = (bf16[128,512]{1,0:T(8,128)(2,1)}, bf16[128,512]{1,0:T(8,128)(2,1)}) custom-call(s32[16]{0:T(128)} %block_ref.7, s32[4]{0:T(128)} %len_ref.5, f32[1,128]{1,0:T(1,128)} %constant.2.clone.freq_hbm, bf16[128,2048]{1,0:T(8,128)(2,1)} %tok_ref.1, f32[1,2048]{1,0:T(1,128)} %bitcast.1, bf16[2048,256]{1,0:T(8,128)(2,1)} %wk_hbm.1, ...), custom_call_target="tpu_custom_call" | custom-call | flops 536870912 | bytes 4194304 | tf_op jit(solution)/shard_map/project/pallas_call | solution.py:371
  5.0 5.1 %collective-permute-start.2 = (bf16[128,512]{1,0:T(8,128)(2,1)}, bf16[128,512]{1,0:T(8,128)(2,1)S(1)}, u32[]{:S(2)}, u32[]{:S(2)}) collective-permute-start(bf16[128,512]{1,0:T(8,128)(2,1)} %get-tuple-element.48.refs_0_), channel_id=1, source_target_pairs={{0,24},{2,26},{4,28},{6,30},{8,0},{10,2},{12,4},{14,6},{16,8},{18,... | collective-permute-start | bytes 393224 | tf_op jit(solution)/shard_map/ppermute | solution.py:357
  10.1 1.0 %collective-permute-start.3 = (bf16[128,512]{1,0:T(8,128)(2,1)}, bf16[128,512]{1,0:T(8,128)(2,1)S(1)}, u32[]{:S(2)}, u32[]{:S(2)}) collective-permute-start(bf16[128,512]{1,0:T(8,128)(2,1)} %get-tuple-element.48.refs_0_), channel_id=1, source_target_pairs={{0,16},{2,18},{4,20},{6,22},{8,24},{10,26},{12,28},{14,30},{16,0},... | collective-permute-start | bytes 393224 | tf_op jit(solution)/shard_map/ppermute | solution.py:357
  11.1 1.5 %collective-permute-start.1 = (bf16[128,512]{1,0:T(8,128)(2,1)}, bf16[128,512]{1,0:T(8,128)(2,1)S(1)}, u32[]{:S(2)}, u32[]{:S(2)}) collective-permute-start(bf16[128,512]{1,0:T(8,128)(2,1)} %get-tuple-element.48.refs_0_), channel_id=1, source_target_pairs={{0,4},{2,6},{4,0},{6,2},{8,12},{10,14},{12,8},{14,10},{16,20},{18,... | collective-permute-start | bytes 393224 | tf_op jit(solution)/shard_map/ppermute | solution.py:336
  12.6 1.7 %collective-permute-done.2.refs_2_ = bf16[128,512]{1,0:T(8,128)(2,1)S(1)} collective-permute-done((bf16[128,512]{1,0:T(8,128)(2,1)}, bf16[128,512]{1,0:T(8,128)(2,1)S(1)}, u32[]{:S(2)}, u32[]{:S(2)}) %collective-permute-start.2) | collective-permute-done | bytes 131104 | tf_op jit(solution)/shard_map/ppermute | solution.py:357
  14.3 1.5 %collective-permute-start.6 = (bf16[128,512]{1,0:T(8,128)(2,1)S(1)}, bf16[128,512]{1,0:T(8,128)(2,1)S(1)}, u32[]{:S(2)}, u32[]{:S(2)}) collective-permute-start(bf16[128,512]{1,0:T(8,128)(2,1)S(1)} %collective-permute-done.2.refs_2_), channel_id=1, source_target_pairs={{0,4},{2,6},{4,0},{6,2},{8,12},{10,14},{12,8},{14,10},{16,20},{18,... | collective-permute-start | bytes 393224 | tf_op jit(solution)/shard_map/ppermute | solution.py:336
  15.8 2.8 %collective-permute-done.5.refs_0_.refs_4_ = bf16[128,512]{1,0:T(8,128)(2,1)S(1)} collective-permute-done((bf16[128,512]{1,0:T(8,128)(2,1)}, bf16[128,512]{1,0:T(8,128)(2,1)S(1)}, u32[]{:S(2)}, u32[]{:S(2)}) %collective-permute-start.5) | collective-permute-done | bytes 131104 | tf_op jit(solution)/shard_map/ppermute | solution.py:357
  18.6 1.5 %collective-permute-start.8 = (bf16[128,512]{1,0:T(8,128)(2,1)S(1)}, bf16[128,512]{1,0:T(8,128)(2,1)S(1)}, u32[]{:S(2)}, u32[]{:S(2)}) collective-permute-start(bf16[128,512]{1,0:T(8,128)(2,1)S(1)} %collective-permute-done.5.refs_0_.refs_4_), channel_id=1, source_target_pairs={{0,4},{2,6},{4,0},{6,2},{8,12},{10,14},{12,8},{14,10},{16,20},{18,... | collective-permute-start | bytes 393224 | tf_op jit(solution)/shard_map/ppermute | solution.py:336
  20.1 1.7 %collective-permute-done.3.refs_3_ = bf16[128,512]{1,0:T(8,128)(2,1)S(1)} collective-permute-done((bf16[128,512]{1,0:T(8,128)(2,1)}, bf16[128,512]{1,0:T(8,128)(2,1)S(1)}, u32[]{:S(2)}, u32[]{:S(2)}) %collective-permute-start.3) | collective-permute-done | bytes 131104 | tf_op jit(solution)/shard_map/ppermute | solution.py:357
  21.8 1.5 %collective-permute-start.9 = (bf16[128,512]{1,0:T(8,128)(2,1)S(1)}, bf16[128,512]{1,0:T(8,128)(2,1)S(1)}, u32[]{:S(2)}, u32[]{:S(2)}) collective-permute-start(bf16[128,512]{1,0:T(8,128)(2,1)S(1)} %collective-permute-done.3.refs_3_), channel_id=1, source_target_pairs={{0,4},{2,6},{4,0},{6,2},{8,12},{10,14},{12,8},{14,10},{16,20},{18,... | collective-permute-start | bytes 393224 | tf_op jit(solution)/shard_map/ppermute | solution.py:336
  23.3 0.9 %copy-done.2 = bf16[128,512]{1,0:T(8,128)(2,1)S(1)} copy-done((bf16[128,512]{1,0:T(8,128)(2,1)S(1)}, bf16[128,512]{1,0:T(8,128)(2,1)}, u32[]{:S(2)}) %copy-start.2) | copy-done | bytes 131096
  24.2 0.9 %copy-done.4 = bf16[128,512]{1,0:T(8,128)(2,1)S(1)} copy-done((bf16[128,512]{1,0:T(8,128)(2,1)S(1)}, bf16[128,512]{1,0:T(8,128)(2,1)}, u32[]{:S(2)}) %copy-start.4) | copy-done | bytes 131096
  25.1 1.6 %attend.3 = (f32[128,512]{1,0:T(8,128)S(1)}, f32[128,128]{1,0:T(8,128)S(1)}, bf16[128,640]{1,0:T(8,128)(2,1)S(1)}) custom-call(s32[16]{0:T(128)S(1)} %copy-done.6, s32[4]{0:T(128)S(1)} %copy-done.7, bf16[128,512]{1,0:T(8,128)(2,1)S(1)} %copy-done.2, bf16[128,512]{1,0:T(8,128)(2,1)S(1)} %collective-permute-done.far_ref, bf16[128,512]{1,0:T(8,128)(2,1)S(1)} %copy-done.4, ...), custom_call_target="tpu_custom_call" | custom-call | flops 268435456 | bytes 524288 | tf_op jit(solution)/shard_map/attend/pallas_call | solution.py:401
  26.9 0.9 %copy-done.3 = bf16[128,512]{1,0:T(8,128)(2,1)S(1)} copy-done((bf16[128,512]{1,0:T(8,128)(2,1)S(1)}, bf16[128,512]{1,0:T(8,128)(2,1)}, u32[]{:S(2)}) %copy-start.3) | copy-done | bytes 131096
  27.8 1.2 %attend.4 = (f32[128,512]{1,0:T(8,128)S(1)}, f32[128,128]{1,0:T(8,128)S(1)}, bf16[128,640]{1,0:T(8,128)(2,1)S(1)}) custom-call(s32[16]{0:T(128)S(1)} %copy-done.6, s32[4]{0:T(128)S(1)} %copy-done.7, bf16[128,512]{1,0:T(8,128)(2,1)S(1)} %copy-done.3, bf16[128,512]{1,0:T(8,128)(2,1)S(1)} %collective-permute-done.far_ref, ...), custom_call_target="tpu_custom_call" | custom-call | flops 134217728 | bytes 262144 | tf_op jit(solution)/shard_map/attend/pallas_call | solution.py:401
  29.0 0.6 %collective-permute-start.7 = (bf16[128,640]{1,0:T(8,128)(2,1)S(1)}, bf16[128,640]{1,0:T(8,128)(2,1)S(1)}, u32[]{:S(2)}, u32[]{:S(2)}) collective-permute-start(bf16[128,640]{1,0:T(8,128)(2,1)S(1)} %get-tuple-element.44), channel_id=1, source_target_pairs={{0,2},{2,0},{4,6},{6,4},{8,10},{10,8},{12,14},{14,12},{16,18},{18,... | collective-permute-start | bytes 491528 | tf_op jit(solution)/shard_map/ppermute | solution.py:336
  29.5 1.2 %attend.5 = (f32[128,512]{1,0:T(8,128)S(1)}, f32[128,128]{1,0:T(8,128)S(1)}, bf16[128,640]{1,0:T(8,128)(2,1)S(1)}) custom-call(s32[16]{0:T(128)S(1)} %copy-done.6, s32[4]{0:T(128)S(1)} %copy-done.7, bf16[128,512]{1,0:T(8,128)(2,1)S(1)} %copy-done.3, bf16[128,512]{1,0:T(8,128)(2,1)S(1)} %collective-permute-done.far_ref, ...), custom_call_target="tpu_custom_call" | custom-call | flops 134217728 | bytes 262144 | tf_op jit(solution)/shard_map/attend/pallas_call | solution.py:401
  30.8 0.9 %copy-done.5 = bf16[128,512]{1,0:T(8,128)(2,1)S(1)} copy-done((bf16[128,512]{1,0:T(8,128)(2,1)S(1)}, bf16[128,512]{1,0:T(8,128)(2,1)}, u32[]{:S(2)}) %copy-start.5) | copy-done | bytes 131096
  31.7 1.2 %cache.1 = (bf16[8,2,32,256]{3,2,1,0:T(8,128)(2,1)S(1)}, bf16[8,2,32,256]{3,2,1,0:T(8,128)(2,1)S(1)}) custom-call(s32[16]{0:T(128)S(1)} %copy-done.6, s32[64]{0:T(128)S(1)} %copy-done.8, bf16[128,512]{1,0:T(8,128)(2,1)S(1)} %copy-done.5, bf16[128,512]{1,0:T(8,128)(2,1)S(1)} %collective-permute-done.1.refs_1_, ...), custom_call_target="tpu_custom_call" | custom-call | bytes 262144 | tf_op jit(solution)/shard_map/cache/pallas_call | solution.py:420
  33.5 1.2 %merge.1 = (bf16[64,2048]{1,0:T(8,128)(2,1)S(1)}, bf16[64,512]{1,0:T(8,128)(2,1)S(1)}) custom-call(bf16[512,2048]{1,0:T(8,128)(2,1)S(1)} %copy-done, f32[128,512]{1,0:T(8,128)S(1)} %get-tuple-element.36.refs_0_, f32[128,128]{1,0:T(8,128)S(1)} %get-tuple-element.38.refs_1_, bf16[128,640]{1,0:T(8,128)(2,1)S(1)} %collective-permute-done.4.refs_2_, ...), custom_call_target="tpu_custom_call" | custom-call | flops 134217728 | bytes 2097152 | tf_op jit(solution)/shard_map/merge/pallas_call | solution.py:430
  34.7 1.6 %collective-permute-start.11 = (bf16[64,2048]{1,0:T(8,128)(2,1)S(1)}, bf16[64,2048]{1,0:T(8,128)(2,1)S(1)}, u32[]{:S(2)}, u32[]{:S(2)}) collective-permute-start(bf16[64,2048]{1,0:T(8,128)(2,1)S(1)} %get-tuple-element.63), channel_id=1, source_target_pairs={{0,1},{1,0},{2,3},{3,2},{4,5},{5,4},{6,7},{7,6},{8,9},{9,8},{10,11... | collective-permute-start | bytes 786440 | tf_op jit(solution)/shard_map/ppermute | solution.py:439
  36.8 0.8 %add.7 = bf16[8,2,32,256]{3,2,1,0:T(8,128)(2,1)} add(bf16[8,2,32,256]{3,2,1,0:T(8,128)(2,1)S(1)} %get-tuple-element.64, bf16[8,2,32,256]{3,2,1,0:T(8,128)(2,1)S(1)} %collective-permute-done.12) | non-fusion elementwise | flops 131072 | bytes 786432 | tf_op jit(solution)/shard_map/add | solution.py:450
  37.6 5.4 %collective-permute-done.11 = bf16[64,2048]{1,0:T(8,128)(2,1)S(1)} collective-permute-done((bf16[64,2048]{1,0:T(8,128)(2,1)S(1)}, bf16[64,2048]{1,0:T(8,128)(2,1)S(1)}, u32[]{:S(2)}, u32[]{:S(2)}) %collective-permute-start.11) | collective-permute-done | bytes 262176 | tf_op jit(solution)/shard_map/ppermute | solution.py:439
  43.0 0.8 %add_convert_fusion = bf16[64,2048]{1,0:T(8,128)(2,1)} fusion(f32[64,2048]{1,0:T(8,128)S(1)} %keep.1, bf16[64,2048]{1,0:T(8,128)(2,1)S(1)} %collective-permute-done.11), kind=kLoop, calls=%fused_computation | loop fusion | flops 393216 | bytes 1048576 | tf_op jit(solution)/shard_map/convert_element_type | solution.py:451
  (29 shorter events, 1.3 us)
Async XLA Ops:
  0.6 22.7 %copy-start.6 = (s32[16]{0:T(128)S(1)}, s32[16]{0:T(128)}, u32[]{:S(2)}) copy-start(s32[16]{0:T(128)} %block_ref.7) | copy-start | bytes 196
  0.6 22.6 %copy-start.7 = (s32[4]{0:T(128)S(1)}, s32[4]{0:T(128)}, u32[]{:S(2)}) copy-start(s32[4]{0:T(128)} %len_ref.5) | copy-start | bytes 52
  0.7 30.2 %copy-start.8 = (s32[64]{0:T(128)S(1)}, s32[64]{0:T(128)}, u32[]{:S(2)}) copy-start(s32[64]{0:T(128)} %slot_ref.1) | copy-start | bytes 772
  5.0 28.5 %copy-start = (bf16[512,2048]{1,0:T(8,128)(2,1)S(1)}, bf16[512,2048]{1,0:T(8,128)(2,1)}, u32[]{:S(2)}) copy-start(bf16[512,2048]{1,0:T(8,128)(2,1)} %wo_ref.3) | copy-start | bytes 6291460
  5.0 9.3 %collective-permute-start.2 = (bf16[128,512]{1,0:T(8,128)(2,1)}, bf16[128,512]{1,0:T(8,128)(2,1)S(1)}, u32[]{:S(2)}, u32[]{:S(2)}) collective-permute-start(bf16[128,512]{1,0:T(8,128)(2,1)} %get-tuple-element.48.refs_0_), channel_id=1, source_target_pairs={{0,24},{2,26},{4,28},{6,30},{8,0},{10,2},{12,4},{14,6},{16,8},{18,... | collective-permute-start | bytes 393224 | tf_op jit(solution)/shard_map/ppermute | solution.py:357
  10.1 8.5 %collective-permute-start.5 = (bf16[128,512]{1,0:T(8,128)(2,1)}, bf16[128,512]{1,0:T(8,128)(2,1)S(1)}, u32[]{:S(2)}, u32[]{:S(2)}) collective-permute-start(bf16[128,512]{1,0:T(8,128)(2,1)} %get-tuple-element.48.refs_0_), channel_id=1, source_target_pairs={{0,8},{2,10},{4,12},{6,14},{8,16},{10,18},{12,20},{14,22},{16,24},... | collective-permute-start | bytes 393224 | tf_op jit(solution)/shard_map/ppermute | solution.py:357
  10.1 11.7 %collective-permute-start.3 = (bf16[128,512]{1,0:T(8,128)(2,1)}, bf16[128,512]{1,0:T(8,128)(2,1)S(1)}, u32[]{:S(2)}, u32[]{:S(2)}) collective-permute-start(bf16[128,512]{1,0:T(8,128)(2,1)} %get-tuple-element.48.refs_0_), channel_id=1, source_target_pairs={{0,16},{2,18},{4,20},{6,22},{8,24},{10,26},{12,28},{14,30},{16,0},... | collective-permute-start | bytes 393224 | tf_op jit(solution)/shard_map/ppermute | solution.py:357
  11.1 12.2 %collective-permute-start = (bf16[128,512]{1,0:T(8,128)(2,1)}, bf16[128,512]{1,0:T(8,128)(2,1)S(1)}, u32[]{:S(2)}, u32[]{:S(2)}) collective-permute-start(bf16[128,512]{1,0:T(8,128)(2,1)} %get-tuple-element.45.q_ref), channel_id=1, source_target_pairs={{0,2},{2,0},{4,6},{6,4},{8,10},{10,8},{12,14},{14,12},{16,18},{18,... | collective-permute-start | bytes 393224 | tf_op jit(solution)/shard_map/ppermute | solution.py:336
  11.1 12.2 %collective-permute-start.1 = (bf16[128,512]{1,0:T(8,128)(2,1)}, bf16[128,512]{1,0:T(8,128)(2,1)S(1)}, u32[]{:S(2)}, u32[]{:S(2)}) collective-permute-start(bf16[128,512]{1,0:T(8,128)(2,1)} %get-tuple-element.48.refs_0_), channel_id=1, source_target_pairs={{0,4},{2,6},{4,0},{6,2},{8,12},{10,14},{12,8},{14,10},{16,20},{18,... | collective-permute-start | bytes 393224 | tf_op jit(solution)/shard_map/ppermute | solution.py:336
  14.3 12.5 %collective-permute-start.6 = (bf16[128,512]{1,0:T(8,128)(2,1)S(1)}, bf16[128,512]{1,0:T(8,128)(2,1)S(1)}, u32[]{:S(2)}, u32[]{:S(2)}) collective-permute-start(bf16[128,512]{1,0:T(8,128)(2,1)S(1)} %collective-permute-done.2.refs_2_), channel_id=1, source_target_pairs={{0,4},{2,6},{4,0},{6,2},{8,12},{10,14},{12,8},{14,10},{16,20},{18,... | collective-permute-start | bytes 393224 | tf_op jit(solution)/shard_map/ppermute | solution.py:336
  18.6 10.9 %collective-permute-start.8 = (bf16[128,512]{1,0:T(8,128)(2,1)S(1)}, bf16[128,512]{1,0:T(8,128)(2,1)S(1)}, u32[]{:S(2)}, u32[]{:S(2)}) collective-permute-start(bf16[128,512]{1,0:T(8,128)(2,1)S(1)} %collective-permute-done.5.refs_0_.refs_4_), channel_id=1, source_target_pairs={{0,4},{2,6},{4,0},{6,2},{8,12},{10,14},{12,8},{14,10},{16,20},{18,... | collective-permute-start | bytes 393224 | tf_op jit(solution)/shard_map/ppermute | solution.py:336
  21.8 7.7 %collective-permute-start.9 = (bf16[128,512]{1,0:T(8,128)(2,1)S(1)}, bf16[128,512]{1,0:T(8,128)(2,1)S(1)}, u32[]{:S(2)}, u32[]{:S(2)}) collective-permute-start(bf16[128,512]{1,0:T(8,128)(2,1)S(1)} %collective-permute-done.3.refs_3_), channel_id=1, source_target_pairs={{0,4},{2,6},{4,0},{6,2},{8,12},{10,14},{12,8},{14,10},{16,20},{18,... | collective-permute-start | bytes 393224 | tf_op jit(solution)/shard_map/ppermute | solution.py:336
  23.3 0.9 %copy-start.2 = (bf16[128,512]{1,0:T(8,128)(2,1)S(1)}, bf16[128,512]{1,0:T(8,128)(2,1)}, u32[]{:S(2)}) copy-start(bf16[128,512]{1,0:T(8,128)(2,1)} %get-tuple-element.45.q_ref) | copy-start | bytes 393220
  24.2 0.9 %copy-start.4 = (bf16[128,512]{1,0:T(8,128)(2,1)S(1)}, bf16[128,512]{1,0:T(8,128)(2,1)}, u32[]{:S(2)}) copy-start(bf16[128,512]{1,0:T(8,128)(2,1)} %get-tuple-element.48.refs_0_) | copy-start | bytes 393220
  26.8 6.7 %collective-permute-start.4 = (bf16[128,640]{1,0:T(8,128)(2,1)S(1)}, bf16[128,640]{1,0:T(8,128)(2,1)S(1)}, u32[]{:S(2)}, u32[]{:S(2)}) collective-permute-start(bf16[128,640]{1,0:T(8,128)(2,1)S(1)} %get-tuple-element.39), channel_id=1, source_target_pairs={{0,2},{2,0},{4,6},{6,4},{8,10},{10,8},{12,14},{14,12},{16,18},{18,... | collective-permute-start | bytes 491528 | tf_op jit(solution)/shard_map/ppermute | solution.py:336
  26.9 0.9 %copy-start.3 = (bf16[128,512]{1,0:T(8,128)(2,1)S(1)}, bf16[128,512]{1,0:T(8,128)(2,1)}, u32[]{:S(2)}) copy-start(bf16[128,512]{1,0:T(8,128)(2,1)} %get-tuple-element.45.q_ref) | copy-start | bytes 393220
  29.0 4.6 %collective-permute-start.7 = (bf16[128,640]{1,0:T(8,128)(2,1)S(1)}, bf16[128,640]{1,0:T(8,128)(2,1)S(1)}, u32[]{:S(2)}, u32[]{:S(2)}) collective-permute-start(bf16[128,640]{1,0:T(8,128)(2,1)S(1)} %get-tuple-element.44), channel_id=1, source_target_pairs={{0,2},{2,0},{4,6},{6,4},{8,10},{10,8},{12,14},{14,12},{16,18},{18,... | collective-permute-start | bytes 491528 | tf_op jit(solution)/shard_map/ppermute | solution.py:336
  30.7 2.8 %collective-permute-start.10 = (bf16[128,640]{1,0:T(8,128)(2,1)S(1)}, bf16[128,640]{1,0:T(8,128)(2,1)S(1)}, u32[]{:S(2)}, u32[]{:S(2)}) collective-permute-start(bf16[128,640]{1,0:T(8,128)(2,1)S(1)} %get-tuple-element.61), channel_id=1, source_target_pairs={{0,2},{2,0},{4,6},{6,4},{8,10},{10,8},{12,14},{14,12},{16,18},{18,... | collective-permute-start | bytes 491528 | tf_op jit(solution)/shard_map/ppermute | solution.py:336
  30.8 0.9 %copy-start.5 = (bf16[128,512]{1,0:T(8,128)(2,1)S(1)}, bf16[128,512]{1,0:T(8,128)(2,1)}, u32[]{:S(2)}) copy-start(bf16[128,512]{1,0:T(8,128)(2,1)} %get-tuple-element.48.refs_0_) | copy-start | bytes 393220
  31.7 4.6 %copy-start.1 = (bf16[128,2048]{1,0:T(8,128)(2,1)S(1)}, bf16[128,2048]{1,0:T(8,128)(2,1)}, u32[]{:S(2)}) copy-start(bf16[128,2048]{1,0:T(8,128)(2,1)} %tok_ref.1) | copy-start | bytes 1572868
  33.0 3.9 %collective-permute-start.12 = (bf16[8,2,32,256]{3,2,1,0:T(8,128)(2,1)S(1)}, bf16[8,2,32,256]{3,2,1,0:T(8,128)(2,1)S(1)}, u32[]{:S(2)}, u32[]{:S(2)}) collective-permute-start(bf16[8,2,32,256]{3,2,1,0:T(8,128)(2,1)S(1)} %get-tuple-element.65), channel_id=1, source_target_pairs={{0,2},{2,0},{4,6},{6,4},{8,10},{10,8},{12,14},{14,12},{16,18},{18,... | collective-permute-start | bytes 786440 | tf_op jit(solution)/shard_map/ppermute | solution.py:336
  34.7 8.3 %collective-permute-start.11 = (bf16[64,2048]{1,0:T(8,128)(2,1)S(1)}, bf16[64,2048]{1,0:T(8,128)(2,1)S(1)}, u32[]{:S(2)}, u32[]{:S(2)}) collective-permute-start(bf16[64,2048]{1,0:T(8,128)(2,1)S(1)} %get-tuple-element.63), channel_id=1, source_target_pairs={{0,1},{1,0},{2,3},{3,2},{4,5},{5,4},{6,7},{7,6},{8,9},{9,8},{10,11... | collective-permute-start | bytes 786440 | tf_op jit(solution)/shard_map/ppermute | solution.py:439

commit v5 on v4

--- a/solution.py
+++ b/solution.py
@@ -159,11 +159,11 @@
         q_ref[:, cols] = rotate(product[:, cols], cosine, sine).astype(bf16)
 
 
-def attend_kernel(sources, block_ref, len_ref, q_ref, far_ref, *refs):
-    pieces, refs = refs[: len(sources)], refs[len(sources) :]
+def attend_kernel(pieces, block_ref, len_ref, q_ref, far_ref, *refs):
+    pieces, refs = with_refs(pieces, refs)
     shard = lax.axis_index("seq")
     rows, q_width = q_ref.shape
-    key_width = pieces[0].shape[1] // 2
+    key_width = pieces[0].arrays[0].shape[1] // 2
     kv_heads = key_width // HEAD
     group = q_width // key_width
     both = 2 * rows
@@ -212,20 +212,21 @@
             jnp.zeros((group * both, HEAD), f32),
         ),
     ) * kv_heads
-    if all(count == 1 for count, _ in sources):
-        for i in range(0, len(sources), 2):
-            span = range(i, min(i + 2, len(sources)))
+    if all(piece.count == 1 for piece in pieces):
+        for i in range(0, len(pieces), 2):
+            pair = pieces[i : i + 2]
             state = absorb(
-                state, [pieces[k][...] for k in span], [sources[k][1](shard, 0) for k in span]
+                state, [loaded(p, shard) for p in pair], [p.source_of(shard, 0) for p in pair]
             )
     else:
-        for ref, (count, source_of) in zip(pieces, sources):
+        for piece in pieces:
 
             def step(i, carried):
                 at = pl.multiple_of(i * rows, rows)
-                return absorb(carried, [ref[pl.ds(at, rows), :]], [source_of(shard, i)])
-
-            state = lax.fori_loop(0, count, step, state)
+                block = piece.arrays[0][pl.ds(at, rows), :]
+                return absorb(carried, [block], [piece.source_of(shard, i)])
+
+            state = lax.fori_loop(0, piece.count, step, state)
 
     mine_ref, stat_ref, packed_ref = refs
     heads = q_width // HEAD
@@ -294,17 +295,18 @@
     out_ref[...] = jnp.dot(context_ref[...], wo_ref[...], preferred_element_type=f32) + residual
 
 
-def cache_kernel(sources, block_ref, slot_ref, *refs):
-    pieces, (mine_ref, other_ref) = refs[: len(sources)], refs[len(sources) :]
+def cache_kernel(pieces, held, block_ref, slot_ref, *refs):
+    pieces, refs = with_refs(pieces, refs)
+    mine_ref, other_ref = refs[-2:]
     shard = lax.axis_index("seq")
     slots = mine_ref.shape[0]
     key_width = mine_ref.shape[3]
     rows = slots * PAGE // 2
     pages = rows // 2 // PAGE
-    mine_ref[...] = jnp.zeros_like(mine_ref)
-    other_ref[...] = jnp.zeros_like(other_ref)
-
-    def place(ref, at, source):
+    for i, target in enumerate((mine_ref, other_ref)):
+        target[...] = refs[i][...] if held else jnp.zeros_like(target)
+
+    def place(ref, at, source, wanted):
         for k, block in enumerate(blocks_of(block_ref, source)):
             for j in range(pages):
                 slot = slot_ref[block * pages + j]
@@ -315,50 +317,64 @@
                     offset = pl.multiple_of(offset, PAGE)
                 for target, owner in ((mine_ref, shard), (other_ref, shard ^ 1)):
 
-                    @pl.when(holder == owner)
+                    @pl.when((holder == owner) & wanted)
                     def _():
                         target[local, 0] = ref[pl.ds(offset, PAGE), :key_width]
                         target[local, 1] = ref[pl.ds(offset, PAGE), key_width:]
 
-    for ref, (count, source_of) in zip(pieces, sources):
-        if count == 1:
-            place(ref, 0, source_of(shard, 0))
+    for piece in pieces:
+        if piece.count == 1:
+            source = piece.source_of(shard, 0)
+            for i, ref in enumerate(piece.arrays):
+                place(ref, 0, source, True if piece.pick is None else piece.pick(shard) == bool(i))
         else:
 
             def step(i, carry):
-                place(ref, i * rows, source_of(shard, i))
+                place(piece.arrays[0], i * rows, piece.source_of(shard, i), True)
                 return carry
 
-            lax.fori_loop(0, count, step, 0)
+            lax.fori_loop(0, piece.count, step, 0)
 
 
 def swap(x, n, bit):
     return lax.ppermute(x, "seq", [(i, i ^ bit) for i in range(n)])
 
 
-def gather_shards(kv, n):
-    if n % 4 or n > 16:
-        same = [list(range(c, n, 2)) for c in range(2)]
-        everyone = lax.all_gather(kv, "seq", axis=0, tiled=True, axis_index_groups=same)
-        return [([everyone], [(n // 2, lambda shard, i: 2 * i + shard % 2)])]
-    outer = n // 4
-
-    def moved(shift, flip):
-        def source_of(shard, i):
-            plane = lax.rem(shard // 4 + outer - shift, outer)
-            return plane * 4 + ((shard % 4) ^ flip)
-
-        return 1, source_of
-
-    own, beside = (kv, moved(0, 0)), (swap(kv, n, 2), moved(0, 2))
-    shifts = sorted(range(1, outer), key=lambda s: (min(s, outer - s), -s))
-    along, across = [], []
-    for shift in shifts:
-        turned = lax.ppermute(kv, "seq", [(i, (i + 4 * shift) % n) for i in range(n)])
-        along.append((turned, moved(shift, 0)))
-        across.append((swap(turned, n, 2), moved(shift, 2)))
-    groups = [[own, beside] + along[::2], along[1::2] + across[:1], across[1:]]
-    return [tuple(zip(*group)) for group in groups if group]
+class Piece:
+    def __init__(self, arrays, source_of, count=1, pick=None):
+        self.arrays, self.source_of, self.count, self.pick = arrays, source_of, count, pick
+
+    def moved(self, arrays):
+        return Piece(arrays, self.source_of, self.count, self.pick)
+
+
+def operands(pieces):
+    return [x for piece in pieces for x in piece.arrays]
+
+
+def with_refs(pieces, refs):
+    out = []
+    for piece in pieces:
+        taken, refs = refs[: len(piece.arrays)], refs[len(piece.arrays) :]
+        out.append(piece.moved(taken))
+    return out, refs
+
+
+def loaded(piece, shard):
+    values = [ref[...] for ref in piece.arrays]
+    return values[0] if piece.pick is None else jnp.where(piece.pick(shard), values[1], values[0])
+
+
+def at_distance(bits):
+    return lambda shard, i: shard ^ bits
+
+
+def move(x, pairs):
+    return lax.ppermute(x, "seq", pairs)
+
+
+def outer_plane(i):
+    return (i // 4 == 0) | (i // 4 == 3)
 
 
 def on_device(
@@ -392,14 +408,13 @@
         block_split, lengths, inverse_frequencies(), tokens, norm_gain.reshape(1, width),
         key_projection, value_projection, w_query,
     )
-    groups = gather_shards(kv, n)
     far_queries = swap(queries, n, 1)
 
-    partials = []
-    for arrays, sources in groups:
-        keys = sum(count for count, _ in sources) * rows
+    def attend(pieces):
+        keys = sum(piece.count for piece in pieces) * rows
+        arrays = operands(pieces)
         mine, stats, packed = pl.pallas_call(
-            functools.partial(attend_kernel, sources),
+            functools.partial(attend_kernel, pieces),
             out_shape=(
                 struct((rows, q_width), f32),
                 struct((rows, HEAD), f32),
@@ -411,22 +426,66 @@
             cost_estimate=cost(8 * rows * keys * q_width, 2 * keys * kv_width),
             name="attend",
         )(block_split, lengths, queries, far_queries, *arrays)
-        partials += [mine, stats, swap(packed, n, 1)]
-        queries, partials[-2] = lax.optimization_barrier((queries, stats))
-    arrays = [x for held, _ in groups for x in held]
-    sources = [s for _, where in groups for s in where]
-    arrays, mine = lax.optimization_barrier((arrays, mine))
-    shape = (2 * rows // PAGE, 2, PAGE, kv_width // 2)
-    cache, other = pl.pallas_call(
-        functools.partial(cache_kernel, sources),
-        out_shape=(struct(shape, bf16),) * 2,
-        in_specs=in_smem(2) + in_vmem(len(arrays)),
-        out_specs=tuple(in_vmem(2)),
-        compiler_params=kernel_params(32),
-        cost_estimate=cost(0, 4 * rows * kv_width),
-        name="cache",
-    )(block_split, page_slot, *arrays)
-    partials[-3], cache, other = lax.optimization_barrier((mine, cache, other))
+        return [mine, stats, swap(packed, n, 1)]
+
+    def place_pages(pieces, held=()):
+        arrays = operands(pieces)
+        shape = (2 * rows // PAGE, 2, PAGE, kv_width // 2)
+        return pl.pallas_call(
+            functools.partial(cache_kernel, pieces, bool(held)),
+            out_shape=(struct(shape, bf16),) * 2,
+            in_specs=in_smem(2) + in_vmem(len(arrays) + len(held)),
+            out_specs=tuple(in_vmem(2)),
+            input_output_aliases={2 + len(arrays) + i: i for i in range(len(held))},
+            compiler_params=kernel_params(32),
+            cost_estimate=cost(0, 4 * rows * kv_width),
+            name="cache",
+        )(block_split, page_slot, *arrays, *held)
+
+    if n == 16:
+        everyone = range(n)
+        inner = [i for i in everyone if not outer_plane(i)]
+        ends = [i for i in everyone if outer_plane(i)]
+        second = move(kv, [(i, i ^ 8) for i in everyone])
+        first = move(kv, [(i, i ^ 4) for i in everyone])
+        beside = move(kv, [(i, i ^ 2) for i in everyone])
+        middle = move(kv, [(i, i ^ 12) for i in inner])
+        onward = move(second, [(i, i ^ 4) for i in inner])
+        early = [
+            Piece([kv], at_distance(0)),
+            Piece([beside], at_distance(2)),
+            Piece([first], at_distance(4)),
+            Piece([second], at_distance(8)),
+        ]
+        partials = attend(early)
+        held = place_pages(early)
+        (middle, onward, *held), partials[1] = lax.optimization_barrier(
+            ((middle, onward, *held), partials[1])
+        )
+        third = Piece([middle, onward], at_distance(12), pick=outer_plane)
+        later = [
+            Piece([move(first, [(i, i ^ 2) for i in everyone])], at_distance(6)),
+            third,
+            Piece([move(second, [(i, i ^ 2) for i in everyone])], at_distance(10)),
+        ]
+        last = third.moved(
+            [move(middle, [(i, i ^ 2) for i in inner]), move(onward, [(i, i ^ 2) for i in ends])]
+        )
+        last.source_of = at_distance(14)
+        queries, partials[1] = lax.optimization_barrier((queries, partials[1]))
+        partials += attend(later)
+        queries, partials[4] = lax.optimization_barrier((queries, partials[4]))
+        partials += attend([last])
+        remaining = later + [last]
+    else:
+        same = [list(range(c, n, 2)) for c in range(2)]
+        gathered = lax.all_gather(kv, "seq", axis=0, tiled=True, axis_index_groups=same)
+        remaining = [Piece([gathered], lambda shard, i: 2 * i + shard % 2, n // 2)]
+        partials, held = attend(remaining), ()
+    arrays, partials[-3] = lax.optimization_barrier((operands(remaining), partials[-3]))
+    remaining, _ = with_refs(remaining, arrays)
+    cache, other = place_pages(remaining, held)
+    partials[-3], cache, other = lax.optimization_barrier((partials[-3], cache, other))
     sent, kept = pl.pallas_call(
         merge_kernel,
         out_shape=(struct((half, width), bf16), struct((half, q_width), bf16)),

time: 44 us -> 45.9 us (1.043)
  starting transfers between devices: 14.9 us -> 18.2 us
  waiting for transfers between devices: 11.6 us -> 8.6 us
  Pallas kernels: 11.3 us -> 12.4 us
    ppermute x3 -> x9, starting transfers between devices: 6.11 us -> 15.3 us  [move(): return lax.ppermute(x, 'seq', pairs)]
    ppermute x9 -> x5, starting transfers between devices: 7.24 us -> 1.25 us  [swap(): return lax.ppermute(x, 'seq', [(i, i ^ bit) for i in range(n)])]
    ppermute x3 -> x9, waiting for transfers between devices: 6.18 us -> 3.2 us  [move(): return lax.ppermute(x, 'seq', pairs)]
    pallas_call x4 -> x5, Pallas kernels: 5.25 us -> 6.46 us  [the longest x3 4.45 us: attend(): pl.pallas_call(functools.partial(attend_kernel, pieces), out_shape=(struc...]
  transfers between devices with their start and end apart: 13 -> 15, of which waited for: 4 -> 3; matrix products, arithmetic and copies ran while one was open for 2% -> 2% of each run, Pallas kernels for 16% -> 18%
where the time goes in v5:
time: 45.9 us; the launch traced here: 45.3 us
  starting transfers between devices  18.2 us (40%)
  Pallas kernels  12.4 us (27%)
  waiting for transfers between devices  8.6 us (19%)
  local copies, waits for them, and re-layouts  3.63 us (8%)
  other arithmetic  1.55 us (3%)
  between operations  0.88 us (2%)
    ppermute x9, starting transfers between devices, move(): return lax.ppermute(x, 'seq', pairs)  15.3 us
    ppermute x1, waiting for transfers between devices, on_device(): lax.ppermute(sent, 'req', [(i, (i + 1) % parts) for i in range(parts)])  5.38 us
    pallas_call x3, Pallas kernels, attend(): pl.pallas_call(functools.partial(attend_kernel, pieces), out_shape=(struc...  4.45 us
    pallas_call x1, Pallas kernels, on_device(): pl.pallas_call(project_kernel, out_shape=(struct((rows, kv_width), bf16),...  4.32 us
    unnamed x18, local copies, waits for them, and re-layouts  3.63 us
    ppermute x9, waiting for transfers between devices, move(): return lax.ppermute(x, 'seq', pairs)  3.2 us
    pallas_call x2, Pallas kernels, place_pages(): pl.pallas_call(functools.partial(cache_kernel, pieces, bool(held)), out_s...  2 us
    ppermute x1, starting transfers between devices, on_device(): lax.ppermute(sent, 'req', [(i, (i + 1) % parts) for i in range(parts)])  1.64 us
  transfers between devices with their start and end apart: 15, of which 3 were waited for; matrix products, arithmetic and copies ran while one was open for 2% of the time, Pallas kernels for 18%

profile of v5, /device:TPU:0, one launch (start us, length us, event | category | flops | bytes accessed | tf_op | source)
XLA Modules:
  0.0 45.3 jit_solution(6515582406576074111)
XLA Ops:
  0.7 4.3 %project.1 = (bf16[128,512]{1,0:T(8,128)(2,1)}, bf16[128,512]{1,0:T(8,128)(2,1)}) custom-call(s32[16]{0:T(128)} %block_ref.9, s32[4]{0:T(128)} %len_ref.5, f32[1,128]{1,0:T(1,128)} %constant.2.clone.freq_hbm, bf16[128,2048]{1,0:T(8,128)(2,1)} %tok_ref.1, f32[1,2048]{1,0:T(1,128)} %bitcast.1, bf16[2048,256]{1,0:T(8,128)(2,1)} %wk_hbm.1, ...), custom_call_target="tpu_custom_call" | custom-call | flops 536870912 | bytes 4194304 | tf_op jit(solution)/shard_map/project/pallas_call | solution.py:387
  5.0 4.1 %collective-permute-start.3 = (bf16[128,512]{1,0:T(8,128)(2,1)}, bf16[128,512]{1,0:T(8,128)(2,1)S(1)}, u32[]{:S(2)}, u32[]{:S(2)}) collective-permute-start(bf16[128,512]{1,0:T(8,128)(2,1)} %get-tuple-element.39.refs_0_), channel_id=1, source_target_pairs={{0,16},{2,18},{4,20},{6,22},{8,24},{10,26},{12,28},{14,30},{16,0},... | collective-permute-start | bytes 393224 | tf_op jit(solution)/shard_map/ppermute | solution.py:373
  9.1 1.6 %collective-permute-start.2 = (bf16[128,512]{1,0:T(8,128)(2,1)}, bf16[128,512]{1,0:T(8,128)(2,1)S(1)}, u32[]{:S(2)}, u32[]{:S(2)}) collective-permute-start(bf16[128,512]{1,0:T(8,128)(2,1)} %get-tuple-element.39.refs_0_), channel_id=1, source_target_pairs={{0,8},{2,10},{4,12},{6,14},{8,0},{10,2},{12,4},{14,6},{16,24},{18,... | collective-permute-start | bytes 393224 | tf_op jit(solution)/shard_map/ppermute | solution.py:373
  10.7 1.5 %collective-permute-start.1 = (bf16[128,512]{1,0:T(8,128)(2,1)}, bf16[128,512]{1,0:T(8,128)(2,1)S(1)}, u32[]{:S(2)}, u32[]{:S(2)}) collective-permute-start(bf16[128,512]{1,0:T(8,128)(2,1)} %get-tuple-element.39.refs_0_), channel_id=1, source_target_pairs={{0,4},{2,6},{4,0},{6,2},{8,12},{10,14},{12,8},{14,10},{16,20},{18,... | collective-permute-start | bytes 393224 | tf_op jit(solution)/shard_map/ppermute | solution.py:373
  12.2 0.7 %collective-permute-start.4 = (bf16[128,512]{1,0:T(8,128)(2,1)}, bf16[128,512]{1,0:T(8,128)(2,1)S(1)}, u32[]{:S(2)}, u32[]{:S(2)}) collective-permute-start(bf16[128,512]{1,0:T(8,128)(2,1)} %get-tuple-element.39.refs_0_), channel_id=1, source_target_pairs={{8,16},{10,18},{12,20},{14,22},{16,8},{18,10},{20,12},{22,14},{9,1... | collective-permute-start | bytes 393224 | tf_op jit(solution)/shard_map/ppermute | solution.py:373
  12.8 2.9 %collective-permute-done.3.refs_3_ = bf16[128,512]{1,0:T(8,128)(2,1)S(1)} collective-permute-done((bf16[128,512]{1,0:T(8,128)(2,1)}, bf16[128,512]{1,0:T(8,128)(2,1)S(1)}, u32[]{:S(2)}, u32[]{:S(2)}) %collective-permute-start.3) | collective-permute-done | bytes 131104 | tf_op jit(solution)/shard_map/ppermute | solution.py:373
  15.7 1.3 %collective-permute-start.5 = (bf16[128,512]{1,0:T(8,128)(2,1)S(1)}, bf16[128,512]{1,0:T(8,128)(2,1)S(1)}, u32[]{:S(2)}, u32[]{:S(2)}) collective-permute-start(bf16[128,512]{1,0:T(8,128)(2,1)S(1)} %collective-permute-done.3.refs_3_), channel_id=1, source_target_pairs={{8,0},{10,2},{12,4},{14,6},{16,24},{18,26},{20,28},{22,30},{9,1},{... | collective-permute-start | bytes 393224 | tf_op jit(solution)/shard_map/ppermute | solution.py:373
  17.0 1.6 %collective-permute-start.8 = (bf16[128,512]{1,0:T(8,128)(2,1)S(1)}, bf16[128,512]{1,0:T(8,128)(2,1)S(1)}, u32[]{:S(2)}, u32[]{:S(2)}) collective-permute-start(bf16[128,512]{1,0:T(8,128)(2,1)S(1)} %collective-permute-done.3.refs_3_), channel_id=1, source_target_pairs={{0,4},{2,6},{4,0},{6,2},{8,12},{10,14},{12,8},{14,10},{16,20},{18,... | collective-permute-start | bytes 393224 | tf_op jit(solution)/shard_map/ppermute | solution.py:373
  19.1 0.9 %copy-done.4 = bf16[128,512]{1,0:T(8,128)(2,1)S(1)} copy-done((bf16[128,512]{1,0:T(8,128)(2,1)S(1)}, bf16[128,512]{1,0:T(8,128)(2,1)}, u32[]{:S(2)}) %copy-start.4) | copy-done | bytes 131096
  20.0 0.9 %cache.2 = (bf16[8,2,32,256]{3,2,1,0:T(8,128)(2,1)S(1)}, bf16[8,2,32,256]{3,2,1,0:T(8,128)(2,1)S(1)}) custom-call(s32[16]{0:T(128)S(1)} %copy-done.6, s32[64]{0:T(128)S(1)} %copy-done.8, bf16[128,512]{1,0:T(8,128)(2,1)S(1)} %copy-done.4, bf16[128,512]{1,0:T(8,128)(2,1)S(1)} %collective-permute-done.1.refs_1_, ...), custom_call_target="tpu_custom_call" | custom-call | bytes 262144 | tf_op jit(solution)/shard_map/cache/pallas_call | solution.py:434
  21.0 0.9 %copy-done.2 = bf16[128,512]{1,0:T(8,128)(2,1)S(1)} copy-done((bf16[128,512]{1,0:T(8,128)(2,1)S(1)}, bf16[128,512]{1,0:T(8,128)(2,1)}, u32[]{:S(2)}) %copy-start.2) | copy-done | bytes 131096
  21.8 0.9 %copy-done.5 = bf16[128,512]{1,0:T(8,128)(2,1)S(1)} copy-done((bf16[128,512]{1,0:T(8,128)(2,1)S(1)}, bf16[128,512]{1,0:T(8,128)(2,1)}, u32[]{:S(2)}) %copy-start.5) | copy-done | bytes 131096
  22.8 1.6 %attend.3 = (f32[128,512]{1,0:T(8,128)S(1)}, f32[128,128]{1,0:T(8,128)S(1)}, bf16[128,640]{1,0:T(8,128)(2,1)S(1)}) custom-call(s32[16]{0:T(128)S(1)} %copy-done.6, s32[4]{0:T(128)S(1)} %copy-done.7, bf16[128,512]{1,0:T(8,128)(2,1)S(1)} %copy-done.2, bf16[128,512]{1,0:T(8,128)(2,1)S(1)} %collective-permute-done.far_ref, bf16[128,512]{1,0:T(8,128)(2,1)S(1)} %copy-done.5, ...), custom_call_target="tpu_custom_call" | custom-call | flops 268435456 | bytes 524288 | tf_op jit(solution)/shard_map/attend/pallas_call | solution.py:416
  24.4 0.7 %collective-permute-start.10 = (bf16[128,512]{1,0:T(8,128)(2,1)S(1)}, bf16[128,512]{1,0:T(8,128)(2,1)S(1)}, u32[]{:S(2)}, u32[]{:S(2)}) collective-permute-start(bf16[128,512]{1,0:T(8,128)(2,1)S(1)} %collective-permute-done.4.refs_1_), channel_id=1, source_target_pairs={{8,12},{10,14},{12,8},{14,10},{16,20},{18,22},{20,16},{22,18},{9,1... | collective-permute-start | bytes 393224 | tf_op jit(solution)/shard_map/ppermute | solution.py:373
  25.1 3.5 %collective-permute-start.11 = (bf16[128,512]{1,0:T(8,128)(2,1)S(1)}, bf16[128,512]{1,0:T(8,128)(2,1)S(1)}, u32[]{:S(2)}, u32[]{:S(2)}) collective-permute-start(bf16[128,512]{1,0:T(8,128)(2,1)S(1)} %collective-permute-done.5.refs_2_), channel_id=1, source_target_pairs={{0,4},{2,6},{4,0},{6,2},{24,28},{26,30},{28,24},{30,26},{1,5},{3,7... | collective-permute-start | bytes 393224 | tf_op jit(solution)/shard_map/ppermute | solution.py:373
  28.7 0.9 %copy-done.3 = bf16[128,512]{1,0:T(8,128)(2,1)S(1)} copy-done((bf16[128,512]{1,0:T(8,128)(2,1)S(1)}, bf16[128,512]{1,0:T(8,128)(2,1)}, u32[]{:S(2)}) %copy-start.3) | copy-done | bytes 131096
  29.6 1.5 %attend.4 = (f32[128,512]{1,0:T(8,128)S(1)}, f32[128,128]{1,0:T(8,128)S(1)}, bf16[128,640]{1,0:T(8,128)(2,1)S(1)}) custom-call(s32[16]{0:T(128)S(1)} %copy-done.6, s32[4]{0:T(128)S(1)} %copy-done.7, bf16[128,512]{1,0:T(8,128)(2,1)S(1)} %copy-done.3, bf16[128,512]{1,0:T(8,128)(2,1)S(1)} %collective-permute-done.far_ref, ...), custom_call_target="tpu_custom_call" | custom-call | flops 201326592 | bytes 393216 | tf_op jit(solution)/shard_map/attend/pallas_call | solution.py:416
  32.0 1.3 %attend.5 = (f32[128,512]{1,0:T(8,128)S(1)}, f32[128,128]{1,0:T(8,128)S(1)}, bf16[128,640]{1,0:T(8,128)(2,1)S(1)}) custom-call(s32[16]{0:T(128)S(1)} %copy-done.6, s32[4]{0:T(128)S(1)} %copy-done.7, bf16[128,512]{1,0:T(8,128)(2,1)S(1)} %copy-done.3, bf16[128,512]{1,0:T(8,128)(2,1)S(1)} %collective-permute-done.far_ref, ...), custom_call_target="tpu_custom_call" | custom-call | flops 67108864 | bytes 131072 | tf_op jit(solution)/shard_map/attend/pallas_call | solution.py:416
  33.3 1.1 %cache.3 = (bf16[8,2,32,256]{3,2,1,0:T(8,128)(2,1)S(1)}, bf16[8,2,32,256]{3,2,1,0:T(8,128)(2,1)S(1)}) custom-call(s32[16]{0:T(128)S(1)} %copy-done.6, s32[64]{0:T(128)S(1)} %copy-done.8, bf16[128,512]{1,0:T(8,128)(2,1)S(1)} %collective-permute-done.7.refs_0_, ...), custom_call_target="tpu_custom_call", output_to_operand_aliasing={{0}: (8, {}), {1}: (9, {})} | custom-call | bytes 262144 | tf_op jit(solution)/shard_map/cache/pallas_call | solution.py:434
  35.1 1.2 %merge.1 = (bf16[64,2048]{1,0:T(8,128)(2,1)S(1)}, bf16[64,512]{1,0:T(8,128)(2,1)S(1)}) custom-call(bf16[512,2048]{1,0:T(8,128)(2,1)S(1)} %copy-done, f32[128,512]{1,0:T(8,128)S(1)} %get-tuple-element.40.refs_0_, f32[128,128]{1,0:T(8,128)S(1)} %get-tuple-element.45.refs_1_, bf16[128,640]{1,0:T(8,128)(2,1)S(1)} %collective-permute-done.6.refs_2_, ...), custom_call_target="tpu_custom_call" | custom-call | flops 134217728 | bytes 2097152 | tf_op jit(solution)/shard_map/merge/pallas_call | solution.py:489
  36.3 1.6 %collective-permute-start.13 = (bf16[64,2048]{1,0:T(8,128)(2,1)S(1)}, bf16[64,2048]{1,0:T(8,128)(2,1)S(1)}, u32[]{:S(2)}, u32[]{:S(2)}) collective-permute-start(bf16[64,2048]{1,0:T(8,128)(2,1)S(1)} %get-tuple-element.71), channel_id=1, source_target_pairs={{0,1},{1,0},{2,3},{3,2},{4,5},{5,4},{6,7},{7,6},{8,9},{9,8},{10,11... | collective-permute-start | bytes 786440 | tf_op jit(solution)/shard_map/ppermute | solution.py:498
  38.4 0.8 %add.7 = bf16[8,2,32,256]{3,2,1,0:T(8,128)(2,1)} add(bf16[8,2,32,256]{3,2,1,0:T(8,128)(2,1)S(1)} %get-tuple-element.72, bf16[8,2,32,256]{3,2,1,0:T(8,128)(2,1)S(1)} %collective-permute-done.14) | non-fusion elementwise | flops 131072 | bytes 786432 | tf_op jit(solution)/shard_map/add | solution.py:509
  39.2 5.4 %collective-permute-done.13 = bf16[64,2048]{1,0:T(8,128)(2,1)S(1)} collective-permute-done((bf16[64,2048]{1,0:T(8,128)(2,1)S(1)}, bf16[64,2048]{1,0:T(8,128)(2,1)S(1)}, u32[]{:S(2)}, u32[]{:S(2)}) %collective-permute-start.13) | collective-permute-done | bytes 262176 | tf_op jit(solution)/shard_map/ppermute | solution.py:498
  44.6 0.8 %add_convert_fusion = bf16[64,2048]{1,0:T(8,128)(2,1)} fusion(f32[64,2048]{1,0:T(8,128)S(1)} %keep.1, bf16[64,2048]{1,0:T(8,128)(2,1)S(1)} %collective-permute-done.13), kind=kLoop, calls=%fused_computation | loop fusion | flops 393216 | bytes 1048576 | tf_op jit(solution)/shard_map/convert_element_type | solution.py:510
  (34 shorter events, 2.6 us)
Async XLA Ops:
  0.6 18.5 %copy-start.6 = (s32[16]{0:T(128)S(1)}, s32[16]{0:T(128)}, u32[]{:S(2)}) copy-start(s32[16]{0:T(128)} %block_ref.9) | copy-start | bytes 196
  0.6 18.5 %copy-start.8 = (s32[64]{0:T(128)S(1)}, s32[64]{0:T(128)}, u32[]{:S(2)}) copy-start(s32[64]{0:T(128)} %slot_ref.3) | copy-start | bytes 772
  0.7 20.3 %copy-start.7 = (s32[4]{0:T(128)S(1)}, s32[4]{0:T(128)}, u32[]{:S(2)}) copy-start(s32[4]{0:T(128)} %len_ref.5) | copy-start | bytes 52
  5.0 30.1 %copy-start = (bf16[512,2048]{1,0:T(8,128)(2,1)S(1)}, bf16[512,2048]{1,0:T(8,128)(2,1)}, u32[]{:S(2)}) copy-start(bf16[512,2048]{1,0:T(8,128)(2,1)} %wo_ref.3) | copy-start | bytes 6291460
  5.0 10.7 %collective-permute-start.3 = (bf16[128,512]{1,0:T(8,128)(2,1)}, bf16[128,512]{1,0:T(8,128)(2,1)S(1)}, u32[]{:S(2)}, u32[]{:S(2)}) collective-permute-start(bf16[128,512]{1,0:T(8,128)(2,1)} %get-tuple-element.39.refs_0_), channel_id=1, source_target_pairs={{0,16},{2,18},{4,20},{6,22},{8,24},{10,26},{12,28},{14,30},{16,0},... | collective-permute-start | bytes 393224 | tf_op jit(solution)/shard_map/ppermute | solution.py:373
  9.1 7.9 %collective-permute-start.2 = (bf16[128,512]{1,0:T(8,128)(2,1)}, bf16[128,512]{1,0:T(8,128)(2,1)S(1)}, u32[]{:S(2)}, u32[]{:S(2)}) collective-permute-start(bf16[128,512]{1,0:T(8,128)(2,1)} %get-tuple-element.39.refs_0_), channel_id=1, source_target_pairs={{0,8},{2,10},{4,12},{6,14},{8,0},{10,2},{12,4},{14,6},{16,24},{18,... | collective-permute-start | bytes 393224 | tf_op jit(solution)/shard_map/ppermute | solution.py:373
  10.7 8.0 %collective-permute-start.1 = (bf16[128,512]{1,0:T(8,128)(2,1)}, bf16[128,512]{1,0:T(8,128)(2,1)S(1)}, u32[]{:S(2)}, u32[]{:S(2)}) collective-permute-start(bf16[128,512]{1,0:T(8,128)(2,1)} %get-tuple-element.39.refs_0_), channel_id=1, source_target_pairs={{0,4},{2,6},{4,0},{6,2},{8,12},{10,14},{12,8},{14,10},{16,20},{18,... | collective-permute-start | bytes 393224 | tf_op jit(solution)/shard_map/ppermute | solution.py:373
  12.2 8.7 %collective-permute-start = (bf16[128,512]{1,0:T(8,128)(2,1)}, bf16[128,512]{1,0:T(8,128)(2,1)S(1)}, u32[]{:S(2)}, u32[]{:S(2)}) collective-permute-start(bf16[128,512]{1,0:T(8,128)(2,1)} %get-tuple-element.54.q_ref), channel_id=1, source_target_pairs={{0,2},{2,0},{4,6},{6,4},{8,10},{10,8},{12,14},{14,12},{16,18},{18,... | collective-permute-start | bytes 393224 | tf_op jit(solution)/shard_map/ppermute | solution.py:340
  12.2 12.2 %collective-permute-start.4 = (bf16[128,512]{1,0:T(8,128)(2,1)}, bf16[128,512]{1,0:T(8,128)(2,1)S(1)}, u32[]{:S(2)}, u32[]{:S(2)}) collective-permute-start(bf16[128,512]{1,0:T(8,128)(2,1)} %get-tuple-element.39.refs_0_), channel_id=1, source_target_pairs={{8,16},{10,18},{12,20},{14,22},{16,8},{18,10},{20,12},{22,14},{9,1... | collective-permute-start | bytes 393224 | tf_op jit(solution)/shard_map/ppermute | solution.py:373
  15.7 8.7 %collective-permute-start.5 = (bf16[128,512]{1,0:T(8,128)(2,1)S(1)}, bf16[128,512]{1,0:T(8,128)(2,1)S(1)}, u32[]{:S(2)}, u32[]{:S(2)}) collective-permute-start(bf16[128,512]{1,0:T(8,128)(2,1)S(1)} %collective-permute-done.3.refs_3_), channel_id=1, source_target_pairs={{8,0},{10,2},{12,4},{14,6},{16,24},{18,26},{20,28},{22,30},{9,1},{... | collective-permute-start | bytes 393224 | tf_op jit(solution)/shard_map/ppermute | solution.py:373
  17.0 11.6 %collective-permute-start.8 = (bf16[128,512]{1,0:T(8,128)(2,1)S(1)}, bf16[128,512]{1,0:T(8,128)(2,1)S(1)}, u32[]{:S(2)}, u32[]{:S(2)}) collective-permute-start(bf16[128,512]{1,0:T(8,128)(2,1)S(1)} %collective-permute-done.3.refs_3_), channel_id=1, source_target_pairs={{0,4},{2,6},{4,0},{6,2},{8,12},{10,14},{12,8},{14,10},{16,20},{18,... | collective-permute-start | bytes 393224 | tf_op jit(solution)/shard_map/ppermute | solution.py:373
  18.6 10.0 %collective-permute-start.7 = (bf16[128,512]{1,0:T(8,128)(2,1)S(1)}, bf16[128,512]{1,0:T(8,128)(2,1)S(1)}, u32[]{:S(2)}, u32[]{:S(2)}) collective-permute-start(bf16[128,512]{1,0:T(8,128)(2,1)S(1)} %collective-permute-done.2.refs_2_), channel_id=1, source_target_pairs={{0,4},{2,6},{4,0},{6,2},{8,12},{10,14},{12,8},{14,10},{16,20},{18,... | collective-permute-start | bytes 393224 | tf_op jit(solution)/shard_map/ppermute | solution.py:373
  19.1 0.9 %copy-start.4 = (bf16[128,512]{1,0:T(8,128)(2,1)S(1)}, bf16[128,512]{1,0:T(8,128)(2,1)}, u32[]{:S(2)}) copy-start(bf16[128,512]{1,0:T(8,128)(2,1)} %get-tuple-element.39.refs_0_) | copy-start | bytes 393220
  20.9 0.9 %copy-start.2 = (bf16[128,512]{1,0:T(8,128)(2,1)S(1)}, bf16[128,512]{1,0:T(8,128)(2,1)}, u32[]{:S(2)}) copy-start(bf16[128,512]{1,0:T(8,128)(2,1)} %get-tuple-element.54.q_ref) | copy-start | bytes 393220
  21.8 0.9 %copy-start.5 = (bf16[128,512]{1,0:T(8,128)(2,1)S(1)}, bf16[128,512]{1,0:T(8,128)(2,1)}, u32[]{:S(2)}) copy-start(bf16[128,512]{1,0:T(8,128)(2,1)} %get-tuple-element.39.refs_0_) | copy-start | bytes 393220
  24.4 7.2 %collective-permute-start.10 = (bf16[128,512]{1,0:T(8,128)(2,1)S(1)}, bf16[128,512]{1,0:T(8,128)(2,1)S(1)}, u32[]{:S(2)}, u32[]{:S(2)}) collective-permute-start(bf16[128,512]{1,0:T(8,128)(2,1)S(1)} %collective-permute-done.4.refs_1_), channel_id=1, source_target_pairs={{8,12},{10,14},{12,8},{14,10},{16,20},{18,22},{20,16},{22,18},{9,1... | collective-permute-start | bytes 393224 | tf_op jit(solution)/shard_map/ppermute | solution.py:373
  25.1 6.9 %collective-permute-start.11 = (bf16[128,512]{1,0:T(8,128)(2,1)S(1)}, bf16[128,512]{1,0:T(8,128)(2,1)S(1)}, u32[]{:S(2)}, u32[]{:S(2)}) collective-permute-start(bf16[128,512]{1,0:T(8,128)(2,1)S(1)} %collective-permute-done.5.refs_2_), channel_id=1, source_target_pairs={{0,4},{2,6},{4,0},{6,2},{24,28},{26,30},{28,24},{30,26},{1,5},{3,7... | collective-permute-start | bytes 393224 | tf_op jit(solution)/shard_map/ppermute | solution.py:373
  28.6 6.5 %collective-permute-start.6 = (bf16[128,640]{1,0:T(8,128)(2,1)S(1)}, bf16[128,640]{1,0:T(8,128)(2,1)S(1)}, u32[]{:S(2)}, u32[]{:S(2)}) collective-permute-start(bf16[128,640]{1,0:T(8,128)(2,1)S(1)} %get-tuple-element.46), channel_id=1, source_target_pairs={{0,2},{2,0},{4,6},{6,4},{8,10},{10,8},{12,14},{14,12},{16,18},{18,... | collective-permute-start | bytes 491528 | tf_op jit(solution)/shard_map/ppermute | solution.py:340
  28.7 0.9 %copy-start.3 = (bf16[128,512]{1,0:T(8,128)(2,1)S(1)}, bf16[128,512]{1,0:T(8,128)(2,1)}, u32[]{:S(2)}) copy-start(bf16[128,512]{1,0:T(8,128)(2,1)} %get-tuple-element.54.q_ref) | copy-start | bytes 393220
  31.1 3.9 %collective-permute-start.9 = (bf16[128,640]{1,0:T(8,128)(2,1)S(1)}, bf16[128,640]{1,0:T(8,128)(2,1)S(1)}, u32[]{:S(2)}, u32[]{:S(2)}) collective-permute-start(bf16[128,640]{1,0:T(8,128)(2,1)S(1)} %get-tuple-element.53), channel_id=1, source_target_pairs={{0,2},{2,0},{4,6},{6,4},{8,10},{10,8},{12,14},{14,12},{16,18},{18,... | collective-permute-start | bytes 491528 | tf_op jit(solution)/shard_map/ppermute | solution.py:340
  33.2 1.8 %collective-permute-start.12 = (bf16[128,640]{1,0:T(8,128)(2,1)S(1)}, bf16[128,640]{1,0:T(8,128)(2,1)S(1)}, u32[]{:S(2)}, u32[]{:S(2)}) collective-permute-start(bf16[128,640]{1,0:T(8,128)(2,1)S(1)} %get-tuple-element.69), channel_id=1, source_target_pairs={{0,2},{2,0},{4,6},{6,4},{8,10},{10,8},{12,14},{14,12},{16,18},{18,... | collective-permute-start | bytes 491528 | tf_op jit(solution)/shard_map/ppermute | solution.py:340
  34.5 3.4 %copy-start.1 = (bf16[128,2048]{1,0:T(8,128)(2,1)S(1)}, bf16[128,2048]{1,0:T(8,128)(2,1)}, u32[]{:S(2)}) copy-start(bf16[128,2048]{1,0:T(8,128)(2,1)} %tok_ref.1) | copy-start | bytes 1572868
  34.5 3.9 %collective-permute-start.14 = (bf16[8,2,32,256]{3,2,1,0:T(8,128)(2,1)S(1)}, bf16[8,2,32,256]{3,2,1,0:T(8,128)(2,1)S(1)}, u32[]{:S(2)}, u32[]{:S(2)}) collective-permute-start(bf16[8,2,32,256]{3,2,1,0:T(8,128)(2,1)S(1)} %get-tuple-element.73), channel_id=1, source_target_pairs={{0,2},{2,0},{4,6},{6,4},{8,10},{10,8},{12,14},{14,12},{16,18},{18,... | collective-permute-start | bytes 786440 | tf_op jit(solution)/shard_map/ppermute | solution.py:340
  36.3 8.3 %collective-permute-start.13 = (bf16[64,2048]{1,0:T(8,128)(2,1)S(1)}, bf16[64,2048]{1,0:T(8,128)(2,1)S(1)}, u32[]{:S(2)}, u32[]{:S(2)}) collective-permute-start(bf16[64,2048]{1,0:T(8,128)(2,1)S(1)} %get-tuple-element.71), channel_id=1, source_target_pairs={{0,1},{1,0},{2,3},{3,2},{4,5},{5,4},{6,7},{7,6},{8,9},{9,8},{10,11... | collective-permute-start | bytes 786440 | tf_op jit(solution)/shard_map/ppermute | solution.py:498

commit v6 on v5

--- a/solution.py
+++ b/solution.py
@@ -216,7 +216,7 @@
         for i in range(0, len(pieces), 2):
             pair = pieces[i : i + 2]
             state = absorb(
-                state, [loaded(p, shard) for p in pair], [p.source_of(shard, 0) for p in pair]
+                state, [p.arrays[0][...] for p in pair], [p.source_of(shard, 0) for p in pair]
             )
     else:
         for piece in pieces:
@@ -306,7 +306,7 @@
     for i, target in enumerate((mine_ref, other_ref)):
         target[...] = refs[i][...] if held else jnp.zeros_like(target)
 
-    def place(ref, at, source, wanted):
+    def place(ref, at, source):
         for k, block in enumerate(blocks_of(block_ref, source)):
             for j in range(pages):
                 slot = slot_ref[block * pages + j]
@@ -317,23 +317,31 @@
                     offset = pl.multiple_of(offset, PAGE)
                 for target, owner in ((mine_ref, shard), (other_ref, shard ^ 1)):
 
-                    @pl.when((holder == owner) & wanted)
+                    @pl.when(holder == owner)
                     def _():
                         target[local, 0] = ref[pl.ds(offset, PAGE), :key_width]
                         target[local, 1] = ref[pl.ds(offset, PAGE), key_width:]
 
     for piece in pieces:
         if piece.count == 1:
-            source = piece.source_of(shard, 0)
-            for i, ref in enumerate(piece.arrays):
-                place(ref, 0, source, True if piece.pick is None else piece.pick(shard) == bool(i))
+            place(piece.arrays[0], 0, piece.source_of(shard, 0))
         else:
 
             def step(i, carry):
-                place(piece.arrays[0], i * rows, piece.source_of(shard, i), True)
+                place(piece.arrays[0], i * rows, piece.source_of(shard, i))
                 return carry
 
             lax.fori_loop(0, piece.count, step, 0)
+
+
+def tied_all(pieces, other):
+    arrays, other = lax.optimization_barrier((operands(pieces), other))
+    return with_refs(pieces, arrays)[0], other
+
+
+def tied(piece, other):
+    (piece,), other = tied_all([piece], other)
+    return piece, other
 
 
 def swap(x, n, bit):
@@ -341,11 +349,11 @@
 
 
 class Piece:
-    def __init__(self, arrays, source_of, count=1, pick=None):
-        self.arrays, self.source_of, self.count, self.pick = arrays, source_of, count, pick
+    def __init__(self, arrays, source_of, count=1):
+        self.arrays, self.source_of, self.count = arrays, source_of, count
 
     def moved(self, arrays):
-        return Piece(arrays, self.source_of, self.count, self.pick)
+        return Piece(arrays, self.source_of, self.count)
 
 
 def operands(pieces):
@@ -360,21 +368,12 @@
     return out, refs
 
 
-def loaded(piece, shard):
-    values = [ref[...] for ref in piece.arrays]
-    return values[0] if piece.pick is None else jnp.where(piece.pick(shard), values[1], values[0])
-
-
 def at_distance(bits):
     return lambda shard, i: shard ^ bits
 
 
 def move(x, pairs):
     return lax.ppermute(x, "seq", pairs)
-
-
-def outer_plane(i):
-    return (i // 4 == 0) | (i // 4 == 3)
 
 
 def on_device(
@@ -444,39 +443,32 @@
 
     if n == 16:
         everyone = range(n)
-        inner = [i for i in everyone if not outer_plane(i)]
-        ends = [i for i in everyone if outer_plane(i)]
-        second = move(kv, [(i, i ^ 8) for i in everyone])
-        first = move(kv, [(i, i ^ 4) for i in everyone])
-        beside = move(kv, [(i, i ^ 2) for i in everyone])
-        middle = move(kv, [(i, i ^ 12) for i in inner])
-        onward = move(second, [(i, i ^ 4) for i in inner])
-        early = [
-            Piece([kv], at_distance(0)),
-            Piece([beside], at_distance(2)),
-            Piece([first], at_distance(4)),
-            Piece([second], at_distance(8)),
-        ]
+
+        def along(shift, kv=kv):
+            source = lambda shard, i: (shard + n - 4 * shift) % n
+            return Piece([move(kv, [(i, (i + 4 * shift) % n) for i in everyone])], source)
+
+        def across(piece):
+            source = lambda shard, i: piece.source_of(shard ^ 2, i)
+            return Piece([swap(piece.arrays[0], n, 2)], source)
+
+        own = Piece([kv], at_distance(0))
+        beside, first, second, third = across(own), along(3), along(1), along(2)
+        first, later_kv = tied(first, kv)
+        third = along(2, later_kv)
+        early = [own, beside, first, second]
+        first_across = across(first)
         partials = attend(early)
-        held = place_pages(early)
-        (middle, onward, *held), partials[1] = lax.optimization_barrier(
-            ((middle, onward, *held), partials[1])
-        )
-        third = Piece([middle, onward], at_distance(12), pick=outer_plane)
-        later = [
-            Piece([move(first, [(i, i ^ 2) for i in everyone])], at_distance(6)),
-            third,
-            Piece([move(second, [(i, i ^ 2) for i in everyone])], at_distance(10)),
-        ]
-        last = third.moved(
-            [move(middle, [(i, i ^ 2) for i in inner]), move(onward, [(i, i ^ 2) for i in ends])]
-        )
-        last.source_of = at_distance(14)
+        third, partials[1] = tied(third, partials[1])
+        later = [third, first_across]
+        last = [across(second), across(third)]
         queries, partials[1] = lax.optimization_barrier((queries, partials[1]))
         partials += attend(later)
-        queries, partials[4] = lax.optimization_barrier((queries, partials[4]))
-        partials += attend([last])
-        remaining = later + [last]
+        placed, partials[4] = tied_all([own, beside, first, second], partials[4])
+        held = place_pages(placed)
+        queries, partials[4], held = lax.optimization_barrier((queries, partials[4], held))
+        partials += attend(last)
+        remaining = [third, first_across] + last
     else:
         same = [list(range(c, n, 2)) for c in range(2)]
         gathered = lax.all_gather(kv, "seq", axis=0, tiled=True, axis_index_groups=same)

time: 45.9 us -> 42.9 us (0.935)
  starting transfers between devices: 18.2 us -> 14.1 us
  waiting for transfers between devices: 8.6 us -> 9.86 us
  local copies, waits for them, and re-layouts: 3.63 us -> 4.53 us
  Pallas kernels: 12.4 us -> 11.8 us
    ppermute x9 -> x3, starting transfers between devices: 15.3 us -> 5.31 us  [move(): return lax.ppermute(x, 'seq', pairs)]
    ppermute x5 -> x9, starting transfers between devices: 1.25 us -> 7.21 us  [swap(): return lax.ppermute(x, 'seq', [(i, i ^ bit) for i in range(n)])]
    ppermute x9 -> x3, waiting for transfers between devices: 3.2 us -> 4.39 us  [move(): return lax.ppermute(x, 'seq', pairs)]
    unnamed x18 -> x20, local copies, waits for them, and re-layouts: 3.63 us -> 4.53 us
  transfers between devices with their start and end apart: 15 -> 13, of which waited for: 3 -> 4; matrix products, arithmetic and copies ran while one was open for 2% -> 2% of each run, Pallas kernels for 18% -> 18%
where the time goes in v6:
time: 42.9 us; the launch traced here: 42.7 us
  starting transfers between devices  14.1 us (33%)
  Pallas kernels  11.8 us (28%)
  waiting for transfers between devices  9.86 us (23%)
  local copies, waits for them, and re-layouts  4.53 us (11%)
  other arithmetic  1.54 us (4%)
  between operations  0.81 us (2%)
    ppermute x9, starting transfers between devices, swap(): return lax.ppermute(x, 'seq', [(i, i ^ bit) for i in range(n)])  7.21 us
    ppermute x1, waiting for transfers between devices, on_device(): lax.ppermute(sent, 'req', [(i, (i + 1) % parts) for i in range(parts)])  5.44 us
    ppermute x3, starting transfers between devices, move(): return lax.ppermute(x, 'seq', pairs)  5.31 us
    unnamed x20, local copies, waits for them, and re-layouts  4.53 us
    ppermute x3, waiting for transfers between devices, move(): return lax.ppermute(x, 'seq', pairs)  4.39 us
    pallas_call x1, Pallas kernels, on_device(): pl.pallas_call(project_kernel, out_shape=(struct((rows, kv_width), bf16),...  4.32 us
    pallas_call x3, Pallas kernels, attend(): pl.pallas_call(functools.partial(attend_kernel, pieces), out_shape=(struc...  4.02 us
    pallas_call x2, Pallas kernels, place_pages(): pl.pallas_call(functools.partial(cache_kernel, pieces, bool(held)), out_s...  1.83 us
  transfers between devices with their start and end apart: 13, of which 4 were waited for; matrix products, arithmetic and copies ran while one was open for 2% of the time, Pallas kernels for 18%

profile of v6, /device:TPU:0, one launch (start us, length us, event | category | flops | bytes accessed | tf_op | source)
XLA Modules:
  0.0 42.7 jit_solution(16913409553600876849)
XLA Ops:
  0.7 4.3 %project.1 = (bf16[128,512]{1,0:T(8,128)(2,1)}, bf16[128,512]{1,0:T(8,128)(2,1)}) custom-call(s32[16]{0:T(128)} %block_ref.9, s32[4]{0:T(128)} %len_ref.5, f32[1,128]{1,0:T(1,128)} %constant.2.clone.freq_hbm, bf16[128,2048]{1,0:T(8,128)(2,1)} %tok_ref.1, f32[1,2048]{1,0:T(1,128)} %bitcast.1, bf16[2048,256]{1,0:T(8,128)(2,1)} %wk_hbm.1, ...), custom_call_target="tpu_custom_call" | custom-call | flops 536870912 | bytes 4194304 | tf_op jit(solution)/shard_map/project/pallas_call | solution.py:386
  5.0 5.1 %collective-permute-start.2 = (bf16[128,512]{1,0:T(8,128)(2,1)}, bf16[128,512]{1,0:T(8,128)(2,1)S(1)}, u32[]{:S(2)}, u32[]{:S(2)}) collective-permute-start(bf16[128,512]{1,0:T(8,128)(2,1)} %get-tuple-element.56.refs_0_), channel_id=1, source_target_pairs={{0,24},{2,26},{4,28},{6,30},{8,0},{10,2},{12,4},{14,6},{16,8},{18,... | collective-permute-start | bytes 393224 | tf_op jit(solution)/shard_map/ppermute | solution.py:376
  10.1 1.5 %collective-permute-start.1 = (bf16[128,512]{1,0:T(8,128)(2,1)}, bf16[128,512]{1,0:T(8,128)(2,1)S(1)}, u32[]{:S(2)}, u32[]{:S(2)}) collective-permute-start(bf16[128,512]{1,0:T(8,128)(2,1)} %get-tuple-element.56.refs_0_), channel_id=1, source_target_pairs={{0,4},{2,6},{4,0},{6,2},{8,12},{10,14},{12,8},{14,10},{16,20},{18,... | collective-permute-start | bytes 393224 | tf_op jit(solution)/shard_map/ppermute | solution.py:348
  11.6 2.7 %collective-permute-done.2.refs_2_ = bf16[128,512]{1,0:T(8,128)(2,1)S(1)} collective-permute-done((bf16[128,512]{1,0:T(8,128)(2,1)}, bf16[128,512]{1,0:T(8,128)(2,1)S(1)}, u32[]{:S(2)}, u32[]{:S(2)}) %collective-permute-start.2) | collective-permute-done | bytes 131104 | tf_op jit(solution)/shard_map/ppermute | solution.py:376
  14.5 1.5 %collective-permute-start.6 = (bf16[128,512]{1,0:T(8,128)(2,1)S(1)}, bf16[128,512]{1,0:T(8,128)(2,1)S(1)}, u32[]{:S(2)}, u32[]{:S(2)}) collective-permute-start(bf16[128,512]{1,0:T(8,128)(2,1)S(1)} %collective-permute-done.2.refs_2_), channel_id=1, source_target_pairs={{0,4},{2,6},{4,0},{6,2},{8,12},{10,14},{12,8},{14,10},{16,20},{18,... | collective-permute-start | bytes 393224 | tf_op jit(solution)/shard_map/ppermute | solution.py:348
  16.0 1.1 %collective-permute-done.3.refs_3_ = bf16[128,512]{1,0:T(8,128)(2,1)S(1)} collective-permute-done((bf16[128,512]{1,0:T(8,128)(2,1)}, bf16[128,512]{1,0:T(8,128)(2,1)S(1)}, u32[]{:S(2)}, u32[]{:S(2)}) %collective-permute-start.3) | collective-permute-done | bytes 131104 | tf_op jit(solution)/shard_map/ppermute | solution.py:376
  17.2 1.5 %collective-permute-start.8 = (bf16[128,512]{1,0:T(8,128)(2,1)S(1)}, bf16[128,512]{1,0:T(8,128)(2,1)S(1)}, u32[]{:S(2)}, u32[]{:S(2)}) collective-permute-start(bf16[128,512]{1,0:T(8,128)(2,1)S(1)} %collective-permute-done.3.refs_3_), channel_id=1, source_target_pairs={{0,4},{2,6},{4,0},{6,2},{8,12},{10,14},{12,8},{14,10},{16,20},{18,... | collective-permute-start | bytes 393224 | tf_op jit(solution)/shard_map/ppermute | solution.py:348
  18.7 0.9 %copy-done.2 = bf16[128,512]{1,0:T(8,128)(2,1)S(1)} copy-done((bf16[128,512]{1,0:T(8,128)(2,1)S(1)}, bf16[128,512]{1,0:T(8,128)(2,1)}, u32[]{:S(2)}) %copy-start.2) | copy-done | bytes 131096
  19.6 0.9 %copy-done.5 = bf16[128,512]{1,0:T(8,128)(2,1)S(1)} copy-done((bf16[128,512]{1,0:T(8,128)(2,1)S(1)}, bf16[128,512]{1,0:T(8,128)(2,1)}, u32[]{:S(2)}) %copy-start.5) | copy-done | bytes 131096
  20.5 1.6 %attend.3 = (f32[128,512]{1,0:T(8,128)S(1)}, f32[128,128]{1,0:T(8,128)S(1)}, bf16[128,640]{1,0:T(8,128)(2,1)S(1)}) custom-call(s32[16]{0:T(128)S(1)} %copy-done.7, s32[4]{0:T(128)S(1)} %copy-done.8, bf16[128,512]{1,0:T(8,128)(2,1)S(1)} %copy-done.2, bf16[128,512]{1,0:T(8,128)(2,1)S(1)} %collective-permute-done.far_ref, bf16[128,512]{1,0:T(8,128)(2,1)S(1)} %copy-done.5, ...), custom_call_target="tpu_custom_call" | custom-call | flops 268435456 | bytes 524288 | tf_op jit(solution)/shard_map/attend/pallas_call | solution.py:415
  22.7 1.5 %collective-permute-start.9 = (bf16[128,512]{1,0:T(8,128)(2,1)S(1)}, bf16[128,512]{1,0:T(8,128)(2,1)S(1)}, u32[]{:S(2)}, u32[]{:S(2)}) collective-permute-start(bf16[128,512]{1,0:T(8,128)(2,1)S(1)} %collective-permute-done.4.refs_0_), channel_id=1, source_target_pairs={{0,4},{2,6},{4,0},{6,2},{8,12},{10,14},{12,8},{14,10},{16,20},{18,... | collective-permute-start | bytes 393224 | tf_op jit(solution)/shard_map/ppermute | solution.py:348
  24.2 0.9 %copy-done.3 = bf16[128,512]{1,0:T(8,128)(2,1)S(1)} copy-done((bf16[128,512]{1,0:T(8,128)(2,1)S(1)}, bf16[128,512]{1,0:T(8,128)(2,1)}, u32[]{:S(2)}) %copy-start.3) | copy-done | bytes 131096
  25.1 1.2 %attend.4 = (f32[128,512]{1,0:T(8,128)S(1)}, f32[128,128]{1,0:T(8,128)S(1)}, bf16[128,640]{1,0:T(8,128)(2,1)S(1)}) custom-call(s32[16]{0:T(128)S(1)} %copy-done.7, s32[4]{0:T(128)S(1)} %copy-done.8, bf16[128,512]{1,0:T(8,128)(2,1)S(1)} %copy-done.3, bf16[128,512]{1,0:T(8,128)(2,1)S(1)} %collective-permute-done.far_ref, ...), custom_call_target="tpu_custom_call" | custom-call | flops 134217728 | bytes 262144 | tf_op jit(solution)/shard_map/attend/pallas_call | solution.py:415
  26.3 0.6 %collective-permute-start.7 = (bf16[128,640]{1,0:T(8,128)(2,1)S(1)}, bf16[128,640]{1,0:T(8,128)(2,1)S(1)}, u32[]{:S(2)}, u32[]{:S(2)}) collective-permute-start(bf16[128,640]{1,0:T(8,128)(2,1)S(1)} %get-tuple-element.63), channel_id=1, source_target_pairs={{0,2},{2,0},{4,6},{6,4},{8,10},{10,8},{12,14},{14,12},{16,18},{18,... | collective-permute-start | bytes 491528 | tf_op jit(solution)/shard_map/ppermute | solution.py:348
  26.9 0.9 %copy-done.6 = bf16[128,512]{1,0:T(8,128)(2,1)S(1)} copy-done((bf16[128,512]{1,0:T(8,128)(2,1)S(1)}, bf16[128,512]{1,0:T(8,128)(2,1)}, u32[]{:S(2)}) %copy-start.6) | copy-done | bytes 131096
  27.8 0.9 %cache.2 = (bf16[8,2,32,256]{3,2,1,0:T(8,128)(2,1)S(1)}, bf16[8,2,32,256]{3,2,1,0:T(8,128)(2,1)S(1)}) custom-call(s32[16]{0:T(128)S(1)} %copy-done.7, s32[64]{0:T(128)S(1)} %copy-done.9, bf16[128,512]{1,0:T(8,128)(2,1)S(1)} %copy-done.6, bf16[128,512]{1,0:T(8,128)(2,1)S(1)} %collective-permute-done.1.refs_1_, ...), custom_call_target="tpu_custom_call" | custom-call | bytes 262144 | tf_op jit(solution)/shard_map/cache/pallas_call | solution.py:433
  28.7 0.9 %copy-done.4 = bf16[128,512]{1,0:T(8,128)(2,1)S(1)} copy-done((bf16[128,512]{1,0:T(8,128)(2,1)S(1)}, bf16[128,512]{1,0:T(8,128)(2,1)}, u32[]{:S(2)}) %copy-start.4) | copy-done | bytes 131096
  29.6 1.2 %attend.5 = (f32[128,512]{1,0:T(8,128)S(1)}, f32[128,128]{1,0:T(8,128)S(1)}, bf16[128,640]{1,0:T(8,128)(2,1)S(1)}) custom-call(s32[16]{0:T(128)S(1)} %copy-done.7, s32[4]{0:T(128)S(1)} %copy-done.8, bf16[128,512]{1,0:T(8,128)(2,1)S(1)} %copy-done.4, bf16[128,512]{1,0:T(8,128)(2,1)S(1)} %collective-permute-done.far_ref, ...), custom_call_target="tpu_custom_call" | custom-call | flops 134217728 | bytes 262144 | tf_op jit(solution)/shard_map/attend/pallas_call | solution.py:415
  30.9 0.9 %cache.3 = (bf16[8,2,32,256]{3,2,1,0:T(8,128)(2,1)S(1)}, bf16[8,2,32,256]{3,2,1,0:T(8,128)(2,1)S(1)}) custom-call(s32[16]{0:T(128)S(1)} %copy-done.7, s32[64]{0:T(128)S(1)} %copy-done.9, bf16[128,512]{1,0:T(8,128)(2,1)S(1)} %collective-permute-done.4.refs_0_, ...), custom_call_target="tpu_custom_call", output_to_operand_aliasing={{0}: (6, {}), {1}: (7, {})} | custom-call | bytes 262144 | tf_op jit(solution)/shard_map/cache/pallas_call | solution.py:433
  32.4 1.2 %merge.1 = (bf16[64,2048]{1,0:T(8,128)(2,1)S(1)}, bf16[64,512]{1,0:T(8,128)(2,1)S(1)}) custom-call(bf16[512,2048]{1,0:T(8,128)(2,1)S(1)} %copy-done, f32[128,512]{1,0:T(8,128)S(1)} %get-tuple-element.45.refs_0_, f32[128,128]{1,0:T(8,128)S(1)} %get-tuple-element.49.refs_1_, bf16[128,640]{1,0:T(8,128)(2,1)S(1)} %collective-permute-done.5.refs_2_, ...), custom_call_target="tpu_custom_call" | custom-call | flops 134217728 | bytes 2097152 | tf_op jit(solution)/shard_map/merge/pallas_call | solution.py:481
  33.6 1.6 %collective-permute-start.11 = (bf16[64,2048]{1,0:T(8,128)(2,1)S(1)}, bf16[64,2048]{1,0:T(8,128)(2,1)S(1)}, u32[]{:S(2)}, u32[]{:S(2)}) collective-permute-start(bf16[64,2048]{1,0:T(8,128)(2,1)S(1)} %get-tuple-element.79), channel_id=1, source_target_pairs={{0,1},{1,0},{2,3},{3,2},{4,5},{5,4},{6,7},{7,6},{8,9},{9,8},{10,11... | collective-permute-start | bytes 786440 | tf_op jit(solution)/shard_map/ppermute | solution.py:490
  35.7 0.8 %add.7 = bf16[8,2,32,256]{3,2,1,0:T(8,128)(2,1)} add(bf16[8,2,32,256]{3,2,1,0:T(8,128)(2,1)S(1)} %get-tuple-element.80, bf16[8,2,32,256]{3,2,1,0:T(8,128)(2,1)S(1)} %collective-permute-done.12) | non-fusion elementwise | flops 131072 | bytes 786432 | tf_op jit(solution)/shard_map/add | solution.py:501
  36.5 5.4 %collective-permute-done.11 = bf16[64,2048]{1,0:T(8,128)(2,1)S(1)} collective-permute-done((bf16[64,2048]{1,0:T(8,128)(2,1)S(1)}, bf16[64,2048]{1,0:T(8,128)(2,1)S(1)}, u32[]{:S(2)}, u32[]{:S(2)}) %collective-permute-start.11) | collective-permute-done | bytes 262176 | tf_op jit(solution)/shard_map/ppermute | solution.py:490
  41.9 0.8 %add_convert_fusion = bf16[64,2048]{1,0:T(8,128)(2,1)} fusion(f32[64,2048]{1,0:T(8,128)S(1)} %keep.1, bf16[64,2048]{1,0:T(8,128)(2,1)S(1)} %collective-permute-done.11), kind=kLoop, calls=%fused_computation | loop fusion | flops 393216 | bytes 1048576 | tf_op jit(solution)/shard_map/convert_element_type | solution.py:502
  (32 shorter events, 1.9 us)
Async XLA Ops:
  0.6 18.0 %copy-start.7 = (s32[16]{0:T(128)S(1)}, s32[16]{0:T(128)}, u32[]{:S(2)}) copy-start(s32[16]{0:T(128)} %block_ref.9) | copy-start | bytes 196
  0.6 18.0 %copy-start.8 = (s32[4]{0:T(128)S(1)}, s32[4]{0:T(128)}, u32[]{:S(2)}) copy-start(s32[4]{0:T(128)} %len_ref.5) | copy-start | bytes 52
  0.7 26.2 %copy-start.9 = (s32[64]{0:T(128)S(1)}, s32[64]{0:T(128)}, u32[]{:S(2)}) copy-start(s32[64]{0:T(128)} %slot_ref.3) | copy-start | bytes 772
  5.0 27.4 %copy-start = (bf16[512,2048]{1,0:T(8,128)(2,1)S(1)}, bf16[512,2048]{1,0:T(8,128)(2,1)}, u32[]{:S(2)}) copy-start(bf16[512,2048]{1,0:T(8,128)(2,1)} %wo_ref.3) | copy-start | bytes 6291460
  5.0 9.3 %collective-permute-start.2 = (bf16[128,512]{1,0:T(8,128)(2,1)}, bf16[128,512]{1,0:T(8,128)(2,1)S(1)}, u32[]{:S(2)}, u32[]{:S(2)}) collective-permute-start(bf16[128,512]{1,0:T(8,128)(2,1)} %get-tuple-element.56.refs_0_), channel_id=1, source_target_pairs={{0,24},{2,26},{4,28},{6,30},{8,0},{10,2},{12,4},{14,6},{16,8},{18,... | collective-permute-start | bytes 393224 | tf_op jit(solution)/shard_map/ppermute | solution.py:376
  10.1 7.1 %collective-permute-start.3 = (bf16[128,512]{1,0:T(8,128)(2,1)}, bf16[128,512]{1,0:T(8,128)(2,1)S(1)}, u32[]{:S(2)}, u32[]{:S(2)}) collective-permute-start(bf16[128,512]{1,0:T(8,128)(2,1)} %get-tuple-element.56.refs_0_), channel_id=1, source_target_pairs={{0,8},{2,10},{4,12},{6,14},{8,16},{10,18},{12,20},{14,22},{16,24},... | collective-permute-start | bytes 393224 | tf_op jit(solution)/shard_map/ppermute | solution.py:376
  10.1 8.6 %collective-permute-start = (bf16[128,512]{1,0:T(8,128)(2,1)}, bf16[128,512]{1,0:T(8,128)(2,1)S(1)}, u32[]{:S(2)}, u32[]{:S(2)}) collective-permute-start(bf16[128,512]{1,0:T(8,128)(2,1)} %get-tuple-element.64.q_ref), channel_id=1, source_target_pairs={{0,2},{2,0},{4,6},{6,4},{8,10},{10,8},{12,14},{14,12},{16,18},{18,... | collective-permute-start | bytes 393224 | tf_op jit(solution)/shard_map/ppermute | solution.py:348
  10.1 8.6 %collective-permute-start.1 = (bf16[128,512]{1,0:T(8,128)(2,1)}, bf16[128,512]{1,0:T(8,128)(2,1)S(1)}, u32[]{:S(2)}, u32[]{:S(2)}) collective-permute-start(bf16[128,512]{1,0:T(8,128)(2,1)} %get-tuple-element.56.refs_0_), channel_id=1, source_target_pairs={{0,4},{2,6},{4,0},{6,2},{8,12},{10,14},{12,8},{14,10},{16,20},{18,... | collective-permute-start | bytes 393224 | tf_op jit(solution)/shard_map/ppermute | solution.py:348
  14.3 8.4 %collective-permute-start.4 = (bf16[128,512]{1,0:T(8,128)(2,1)}, bf16[128,512]{1,0:T(8,128)(2,1)S(1)}, u32[]{:S(2)}, u32[]{:S(2)}) collective-permute-start(bf16[128,512]{1,0:T(8,128)(2,1)} %get-tuple-element.56.refs_0_), channel_id=1, source_target_pairs={{0,16},{2,18},{4,20},{6,22},{8,24},{10,26},{12,28},{14,30},{16,0},... | collective-permute-start | bytes 393224 | tf_op jit(solution)/shard_map/ppermute | solution.py:376
  14.5 9.7 %collective-permute-start.6 = (bf16[128,512]{1,0:T(8,128)(2,1)S(1)}, bf16[128,512]{1,0:T(8,128)(2,1)S(1)}, u32[]{:S(2)}, u32[]{:S(2)}) collective-permute-start(bf16[128,512]{1,0:T(8,128)(2,1)S(1)} %collective-permute-done.2.refs_2_), channel_id=1, source_target_pairs={{0,4},{2,6},{4,0},{6,2},{8,12},{10,14},{12,8},{14,10},{16,20},{18,... | collective-permute-start | bytes 393224 | tf_op jit(solution)/shard_map/ppermute | solution.py:348
  17.2 11.5 %collective-permute-start.8 = (bf16[128,512]{1,0:T(8,128)(2,1)S(1)}, bf16[128,512]{1,0:T(8,128)(2,1)S(1)}, u32[]{:S(2)}, u32[]{:S(2)}) collective-permute-start(bf16[128,512]{1,0:T(8,128)(2,1)S(1)} %collective-permute-done.3.refs_3_), channel_id=1, source_target_pairs={{0,4},{2,6},{4,0},{6,2},{8,12},{10,14},{12,8},{14,10},{16,20},{18,... | collective-permute-start | bytes 393224 | tf_op jit(solution)/shard_map/ppermute | solution.py:348
  18.7 0.9 %copy-start.2 = (bf16[128,512]{1,0:T(8,128)(2,1)S(1)}, bf16[128,512]{1,0:T(8,128)(2,1)}, u32[]{:S(2)}) copy-start(bf16[128,512]{1,0:T(8,128)(2,1)} %get-tuple-element.64.q_ref) | copy-start | bytes 393220
  19.6 0.9 %copy-start.5 = (bf16[128,512]{1,0:T(8,128)(2,1)S(1)}, bf16[128,512]{1,0:T(8,128)(2,1)}, u32[]{:S(2)}) copy-start(bf16[128,512]{1,0:T(8,128)(2,1)} %get-tuple-element.56.refs_0_) | copy-start | bytes 393220
  22.7 6.0 %collective-permute-start.9 = (bf16[128,512]{1,0:T(8,128)(2,1)S(1)}, bf16[128,512]{1,0:T(8,128)(2,1)S(1)}, u32[]{:S(2)}, u32[]{:S(2)}) collective-permute-start(bf16[128,512]{1,0:T(8,128)(2,1)S(1)} %collective-permute-done.4.refs_0_), channel_id=1, source_target_pairs={{0,4},{2,6},{4,0},{6,2},{8,12},{10,14},{12,8},{14,10},{16,20},{18,... | collective-permute-start | bytes 393224 | tf_op jit(solution)/shard_map/ppermute | solution.py:348
  24.2 8.2 %collective-permute-start.5 = (bf16[128,640]{1,0:T(8,128)(2,1)S(1)}, bf16[128,640]{1,0:T(8,128)(2,1)S(1)}, u32[]{:S(2)}, u32[]{:S(2)}) collective-permute-start(bf16[128,640]{1,0:T(8,128)(2,1)S(1)} %get-tuple-element.50), channel_id=1, source_target_pairs={{0,2},{2,0},{4,6},{6,4},{8,10},{10,8},{12,14},{14,12},{16,18},{18,... | collective-permute-start | bytes 491528 | tf_op jit(solution)/shard_map/ppermute | solution.py:348
  24.2 0.9 %copy-start.3 = (bf16[128,512]{1,0:T(8,128)(2,1)S(1)}, bf16[128,512]{1,0:T(8,128)(2,1)}, u32[]{:S(2)}) copy-start(bf16[128,512]{1,0:T(8,128)(2,1)} %get-tuple-element.64.q_ref) | copy-start | bytes 393220
  26.3 6.1 %collective-permute-start.7 = (bf16[128,640]{1,0:T(8,128)(2,1)S(1)}, bf16[128,640]{1,0:T(8,128)(2,1)S(1)}, u32[]{:S(2)}, u32[]{:S(2)}) collective-permute-start(bf16[128,640]{1,0:T(8,128)(2,1)S(1)} %get-tuple-element.63), channel_id=1, source_target_pairs={{0,2},{2,0},{4,6},{6,4},{8,10},{10,8},{12,14},{14,12},{16,18},{18,... | collective-permute-start | bytes 491528 | tf_op jit(solution)/shard_map/ppermute | solution.py:348
  26.9 0.9 %copy-start.6 = (bf16[128,512]{1,0:T(8,128)(2,1)S(1)}, bf16[128,512]{1,0:T(8,128)(2,1)}, u32[]{:S(2)}) copy-start(bf16[128,512]{1,0:T(8,128)(2,1)} %get-tuple-element.56.refs_0_) | copy-start | bytes 393220
  28.7 0.9 %copy-start.4 = (bf16[128,512]{1,0:T(8,128)(2,1)S(1)}, bf16[128,512]{1,0:T(8,128)(2,1)}, u32[]{:S(2)}) copy-start(bf16[128,512]{1,0:T(8,128)(2,1)} %get-tuple-element.64.q_ref) | copy-start | bytes 393220
  30.8 1.6 %collective-permute-start.10 = (bf16[128,640]{1,0:T(8,128)(2,1)S(1)}, bf16[128,640]{1,0:T(8,128)(2,1)S(1)}, u32[]{:S(2)}, u32[]{:S(2)}) collective-permute-start(bf16[128,640]{1,0:T(8,128)(2,1)S(1)} %get-tuple-element.77), channel_id=1, source_target_pairs={{0,2},{2,0},{4,6},{6,4},{8,10},{10,8},{12,14},{14,12},{16,18},{18,... | collective-permute-start | bytes 491528 | tf_op jit(solution)/shard_map/ppermute | solution.py:348
  30.9 4.3 %copy-start.1 = (bf16[128,2048]{1,0:T(8,128)(2,1)S(1)}, bf16[128,2048]{1,0:T(8,128)(2,1)}, u32[]{:S(2)}) copy-start(bf16[128,2048]{1,0:T(8,128)(2,1)} %tok_ref.1) | copy-start | bytes 1572868
  31.8 3.8 %collective-permute-start.12 = (bf16[8,2,32,256]{3,2,1,0:T(8,128)(2,1)S(1)}, bf16[8,2,32,256]{3,2,1,0:T(8,128)(2,1)S(1)}, u32[]{:S(2)}, u32[]{:S(2)}) collective-permute-start(bf16[8,2,32,256]{3,2,1,0:T(8,128)(2,1)S(1)} %get-tuple-element.81), channel_id=1, source_target_pairs={{0,2},{2,0},{4,6},{6,4},{8,10},{10,8},{12,14},{14,12},{16,18},{18,... | collective-permute-start | bytes 786440 | tf_op jit(solution)/shard_map/ppermute | solution.py:348
  33.6 8.3 %collective-permute-start.11 = (bf16[64,2048]{1,0:T(8,128)(2,1)S(1)}, bf16[64,2048]{1,0:T(8,128)(2,1)S(1)}, u32[]{:S(2)}, u32[]{:S(2)}) collective-permute-start(bf16[64,2048]{1,0:T(8,128)(2,1)S(1)} %get-tuple-element.79), channel_id=1, source_target_pairs={{0,1},{1,0},{2,3},{3,2},{4,5},{5,4},{6,7},{7,6},{8,9},{9,8},{10,11... | collective-permute-start | bytes 786440 | tf_op jit(solution)/shard_map/ppermute | solution.py:490

commit v7 on v6

--- a/solution.py
+++ b/solution.py
@@ -254,45 +254,54 @@
     packed_ref[:, q_width:] = parts.astype(bf16)
 
 
-def merge_kernel(wo_ref, *refs):
-    partials, (sent_ref, kept_ref) = refs[:-2], refs[-2:]
-    rows, q_width = partials[0].shape
+def stage_kernel(q_ref, kv_ref, q_out, kv_out):
+    q_out[...] = q_ref[...]
+    kv_out[...] = kv_ref[...]
+
+
+def joined_rows(partials, first, half):
+    q_width = partials[0].shape[1]
     heads = q_width // HEAD
-    half = rows // 2
+    span = pl.ds(pl.multiple_of(first, half), half)
     held = []
     for mine_ref, stat_ref, packed_ref in zip(partials[::3], partials[1::3], partials[2::3]):
-        parts = packed_ref[:, q_width:].astype(f32)
+        parts = packed_ref[span, q_width:].astype(f32)
         stats = parts
         for t in (1, 2):
             stats = stats + pltpu.roll(parts, HEAD - 2 * heads * t, 1)
-        held += [(mine_ref, stat_ref[...]), (packed_ref, stats)]
+        held += [(mine_ref, stat_ref[span, :]), (packed_ref, stats)]
     top = functools.reduce(jnp.maximum, [stats for _, stats in held])
     shares = [jnp.exp2(stats - top) for _, stats in held]
     total = sum(
         share * pltpu.roll(stats, HEAD - heads, 1) for share, (_, stats) in zip(shares, held)
     )
     shares = [share / total for share in shares]
-    joined = []
+    context = []
     for h in range(heads):
         cols = slice(h * HEAD, (h + 1) * HEAD)
-        joined.append(
+        context.append(
             sum(
-                ref[:, cols].astype(f32) * share[:, h : h + 1]
+                ref[span, cols].astype(f32) * share[:, h : h + 1]
                 for (ref, _), share in zip(held, shares)
             ).astype(bf16)
         )
-    context = jnp.concatenate(joined, 1)
-    upper = lax.axis_index("req") == 0
-    kept_ref[...] = jnp.where(upper, context[:half], context[half:])
-    leaving = jnp.where(upper, context[half:], context[:half])
-    sent_ref[...] = jnp.dot(leaving, wo_ref[...], preferred_element_type=f32).astype(bf16)
-
-
-def keep_kernel(context_ref, wo_ref, tok_ref, out_ref):
-    half = context_ref.shape[0]
-    first = pl.multiple_of(lax.axis_index("req") * half, half)
-    residual = tok_ref[pl.ds(first, half), :].astype(f32)
-    out_ref[...] = jnp.dot(context_ref[...], wo_ref[...], preferred_element_type=f32) + residual
+    return jnp.concatenate(context, 1)
+
+
+def leave_kernel(wo_ref, *refs):
+    partials, sent_ref = refs[:-1], refs[-1]
+    half = sent_ref.shape[0]
+    context = joined_rows(partials, (1 - lax.axis_index("req")) * half, half)
+    sent_ref[...] = jnp.dot(context, wo_ref[...], preferred_element_type=f32).astype(bf16)
+
+
+def keep_kernel(wo_ref, tok_ref, *refs):
+    partials, out_ref = refs[:-1], refs[-1]
+    half = out_ref.shape[0]
+    first = lax.axis_index("req") * half
+    context = joined_rows(partials, first, half)
+    residual = tok_ref[pl.ds(pl.multiple_of(first, half), half), :].astype(f32)
+    out_ref[...] = jnp.dot(context, wo_ref[...], preferred_element_type=f32) + residual
 
 
 def cache_kernel(pieces, held, block_ref, slot_ref, *refs):
@@ -442,33 +451,33 @@
         )(block_split, page_slot, *arrays, *held)
 
     if n == 16:
-        everyone = range(n)
-
-        def along(shift, kv=kv):
-            source = lambda shard, i: (shard + n - 4 * shift) % n
-            return Piece([move(kv, [(i, (i + 4 * shift) % n) for i in everyone])], source)
-
-        def across(piece):
-            source = lambda shard, i: piece.source_of(shard ^ 2, i)
-            return Piece([swap(piece.arrays[0], n, 2)], source)
+
+        def swapped(piece, bits):
+            source = lambda shard, i: piece.source_of(shard ^ bits, i)
+            return Piece([swap(piece.arrays[0], n, bits)], source)
 
         own = Piece([kv], at_distance(0))
-        beside, first, second, third = across(own), along(3), along(1), along(2)
-        first, later_kv = tied(first, kv)
-        third = along(2, later_kv)
-        early = [own, beside, first, second]
-        first_across = across(first)
+        second, first, beside = swapped(own, 8), swapped(own, 4), swapped(own, 2)
+        queries, kv = pl.pallas_call(
+            stage_kernel,
+            out_shape=(struct(queries.shape, bf16), struct(kv.shape, bf16)),
+            in_specs=in_vmem(2),
+            out_specs=tuple(in_vmem(2)),
+            compiler_params=kernel_params(24),
+            cost_estimate=cost(0, 8 * rows * kv_width),
+            name="stage",
+        )(queries, kv)
+        (second, beside), kv = tied_all([second, beside], kv)
+        own = own.moved([kv])
+        third = swapped(second, 4)
+        early = [own, beside, first, second, third]
+        late = [swapped(second, 2), swapped(first, 2), swapped(third, 2)]
         partials = attend(early)
-        third, partials[1] = tied(third, partials[1])
-        later = [third, first_across]
-        last = [across(second), across(third)]
-        queries, partials[1] = lax.optimization_barrier((queries, partials[1]))
-        partials += attend(later)
-        placed, partials[4] = tied_all([own, beside, first, second], partials[4])
+        placed, partials[1] = tied_all(early, partials[1])
         held = place_pages(placed)
-        queries, partials[4], held = lax.optimization_barrier((queries, partials[4], held))
-        partials += attend(last)
-        remaining = [third, first_across] + last
+        queries, partials[1], held = lax.optimization_barrier((queries, partials[1], held))
+        partials += attend(late)
+        remaining = late
     else:
         same = [list(range(c, n, 2)) for c in range(2)]
         gathered = lax.all_gather(kv, "seq", axis=0, tiled=True, axis_index_groups=same)
@@ -478,26 +487,25 @@
     remaining, _ = with_refs(remaining, arrays)
     cache, other = place_pages(remaining, held)
     partials[-3], cache, other = lax.optimization_barrier((partials[-3], cache, other))
-    sent, kept = pl.pallas_call(
-        merge_kernel,
-        out_shape=(struct((half, width), bf16), struct((half, q_width), bf16)),
+    sent = pl.pallas_call(
+        leave_kernel,
+        out_shape=struct((half, width), bf16),
         in_specs=in_vmem(1 + len(partials)),
-        out_specs=tuple(in_vmem(2)),
+        out_specs=in_vmem(1)[0],
         compiler_params=kernel_params(24),
         cost_estimate=cost(rows * width * q_width, 2 * width * q_width),
-        name="merge",
+        name="leave",
     )(w_out, *partials)
     received = lax.ppermute(sent, "req", [(i, (i + 1) % parts) for i in range(parts)])
     kept = pl.pallas_call(
         keep_kernel,
         out_shape=struct((half, width), f32),
-        in_specs=in_vmem(3),
+        in_specs=in_vmem(2 + len(partials)),
         out_specs=in_vmem(1)[0],
         compiler_params=kernel_params(24),
         cost_estimate=cost(rows * width * q_width, 2 * width * q_width),
         name="keep",
-    )(kept, w_out, tokens)
-
+    )(w_out, tokens, *partials)
     cache = cache + swap(other, n, 1)
     hidden = (kept + received.astype(f32)).astype(bf16)
     return hidden, cache

time: 42.9 us -> 42.3 us (0.986)
  waiting for transfers between devices: 9.86 us -> 14.2 us
  local copies, waits for them, and re-layouts: 4.53 us -> 1.83 us
  starting transfers between devices: 14.1 us -> 12.6 us
  Pallas kernels: 11.8 us -> 11.2 us
    ppermute x9 -> x11, waiting for transfers between devices: 0.02 us -> 8.97 us  [swap(): return lax.ppermute(x, 'seq', [(i, i ^ bit) for i in range(n)])]
    ppermute x3 -> x0, starting transfers between devices: 5.31 us -> none  [move(): return lax.ppermute(x, 'seq', pairs)]
    ppermute x3 -> x0, waiting for transfers between devices: 4.39 us -> none  [move(): return lax.ppermute(x, 'seq', pairs)]
    ppermute x9 -> x11, starting transfers between devices: 7.21 us -> 11 us  [swap(): return lax.ppermute(x, 'seq', [(i, i ^ bit) for i in range(n)])]
    unnamed x20 -> x14, local copies, waits for them, and re-layouts: 4.53 us -> 1.83 us
    pallas_call x3 -> x2, Pallas kernels: 4.02 us -> 3.46 us  [attend(): pl.pallas_call(functools.partial(attend_kernel, pieces), out_shape=(struc...]
    pallas_call x1 -> x2, Pallas kernels: 1.19 us -> 0.81 us  [the longest x1 0.79 us: on_device(): pl.pallas_call(leave_kernel, out_shape=struct((half, width), bf16), in_sp...]
  transfers between devices with their start and end apart: 13 -> 12, of which waited for: 4 -> 5; matrix products, arithmetic and copies ran while one was open for 2% -> 2% of each run, Pallas kernels for 18% -> 16%
where the time goes in v7:
time: 42.3 us; the launch traced here: 42.1 us
  waiting for transfers between devices  14.2 us (34%)
  starting transfers between devices  12.6 us (30%)
  Pallas kernels  11.2 us (26%)
  local copies, waits for them, and re-layouts  1.83 us (4%)
  other arithmetic  1.54 us (4%)
  between operations  0.79 us (2%)
    ppermute x11, starting transfers between devices, swap(): return lax.ppermute(x, 'seq', [(i, i ^ bit) for i in range(n)])  11 us
    ppermute x11, waiting for transfers between devices, swap(): return lax.ppermute(x, 'seq', [(i, i ^ bit) for i in range(n)])  8.97 us
    ppermute x1, waiting for transfers between devices, on_device(): lax.ppermute(sent, 'req', [(i, (i + 1) % parts) for i in range(parts)])  5.19 us
    pallas_call x1, Pallas kernels, on_device(): pl.pallas_call(project_kernel, out_shape=(struct((rows, kv_width), bf16),...  4.32 us
    pallas_call x2, Pallas kernels, attend(): pl.pallas_call(functools.partial(attend_kernel, pieces), out_shape=(struc...  3.46 us
    unnamed x14, local copies, waits for them, and re-layouts  1.83 us
    pallas_call x2, Pallas kernels, place_pages(): pl.pallas_call(functools.partial(cache_kernel, pieces, bool(held)), out_s...  1.82 us
    ppermute x1, starting transfers between devices, on_device(): lax.ppermute(sent, 'req', [(i, (i + 1) % parts) for i in range(parts)])  1.58 us
  transfers between devices with their start and end apart: 12, of which 5 were waited for; matrix products, arithmetic and copies ran while one was open for 2% of the time, Pallas kernels for 16%

profile of v7, /device:TPU:0, one launch (start us, length us, event | category | flops | bytes accessed | tf_op | source)
XLA Modules:
  0.0 42.1 jit_solution(17065105527979905037)
XLA Ops:
  0.7 4.3 %project.1 = (bf16[128,512]{1,0:T(8,128)(2,1)}, bf16[128,512]{1,0:T(8,128)(2,1)}) custom-call(s32[16]{0:T(128)} %block_ref.7, s32[4]{0:T(128)} %len_ref.3, f32[1,128]{1,0:T(1,128)} %constant.2.clone.freq_hbm, bf16[128,2048]{1,0:T(8,128)(2,1)} %tok_ref.1, f32[1,2048]{1,0:T(1,128)} %bitcast.1, bf16[2048,256]{1,0:T(8,128)(2,1)} %wk_hbm.1, ...), custom_call_target="tpu_custom_call" | custom-call | flops 536870912 | bytes 4194304 | tf_op jit(solution)/shard_map/project/pallas_call | solution.py:395
  5.0 3.0 %collective-permute-start.2 = (bf16[128,512]{1,0:T(8,128)(2,1)}, bf16[128,512]{1,0:T(8,128)(2,1)S(1)}, u32[]{:S(2)}, u32[]{:S(2)}) collective-permute-start(bf16[128,512]{1,0:T(8,128)(2,1)} %get-tuple-element.37.kv_ref), channel_id=1, source_target_pairs={{0,4},{2,6},{4,0},{6,2},{8,12},{10,14},{12,8},{14,10},{16,20},{18,... | collective-permute-start | bytes 393224 | tf_op jit(solution)/shard_map/ppermute | solution.py:357
  8.0 2.6 %collective-permute-start.1 = (bf16[128,512]{1,0:T(8,128)(2,1)}, bf16[128,512]{1,0:T(8,128)(2,1)S(1)}, u32[]{:S(2)}, u32[]{:S(2)}) collective-permute-start(bf16[128,512]{1,0:T(8,128)(2,1)} %get-tuple-element.37.kv_ref), channel_id=1, source_target_pairs={{0,16},{2,18},{4,20},{6,22},{8,24},{10,26},{12,28},{14,30},{16,0},... | collective-permute-start | bytes 393224 | tf_op jit(solution)/shard_map/ppermute | solution.py:357
  10.6 1.6 %collective-permute-start.3 = (bf16[128,512]{1,0:T(8,128)(2,1)}, bf16[128,512]{1,0:T(8,128)(2,1)S(1)}, u32[]{:S(2)}, u32[]{:S(2)}) collective-permute-start(bf16[128,512]{1,0:T(8,128)(2,1)} %get-tuple-element.37.kv_ref), channel_id=1, source_target_pairs={{0,8},{2,10},{4,12},{6,14},{8,0},{10,2},{12,4},{14,6},{16,24},{18,... | collective-permute-start | bytes 393224 | tf_op jit(solution)/shard_map/ppermute | solution.py:357
  12.2 0.9 %copy-done.2 = bf16[128,512]{1,0:T(8,128)(2,1)S(1)} copy-done((bf16[128,512]{1,0:T(8,128)(2,1)S(1)}, bf16[128,512]{1,0:T(8,128)(2,1)}, u32[]{:S(2)}) %copy-start.2) | copy-done | bytes 131096
  13.1 0.9 %copy-done.3 = bf16[128,512]{1,0:T(8,128)(2,1)S(1)} copy-done((bf16[128,512]{1,0:T(8,128)(2,1)S(1)}, bf16[128,512]{1,0:T(8,128)(2,1)}, u32[]{:S(2)}) %copy-start.3) | copy-done | bytes 131096
  14.0 3.0 %collective-permute-done.1.refs_3_ = bf16[128,512]{1,0:T(8,128)(2,1)S(1)} collective-permute-done((bf16[128,512]{1,0:T(8,128)(2,1)}, bf16[128,512]{1,0:T(8,128)(2,1)S(1)}, u32[]{:S(2)}, u32[]{:S(2)}) %collective-permute-start.1) | collective-permute-done | bytes 131104 | tf_op jit(solution)/shard_map/ppermute | solution.py:357
  17.0 0.7 %collective-permute-start.4 = (bf16[128,512]{1,0:T(8,128)(2,1)S(1)}, bf16[128,512]{1,0:T(8,128)(2,1)S(1)}, u32[]{:S(2)}, u32[]{:S(2)}) collective-permute-start(bf16[128,512]{1,0:T(8,128)(2,1)S(1)} %collective-permute-done.1.refs_3_), channel_id=1, source_target_pairs={{0,8},{2,10},{4,12},{6,14},{8,0},{10,2},{12,4},{14,6},{16,24},{18,... | collective-permute-start | bytes 393224 | tf_op jit(solution)/shard_map/ppermute | solution.py:357
  17.7 0.5 %collective-permute-start.6 = (bf16[128,512]{1,0:T(8,128)(2,1)S(1)}, bf16[128,512]{1,0:T(8,128)(2,1)S(1)}, u32[]{:S(2)}, u32[]{:S(2)}) collective-permute-start(bf16[128,512]{1,0:T(8,128)(2,1)S(1)} %collective-permute-done.1.refs_3_), channel_id=1, source_target_pairs={{0,4},{2,6},{4,0},{6,2},{8,12},{10,14},{12,8},{14,10},{16,20},{18,... | collective-permute-start | bytes 393224 | tf_op jit(solution)/shard_map/ppermute | solution.py:357
  18.2 1.5 %collective-permute-start.7 = (bf16[128,512]{1,0:T(8,128)(2,1)S(1)}, bf16[128,512]{1,0:T(8,128)(2,1)S(1)}, u32[]{:S(2)}, u32[]{:S(2)}) collective-permute-start(bf16[128,512]{1,0:T(8,128)(2,1)S(1)} %collective-permute-done.3.refs_2_), channel_id=1, source_target_pairs={{0,4},{2,6},{4,0},{6,2},{8,12},{10,14},{12,8},{14,10},{16,20},{18,... | collective-permute-start | bytes 393224 | tf_op jit(solution)/shard_map/ppermute | solution.py:357
  19.7 2.3 %collective-permute-done.4.refs_4_ = bf16[128,512]{1,0:T(8,128)(2,1)S(1)} collective-permute-done((bf16[128,512]{1,0:T(8,128)(2,1)S(1)}, bf16[128,512]{1,0:T(8,128)(2,1)S(1)}, u32[]{:S(2)}, u32[]{:S(2)}) %collective-permute-start.4) | collective-permute-done | bytes 131104 | tf_op jit(solution)/shard_map/ppermute | solution.py:357
  22.5 2.0 %attend.2 = (f32[128,512]{1,0:T(8,128)S(1)}, f32[128,128]{1,0:T(8,128)S(1)}, bf16[128,640]{1,0:T(8,128)(2,1)S(1)}) custom-call(s32[16]{0:T(128)S(1)} %copy-done.4, s32[4]{0:T(128)S(1)} %copy-done.6, bf16[128,512]{1,0:T(8,128)(2,1)S(1)} %get-tuple-element.55.q_ref, bf16[128,512]{1,0:T(8,128)(2,1)S(1)} %collective-permute-done.far_ref, ...), custom_call_target="tpu_custom_call" | custom-call | flops 335544320 | bytes 655360 | tf_op jit(solution)/shard_map/attend/pallas_call | solution.py:424
  24.5 1.0 %cache.2 = (bf16[8,2,32,256]{3,2,1,0:T(8,128)(2,1)S(1)}, bf16[8,2,32,256]{3,2,1,0:T(8,128)(2,1)S(1)}) custom-call(s32[16]{0:T(128)S(1)} %copy-done.4, s32[64]{0:T(128)S(1)} %copy-done.5, bf16[128,512]{1,0:T(8,128)(2,1)S(1)} %get-tuple-element.46.refs_0_, bf16[128,512]{1,0:T(8,128)(2,1)S(1)} %collective-permute-done.2.refs_1_, ...), custom_call_target="tpu_custom_call" | custom-call | bytes 262144 | tf_op jit(solution)/shard_map/cache/pallas_call | solution.py:442
  25.5 1.3 %collective-permute-done.7.refs_1_ = bf16[128,512]{1,0:T(8,128)(2,1)S(1)} collective-permute-done((bf16[128,512]{1,0:T(8,128)(2,1)S(1)}, bf16[128,512]{1,0:T(8,128)(2,1)S(1)}, u32[]{:S(2)}, u32[]{:S(2)}) %collective-permute-start.7) | collective-permute-done | bytes 131104 | tf_op jit(solution)/shard_map/ppermute | solution.py:357
  26.8 2.4 %collective-permute-done.8.refs_2_ = bf16[128,512]{1,0:T(8,128)(2,1)S(1)} collective-permute-done((bf16[128,512]{1,0:T(8,128)(2,1)S(1)}, bf16[128,512]{1,0:T(8,128)(2,1)S(1)}, u32[]{:S(2)}, u32[]{:S(2)}) %collective-permute-start.8) | collective-permute-done | bytes 131104 | tf_op jit(solution)/shard_map/ppermute | solution.py:357
  29.2 1.5 %attend.3 = (f32[128,512]{1,0:T(8,128)S(1)}, f32[128,128]{1,0:T(8,128)S(1)}, bf16[128,640]{1,0:T(8,128)(2,1)S(1)}) custom-call(s32[16]{0:T(128)S(1)} %copy-done.4, s32[4]{0:T(128)S(1)} %copy-done.6, bf16[128,512]{1,0:T(8,128)(2,1)S(1)} %get-tuple-element.55.q_ref, bf16[128,512]{1,0:T(8,128)(2,1)S(1)} %collective-permute-done.far_ref, ...), custom_call_target="tpu_custom_call" | custom-call | flops 201326592 | bytes 393216 | tf_op jit(solution)/shard_map/attend/pallas_call | solution.py:424
  30.8 0.8 %cache.3 = (bf16[8,2,32,256]{3,2,1,0:T(8,128)(2,1)S(1)}, bf16[8,2,32,256]{3,2,1,0:T(8,128)(2,1)S(1)}) custom-call(s32[16]{0:T(128)S(1)} %copy-done.4, s32[64]{0:T(128)S(1)} %copy-done.5, bf16[128,512]{1,0:T(8,128)(2,1)S(1)} %collective-permute-done.6.refs_0_, ...), custom_call_target="tpu_custom_call", output_to_operand_aliasing={{0}: (5, {}), {1}: (6, {})} | custom-call | bytes 262144 | tf_op jit(solution)/shard_map/cache/pallas_call | solution.py:442
  31.6 0.5 %collective-permute-start.11 = (bf16[8,2,32,256]{3,2,1,0:T(8,128)(2,1)S(1)}, bf16[8,2,32,256]{3,2,1,0:T(8,128)(2,1)S(1)}, u32[]{:S(2)}, u32[]{:S(2)}) collective-permute-start(bf16[8,2,32,256]{3,2,1,0:T(8,128)(2,1)S(1)} %get-tuple-element.69), channel_id=1, source_target_pairs={{0,2},{2,0},{4,6},{6,4},{8,10},{10,8},{12,14},{14,12},{16,18},{18,... | collective-permute-start | bytes 786440 | tf_op jit(solution)/shard_map/ppermute | solution.py:357
  32.2 0.8 %leave.1 = bf16[64,2048]{1,0:T(8,128)(2,1)S(1)} custom-call(bf16[512,2048]{1,0:T(8,128)(2,1)S(1)} %copy-done, f32[128,512]{1,0:T(8,128)S(1)} %get-tuple-element.43.refs_0_, f32[128,128]{1,0:T(8,128)S(1)} %get-tuple-element.53.refs_1_, bf16[128,640]{1,0:T(8,128)(2,1)S(1)} %collective-permute-done.5.refs_2_, f32[128,512]{1,0:T(8,128)S(1)} %get-tuple-element.65.refs_3_, ...), custom_call_target="tpu_custom_call" | custom-call | flops 134217728 | bytes 2097152 | tf_op jit(solution)/shard_map/leave/pallas_call | solution.py:490
  33.0 1.6 %collective-permute-start.10 = (bf16[64,2048]{1,0:T(8,128)(2,1)S(1)}, bf16[64,2048]{1,0:T(8,128)(2,1)S(1)}, u32[]{:S(2)}, u32[]{:S(2)}) collective-permute-start(bf16[64,2048]{1,0:T(8,128)(2,1)S(1)} %leave.1), channel_id=1, source_target_pairs={{0,1},{1,0},{2,3},{3,2},{4,5},{5,4},{6,7},{7,6},{8,9},{9,8},{10,11... | collective-permute-start | bytes 786440 | tf_op jit(solution)/shard_map/ppermute | solution.py:499
  34.6 0.8 %keep.1 = f32[64,2048]{1,0:T(8,128)S(1)} custom-call(bf16[512,2048]{1,0:T(8,128)(2,1)S(1)} %copy-done, bf16[128,2048]{1,0:T(8,128)(2,1)S(1)} %copy-done.1, f32[128,512]{1,0:T(8,128)S(1)} %get-tuple-element.43.refs_0_, f32[128,128]{1,0:T(8,128)S(1)} %get-tuple-element.53.refs_1_, bf16[128,640]{1,0:T(8,128)(2,1)S(1)} %collective-permute-done.5.refs_2_, ...), custom_call_target="tpu_custom_call" | custom-call | flops 134217728 | bytes 2097152 | tf_op jit(solution)/shard_map/keep/pallas_call | solution.py:500
  35.4 0.8 %add.7 = bf16[8,2,32,256]{3,2,1,0:T(8,128)(2,1)} add(bf16[8,2,32,256]{3,2,1,0:T(8,128)(2,1)S(1)} %get-tuple-element.68, bf16[8,2,32,256]{3,2,1,0:T(8,128)(2,1)S(1)} %collective-permute-done.11) | non-fusion elementwise | flops 131072 | bytes 786432 | tf_op jit(solution)/shard_map/add | solution.py:509
  36.2 5.2 %collective-permute-done.10 = bf16[64,2048]{1,0:T(8,128)(2,1)S(1)} collective-permute-done((bf16[64,2048]{1,0:T(8,128)(2,1)S(1)}, bf16[64,2048]{1,0:T(8,128)(2,1)S(1)}, u32[]{:S(2)}, u32[]{:S(2)}) %collective-permute-start.10) | collective-permute-done | bytes 262176 | tf_op jit(solution)/shard_map/ppermute | solution.py:499
  41.4 0.8 %add_convert_fusion = bf16[64,2048]{1,0:T(8,128)(2,1)} fusion(f32[64,2048]{1,0:T(8,128)S(1)} %keep.1, bf16[64,2048]{1,0:T(8,128)(2,1)S(1)} %collective-permute-done.10), kind=kLoop, calls=%fused_computation | loop fusion | flops 393216 | bytes 1048576 | tf_op jit(solution)/shard_map/convert_element_type | solution.py:510
  (24 shorter events, 0.7 us)
Async XLA Ops:
  0.6 21.8 %copy-start.4 = (s32[16]{0:T(128)S(1)}, s32[16]{0:T(128)}, u32[]{:S(2)}) copy-start(s32[16]{0:T(128)} %block_ref.7) | copy-start | bytes 196
  0.6 21.8 %copy-start.6 = (s32[4]{0:T(128)S(1)}, s32[4]{0:T(128)}, u32[]{:S(2)}) copy-start(s32[4]{0:T(128)} %len_ref.3) | copy-start | bytes 52
  0.7 23.9 %copy-start.5 = (s32[64]{0:T(128)S(1)}, s32[64]{0:T(128)}, u32[]{:S(2)}) copy-start(s32[64]{0:T(128)} %slot_ref.3) | copy-start | bytes 772
  5.0 27.2 %copy-start = (bf16[512,2048]{1,0:T(8,128)(2,1)S(1)}, bf16[512,2048]{1,0:T(8,128)(2,1)}, u32[]{:S(2)}) copy-start(bf16[512,2048]{1,0:T(8,128)(2,1)} %wo_ref.3) | copy-start | bytes 6291460
  5.0 9.0 %collective-permute-start.2 = (bf16[128,512]{1,0:T(8,128)(2,1)}, bf16[128,512]{1,0:T(8,128)(2,1)S(1)}, u32[]{:S(2)}, u32[]{:S(2)}) collective-permute-start(bf16[128,512]{1,0:T(8,128)(2,1)} %get-tuple-element.37.kv_ref), channel_id=1, source_target_pairs={{0,4},{2,6},{4,0},{6,2},{8,12},{10,14},{12,8},{14,10},{16,20},{18,... | collective-permute-start | bytes 393224 | tf_op jit(solution)/shard_map/ppermute | solution.py:357
  8.0 9.0 %collective-permute-start.1 = (bf16[128,512]{1,0:T(8,128)(2,1)}, bf16[128,512]{1,0:T(8,128)(2,1)S(1)}, u32[]{:S(2)}, u32[]{:S(2)}) collective-permute-start(bf16[128,512]{1,0:T(8,128)(2,1)} %get-tuple-element.37.kv_ref), channel_id=1, source_target_pairs={{0,16},{2,18},{4,20},{6,22},{8,24},{10,26},{12,28},{14,30},{16,0},... | collective-permute-start | bytes 393224 | tf_op jit(solution)/shard_map/ppermute | solution.py:357
  10.6 7.6 %collective-permute-start.3 = (bf16[128,512]{1,0:T(8,128)(2,1)}, bf16[128,512]{1,0:T(8,128)(2,1)S(1)}, u32[]{:S(2)}, u32[]{:S(2)}) collective-permute-start(bf16[128,512]{1,0:T(8,128)(2,1)} %get-tuple-element.37.kv_ref), channel_id=1, source_target_pairs={{0,8},{2,10},{4,12},{6,14},{8,0},{10,2},{12,4},{14,6},{16,24},{18,... | collective-permute-start | bytes 393224 | tf_op jit(solution)/shard_map/ppermute | solution.py:357
  12.2 0.9 %copy-start.2 = (bf16[128,512]{1,0:T(8,128)(2,1)S(1)}, bf16[128,512]{1,0:T(8,128)(2,1)}, u32[]{:S(2)}) copy-start(bf16[128,512]{1,0:T(8,128)(2,1)} %get-tuple-element.36.q_ref) | copy-start | bytes 393220
  13.1 0.9 %copy-start.3 = (bf16[128,512]{1,0:T(8,128)(2,1)S(1)}, bf16[128,512]{1,0:T(8,128)(2,1)}, u32[]{:S(2)}) copy-start(bf16[128,512]{1,0:T(8,128)(2,1)} %get-tuple-element.37.kv_ref) | copy-start | bytes 393220
  17.0 5.0 %collective-permute-start.4 = (bf16[128,512]{1,0:T(8,128)(2,1)S(1)}, bf16[128,512]{1,0:T(8,128)(2,1)S(1)}, u32[]{:S(2)}, u32[]{:S(2)}) collective-permute-start(bf16[128,512]{1,0:T(8,128)(2,1)S(1)} %collective-permute-done.1.refs_3_), channel_id=1, source_target_pairs={{0,8},{2,10},{4,12},{6,14},{8,0},{10,2},{12,4},{14,6},{16,24},{18,... | collective-permute-start | bytes 393224 | tf_op jit(solution)/shard_map/ppermute | solution.py:357
  17.7 4.8 %collective-permute-start = (bf16[128,512]{1,0:T(8,128)(2,1)S(1)}, bf16[128,512]{1,0:T(8,128)(2,1)S(1)}, u32[]{:S(2)}, u32[]{:S(2)}) collective-permute-start(bf16[128,512]{1,0:T(8,128)(2,1)S(1)} %copy-done.2), channel_id=1, source_target_pairs={{0,2},{2,0},{4,6},{6,4},{8,10},{10,8},{12,14},{14,12},{16,18},{18,... | collective-permute-start | bytes 393224 | tf_op jit(solution)/shard_map/ppermute | solution.py:357
  17.7 9.1 %collective-permute-start.6 = (bf16[128,512]{1,0:T(8,128)(2,1)S(1)}, bf16[128,512]{1,0:T(8,128)(2,1)S(1)}, u32[]{:S(2)}, u32[]{:S(2)}) collective-permute-start(bf16[128,512]{1,0:T(8,128)(2,1)S(1)} %collective-permute-done.1.refs_3_), channel_id=1, source_target_pairs={{0,4},{2,6},{4,0},{6,2},{8,12},{10,14},{12,8},{14,10},{16,20},{18,... | collective-permute-start | bytes 393224 | tf_op jit(solution)/shard_map/ppermute | solution.py:357
  18.2 8.6 %collective-permute-start.7 = (bf16[128,512]{1,0:T(8,128)(2,1)S(1)}, bf16[128,512]{1,0:T(8,128)(2,1)S(1)}, u32[]{:S(2)}, u32[]{:S(2)}) collective-permute-start(bf16[128,512]{1,0:T(8,128)(2,1)S(1)} %collective-permute-done.3.refs_2_), channel_id=1, source_target_pairs={{0,4},{2,6},{4,0},{6,2},{8,12},{10,14},{12,8},{14,10},{16,20},{18,... | collective-permute-start | bytes 393224 | tf_op jit(solution)/shard_map/ppermute | solution.py:357
  22.0 7.2 %collective-permute-start.8 = (bf16[128,512]{1,0:T(8,128)(2,1)S(1)}, bf16[128,512]{1,0:T(8,128)(2,1)S(1)}, u32[]{:S(2)}, u32[]{:S(2)}) collective-permute-start(bf16[128,512]{1,0:T(8,128)(2,1)S(1)} %collective-permute-done.4.refs_4_), channel_id=1, source_target_pairs={{0,4},{2,6},{4,0},{6,2},{8,12},{10,14},{12,8},{14,10},{16,20},{18,... | collective-permute-start | bytes 393224 | tf_op jit(solution)/shard_map/ppermute | solution.py:357
  24.4 7.8 %collective-permute-start.5 = (bf16[128,640]{1,0:T(8,128)(2,1)S(1)}, bf16[128,640]{1,0:T(8,128)(2,1)S(1)}, u32[]{:S(2)}, u32[]{:S(2)}) collective-permute-start(bf16[128,640]{1,0:T(8,128)(2,1)S(1)} %get-tuple-element.54), channel_id=1, source_target_pairs={{0,2},{2,0},{4,6},{6,4},{8,10},{10,8},{12,14},{14,12},{16,18},{18,... | collective-permute-start | bytes 491528 | tf_op jit(solution)/shard_map/ppermute | solution.py:357
  30.7 1.5 %collective-permute-start.9 = (bf16[128,640]{1,0:T(8,128)(2,1)S(1)}, bf16[128,640]{1,0:T(8,128)(2,1)S(1)}, u32[]{:S(2)}, u32[]{:S(2)}) collective-permute-start(bf16[128,640]{1,0:T(8,128)(2,1)S(1)} %get-tuple-element.67), channel_id=1, source_target_pairs={{0,2},{2,0},{4,6},{6,4},{8,10},{10,8},{12,14},{14,12},{16,18},{18,... | collective-permute-start | bytes 491528 | tf_op jit(solution)/shard_map/ppermute | solution.py:357
  30.8 3.8 %copy-start.1 = (bf16[128,2048]{1,0:T(8,128)(2,1)S(1)}, bf16[128,2048]{1,0:T(8,128)(2,1)}, u32[]{:S(2)}) copy-start(bf16[128,2048]{1,0:T(8,128)(2,1)} %tok_ref.1) | copy-start | bytes 1572868
  31.6 3.7 %collective-permute-start.11 = (bf16[8,2,32,256]{3,2,1,0:T(8,128)(2,1)S(1)}, bf16[8,2,32,256]{3,2,1,0:T(8,128)(2,1)S(1)}, u32[]{:S(2)}, u32[]{:S(2)}) collective-permute-start(bf16[8,2,32,256]{3,2,1,0:T(8,128)(2,1)S(1)} %get-tuple-element.69), channel_id=1, source_target_pairs={{0,2},{2,0},{4,6},{6,4},{8,10},{10,8},{12,14},{14,12},{16,18},{18,... | collective-permute-start | bytes 786440 | tf_op jit(solution)/shard_map/ppermute | solution.py:357
  33.0 8.4 %collective-permute-start.10 = (bf16[64,2048]{1,0:T(8,128)(2,1)S(1)}, bf16[64,2048]{1,0:T(8,128)(2,1)S(1)}, u32[]{:S(2)}, u32[]{:S(2)}) collective-permute-start(bf16[64,2048]{1,0:T(8,128)(2,1)S(1)} %leave.1), channel_id=1, source_target_pairs={{0,1},{1,0},{2,3},{3,2},{4,5},{5,4},{6,7},{7,6},{8,9},{9,8},{10,11... | collective-permute-start | bytes 786440 | tf_op jit(solution)/shard_map/ppermute | solution.py:499

commit v8 on v7

--- a/solution.py
+++ b/solution.py
@@ -467,11 +467,12 @@
             cost_estimate=cost(0, 8 * rows * kv_width),
             name="stage",
         )(queries, kv)
-        (second, beside), kv = tied_all([second, beside], kv)
+        first_across = swapped(first, 2)
+        (second, beside, first_across), kv = tied_all([second, beside, first_across], kv)
         own = own.moved([kv])
         third = swapped(second, 4)
-        early = [own, beside, first, second, third]
-        late = [swapped(second, 2), swapped(first, 2), swapped(third, 2)]
+        early = [own, beside, first, second, first_across]
+        late = [third, swapped(second, 2), swapped(third, 2)]
         partials = attend(early)
         placed, partials[1] = tied_all(early, partials[1])
         held = place_pages(placed)

time: 42.3 us -> 41.4 us (0.979)
  waiting for transfers between devices: 14.2 us -> 10 us
  starting transfers between devices: 12.6 us -> 15.9 us
    ppermute x11, waiting for transfers between devices: 8.97 us -> 4.65 us  [swap(): return lax.ppermute(x, 'seq', [(i, i ^ bit) for i in range(n)])]
    ppermute x11, starting transfers between devices: 11 us -> 14.3 us  [swap(): return lax.ppermute(x, 'seq', [(i, i ^ bit) for i in range(n)])]
  transfers between devices with their start and end apart: 12 -> 12, of which waited for: 5 -> 4; matrix products, arithmetic and copies ran while one was open for 2% -> 2% of each run, Pallas kernels for 16% -> 17%
where the time goes in v8:
time: 41.4 us; the launch traced here: 41.3 us
  starting transfers between devices  15.9 us (38%)
  Pallas kernels  11.2 us (27%)
  waiting for transfers between devices  10 us (24%)
  local copies, waits for them, and re-layouts  1.83 us (4%)
  other arithmetic  1.54 us (4%)
  between operations  0.78 us (2%)
    ppermute x11, starting transfers between devices, swap(): return lax.ppermute(x, 'seq', [(i, i ^ bit) for i in range(n)])  14.3 us
    ppermute x1, waiting for transfers between devices, on_device(): lax.ppermute(sent, 'req', [(i, (i + 1) % parts) for i in range(parts)])  5.37 us
    ppermute x11, waiting for transfers between devices, swap(): return lax.ppermute(x, 'seq', [(i, i ^ bit) for i in range(n)])  4.65 us
    pallas_call x1, Pallas kernels, on_device(): pl.pallas_call(project_kernel, out_shape=(struct((rows, kv_width), bf16),...  4.32 us
    pallas_call x2, Pallas kernels, attend(): pl.pallas_call(functools.partial(attend_kernel, pieces), out_shape=(struc...  3.46 us
    unnamed x14, local copies, waits for them, and re-layouts  1.83 us
    pallas_call x2, Pallas kernels, place_pages(): pl.pallas_call(functools.partial(cache_kernel, pieces, bool(held)), out_s...  1.81 us
    ppermute x1, starting transfers between devices, on_device(): lax.ppermute(sent, 'req', [(i, (i + 1) % parts) for i in range(parts)])  1.59 us
  transfers between devices with their start and end apart: 12, of which 4 were waited for; matrix products, arithmetic and copies ran while one was open for 2% of the time, Pallas kernels for 17%

profile of v8, /device:TPU:0, one launch (start us, length us, event | category | flops | bytes accessed | tf_op | source)
XLA Modules:
  0.0 41.3 jit_solution(9761570564598328893)
XLA Ops:
  0.7 4.3 %project.1 = (bf16[128,512]{1,0:T(8,128)(2,1)}, bf16[128,512]{1,0:T(8,128)(2,1)}) custom-call(s32[16]{0:T(128)} %block_ref.7, s32[4]{0:T(128)} %len_ref.3, f32[1,128]{1,0:T(1,128)} %constant.2.clone.freq_hbm, bf16[128,2048]{1,0:T(8,128)(2,1)} %tok_ref.1, f32[1,2048]{1,0:T(1,128)} %bitcast.1, bf16[2048,256]{1,0:T(8,128)(2,1)} %wk_hbm.1, ...), custom_call_target="tpu_custom_call" | custom-call | flops 536870912 | bytes 4194304 | tf_op jit(solution)/shard_map/project/pallas_call | solution.py:395
  5.0 3.1 %collective-permute-start.3 = (bf16[128,512]{1,0:T(8,128)(2,1)}, bf16[128,512]{1,0:T(8,128)(2,1)S(1)}, u32[]{:S(2)}, u32[]{:S(2)}) collective-permute-start(bf16[128,512]{1,0:T(8,128)(2,1)} %get-tuple-element.38.kv_ref), channel_id=1, source_target_pairs={{0,8},{2,10},{4,12},{6,14},{8,0},{10,2},{12,4},{14,6},{16,24},{18,... | collective-permute-start | bytes 393224 | tf_op jit(solution)/shard_map/ppermute | solution.py:357
  8.1 1.5 %collective-permute-start.2 = (bf16[128,512]{1,0:T(8,128)(2,1)}, bf16[128,512]{1,0:T(8,128)(2,1)S(1)}, u32[]{:S(2)}, u32[]{:S(2)}) collective-permute-start(bf16[128,512]{1,0:T(8,128)(2,1)} %get-tuple-element.38.kv_ref), channel_id=1, source_target_pairs={{0,4},{2,6},{4,0},{6,2},{8,12},{10,14},{12,8},{14,10},{16,20},{18,... | collective-permute-start | bytes 393224 | tf_op jit(solution)/shard_map/ppermute | solution.py:357
  9.6 2.6 %collective-permute-start.1 = (bf16[128,512]{1,0:T(8,128)(2,1)}, bf16[128,512]{1,0:T(8,128)(2,1)S(1)}, u32[]{:S(2)}, u32[]{:S(2)}) collective-permute-start(bf16[128,512]{1,0:T(8,128)(2,1)} %get-tuple-element.38.kv_ref), channel_id=1, source_target_pairs={{0,16},{2,18},{4,20},{6,22},{8,24},{10,26},{12,28},{14,30},{16,0},... | collective-permute-start | bytes 393224 | tf_op jit(solution)/shard_map/ppermute | solution.py:357
  12.2 2.7 %collective-permute-start.4 = (bf16[128,512]{1,0:T(8,128)(2,1)S(1)}, bf16[128,512]{1,0:T(8,128)(2,1)S(1)}, u32[]{:S(2)}, u32[]{:S(2)}) collective-permute-start(bf16[128,512]{1,0:T(8,128)(2,1)S(1)} %collective-permute-done.3.refs_2_), channel_id=1, source_target_pairs={{0,4},{2,6},{4,0},{6,2},{8,12},{10,14},{12,8},{14,10},{16,20},{18,... | collective-permute-start | bytes 393224 | tf_op jit(solution)/shard_map/ppermute | solution.py:357
  14.9 0.9 %copy-done.2 = bf16[128,512]{1,0:T(8,128)(2,1)S(1)} copy-done((bf16[128,512]{1,0:T(8,128)(2,1)S(1)}, bf16[128,512]{1,0:T(8,128)(2,1)}, u32[]{:S(2)}) %copy-start.2) | copy-done | bytes 131096
  15.8 0.9 %copy-done.3 = bf16[128,512]{1,0:T(8,128)(2,1)S(1)} copy-done((bf16[128,512]{1,0:T(8,128)(2,1)S(1)}, bf16[128,512]{1,0:T(8,128)(2,1)}, u32[]{:S(2)}) %copy-start.3) | copy-done | bytes 131096
  16.8 1.4 %collective-permute-done.1.refs_3_ = bf16[128,512]{1,0:T(8,128)(2,1)S(1)} collective-permute-done((bf16[128,512]{1,0:T(8,128)(2,1)}, bf16[128,512]{1,0:T(8,128)(2,1)S(1)}, u32[]{:S(2)}, u32[]{:S(2)}) %collective-permute-start.1) | collective-permute-done | bytes 131104 | tf_op jit(solution)/shard_map/ppermute | solution.py:357
  18.2 0.3 collective-permute-start.6
  18.5 1.7 %collective-permute-start.7 = (bf16[128,512]{1,0:T(8,128)(2,1)S(1)}, bf16[128,512]{1,0:T(8,128)(2,1)S(1)}, u32[]{:S(2)}, u32[]{:S(2)}) collective-permute-start(bf16[128,512]{1,0:T(8,128)(2,1)S(1)} %collective-permute-done.1.refs_3_), channel_id=1, source_target_pairs={{0,4},{2,6},{4,0},{6,2},{8,12},{10,14},{12,8},{14,10},{16,20},{18,... | collective-permute-start | bytes 393224 | tf_op jit(solution)/shard_map/ppermute | solution.py:357
  20.2 3.0 %collective-permute-done.6.refs_0_ = bf16[128,512]{1,0:T(8,128)(2,1)S(1)} collective-permute-done((bf16[128,512]{1,0:T(8,128)(2,1)S(1)}, bf16[128,512]{1,0:T(8,128)(2,1)S(1)}, u32[]{:S(2)}, u32[]{:S(2)}) %collective-permute-start.6) | collective-permute-done | bytes 131104 | tf_op jit(solution)/shard_map/ppermute | solution.py:357
  23.2 1.7 %collective-permute-start.8 = (bf16[128,512]{1,0:T(8,128)(2,1)S(1)}, bf16[128,512]{1,0:T(8,128)(2,1)S(1)}, u32[]{:S(2)}, u32[]{:S(2)}) collective-permute-start(bf16[128,512]{1,0:T(8,128)(2,1)S(1)} %collective-permute-done.6.refs_0_), channel_id=1, source_target_pairs={{0,4},{2,6},{4,0},{6,2},{8,12},{10,14},{12,8},{14,10},{16,20},{18,... | collective-permute-start | bytes 393224 | tf_op jit(solution)/shard_map/ppermute | solution.py:357
  24.9 2.0 %attend.2 = (f32[128,512]{1,0:T(8,128)S(1)}, f32[128,128]{1,0:T(8,128)S(1)}, bf16[128,640]{1,0:T(8,128)(2,1)S(1)}) custom-call(s32[16]{0:T(128)S(1)} %copy-done.4, s32[4]{0:T(128)S(1)} %copy-done.6, bf16[128,512]{1,0:T(8,128)(2,1)S(1)} %get-tuple-element.57.q_ref, bf16[128,512]{1,0:T(8,128)(2,1)S(1)} %collective-permute-done.far_ref, ...), custom_call_target="tpu_custom_call" | custom-call | flops 335544320 | bytes 655360 | tf_op jit(solution)/shard_map/attend/pallas_call | solution.py:424
  26.9 1.0 %cache.2 = (bf16[8,2,32,256]{3,2,1,0:T(8,128)(2,1)S(1)}, bf16[8,2,32,256]{3,2,1,0:T(8,128)(2,1)S(1)}) custom-call(s32[16]{0:T(128)S(1)} %copy-done.4, s32[64]{0:T(128)S(1)} %copy-done.5, bf16[128,512]{1,0:T(8,128)(2,1)S(1)} %get-tuple-element.48.refs_0_, bf16[128,512]{1,0:T(8,128)(2,1)S(1)} %collective-permute-done.2.refs_1_, ...), custom_call_target="tpu_custom_call" | custom-call | bytes 262144 | tf_op jit(solution)/shard_map/cache/pallas_call | solution.py:442
  28.1 1.5 %attend.3 = (f32[128,512]{1,0:T(8,128)S(1)}, f32[128,128]{1,0:T(8,128)S(1)}, bf16[128,640]{1,0:T(8,128)(2,1)S(1)}) custom-call(s32[16]{0:T(128)S(1)} %copy-done.4, s32[4]{0:T(128)S(1)} %copy-done.6, bf16[128,512]{1,0:T(8,128)(2,1)S(1)} %get-tuple-element.57.q_ref, bf16[128,512]{1,0:T(8,128)(2,1)S(1)} %collective-permute-done.far_ref, ...), custom_call_target="tpu_custom_call" | custom-call | flops 201326592 | bytes 393216 | tf_op jit(solution)/shard_map/attend/pallas_call | solution.py:424
  29.6 0.3 collective-permute-start.9
  30.0 0.8 %cache.3 = (bf16[8,2,32,256]{3,2,1,0:T(8,128)(2,1)S(1)}, bf16[8,2,32,256]{3,2,1,0:T(8,128)(2,1)S(1)}) custom-call(s32[16]{0:T(128)S(1)} %copy-done.4, s32[64]{0:T(128)S(1)} %copy-done.5, bf16[128,512]{1,0:T(8,128)(2,1)S(1)} %collective-permute-done.6.refs_0_, ...), custom_call_target="tpu_custom_call", output_to_operand_aliasing={{0}: (5, {}), {1}: (6, {})} | custom-call | bytes 262144 | tf_op jit(solution)/shard_map/cache/pallas_call | solution.py:442
  30.8 0.3 collective-permute-start.11
  31.2 0.8 %leave.1 = bf16[64,2048]{1,0:T(8,128)(2,1)S(1)} custom-call(bf16[512,2048]{1,0:T(8,128)(2,1)S(1)} %copy-done, f32[128,512]{1,0:T(8,128)S(1)} %get-tuple-element.45.refs_0_, f32[128,128]{1,0:T(8,128)S(1)} %get-tuple-element.55.refs_1_, bf16[128,640]{1,0:T(8,128)(2,1)S(1)} %collective-permute-done.5.refs_2_, f32[128,512]{1,0:T(8,128)S(1)} %get-tuple-element.67.refs_3_, ...), custom_call_target="tpu_custom_call" | custom-call | flops 134217728 | bytes 2097152 | tf_op jit(solution)/shard_map/leave/pallas_call | solution.py:491
  31.9 1.6 %collective-permute-start.10 = (bf16[64,2048]{1,0:T(8,128)(2,1)S(1)}, bf16[64,2048]{1,0:T(8,128)(2,1)S(1)}, u32[]{:S(2)}, u32[]{:S(2)}) collective-permute-start(bf16[64,2048]{1,0:T(8,128)(2,1)S(1)} %leave.1), channel_id=1, source_target_pairs={{0,1},{1,0},{2,3},{3,2},{4,5},{5,4},{6,7},{7,6},{8,9},{9,8},{10,11... | collective-permute-start | bytes 786440 | tf_op jit(solution)/shard_map/ppermute | solution.py:500
  33.5 0.8 %keep.1 = f32[64,2048]{1,0:T(8,128)S(1)} custom-call(bf16[512,2048]{1,0:T(8,128)(2,1)S(1)} %copy-done, bf16[128,2048]{1,0:T(8,128)(2,1)S(1)} %copy-done.1, f32[128,512]{1,0:T(8,128)S(1)} %get-tuple-element.45.refs_0_, f32[128,128]{1,0:T(8,128)S(1)} %get-tuple-element.55.refs_1_, bf16[128,640]{1,0:T(8,128)(2,1)S(1)} %collective-permute-done.5.refs_2_, ...), custom_call_target="tpu_custom_call" | custom-call | flops 134217728 | bytes 2097152 | tf_op jit(solution)/shard_map/keep/pallas_call | solution.py:501
  34.3 0.8 %add.7 = bf16[8,2,32,256]{3,2,1,0:T(8,128)(2,1)} add(bf16[8,2,32,256]{3,2,1,0:T(8,128)(2,1)S(1)} %get-tuple-element.70, bf16[8,2,32,256]{3,2,1,0:T(8,128)(2,1)S(1)} %collective-permute-done.11) | non-fusion elementwise | flops 131072 | bytes 786432 | tf_op jit(solution)/shard_map/add | solution.py:510
  35.1 5.4 %collective-permute-done.10 = bf16[64,2048]{1,0:T(8,128)(2,1)S(1)} collective-permute-done((bf16[64,2048]{1,0:T(8,128)(2,1)S(1)}, bf16[64,2048]{1,0:T(8,128)(2,1)S(1)}, u32[]{:S(2)}, u32[]{:S(2)}) %collective-permute-start.10) | collective-permute-done | bytes 262176 | tf_op jit(solution)/shard_map/ppermute | solution.py:500
  40.5 0.8 %add_convert_fusion = bf16[64,2048]{1,0:T(8,128)(2,1)} fusion(f32[64,2048]{1,0:T(8,128)S(1)} %keep.1, bf16[64,2048]{1,0:T(8,128)(2,1)S(1)} %collective-permute-done.10), kind=kLoop, calls=%fused_computation | loop fusion | flops 393216 | bytes 1048576 | tf_op jit(solution)/shard_map/convert_element_type | solution.py:511
  (24 shorter events, 0.4 us)
Async XLA Ops:
  0.6 24.2 %copy-start.4 = (s32[16]{0:T(128)S(1)}, s32[16]{0:T(128)}, u32[]{:S(2)}) copy-start(s32[16]{0:T(128)} %block_ref.7) | copy-start | bytes 196
  0.6 24.2 %copy-start.6 = (s32[4]{0:T(128)S(1)}, s32[4]{0:T(128)}, u32[]{:S(2)}) copy-start(s32[4]{0:T(128)} %len_ref.3) | copy-start | bytes 52
  0.7 26.3 %copy-start.5 = (s32[64]{0:T(128)S(1)}, s32[64]{0:T(128)}, u32[]{:S(2)}) copy-start(s32[64]{0:T(128)} %slot_ref.3) | copy-start | bytes 772
  5.0 26.2 %copy-start = (bf16[512,2048]{1,0:T(8,128)(2,1)S(1)}, bf16[512,2048]{1,0:T(8,128)(2,1)}, u32[]{:S(2)}) copy-start(bf16[512,2048]{1,0:T(8,128)(2,1)} %wo_ref.3) | copy-start | bytes 6291460
  5.0 7.2 %collective-permute-start.3 = (bf16[128,512]{1,0:T(8,128)(2,1)}, bf16[128,512]{1,0:T(8,128)(2,1)S(1)}, u32[]{:S(2)}, u32[]{:S(2)}) collective-permute-start(bf16[128,512]{1,0:T(8,128)(2,1)} %get-tuple-element.38.kv_ref), channel_id=1, source_target_pairs={{0,8},{2,10},{4,12},{6,14},{8,0},{10,2},{12,4},{14,6},{16,24},{18,... | collective-permute-start | bytes 393224 | tf_op jit(solution)/shard_map/ppermute | solution.py:357
  8.1 8.7 %collective-permute-start.2 = (bf16[128,512]{1,0:T(8,128)(2,1)}, bf16[128,512]{1,0:T(8,128)(2,1)S(1)}, u32[]{:S(2)}, u32[]{:S(2)}) collective-permute-start(bf16[128,512]{1,0:T(8,128)(2,1)} %get-tuple-element.38.kv_ref), channel_id=1, source_target_pairs={{0,4},{2,6},{4,0},{6,2},{8,12},{10,14},{12,8},{14,10},{16,20},{18,... | collective-permute-start | bytes 393224 | tf_op jit(solution)/shard_map/ppermute | solution.py:357
  9.6 8.6 %collective-permute-start.1 = (bf16[128,512]{1,0:T(8,128)(2,1)}, bf16[128,512]{1,0:T(8,128)(2,1)S(1)}, u32[]{:S(2)}, u32[]{:S(2)}) collective-permute-start(bf16[128,512]{1,0:T(8,128)(2,1)} %get-tuple-element.38.kv_ref), channel_id=1, source_target_pairs={{0,16},{2,18},{4,20},{6,22},{8,24},{10,26},{12,28},{14,30},{16,0},... | collective-permute-start | bytes 393224 | tf_op jit(solution)/shard_map/ppermute | solution.py:357
  12.2 6.0 %collective-permute-start.4 = (bf16[128,512]{1,0:T(8,128)(2,1)S(1)}, bf16[128,512]{1,0:T(8,128)(2,1)S(1)}, u32[]{:S(2)}, u32[]{:S(2)}) collective-permute-start(bf16[128,512]{1,0:T(8,128)(2,1)S(1)} %collective-permute-done.3.refs_2_), channel_id=1, source_target_pairs={{0,4},{2,6},{4,0},{6,2},{8,12},{10,14},{12,8},{14,10},{16,20},{18,... | collective-permute-start | bytes 393224 | tf_op jit(solution)/shard_map/ppermute | solution.py:357
  14.9 0.9 %copy-start.2 = (bf16[128,512]{1,0:T(8,128)(2,1)S(1)}, bf16[128,512]{1,0:T(8,128)(2,1)}, u32[]{:S(2)}) copy-start(bf16[128,512]{1,0:T(8,128)(2,1)} %get-tuple-element.37.q_ref) | copy-start | bytes 393220
  15.8 0.9 %copy-start.3 = (bf16[128,512]{1,0:T(8,128)(2,1)S(1)}, bf16[128,512]{1,0:T(8,128)(2,1)}, u32[]{:S(2)}) copy-start(bf16[128,512]{1,0:T(8,128)(2,1)} %get-tuple-element.38.kv_ref) | copy-start | bytes 393220
  18.2 5.0 %collective-permute-start.6 = (bf16[128,512]{1,0:T(8,128)(2,1)S(1)}, bf16[128,512]{1,0:T(8,128)(2,1)S(1)}, u32[]{:S(2)}, u32[]{:S(2)}) collective-permute-start(bf16[128,512]{1,0:T(8,128)(2,1)S(1)} %collective-permute-done.1.refs_3_), channel_id=1, source_target_pairs={{0,8},{2,10},{4,12},{6,14},{8,0},{10,2},{12,4},{14,6},{16,24},{18,... | collective-permute-start | bytes 393224 | tf_op jit(solution)/shard_map/ppermute | solution.py:357
  18.5 6.4 %collective-permute-start = (bf16[128,512]{1,0:T(8,128)(2,1)S(1)}, bf16[128,512]{1,0:T(8,128)(2,1)S(1)}, u32[]{:S(2)}, u32[]{:S(2)}) collective-permute-start(bf16[128,512]{1,0:T(8,128)(2,1)S(1)} %copy-done.2), channel_id=1, source_target_pairs={{0,2},{2,0},{4,6},{6,4},{8,10},{10,8},{12,14},{14,12},{16,18},{18,... | collective-permute-start | bytes 393224 | tf_op jit(solution)/shard_map/ppermute | solution.py:357
  18.5 9.4 %collective-permute-start.7 = (bf16[128,512]{1,0:T(8,128)(2,1)S(1)}, bf16[128,512]{1,0:T(8,128)(2,1)S(1)}, u32[]{:S(2)}, u32[]{:S(2)}) collective-permute-start(bf16[128,512]{1,0:T(8,128)(2,1)S(1)} %collective-permute-done.1.refs_3_), channel_id=1, source_target_pairs={{0,4},{2,6},{4,0},{6,2},{8,12},{10,14},{12,8},{14,10},{16,20},{18,... | collective-permute-start | bytes 393224 | tf_op jit(solution)/shard_map/ppermute | solution.py:357
  23.2 5.0 %collective-permute-start.8 = (bf16[128,512]{1,0:T(8,128)(2,1)S(1)}, bf16[128,512]{1,0:T(8,128)(2,1)S(1)}, u32[]{:S(2)}, u32[]{:S(2)}) collective-permute-start(bf16[128,512]{1,0:T(8,128)(2,1)S(1)} %collective-permute-done.6.refs_0_), channel_id=1, source_target_pairs={{0,4},{2,6},{4,0},{6,2},{8,12},{10,14},{12,8},{14,10},{16,20},{18,... | collective-permute-start | bytes 393224 | tf_op jit(solution)/shard_map/ppermute | solution.py:357
  26.8 4.3 %collective-permute-start.5 = (bf16[128,640]{1,0:T(8,128)(2,1)S(1)}, bf16[128,640]{1,0:T(8,128)(2,1)S(1)}, u32[]{:S(2)}, u32[]{:S(2)}) collective-permute-start(bf16[128,640]{1,0:T(8,128)(2,1)S(1)} %get-tuple-element.56), channel_id=1, source_target_pairs={{0,2},{2,0},{4,6},{6,4},{8,10},{10,8},{12,14},{14,12},{16,18},{18,... | collective-permute-start | bytes 491528 | tf_op jit(solution)/shard_map/ppermute | solution.py:357
  29.6 1.5 %collective-permute-start.9 = (bf16[128,640]{1,0:T(8,128)(2,1)S(1)}, bf16[128,640]{1,0:T(8,128)(2,1)S(1)}, u32[]{:S(2)}, u32[]{:S(2)}) collective-permute-start(bf16[128,640]{1,0:T(8,128)(2,1)S(1)} %get-tuple-element.69), channel_id=1, source_target_pairs={{0,2},{2,0},{4,6},{6,4},{8,10},{10,8},{12,14},{14,12},{16,18},{18,... | collective-permute-start | bytes 491528 | tf_op jit(solution)/shard_map/ppermute | solution.py:357
  30.0 3.6 %copy-start.1 = (bf16[128,2048]{1,0:T(8,128)(2,1)S(1)}, bf16[128,2048]{1,0:T(8,128)(2,1)}, u32[]{:S(2)}) copy-start(bf16[128,2048]{1,0:T(8,128)(2,1)} %tok_ref.1) | copy-start | bytes 1572868
  30.8 3.5 %collective-permute-start.11 = (bf16[8,2,32,256]{3,2,1,0:T(8,128)(2,1)S(1)}, bf16[8,2,32,256]{3,2,1,0:T(8,128)(2,1)S(1)}, u32[]{:S(2)}, u32[]{:S(2)}) collective-permute-start(bf16[8,2,32,256]{3,2,1,0:T(8,128)(2,1)S(1)} %get-tuple-element.71), channel_id=1, source_target_pairs={{0,2},{2,0},{4,6},{6,4},{8,10},{10,8},{12,14},{14,12},{16,18},{18,... | collective-permute-start | bytes 786440 | tf_op jit(solution)/shard_map/ppermute | solution.py:357
  31.9 8.6 %collective-permute-start.10 = (bf16[64,2048]{1,0:T(8,128)(2,1)S(1)}, bf16[64,2048]{1,0:T(8,128)(2,1)S(1)}, u32[]{:S(2)}, u32[]{:S(2)}) collective-permute-start(bf16[64,2048]{1,0:T(8,128)(2,1)S(1)} %leave.1), channel_id=1, source_target_pairs={{0,1},{1,0},{2,3},{3,2},{4,5},{5,4},{6,7},{7,6},{8,9},{9,8},{10,11... | collective-permute-start | bytes 786440 | tf_op jit(solution)/shard_map/ppermute | solution.py:500

commit v9 on v8

--- a/solution.py
+++ b/solution.py
@@ -64,10 +64,8 @@
     return begin
 
 
-def positions(block_ref, shards, rows, dim, shape):
-    half = rows // 2
+def positions(blocks, half, dim, shape):
     index = lax.broadcasted_iota(jnp.int32, shape, dim)
-    blocks = [block for shard in shards for block in blocks_of(block_ref, shard)]
     offset = blocks[0] * half
     for i, block in enumerate(blocks[1:], 1):
         offset = jnp.where(index >= i * half, (block - i) * half, offset)
@@ -137,7 +135,7 @@
     rows = tok_ref.shape[0]
     for copy in small[:3]:
         copy.wait()
-    position = positions(block_ref, [lax.axis_index("seq")], rows, 0, (rows, HEAD))
+    position = positions(blocks_of(block_ref, lax.axis_index("seq")), rows // 2, 0, (rows, HEAD))
     angle = (position - prompt_begin(position, len_ref)).astype(f32) * freq_ref[...]
     cosine, sine = jnp.cos(angle), jnp.sin(angle)
     lane = lax.broadcasted_iota(jnp.int32, (rows, HEAD), 1)
@@ -159,20 +157,30 @@
         q_ref[:, cols] = rotate(product[:, cols], cosine, sine).astype(bf16)
 
 
-def attend_kernel(pieces, block_ref, len_ref, q_ref, far_ref, *refs):
+def attend_kernel(pieces, side, block_ref, len_ref, q_ref, far_ref, *refs):
     pieces, refs = with_refs(pieces, refs)
     shard = lax.axis_index("seq")
     rows, q_width = q_ref.shape
     key_width = pieces[0].arrays[0].shape[1] // 2
     kv_heads = key_width // HEAD
     group = q_width // key_width
-    both = 2 * rows
-    q_pos = positions(block_ref, [shard, shard ^ 1], rows, 0, (both, 1))
+    shards = [shard, shard ^ 1]
+    if side is None:
+        taken, span = rows, slice(None)
+        blocks = [block for s in shards for block in blocks_of(block_ref, s)]
+    else:
+        part = lax.axis_index("req")
+        part = 1 - part if side else part
+        taken = rows // 2
+        span = pl.ds(pl.multiple_of(part * taken, taken), taken)
+        blocks = [jnp.where(part == 0, *blocks_of(block_ref, s)) for s in shards]
+    both = 2 * taken
+    q_pos = positions(blocks, rows // 2, 0, (both, 1))
     q_begin = prompt_begin(q_pos, len_ref)
     queries = [
         jnp.concatenate(
             [
-                ref[:, h * HEAD : (h + 1) * HEAD]
+                ref[span, h * HEAD : (h + 1) * HEAD]
                 for h in range(g * group, (g + 1) * group)
                 for ref in (q_ref, far_ref)
             ],
@@ -181,9 +189,10 @@
         for g in range(kv_heads)
     ]
 
-    def absorb(state, blocks, shards):
+    def absorb(state, blocks, sources):
         width = rows * len(blocks)
-        key_pos = positions(block_ref, shards, rows, 1, (1, width))
+        held = [block for s in sources for block in blocks_of(block_ref, s)]
+        key_pos = positions(held, rows // 2, 1, (1, width))
         bias = jnp.where((key_pos >= q_begin) & (key_pos <= q_pos), 0.0, MASKED)
         bias = jnp.concatenate([bias] * group, 0)
         out = []
@@ -230,16 +239,16 @@
 
     mine_ref, stat_ref, packed_ref = refs
     heads = q_width // HEAD
-    lane = lax.broadcasted_iota(jnp.int32, (rows, HEAD), 1)
-    mine = jnp.zeros((rows, HEAD), f32)
-    theirs = jnp.zeros((rows, HEAD), f32)
+    lane = lax.broadcasted_iota(jnp.int32, (taken, HEAD), 1)
+    mine = jnp.zeros((taken, HEAD), f32)
+    theirs = jnp.zeros((taken, HEAD), f32)
     for g in range(kv_heads):
         top, total, acc = state[g]
         for j in range(group):
             h = g * group + j
             cols = slice(h * HEAD, (h + 1) * HEAD)
-            near = slice(j * both, j * both + rows)
-            far = slice(j * both + rows, (j + 1) * both)
+            near = slice(j * both, j * both + taken)
+            far = slice(j * both + taken, (j + 1) * both)
             mine_ref[:, cols] = acc[near]
             packed_ref[:, cols] = acc[far].astype(bf16)
             for value, at in ((top, h), (total, heads + h)):
@@ -262,18 +271,19 @@
 def joined_rows(partials, first, half):
     q_width = partials[0].shape[1]
     heads = q_width // HEAD
-    span = pl.ds(pl.multiple_of(first, half), half)
+    part = pl.ds(pl.multiple_of(first, half), half)
     held = []
     for mine_ref, stat_ref, packed_ref in zip(partials[::3], partials[1::3], partials[2::3]):
+        span = slice(None) if mine_ref.shape[0] == half else part
         parts = packed_ref[span, q_width:].astype(f32)
         stats = parts
         for t in (1, 2):
             stats = stats + pltpu.roll(parts, HEAD - 2 * heads * t, 1)
-        held += [(mine_ref, stat_ref[span, :]), (packed_ref, stats)]
-    top = functools.reduce(jnp.maximum, [stats for _, stats in held])
-    shares = [jnp.exp2(stats - top) for _, stats in held]
+        held += [(mine_ref, span, stat_ref[span, :]), (packed_ref, span, stats)]
+    top = functools.reduce(jnp.maximum, [stats for _, _, stats in held])
+    shares = [jnp.exp2(stats - top) for _, _, stats in held]
     total = sum(
-        share * pltpu.roll(stats, HEAD - heads, 1) for share, (_, stats) in zip(shares, held)
+        share * pltpu.roll(stats, HEAD - heads, 1) for share, (_, _, stats) in zip(shares, held)
     )
     shares = [share / total for share in shares]
     context = []
@@ -282,7 +292,7 @@
         context.append(
             sum(
                 ref[span, cols].astype(f32) * share[:, h : h + 1]
-                for (ref, _), share in zip(held, shares)
+                for (ref, span, _), share in zip(held, shares)
             ).astype(bf16)
         )
     return jnp.concatenate(context, 1)
@@ -302,6 +312,11 @@
     context = joined_rows(partials, first, half)
     residual = tok_ref[pl.ds(pl.multiple_of(first, half), half), :].astype(f32)
     out_ref[...] = jnp.dot(context, wo_ref[...], preferred_element_type=f32) + residual
+
+
+def finish_kernel(kept_ref, received_ref, mine_ref, other_ref, hidden_ref, cache_ref):
+    hidden_ref[...] = (kept_ref[...] + received_ref[...].astype(f32)).astype(bf16)
+    cache_ref[...] = mine_ref[...] + other_ref[...]
 
 
 def cache_kernel(pieces, held, block_ref, slot_ref, *refs):
@@ -418,20 +433,20 @@
     )
     far_queries = swap(queries, n, 1)
 
-    def attend(pieces):
-        keys = sum(piece.count for piece in pieces) * rows
+    def attend(pieces, side=None):
         arrays = operands(pieces)
+        taken = rows if side is None else half
         mine, stats, packed = pl.pallas_call(
-            functools.partial(attend_kernel, pieces),
+            functools.partial(attend_kernel, pieces, side),
             out_shape=(
-                struct((rows, q_width), f32),
-                struct((rows, HEAD), f32),
-                struct((rows, q_width + HEAD), bf16),
+                struct((taken, q_width), f32),
+                struct((taken, HEAD), f32),
+                struct((taken, q_width + HEAD), bf16),
             ),
             in_specs=in_smem(2) + in_vmem(2 + len(arrays)),
             out_specs=tuple(in_vmem(3)),
             compiler_params=kernel_params(32),
-            cost_estimate=cost(8 * rows * keys * q_width, 2 * keys * kv_width),
+            cost_estimate=cost(0, 0),
             name="attend",
         )(block_split, lengths, queries, far_queries, *arrays)
         return [mine, stats, swap(packed, n, 1)]
@@ -446,7 +461,7 @@
             out_specs=tuple(in_vmem(2)),
             input_output_aliases={2 + len(arrays) + i: i for i in range(len(held))},
             compiler_params=kernel_params(32),
-            cost_estimate=cost(0, 4 * rows * kv_width),
+            cost_estimate=cost(0, 0),
             name="cache",
         )(block_split, page_slot, *arrays, *held)
 
@@ -471,45 +486,52 @@
         (second, beside, first_across), kv = tied_all([second, beside, first_across], kv)
         own = own.moved([kv])
         third = swapped(second, 4)
-        early = [own, beside, first, second, first_across]
-        late = [third, swapped(second, 2), swapped(third, 2)]
+        early = [own, beside, first, second, first_across, third]
+        late = [swapped(second, 2), swapped(third, 2)]
         partials = attend(early)
         placed, partials[1] = tied_all(early, partials[1])
         held = place_pages(placed)
         queries, partials[1], held = lax.optimization_barrier((queries, partials[1], held))
-        partials += attend(late)
         remaining = late
     else:
         same = [list(range(c, n, 2)) for c in range(2)]
         gathered = lax.all_gather(kv, "seq", axis=0, tiled=True, axis_index_groups=same)
         remaining = [Piece([gathered], lambda shard, i: 2 * i + shard % 2, n // 2)]
-        partials, held = attend(remaining), ()
-    arrays, partials[-3] = lax.optimization_barrier((operands(remaining), partials[-3]))
-    remaining, _ = with_refs(remaining, arrays)
-    cache, other = place_pages(remaining, held)
-    partials[-3], cache, other = lax.optimization_barrier((partials[-3], cache, other))
+        partials, held = [], ()
+    leaving = attend(remaining, 1)
+    queries, leaving[1] = lax.optimization_barrier((queries, leaving[1]))
+    staying = attend(remaining, 0)
+    leaving[0], staying[1] = lax.optimization_barrier((leaving[0], staying[1]))
     sent = pl.pallas_call(
         leave_kernel,
         out_shape=struct((half, width), bf16),
-        in_specs=in_vmem(1 + len(partials)),
+        in_specs=in_vmem(4 + len(partials)),
         out_specs=in_vmem(1)[0],
         compiler_params=kernel_params(24),
-        cost_estimate=cost(rows * width * q_width, 2 * width * q_width),
+        cost_estimate=cost(0, 0),
         name="leave",
-    )(w_out, *partials)
+    )(w_out, *partials, *leaving)
     received = lax.ppermute(sent, "req", [(i, (i + 1) % parts) for i in range(parts)])
+    remaining, sent = tied_all(remaining, sent)
+    cache, other = place_pages(remaining, held)
     kept = pl.pallas_call(
         keep_kernel,
         out_shape=struct((half, width), f32),
-        in_specs=in_vmem(2 + len(partials)),
+        in_specs=in_vmem(5 + len(partials)),
         out_specs=in_vmem(1)[0],
         compiler_params=kernel_params(24),
-        cost_estimate=cost(rows * width * q_width, 2 * width * q_width),
+        cost_estimate=cost(0, 0),
         name="keep",
-    )(w_out, tokens, *partials)
-    cache = cache + swap(other, n, 1)
-    hidden = (kept + received.astype(f32)).astype(bf16)
-    return hidden, cache
+    )(w_out, tokens, *partials, *staying)
+    return pl.pallas_call(
+        finish_kernel,
+        out_shape=(struct((half, width), bf16), struct(cache.shape, bf16)),
+        in_specs=in_vmem(4),
+        out_specs=tuple(in_vmem(2)),
+        compiler_params=kernel_params(24),
+        cost_estimate=cost(0, 0),
+        name="finish",
+    )(kept, received, cache, swap(other, n, 1))
 
 
 def solution(mesh):

time: 41.4 us -> 41.9 us (1.012)
  Pallas kernels: 11.2 us -> 13.2 us
  other arithmetic: 1.54 us -> 0 us
    ppermute x11 -> x12, waiting for transfers between devices: 4.65 us -> 6.78 us  [swap(): return lax.ppermute(x, 'seq', [(i, i ^ bit) for i in range(n)])]
    pallas_call x2 -> x4, Pallas kernels: 3.46 us -> 5.46 us  [the longest x3 4.61 us: attend(): pl.pallas_call(functools.partial(attend_kernel, pieces, side), out_shape=...]
    ppermute x1, waiting for transfers between devices: 5.37 us -> 3.45 us  [on_device(): lax.ppermute(sent, 'req', [(i, (i + 1) % parts) for i in range(parts)])]
    add x1 -> x0, other arithmetic: 0.79 us -> none  [on_device(): cache = cache + swap(other, n, 1)]
    convert_element_type x1 -> x0, other arithmetic: 0.75 us -> none  [on_device(): hidden = (kept + received.astype(f32)).astype(bf16)]
    ppermute x11 -> x12, starting transfers between devices: 14.3 us -> 14.1 us  [swap(): return lax.ppermute(x, 'seq', [(i, i ^ bit) for i in range(n)])]
  transfers between devices with their start and end apart: 12 -> 13, of which waited for: 4 -> 5; matrix products, arithmetic and copies ran while one was open for 2% -> 0% of each run, Pallas kernels for 17% -> 17%
where the time goes in v9:
time: 41.9 us; the launch traced here: 41.7 us
  starting transfers between devices  15.7 us (37%)
  Pallas kernels  13.2 us (32%)
  waiting for transfers between devices  10.2 us (24%)
  local copies, waits for them, and re-layouts  1.83 us (4%)
  between operations  0.82 us (2%)
    ppermute x12, starting transfers between devices, swap(): return lax.ppermute(x, 'seq', [(i, i ^ bit) for i in range(n)])  14.1 us
    ppermute x12, waiting for transfers between devices, swap(): return lax.ppermute(x, 'seq', [(i, i ^ bit) for i in range(n)])  6.78 us
    pallas_call x3, Pallas kernels, attend(): pl.pallas_call(functools.partial(attend_kernel, pieces, side), out_shape=...  4.61 us
    pallas_call x1, Pallas kernels, on_device(): pl.pallas_call(project_kernel, out_shape=(struct((rows, kv_width), bf16),...  4.32 us
    ppermute x1, waiting for transfers between devices, on_device(): lax.ppermute(sent, 'req', [(i, (i + 1) % parts) for i in range(parts)])  3.45 us
    unnamed x14, local copies, waits for them, and re-layouts  1.83 us
    pallas_call x2, Pallas kernels, place_pages(): pl.pallas_call(functools.partial(cache_kernel, pieces, bool(held)), out_s...  1.81 us
    ppermute x1, starting transfers between devices, on_device(): lax.ppermute(sent, 'req', [(i, (i + 1) % parts) for i in range(parts)])  1.56 us
  transfers between devices with their start and end apart: 13, of which 5 were waited for; matrix products, arithmetic and copies ran while one was open for 0% of the time, Pallas kernels for 17%

profile of v9, /device:TPU:0, one launch (start us, length us, event | category | flops | bytes accessed | tf_op | source)
XLA Modules:
  0.0 41.7 jit_solution(1875959899093518484)
XLA Ops:
  0.7 4.3 %project.1 = (bf16[128,512]{1,0:T(8,128)(2,1)}, bf16[128,512]{1,0:T(8,128)(2,1)}) custom-call(s32[16]{0:T(128)} %block_ref.9, s32[4]{0:T(128)} %len_ref.5, f32[1,128]{1,0:T(1,128)} %constant.2.clone.freq_hbm, bf16[128,2048]{1,0:T(8,128)(2,1)} %tok_ref.1, f32[1,2048]{1,0:T(1,128)} %bitcast.1, bf16[2048,256]{1,0:T(8,128)(2,1)} %wk_hbm.1, ...), custom_call_target="tpu_custom_call" | custom-call | flops 536870912 | bytes 4194304 | tf_op jit(solution)/shard_map/project/pallas_call | solution.py:410
  5.0 3.1 %collective-permute-start.3 = (bf16[128,512]{1,0:T(8,128)(2,1)}, bf16[128,512]{1,0:T(8,128)(2,1)S(1)}, u32[]{:S(2)}, u32[]{:S(2)}) collective-permute-start(bf16[128,512]{1,0:T(8,128)(2,1)} %get-tuple-element.41.kv_ref), channel_id=1, source_target_pairs={{0,8},{2,10},{4,12},{6,14},{8,0},{10,2},{12,4},{14,6},{16,24},{18,... | collective-permute-start | bytes 393224 | tf_op jit(solution)/shard_map/ppermute | solution.py:372
  8.1 2.6 %collective-permute-start.1 = (bf16[128,512]{1,0:T(8,128)(2,1)}, bf16[128,512]{1,0:T(8,128)(2,1)S(1)}, u32[]{:S(2)}, u32[]{:S(2)}) collective-permute-start(bf16[128,512]{1,0:T(8,128)(2,1)} %get-tuple-element.41.kv_ref), channel_id=1, source_target_pairs={{0,16},{2,18},{4,20},{6,22},{8,24},{10,26},{12,28},{14,30},{16,0},... | collective-permute-start | bytes 393224 | tf_op jit(solution)/shard_map/ppermute | solution.py:372
  10.7 1.5 %collective-permute-start.2 = (bf16[128,512]{1,0:T(8,128)(2,1)}, bf16[128,512]{1,0:T(8,128)(2,1)S(1)}, u32[]{:S(2)}, u32[]{:S(2)}) collective-permute-start(bf16[128,512]{1,0:T(8,128)(2,1)} %get-tuple-element.41.kv_ref), channel_id=1, source_target_pairs={{0,4},{2,6},{4,0},{6,2},{8,12},{10,14},{12,8},{14,10},{16,20},{18,... | collective-permute-start | bytes 393224 | tf_op jit(solution)/shard_map/ppermute | solution.py:372
  12.2 1.4 %collective-permute-done.3.refs_2_ = bf16[128,512]{1,0:T(8,128)(2,1)S(1)} collective-permute-done((bf16[128,512]{1,0:T(8,128)(2,1)}, bf16[128,512]{1,0:T(8,128)(2,1)S(1)}, u32[]{:S(2)}, u32[]{:S(2)}) %collective-permute-start.3) | collective-permute-done | bytes 131104 | tf_op jit(solution)/shard_map/ppermute | solution.py:372
  13.6 1.8 %collective-permute-start.4 = (bf16[128,512]{1,0:T(8,128)(2,1)S(1)}, bf16[128,512]{1,0:T(8,128)(2,1)S(1)}, u32[]{:S(2)}, u32[]{:S(2)}) collective-permute-start(bf16[128,512]{1,0:T(8,128)(2,1)S(1)} %collective-permute-done.3.refs_2_), channel_id=1, source_target_pairs={{0,4},{2,6},{4,0},{6,2},{8,12},{10,14},{12,8},{14,10},{16,20},{18,... | collective-permute-start | bytes 393224 | tf_op jit(solution)/shard_map/ppermute | solution.py:372
  15.4 0.9 %copy-done.2 = bf16[128,512]{1,0:T(8,128)(2,1)S(1)} copy-done((bf16[128,512]{1,0:T(8,128)(2,1)S(1)}, bf16[128,512]{1,0:T(8,128)(2,1)}, u32[]{:S(2)}) %copy-start.2) | copy-done | bytes 131096
  16.3 0.9 %copy-done.3 = bf16[128,512]{1,0:T(8,128)(2,1)S(1)} copy-done((bf16[128,512]{1,0:T(8,128)(2,1)S(1)}, bf16[128,512]{1,0:T(8,128)(2,1)}, u32[]{:S(2)}) %copy-start.3) | copy-done | bytes 131096
  17.3 1.3 %collective-permute-done.4.refs_4_ = bf16[128,512]{1,0:T(8,128)(2,1)S(1)} collective-permute-done((bf16[128,512]{1,0:T(8,128)(2,1)S(1)}, bf16[128,512]{1,0:T(8,128)(2,1)S(1)}, u32[]{:S(2)}, u32[]{:S(2)}) %collective-permute-start.4) | collective-permute-done | bytes 131104 | tf_op jit(solution)/shard_map/ppermute | solution.py:372
  19.1 1.5 %collective-permute-start.7 = (bf16[128,512]{1,0:T(8,128)(2,1)S(1)}, bf16[128,512]{1,0:T(8,128)(2,1)S(1)}, u32[]{:S(2)}, u32[]{:S(2)}) collective-permute-start(bf16[128,512]{1,0:T(8,128)(2,1)S(1)} %collective-permute-done.1.refs_3_), channel_id=1, source_target_pairs={{0,4},{2,6},{4,0},{6,2},{8,12},{10,14},{12,8},{14,10},{16,20},{18,... | collective-permute-start | bytes 393224 | tf_op jit(solution)/shard_map/ppermute | solution.py:372
  20.6 2.9 %collective-permute-done.5.refs_5_ = bf16[128,512]{1,0:T(8,128)(2,1)S(1)} collective-permute-done((bf16[128,512]{1,0:T(8,128)(2,1)S(1)}, bf16[128,512]{1,0:T(8,128)(2,1)S(1)}, u32[]{:S(2)}, u32[]{:S(2)}) %collective-permute-start.5) | collective-permute-done | bytes 131104 | tf_op jit(solution)/shard_map/ppermute | solution.py:372
  23.5 1.8 %collective-permute-start.8 = (bf16[128,512]{1,0:T(8,128)(2,1)S(1)}, bf16[128,512]{1,0:T(8,128)(2,1)S(1)}, u32[]{:S(2)}, u32[]{:S(2)}) collective-permute-start(bf16[128,512]{1,0:T(8,128)(2,1)S(1)} %collective-permute-done.5.refs_5_), channel_id=1, source_target_pairs={{0,4},{2,6},{4,0},{6,2},{8,12},{10,14},{12,8},{14,10},{16,20},{18,... | collective-permute-start | bytes 393224 | tf_op jit(solution)/shard_map/ppermute | solution.py:372
  25.4 2.1 %attend.3 = (f32[128,512]{1,0:T(8,128)S(1)}, f32[128,128]{1,0:T(8,128)S(1)}, bf16[128,640]{1,0:T(8,128)(2,1)S(1)}) custom-call(s32[16]{0:T(128)S(1)} %copy-done.4, s32[4]{0:T(128)S(1)} %copy-done.5, bf16[128,512]{1,0:T(8,128)(2,1)S(1)} %get-tuple-element.63.q_ref, bf16[128,512]{1,0:T(8,128)(2,1)S(1)} %collective-permute-done.far_ref, ...), custom_call_target="tpu_custom_call" | custom-call | tf_op jit(solution)/shard_map/attend/pallas_call | solution.py:439
  27.6 1.1 %cache.2 = (bf16[8,2,32,256]{3,2,1,0:T(8,128)(2,1)S(1)}, bf16[8,2,32,256]{3,2,1,0:T(8,128)(2,1)S(1)}) custom-call(s32[16]{0:T(128)S(1)} %copy-done.4, s32[64]{0:T(128)S(1)} %copy-done.6, bf16[128,512]{1,0:T(8,128)(2,1)S(1)} %get-tuple-element.51.refs_0_, bf16[128,512]{1,0:T(8,128)(2,1)S(1)} %collective-permute-done.2.refs_1_, ...), custom_call_target="tpu_custom_call" | custom-call | tf_op jit(solution)/shard_map/cache/pallas_call | solution.py:457
  28.7 1.2 %attend.4 = (f32[64,512]{1,0:T(8,128)S(1)}, f32[64,128]{1,0:T(8,128)S(1)}, bf16[64,640]{1,0:T(8,128)(2,1)S(1)}) custom-call(s32[16]{0:T(128)S(1)} %copy-done.4, s32[4]{0:T(128)S(1)} %copy-done.5, bf16[128,512]{1,0:T(8,128)(2,1)S(1)} %get-tuple-element.63.q_ref, bf16[128,512]{1,0:T(8,128)(2,1)S(1)} %collective-permute-done.far_ref, ...), custom_call_target="tpu_custom_call" | custom-call | tf_op jit(solution)/shard_map/attend/pallas_call | solution.py:439
  29.9 0.6 %collective-permute-start.10 = (bf16[64,640]{1,0:T(8,128)(2,1)S(1)}, bf16[64,640]{1,0:T(8,128)(2,1)S(1)}, u32[]{:S(2)}, u32[]{:S(2)}) collective-permute-start(bf16[64,640]{1,0:T(8,128)(2,1)S(1)} %get-tuple-element.71), channel_id=1, source_target_pairs={{0,2},{2,0},{4,6},{6,4},{8,10},{10,8},{12,14},{14,12},{16,18},{18,... | collective-permute-start | bytes 245768 | tf_op jit(solution)/shard_map/ppermute | solution.py:372
  30.5 1.2 %attend.5 = (f32[64,512]{1,0:T(8,128)S(1)}, f32[64,128]{1,0:T(8,128)S(1)}, bf16[64,640]{1,0:T(8,128)(2,1)S(1)}) custom-call(s32[16]{0:T(128)S(1)} %copy-done.4, s32[4]{0:T(128)S(1)} %copy-done.5, bf16[128,512]{1,0:T(8,128)(2,1)S(1)} %get-tuple-element.63.q_ref, bf16[128,512]{1,0:T(8,128)(2,1)S(1)} %collective-permute-done.far_ref, ...), custom_call_target="tpu_custom_call" | custom-call | tf_op jit(solution)/shard_map/attend/pallas_call | solution.py:439
  31.8 0.8 %leave.1 = bf16[64,2048]{1,0:T(8,128)(2,1)S(1)} custom-call(bf16[512,2048]{1,0:T(8,128)(2,1)S(1)} %copy-done, f32[128,512]{1,0:T(8,128)S(1)} %get-tuple-element.48.refs_0_, f32[128,128]{1,0:T(8,128)S(1)} %get-tuple-element.59.refs_1_, bf16[128,640]{1,0:T(8,128)(2,1)S(1)} %collective-permute-done.6.refs_2_, f32[64,512]{1,0:T(8,128)S(1)} %get-tuple-element.69.refs_3_, ...), custom_call_target="tpu_custom_call" | custom-call | tf_op jit(solution)/shard_map/leave/pallas_call | solution.py:505
  32.6 1.6 %collective-permute-start.11 = (bf16[64,2048]{1,0:T(8,128)(2,1)S(1)}, bf16[64,2048]{1,0:T(8,128)(2,1)S(1)}, u32[]{:S(2)}, u32[]{:S(2)}) collective-permute-start(bf16[64,2048]{1,0:T(8,128)(2,1)S(1)} %leave.1), channel_id=1, source_target_pairs={{0,1},{1,0},{2,3},{3,2},{4,5},{5,4},{6,7},{7,6},{8,9},{9,8},{10,11... | collective-permute-start | bytes 786440 | tf_op jit(solution)/shard_map/ppermute | solution.py:514
  34.1 0.8 %cache.3 = (bf16[8,2,32,256]{3,2,1,0:T(8,128)(2,1)S(1)}, bf16[8,2,32,256]{3,2,1,0:T(8,128)(2,1)S(1)}) custom-call(s32[16]{0:T(128)S(1)} %copy-done.4, s32[64]{0:T(128)S(1)} %copy-done.6, bf16[128,512]{1,0:T(8,128)(2,1)S(1)} %collective-permute-done.7.refs_0_, ...), custom_call_target="tpu_custom_call", output_to_operand_aliasing={{0}: (4, {}), {1}: (5, {})} | custom-call | tf_op jit(solution)/shard_map/cache/pallas_call | solution.py:457
  35.5 1.1 %collective-permute-done.9.refs_5_ = bf16[64,640]{1,0:T(8,128)(2,1)S(1)} collective-permute-done((bf16[64,640]{1,0:T(8,128)(2,1)S(1)}, bf16[64,640]{1,0:T(8,128)(2,1)S(1)}, u32[]{:S(2)}, u32[]{:S(2)}) %collective-permute-start.9) | collective-permute-done | bytes 81952 | tf_op jit(solution)/shard_map/ppermute | solution.py:372
  36.6 0.8 %keep.1.kept_ref = f32[64,2048]{1,0:T(8,128)S(1)} custom-call(bf16[512,2048]{1,0:T(8,128)(2,1)S(1)} %copy-done, bf16[128,2048]{1,0:T(8,128)(2,1)S(1)} %copy-done.1, f32[128,512]{1,0:T(8,128)S(1)} %get-tuple-element.48.refs_0_, f32[128,128]{1,0:T(8,128)S(1)} %get-tuple-element.59.refs_1_, bf16[128,640]{1,0:T(8,128)(2,1)S(1)} %collective-permute-done.6.refs_2_, ...), custom_call_target="tpu_custom_call" | custom-call | tf_op jit(solution)/shard_map/keep/pallas_call | solution.py:517
  37.4 3.5 %collective-permute-done.11.received_ref = bf16[64,2048]{1,0:T(8,128)(2,1)S(1)} collective-permute-done((bf16[64,2048]{1,0:T(8,128)(2,1)S(1)}, bf16[64,2048]{1,0:T(8,128)(2,1)S(1)}, u32[]{:S(2)}, u32[]{:S(2)}) %collective-permute-start.11) | collective-permute-done | bytes 262176 | tf_op jit(solution)/shard_map/ppermute | solution.py:514
  40.9 0.9 %finish.1 = (bf16[64,2048]{1,0:T(8,128)(2,1)}, bf16[8,2,32,256]{3,2,1,0:T(8,128)(2,1)}) custom-call(f32[64,2048]{1,0:T(8,128)S(1)} %keep.1.kept_ref, bf16[64,2048]{1,0:T(8,128)(2,1)S(1)} %collective-permute-done.11.received_ref, bf16[8,2,32,256]{3,2,1,0:T(8,128)(2,1)S(1)} %get-tuple-element.76.mine_ref, ...), custom_call_target="tpu_custom_call" | custom-call | tf_op jit(solution)/shard_map/finish/pallas_call | solution.py:526
  (26 shorter events, 1.3 us)
Async XLA Ops:
  0.6 24.7 %copy-start.4 = (s32[16]{0:T(128)S(1)}, s32[16]{0:T(128)}, u32[]{:S(2)}) copy-start(s32[16]{0:T(128)} %block_ref.9) | copy-start | bytes 196
  0.6 24.7 %copy-start.5 = (s32[4]{0:T(128)S(1)}, s32[4]{0:T(128)}, u32[]{:S(2)}) copy-start(s32[4]{0:T(128)} %len_ref.5) | copy-start | bytes 52
  0.7 27.0 %copy-start.6 = (s32[64]{0:T(128)S(1)}, s32[64]{0:T(128)}, u32[]{:S(2)}) copy-start(s32[64]{0:T(128)} %slot_ref.3) | copy-start | bytes 772
  5.0 26.8 %copy-start = (bf16[512,2048]{1,0:T(8,128)(2,1)S(1)}, bf16[512,2048]{1,0:T(8,128)(2,1)}, u32[]{:S(2)}) copy-start(bf16[512,2048]{1,0:T(8,128)(2,1)} %wo_ref.3) | copy-start | bytes 6291460
  5.0 8.6 %collective-permute-start.3 = (bf16[128,512]{1,0:T(8,128)(2,1)}, bf16[128,512]{1,0:T(8,128)(2,1)S(1)}, u32[]{:S(2)}, u32[]{:S(2)}) collective-permute-start(bf16[128,512]{1,0:T(8,128)(2,1)} %get-tuple-element.41.kv_ref), channel_id=1, source_target_pairs={{0,8},{2,10},{4,12},{6,14},{8,0},{10,2},{12,4},{14,6},{16,24},{18,... | collective-permute-start | bytes 393224 | tf_op jit(solution)/shard_map/ppermute | solution.py:372
  8.1 9.2 %collective-permute-start.1 = (bf16[128,512]{1,0:T(8,128)(2,1)}, bf16[128,512]{1,0:T(8,128)(2,1)S(1)}, u32[]{:S(2)}, u32[]{:S(2)}) collective-permute-start(bf16[128,512]{1,0:T(8,128)(2,1)} %get-tuple-element.41.kv_ref), channel_id=1, source_target_pairs={{0,16},{2,18},{4,20},{6,22},{8,24},{10,26},{12,28},{14,30},{16,0},... | collective-permute-start | bytes 393224 | tf_op jit(solution)/shard_map/ppermute | solution.py:372
  10.7 6.6 %collective-permute-start.2 = (bf16[128,512]{1,0:T(8,128)(2,1)}, bf16[128,512]{1,0:T(8,128)(2,1)S(1)}, u32[]{:S(2)}, u32[]{:S(2)}) collective-permute-start(bf16[128,512]{1,0:T(8,128)(2,1)} %get-tuple-element.41.kv_ref), channel_id=1, source_target_pairs={{0,4},{2,6},{4,0},{6,2},{8,12},{10,14},{12,8},{14,10},{16,20},{18,... | collective-permute-start | bytes 393224 | tf_op jit(solution)/shard_map/ppermute | solution.py:372
  13.6 5.0 %collective-permute-start.4 = (bf16[128,512]{1,0:T(8,128)(2,1)S(1)}, bf16[128,512]{1,0:T(8,128)(2,1)S(1)}, u32[]{:S(2)}, u32[]{:S(2)}) collective-permute-start(bf16[128,512]{1,0:T(8,128)(2,1)S(1)} %collective-permute-done.3.refs_2_), channel_id=1, source_target_pairs={{0,4},{2,6},{4,0},{6,2},{8,12},{10,14},{12,8},{14,10},{16,20},{18,... | collective-permute-start | bytes 393224 | tf_op jit(solution)/shard_map/ppermute | solution.py:372
  15.4 0.9 %copy-start.2 = (bf16[128,512]{1,0:T(8,128)(2,1)S(1)}, bf16[128,512]{1,0:T(8,128)(2,1)}, u32[]{:S(2)}) copy-start(bf16[128,512]{1,0:T(8,128)(2,1)} %get-tuple-element.40.q_ref) | copy-start | bytes 393220
  16.3 0.9 %copy-start.3 = (bf16[128,512]{1,0:T(8,128)(2,1)S(1)}, bf16[128,512]{1,0:T(8,128)(2,1)}, u32[]{:S(2)}) copy-start(bf16[128,512]{1,0:T(8,128)(2,1)} %get-tuple-element.41.kv_ref) | copy-start | bytes 393220
  18.6 5.0 %collective-permute-start.5 = (bf16[128,512]{1,0:T(8,128)(2,1)S(1)}, bf16[128,512]{1,0:T(8,128)(2,1)S(1)}, u32[]{:S(2)}, u32[]{:S(2)}) collective-permute-start(bf16[128,512]{1,0:T(8,128)(2,1)S(1)} %collective-permute-done.1.refs_3_), channel_id=1, source_target_pairs={{0,8},{2,10},{4,12},{6,14},{8,0},{10,2},{12,4},{14,6},{16,24},{18,... | collective-permute-start | bytes 393224 | tf_op jit(solution)/shard_map/ppermute | solution.py:372
  19.1 6.3 %collective-permute-start = (bf16[128,512]{1,0:T(8,128)(2,1)}, bf16[128,512]{1,0:T(8,128)(2,1)S(1)}, u32[]{:S(2)}, u32[]{:S(2)}) collective-permute-start(bf16[128,512]{1,0:T(8,128)(2,1)} %get-tuple-element.40.q_ref), channel_id=1, source_target_pairs={{0,2},{2,0},{4,6},{6,4},{8,10},{10,8},{12,14},{14,12},{16,18},{18,... | collective-permute-start | bytes 393224 | tf_op jit(solution)/shard_map/ppermute | solution.py:372
  19.1 9.6 %collective-permute-start.7 = (bf16[128,512]{1,0:T(8,128)(2,1)S(1)}, bf16[128,512]{1,0:T(8,128)(2,1)S(1)}, u32[]{:S(2)}, u32[]{:S(2)}) collective-permute-start(bf16[128,512]{1,0:T(8,128)(2,1)S(1)} %collective-permute-done.1.refs_3_), channel_id=1, source_target_pairs={{0,4},{2,6},{4,0},{6,2},{8,12},{10,14},{12,8},{14,10},{16,20},{18,... | collective-permute-start | bytes 393224 | tf_op jit(solution)/shard_map/ppermute | solution.py:372
  23.5 5.2 %collective-permute-start.8 = (bf16[128,512]{1,0:T(8,128)(2,1)S(1)}, bf16[128,512]{1,0:T(8,128)(2,1)S(1)}, u32[]{:S(2)}, u32[]{:S(2)}) collective-permute-start(bf16[128,512]{1,0:T(8,128)(2,1)S(1)} %collective-permute-done.5.refs_5_), channel_id=1, source_target_pairs={{0,4},{2,6},{4,0},{6,2},{8,12},{10,14},{12,8},{14,10},{16,20},{18,... | collective-permute-start | bytes 393224 | tf_op jit(solution)/shard_map/ppermute | solution.py:372
  27.5 4.2 %collective-permute-start.6 = (bf16[128,640]{1,0:T(8,128)(2,1)S(1)}, bf16[128,640]{1,0:T(8,128)(2,1)S(1)}, u32[]{:S(2)}, u32[]{:S(2)}) collective-permute-start(bf16[128,640]{1,0:T(8,128)(2,1)S(1)} %get-tuple-element.60), channel_id=1, source_target_pairs={{0,2},{2,0},{4,6},{6,4},{8,10},{10,8},{12,14},{14,12},{16,18},{18,... | collective-permute-start | bytes 491528 | tf_op jit(solution)/shard_map/ppermute | solution.py:372
  29.9 1.8 %collective-permute-start.10 = (bf16[64,640]{1,0:T(8,128)(2,1)S(1)}, bf16[64,640]{1,0:T(8,128)(2,1)S(1)}, u32[]{:S(2)}, u32[]{:S(2)}) collective-permute-start(bf16[64,640]{1,0:T(8,128)(2,1)S(1)} %get-tuple-element.71), channel_id=1, source_target_pairs={{0,2},{2,0},{4,6},{6,4},{8,10},{10,8},{12,14},{14,12},{16,18},{18,... | collective-permute-start | bytes 245768 | tf_op jit(solution)/shard_map/ppermute | solution.py:372
  30.5 6.1 %copy-start.1 = (bf16[128,2048]{1,0:T(8,128)(2,1)S(1)}, bf16[128,2048]{1,0:T(8,128)(2,1)}, u32[]{:S(2)}) copy-start(bf16[128,2048]{1,0:T(8,128)(2,1)} %tok_ref.1) | copy-start | bytes 1572868
  32.6 8.3 %collective-permute-start.11 = (bf16[64,2048]{1,0:T(8,128)(2,1)S(1)}, bf16[64,2048]{1,0:T(8,128)(2,1)S(1)}, u32[]{:S(2)}, u32[]{:S(2)}) collective-permute-start(bf16[64,2048]{1,0:T(8,128)(2,1)S(1)} %leave.1), channel_id=1, source_target_pairs={{0,1},{1,0},{2,3},{3,2},{4,5},{5,4},{6,7},{7,6},{8,9},{9,8},{10,11... | collective-permute-start | bytes 786440 | tf_op jit(solution)/shard_map/ppermute | solution.py:514
  34.9 6.0 %collective-permute-start.12 = (bf16[8,2,32,256]{3,2,1,0:T(8,128)(2,1)S(1)}, bf16[8,2,32,256]{3,2,1,0:T(8,128)(2,1)S(1)}, u32[]{:S(2)}, u32[]{:S(2)}) collective-permute-start(bf16[8,2,32,256]{3,2,1,0:T(8,128)(2,1)S(1)} %get-tuple-element.77), channel_id=1, source_target_pairs={{0,2},{2,0},{4,6},{6,4},{8,10},{10,8},{12,14},{14,12},{16,18},{18,... | collective-permute-start | bytes 786440 | tf_op jit(solution)/shard_map/ppermute | solution.py:372
  35.0 1.6 %collective-permute-start.9 = (bf16[64,640]{1,0:T(8,128)(2,1)S(1)}, bf16[64,640]{1,0:T(8,128)(2,1)S(1)}, u32[]{:S(2)}, u32[]{:S(2)}) collective-permute-start(bf16[64,640]{1,0:T(8,128)(2,1)S(1)} %get-tuple-element.68), channel_id=1, source_target_pairs={{0,2},{2,0},{4,6},{6,4},{8,10},{10,8},{12,14},{14,12},{16,18},{18,... | collective-permute-start | bytes 245768 | tf_op jit(solution)/shard_map/ppermute | solution.py:372

commit v10 on v9

--- a/solution.py
+++ b/solution.py
@@ -111,7 +111,7 @@
 
 def project_kernel(
     block_hbm, len_hbm, freq_hbm, tok_hbm, gain_hbm, wk_hbm, wv_hbm, wq_hbm,
-    kv_ref, q_ref,
+    kv_ref, both_ref,
     block_ref, len_ref, freq_ref, tok_ref, gain_ref, kv_weights, q_weights, small_sems, kv_sems, q_sems,
 ):
     small = [
@@ -151,10 +151,12 @@
         cols = slice(h * HEAD, (h + 1) * HEAD)
         kv_ref[:, cols] = rotate(product[:, cols], cosine, sine).astype(bf16)
     kv_ref[:, key_width:] = product[:, key_width:].astype(bf16)
+    both_ref[:, : kv_ref.shape[1]] = kv_ref[...]
     product = stepped_dot(normed, q_copies, q_weights)
     for h in range(wq_hbm.shape[1] // HEAD):
         cols = slice(h * HEAD, (h + 1) * HEAD)
-        q_ref[:, cols] = rotate(product[:, cols], cosine, sine).astype(bf16)
+        turned = rotate(product[:, cols], cosine, sine).astype(bf16)
+        both_ref[:, pl.ds(kv_ref.shape[1] + h * HEAD, HEAD)] = turned
 
 
 def attend_kernel(pieces, side, block_ref, len_ref, q_ref, far_ref, *refs):
@@ -263,9 +265,9 @@
     packed_ref[:, q_width:] = parts.astype(bf16)
 
 
-def stage_kernel(q_ref, kv_ref, q_out, kv_out):
-    q_out[...] = q_ref[...]
-    kv_out[...] = kv_ref[...]
+def stage_kernel(both_ref, kv_out, q_out):
+    kv_out[...] = both_ref[:, : kv_out.shape[1]]
+    q_out[...] = both_ref[:, kv_out.shape[1] :]
 
 
 def joined_rows(partials, first, half):
@@ -319,16 +321,15 @@
     cache_ref[...] = mine_ref[...] + other_ref[...]
 
 
-def cache_kernel(pieces, held, block_ref, slot_ref, *refs):
-    pieces, refs = with_refs(pieces, refs)
-    mine_ref, other_ref = refs[-2:]
+def cache_kernel(pieces, block_ref, slot_ref, *refs):
+    pieces, (mine_ref, other_ref) = with_refs(pieces, refs)
     shard = lax.axis_index("seq")
     slots = mine_ref.shape[0]
     key_width = mine_ref.shape[3]
     rows = slots * PAGE // 2
     pages = rows // 2 // PAGE
-    for i, target in enumerate((mine_ref, other_ref)):
-        target[...] = refs[i][...] if held else jnp.zeros_like(target)
+    for target in (mine_ref, other_ref):
+        target[...] = jnp.zeros_like(target)
 
     def place(ref, at, source):
         for k, block in enumerate(blocks_of(block_ref, source)):
@@ -407,9 +408,9 @@
     half = rows // 2
     q_width = w_query.shape[1]
     kv_width = key_projection.shape[1] + value_projection.shape[1]
-    kv, queries = pl.pallas_call(
+    kv, both = pl.pallas_call(
         project_kernel,
-        out_shape=(struct((rows, kv_width), bf16), struct((rows, q_width), bf16)),
+        out_shape=(struct((rows, kv_width), bf16), struct((rows, kv_width + q_width), bf16)),
         in_specs=in_hbm(8),
         out_specs=tuple(in_vmem(2)),
         scratch_shapes=[
@@ -431,6 +432,15 @@
         block_split, lengths, inverse_frequencies(), tokens, norm_gain.reshape(1, width),
         key_projection, value_projection, w_query,
     )
+    staged, queries = pl.pallas_call(
+        stage_kernel,
+        out_shape=(struct((rows, kv_width), bf16), struct((rows, q_width), bf16)),
+        in_specs=in_vmem(1),
+        out_specs=tuple(in_vmem(2)),
+        compiler_params=kernel_params(24),
+        cost_estimate=cost(0, 0),
+        name="stage",
+    )(both)
     far_queries = swap(queries, n, 1)
 
     def attend(pieces, side=None):
@@ -451,19 +461,18 @@
         )(block_split, lengths, queries, far_queries, *arrays)
         return [mine, stats, swap(packed, n, 1)]
 
-    def place_pages(pieces, held=()):
+    def place_pages(pieces):
         arrays = operands(pieces)
         shape = (2 * rows // PAGE, 2, PAGE, kv_width // 2)
         return pl.pallas_call(
-            functools.partial(cache_kernel, pieces, bool(held)),
+            functools.partial(cache_kernel, pieces),
             out_shape=(struct(shape, bf16),) * 2,
-            in_specs=in_smem(2) + in_vmem(len(arrays) + len(held)),
+            in_specs=in_smem(2) + in_vmem(len(arrays)),
             out_specs=tuple(in_vmem(2)),
-            input_output_aliases={2 + len(arrays) + i: i for i in range(len(held))},
             compiler_params=kernel_params(32),
             cost_estimate=cost(0, 0),
             name="cache",
-        )(block_split, page_slot, *arrays, *held)
+        )(block_split, page_slot, *arrays)
 
     if n == 16:
 
@@ -473,31 +482,20 @@
 
         own = Piece([kv], at_distance(0))
         second, first, beside = swapped(own, 8), swapped(own, 4), swapped(own, 2)
-        queries, kv = pl.pallas_call(
-            stage_kernel,
-            out_shape=(struct(queries.shape, bf16), struct(kv.shape, bf16)),
-            in_specs=in_vmem(2),
-            out_specs=tuple(in_vmem(2)),
-            compiler_params=kernel_params(24),
-            cost_estimate=cost(0, 8 * rows * kv_width),
-            name="stage",
-        )(queries, kv)
         first_across = swapped(first, 2)
-        (second, beside, first_across), kv = tied_all([second, beside, first_across], kv)
-        own = own.moved([kv])
+        second, staged = tied(second, staged)
+        own = own.moved([staged])
         third = swapped(second, 4)
-        early = [own, beside, first, second, first_across, third]
-        late = [swapped(second, 2), swapped(third, 2)]
-        partials = attend(early)
-        placed, partials[1] = tied_all(early, partials[1])
-        held = place_pages(placed)
-        queries, partials[1], held = lax.optimization_barrier((queries, partials[1], held))
-        remaining = late
+        (second, first_across, beside), _ = tied_all([second, first_across, beside], ())
+        partials = attend([own, beside, first, second, first_across, third])
+        queries, partials[1] = lax.optimization_barrier((queries, partials[1]))
+        remaining = [swapped(second, 2), swapped(third, 2)]
+        placed = [own, beside, first, second, first_across, third] + remaining
     else:
         same = [list(range(c, n, 2)) for c in range(2)]
         gathered = lax.all_gather(kv, "seq", axis=0, tiled=True, axis_index_groups=same)
         remaining = [Piece([gathered], lambda shard, i: 2 * i + shard % 2, n // 2)]
-        partials, held = [], ()
+        partials, placed = [], remaining
     leaving = attend(remaining, 1)
     queries, leaving[1] = lax.optimization_barrier((queries, leaving[1]))
     staying = attend(remaining, 0)
@@ -512,8 +510,9 @@
         name="leave",
     )(w_out, *partials, *leaving)
     received = lax.ppermute(sent, "req", [(i, (i + 1) % parts) for i in range(parts)])
-    remaining, sent = tied_all(remaining, sent)
-    cache, other = place_pages(remaining, held)
+    placed, (staging, sent) = tied_all(placed, (staying[2], sent))
+    staying[2] = staging
+    cache, other = place_pages(placed)
     kept = pl.pallas_call(
         keep_kernel,
         out_shape=struct((half, width), f32),

time: 41.9 us -> 40.3 us (0.962)
  local copies, waits for them, and re-layouts: 1.83 us -> 0.98 us
  starting transfers between devices: 15.7 us -> 15 us
  Pallas kernels: 13.2 us -> 12.7 us
  waiting for transfers between devices: 10.2 us -> 10.7 us
    ppermute x1, waiting for transfers between devices: 3.45 us -> 4.6 us  [on_device(): lax.ppermute(sent, 'req', [(i, (i + 1) % parts) for i in range(parts)])]
    unnamed x14 -> x12, local copies, waits for them, and re-layouts: 1.83 us -> 0.98 us
    ppermute x12, waiting for transfers between devices: 6.78 us -> 6.06 us  [swap(): return lax.ppermute(x, 'seq', [(i, i ^ bit) for i in range(n)])]
    ppermute x12, starting transfers between devices: 14.1 us -> 13.4 us  [swap(): return lax.ppermute(x, 'seq', [(i, i ^ bit) for i in range(n)])]
    pallas_call x3 -> x2, Pallas kernels: 1.83 us -> 1.23 us  [the longest x1 1.21 us: place_pages(): pl.pallas_call(functools.partial(cache_kernel, pieces), out_shape=(struct...]
  transfers between devices with their start and end apart: 13 -> 13, of which waited for: 5 -> 6; matrix products, arithmetic and copies ran while one was open for 0% -> 0% of each run, Pallas kernels for 17% -> 19%
where the time goes in v10:
time: 40.3 us; the launch traced here: 40.2 us
  starting transfers between devices  15 us (37%)
  Pallas kernels  12.7 us (32%)
  waiting for transfers between devices  10.7 us (27%)
  local copies, waits for them, and re-layouts  0.98 us (2%)
  between operations  0.78 us (2%)
    ppermute x12, starting transfers between devices, swap(): return lax.ppermute(x, 'seq', [(i, i ^ bit) for i in range(n)])  13.4 us
    ppermute x12, waiting for transfers between devices, swap(): return lax.ppermute(x, 'seq', [(i, i ^ bit) for i in range(n)])  6.06 us
    pallas_call x3, Pallas kernels, attend(): pl.pallas_call(functools.partial(attend_kernel, pieces, side), out_shape=...  4.63 us
    ppermute x1, waiting for transfers between devices, on_device(): lax.ppermute(sent, 'req', [(i, (i + 1) % parts) for i in range(parts)])  4.6 us
    pallas_call x1, Pallas kernels, on_device(): pl.pallas_call(project_kernel, out_shape=(struct((rows, kv_width), bf16),...  4.38 us
    ppermute x1, starting transfers between devices, on_device(): lax.ppermute(sent, 'req', [(i, (i + 1) % parts) for i in range(parts)])  1.58 us
    pallas_call x1, Pallas kernels, place_pages(): pl.pallas_call(functools.partial(cache_kernel, pieces), out_shape=(struct...  1.21 us
    unnamed x12, local copies, waits for them, and re-layouts  0.98 us
  transfers between devices with their start and end apart: 13, of which 6 were waited for; matrix products, arithmetic and copies ran while one was open for 0% of the time, Pallas kernels for 19%

profile of v10, /device:TPU:0, one launch (start us, length us, event | category | flops | bytes accessed | tf_op | source)
XLA Modules:
  0.0 40.2 jit_solution(16253766233952954852)
XLA Ops:
  0.7 4.4 %project.1 = (bf16[128,512]{1,0:T(8,128)(2,1)}, bf16[128,1024]{1,0:T(8,128)(2,1)}) custom-call(s32[16]{0:T(128)} %block_ref.7, s32[4]{0:T(128)} %len_ref.5, f32[1,128]{1,0:T(1,128)} %constant.2.clone.freq_hbm, bf16[128,2048]{1,0:T(8,128)(2,1)} %tok_ref.1, f32[1,2048]{1,0:T(1,128)} %bitcast.1, bf16[2048,256]{1,0:T(8,128)(2,1)} %wk_hbm.1, ...), custom_call_target="tpu_custom_call" | custom-call | flops 536870912 | bytes 4194304 | tf_op jit(solution)/shard_map/project/pallas_call | solution.py:411
  5.1 3.1 %collective-permute-start.2 = (bf16[128,512]{1,0:T(8,128)(2,1)}, bf16[128,512]{1,0:T(8,128)(2,1)S(1)}, u32[]{:S(2)}, u32[]{:S(2)}) collective-permute-start(bf16[128,512]{1,0:T(8,128)(2,1)} %get-tuple-element.39), channel_id=1, source_target_pairs={{0,8},{2,10},{4,12},{6,14},{8,0},{10,2},{12,4},{14,6},{16,24},{18,... | collective-permute-start | bytes 393224 | tf_op jit(solution)/shard_map/ppermute | solution.py:373
  8.1 2.6 %collective-permute-start.1 = (bf16[128,512]{1,0:T(8,128)(2,1)}, bf16[128,512]{1,0:T(8,128)(2,1)S(1)}, u32[]{:S(2)}, u32[]{:S(2)}) collective-permute-start(bf16[128,512]{1,0:T(8,128)(2,1)} %get-tuple-element.39), channel_id=1, source_target_pairs={{0,16},{2,18},{4,20},{6,22},{8,24},{10,26},{12,28},{14,30},{16,0},... | collective-permute-start | bytes 393224 | tf_op jit(solution)/shard_map/ppermute | solution.py:373
  10.7 1.5 %collective-permute-start.4 = (bf16[128,512]{1,0:T(8,128)(2,1)}, bf16[128,512]{1,0:T(8,128)(2,1)S(1)}, u32[]{:S(2)}, u32[]{:S(2)}) collective-permute-start(bf16[128,512]{1,0:T(8,128)(2,1)} %get-tuple-element.39), channel_id=1, source_target_pairs={{0,4},{2,6},{4,0},{6,2},{8,12},{10,14},{12,8},{14,10},{16,20},{18,... | collective-permute-start | bytes 393224 | tf_op jit(solution)/shard_map/ppermute | solution.py:373
  12.2 0.9 %copy-done.2 = bf16[128,1024]{1,0:T(8,128)(2,1)S(1)} copy-done((bf16[128,1024]{1,0:T(8,128)(2,1)S(1)}, bf16[128,1024]{1,0:T(8,128)(2,1)}, u32[]{:S(2)}) %copy-start.2) | copy-done | bytes 262168
  13.2 0.5 %collective-permute-done.2.refs_2_ = bf16[128,512]{1,0:T(8,128)(2,1)S(1)} collective-permute-done((bf16[128,512]{1,0:T(8,128)(2,1)}, bf16[128,512]{1,0:T(8,128)(2,1)S(1)}, u32[]{:S(2)}, u32[]{:S(2)}) %collective-permute-start.2) | collective-permute-done | bytes 131104 | tf_op jit(solution)/shard_map/ppermute | solution.py:373
  13.7 1.8 %collective-permute-start.3 = (bf16[128,512]{1,0:T(8,128)(2,1)S(1)}, bf16[128,512]{1,0:T(8,128)(2,1)S(1)}, u32[]{:S(2)}, u32[]{:S(2)}) collective-permute-start(bf16[128,512]{1,0:T(8,128)(2,1)S(1)} %collective-permute-done.2.refs_2_), channel_id=1, source_target_pairs={{0,4},{2,6},{4,0},{6,2},{8,12},{10,14},{12,8},{14,10},{16,20},{18,... | collective-permute-start | bytes 393224 | tf_op jit(solution)/shard_map/ppermute | solution.py:373
  15.5 1.6 %collective-permute-done.1.refs_3_ = bf16[128,512]{1,0:T(8,128)(2,1)S(1)} collective-permute-done((bf16[128,512]{1,0:T(8,128)(2,1)}, bf16[128,512]{1,0:T(8,128)(2,1)S(1)}, u32[]{:S(2)}, u32[]{:S(2)}) %collective-permute-start.1) | collective-permute-done | bytes 131104 | tf_op jit(solution)/shard_map/ppermute | solution.py:373
  17.1 0.4 %collective-permute-start.5 = (bf16[128,512]{1,0:T(8,128)(2,1)S(1)}, bf16[128,512]{1,0:T(8,128)(2,1)S(1)}, u32[]{:S(2)}, u32[]{:S(2)}) collective-permute-start(bf16[128,512]{1,0:T(8,128)(2,1)S(1)} %collective-permute-done.1.refs_3_), channel_id=1, source_target_pairs={{0,8},{2,10},{4,12},{6,14},{8,0},{10,2},{12,4},{14,6},{16,24},{18,... | collective-permute-start | bytes 393224 | tf_op jit(solution)/shard_map/ppermute | solution.py:373
  17.5 1.2 %collective-permute-done.3.refs_4_ = bf16[128,512]{1,0:T(8,128)(2,1)S(1)} collective-permute-done((bf16[128,512]{1,0:T(8,128)(2,1)S(1)}, bf16[128,512]{1,0:T(8,128)(2,1)S(1)}, u32[]{:S(2)}, u32[]{:S(2)}) %collective-permute-start.3) | collective-permute-done | bytes 131104 | tf_op jit(solution)/shard_map/ppermute | solution.py:373
  18.7 1.7 %collective-permute-start.7 = (bf16[128,512]{1,0:T(8,128)(2,1)S(1)}, bf16[128,512]{1,0:T(8,128)(2,1)S(1)}, u32[]{:S(2)}, u32[]{:S(2)}) collective-permute-start(bf16[128,512]{1,0:T(8,128)(2,1)S(1)} %collective-permute-done.1.refs_3_), channel_id=1, source_target_pairs={{0,4},{2,6},{4,0},{6,2},{8,12},{10,14},{12,8},{14,10},{16,20},{18,... | collective-permute-start | bytes 393224 | tf_op jit(solution)/shard_map/ppermute | solution.py:373
  20.5 1.6 %collective-permute-done.5.refs_5_ = bf16[128,512]{1,0:T(8,128)(2,1)S(1)} collective-permute-done((bf16[128,512]{1,0:T(8,128)(2,1)S(1)}, bf16[128,512]{1,0:T(8,128)(2,1)S(1)}, u32[]{:S(2)}, u32[]{:S(2)}) %collective-permute-start.5) | collective-permute-done | bytes 131104 | tf_op jit(solution)/shard_map/ppermute | solution.py:373
  22.0 1.5 %collective-permute-start.8 = (bf16[128,512]{1,0:T(8,128)(2,1)S(1)}, bf16[128,512]{1,0:T(8,128)(2,1)S(1)}, u32[]{:S(2)}, u32[]{:S(2)}) collective-permute-start(bf16[128,512]{1,0:T(8,128)(2,1)S(1)} %collective-permute-done.5.refs_5_), channel_id=1, source_target_pairs={{0,4},{2,6},{4,0},{6,2},{8,12},{10,14},{12,8},{14,10},{16,20},{18,... | collective-permute-start | bytes 393224 | tf_op jit(solution)/shard_map/ppermute | solution.py:373
  23.5 2.2 %attend.3 = (f32[128,512]{1,0:T(8,128)S(1)}, f32[128,128]{1,0:T(8,128)S(1)}, bf16[128,640]{1,0:T(8,128)(2,1)S(1)}) custom-call(s32[16]{0:T(128)S(1)} %copy-done.3, s32[4]{0:T(128)S(1)} %copy-done.4, bf16[128,512]{1,0:T(8,128)(2,1)S(1)} %get-tuple-element.52.q_ref, bf16[128,512]{1,0:T(8,128)(2,1)S(1)} %collective-permute-done.far_ref, ...), custom_call_target="tpu_custom_call" | custom-call | tf_op jit(solution)/shard_map/attend/pallas_call | solution.py:449
  25.8 1.2 %collective-permute-done.8.refs_1_.refs_7_ = bf16[128,512]{1,0:T(8,128)(2,1)S(1)} collective-permute-done((bf16[128,512]{1,0:T(8,128)(2,1)S(1)}, bf16[128,512]{1,0:T(8,128)(2,1)S(1)}, u32[]{:S(2)}, u32[]{:S(2)}) %collective-permute-start.8) | collective-permute-done | bytes 131104 | tf_op jit(solution)/shard_map/ppermute | solution.py:373
  27.0 1.2 %attend.4 = (f32[64,512]{1,0:T(8,128)S(1)}, f32[64,128]{1,0:T(8,128)S(1)}, bf16[64,640]{1,0:T(8,128)(2,1)S(1)}) custom-call(s32[16]{0:T(128)S(1)} %copy-done.3, s32[4]{0:T(128)S(1)} %copy-done.4, bf16[128,512]{1,0:T(8,128)(2,1)S(1)} %get-tuple-element.52.q_ref, bf16[128,512]{1,0:T(8,128)(2,1)S(1)} %collective-permute-done.far_ref, ...), custom_call_target="tpu_custom_call" | custom-call | tf_op jit(solution)/shard_map/attend/pallas_call | solution.py:449
  28.3 1.2 %attend.5 = (f32[64,512]{1,0:T(8,128)S(1)}, f32[64,128]{1,0:T(8,128)S(1)}, bf16[64,640]{1,0:T(8,128)(2,1)S(1)}) custom-call(s32[16]{0:T(128)S(1)} %copy-done.3, s32[4]{0:T(128)S(1)} %copy-done.4, bf16[128,512]{1,0:T(8,128)(2,1)S(1)} %get-tuple-element.52.q_ref, bf16[128,512]{1,0:T(8,128)(2,1)S(1)} %collective-permute-done.far_ref, ...), custom_call_target="tpu_custom_call" | custom-call | tf_op jit(solution)/shard_map/attend/pallas_call | solution.py:449
  29.6 0.6 %collective-permute-start.9 = (bf16[64,640]{1,0:T(8,128)(2,1)S(1)}, bf16[64,640]{1,0:T(8,128)(2,1)S(1)}, u32[]{:S(2)}, u32[]{:S(2)}) collective-permute-start(bf16[64,640]{1,0:T(8,128)(2,1)S(1)} %get-tuple-element.57), channel_id=1, source_target_pairs={{0,2},{2,0},{4,6},{6,4},{8,10},{10,8},{12,14},{14,12},{16,18},{18,... | collective-permute-start | bytes 245768 | tf_op jit(solution)/shard_map/ppermute | solution.py:373
  30.2 0.8 %leave.1 = bf16[64,2048]{1,0:T(8,128)(2,1)S(1)} custom-call(bf16[512,2048]{1,0:T(8,128)(2,1)S(1)} %copy-done, f32[128,512]{1,0:T(8,128)S(1)} %get-tuple-element.46.refs_0_, f32[128,128]{1,0:T(8,128)S(1)} %get-tuple-element.48.refs_1_, bf16[128,640]{1,0:T(8,128)(2,1)S(1)} %collective-permute-done.6.refs_2_, f32[64,512]{1,0:T(8,128)S(1)} %get-tuple-element.58.refs_3_, ...), custom_call_target="tpu_custom_call" | custom-call | tf_op jit(solution)/shard_map/leave/pallas_call | solution.py:503
  31.0 1.6 %collective-permute-start.11 = (bf16[64,2048]{1,0:T(8,128)(2,1)S(1)}, bf16[64,2048]{1,0:T(8,128)(2,1)S(1)}, u32[]{:S(2)}, u32[]{:S(2)}) collective-permute-start(bf16[64,2048]{1,0:T(8,128)(2,1)S(1)} %leave.1), channel_id=1, source_target_pairs={{0,1},{1,0},{2,3},{3,2},{4,5},{5,4},{6,7},{7,6},{8,9},{9,8},{10,11... | collective-permute-start | bytes 786440 | tf_op jit(solution)/shard_map/ppermute | solution.py:512
  32.6 1.2 %cache.1 = (bf16[8,2,32,256]{3,2,1,0:T(8,128)(2,1)S(1)}, bf16[8,2,32,256]{3,2,1,0:T(8,128)(2,1)S(1)}) custom-call(s32[16]{0:T(128)S(1)} %copy-done.3, s32[64]{0:T(128)S(1)} %copy-done.5, bf16[128,512]{1,0:T(8,128)(2,1)S(1)} %get-tuple-element.62.refs_0_, bf16[128,512]{1,0:T(8,128)(2,1)S(1)} %collective-permute-done.4.refs_1_, ...), custom_call_target="tpu_custom_call" | custom-call | tf_op jit(solution)/shard_map/cache/pallas_call | solution.py:467
  33.9 0.8 %keep.1.kept_ref = f32[64,2048]{1,0:T(8,128)S(1)} custom-call(bf16[512,2048]{1,0:T(8,128)(2,1)S(1)} %copy-done, bf16[128,2048]{1,0:T(8,128)(2,1)S(1)} %copy-done.1, f32[128,512]{1,0:T(8,128)S(1)} %get-tuple-element.46.refs_0_, f32[128,128]{1,0:T(8,128)S(1)} %get-tuple-element.48.refs_1_, bf16[128,640]{1,0:T(8,128)(2,1)S(1)} %collective-permute-done.6.refs_2_, ...), custom_call_target="tpu_custom_call" | custom-call | tf_op jit(solution)/shard_map/keep/pallas_call | solution.py:516
  34.7 4.6 %collective-permute-done.11.received_ref = bf16[64,2048]{1,0:T(8,128)(2,1)S(1)} collective-permute-done((bf16[64,2048]{1,0:T(8,128)(2,1)S(1)}, bf16[64,2048]{1,0:T(8,128)(2,1)S(1)}, u32[]{:S(2)}, u32[]{:S(2)}) %collective-permute-start.11) | collective-permute-done | bytes 262176 | tf_op jit(solution)/shard_map/ppermute | solution.py:512
  39.3 0.9 %finish.1 = (bf16[64,2048]{1,0:T(8,128)(2,1)}, bf16[8,2,32,256]{3,2,1,0:T(8,128)(2,1)}) custom-call(f32[64,2048]{1,0:T(8,128)S(1)} %keep.1.kept_ref, bf16[64,2048]{1,0:T(8,128)(2,1)S(1)} %collective-permute-done.11.received_ref, bf16[8,2,32,256]{3,2,1,0:T(8,128)(2,1)S(1)} %get-tuple-element.70.mine_ref, ...), custom_call_target="tpu_custom_call" | custom-call | tf_op jit(solution)/shard_map/finish/pallas_call | solution.py:525
  (23 shorter events, 0.3 us)
Async XLA Ops:
  0.6 22.9 %copy-start.3 = (s32[16]{0:T(128)S(1)}, s32[16]{0:T(128)}, u32[]{:S(2)}) copy-start(s32[16]{0:T(128)} %block_ref.7) | copy-start | bytes 196
  0.6 22.9 %copy-start.4 = (s32[4]{0:T(128)S(1)}, s32[4]{0:T(128)}, u32[]{:S(2)}) copy-start(s32[4]{0:T(128)} %len_ref.5) | copy-start | bytes 52
  5.0 25.1 %copy-start = (bf16[512,2048]{1,0:T(8,128)(2,1)S(1)}, bf16[512,2048]{1,0:T(8,128)(2,1)}, u32[]{:S(2)}) copy-start(bf16[512,2048]{1,0:T(8,128)(2,1)} %wo_ref.3) | copy-start | bytes 6291460
  5.1 8.6 %collective-permute-start.2 = (bf16[128,512]{1,0:T(8,128)(2,1)}, bf16[128,512]{1,0:T(8,128)(2,1)S(1)}, u32[]{:S(2)}, u32[]{:S(2)}) collective-permute-start(bf16[128,512]{1,0:T(8,128)(2,1)} %get-tuple-element.39), channel_id=1, source_target_pairs={{0,8},{2,10},{4,12},{6,14},{8,0},{10,2},{12,4},{14,6},{16,24},{18,... | collective-permute-start | bytes 393224 | tf_op jit(solution)/shard_map/ppermute | solution.py:373
  8.1 8.9 %collective-permute-start.1 = (bf16[128,512]{1,0:T(8,128)(2,1)}, bf16[128,512]{1,0:T(8,128)(2,1)S(1)}, u32[]{:S(2)}, u32[]{:S(2)}) collective-permute-start(bf16[128,512]{1,0:T(8,128)(2,1)} %get-tuple-element.39), channel_id=1, source_target_pairs={{0,16},{2,18},{4,20},{6,22},{8,24},{10,26},{12,28},{14,30},{16,0},... | collective-permute-start | bytes 393224 | tf_op jit(solution)/shard_map/ppermute | solution.py:373
  10.7 6.8 %collective-permute-start.4 = (bf16[128,512]{1,0:T(8,128)(2,1)}, bf16[128,512]{1,0:T(8,128)(2,1)S(1)}, u32[]{:S(2)}, u32[]{:S(2)}) collective-permute-start(bf16[128,512]{1,0:T(8,128)(2,1)} %get-tuple-element.39), channel_id=1, source_target_pairs={{0,4},{2,6},{4,0},{6,2},{8,12},{10,14},{12,8},{14,10},{16,20},{18,... | collective-permute-start | bytes 393224 | tf_op jit(solution)/shard_map/ppermute | solution.py:373
  12.2 0.9 %copy-start.2 = (bf16[128,1024]{1,0:T(8,128)(2,1)S(1)}, bf16[128,1024]{1,0:T(8,128)(2,1)}, u32[]{:S(2)}) copy-start(bf16[128,1024]{1,0:T(8,128)(2,1)} %get-tuple-element.37.both_ref) | copy-start | bytes 786436
  13.7 5.1 %collective-permute-start.3 = (bf16[128,512]{1,0:T(8,128)(2,1)S(1)}, bf16[128,512]{1,0:T(8,128)(2,1)S(1)}, u32[]{:S(2)}, u32[]{:S(2)}) collective-permute-start(bf16[128,512]{1,0:T(8,128)(2,1)S(1)} %collective-permute-done.2.refs_2_), channel_id=1, source_target_pairs={{0,4},{2,6},{4,0},{6,2},{8,12},{10,14},{12,8},{14,10},{16,20},{18,... | collective-permute-start | bytes 393224 | tf_op jit(solution)/shard_map/ppermute | solution.py:373
  17.1 5.0 %collective-permute-start.5 = (bf16[128,512]{1,0:T(8,128)(2,1)S(1)}, bf16[128,512]{1,0:T(8,128)(2,1)S(1)}, u32[]{:S(2)}, u32[]{:S(2)}) collective-permute-start(bf16[128,512]{1,0:T(8,128)(2,1)S(1)} %collective-permute-done.1.refs_3_), channel_id=1, source_target_pairs={{0,8},{2,10},{4,12},{6,14},{8,0},{10,2},{12,4},{14,6},{16,24},{18,... | collective-permute-start | bytes 393224 | tf_op jit(solution)/shard_map/ppermute | solution.py:373
  17.5 6.0 %collective-permute-start = (bf16[128,512]{1,0:T(8,128)(2,1)S(1)}, bf16[128,512]{1,0:T(8,128)(2,1)S(1)}, u32[]{:S(2)}, u32[]{:S(2)}) collective-permute-start(bf16[128,512]{1,0:T(8,128)(2,1)S(1)} %get-tuple-element.52.q_ref), channel_id=1, source_target_pairs={{0,2},{2,0},{4,6},{6,4},{8,10},{10,8},{12,14},{14,12},{16,18},{18,... | collective-permute-start | bytes 393224 | tf_op jit(solution)/shard_map/ppermute | solution.py:373
  18.7 7.1 %collective-permute-start.7 = (bf16[128,512]{1,0:T(8,128)(2,1)S(1)}, bf16[128,512]{1,0:T(8,128)(2,1)S(1)}, u32[]{:S(2)}, u32[]{:S(2)}) collective-permute-start(bf16[128,512]{1,0:T(8,128)(2,1)S(1)} %collective-permute-done.1.refs_3_), channel_id=1, source_target_pairs={{0,4},{2,6},{4,0},{6,2},{8,12},{10,14},{12,8},{14,10},{16,20},{18,... | collective-permute-start | bytes 393224 | tf_op jit(solution)/shard_map/ppermute | solution.py:373
  22.0 5.0 %collective-permute-start.8 = (bf16[128,512]{1,0:T(8,128)(2,1)S(1)}, bf16[128,512]{1,0:T(8,128)(2,1)S(1)}, u32[]{:S(2)}, u32[]{:S(2)}) collective-permute-start(bf16[128,512]{1,0:T(8,128)(2,1)S(1)} %collective-permute-done.5.refs_5_), channel_id=1, source_target_pairs={{0,4},{2,6},{4,0},{6,2},{8,12},{10,14},{12,8},{14,10},{16,20},{18,... | collective-permute-start | bytes 393224 | tf_op jit(solution)/shard_map/ppermute | solution.py:373
  25.7 6.8 %copy-start.5 = (s32[64]{0:T(128)S(1)}, s32[64]{0:T(128)}, u32[]{:S(2)}) copy-start(s32[64]{0:T(128)} %slot_ref.1) | copy-start | bytes 772
  25.7 4.4 %collective-permute-start.6 = (bf16[128,640]{1,0:T(8,128)(2,1)S(1)}, bf16[128,640]{1,0:T(8,128)(2,1)S(1)}, u32[]{:S(2)}, u32[]{:S(2)}) collective-permute-start(bf16[128,640]{1,0:T(8,128)(2,1)S(1)} %get-tuple-element.49), channel_id=1, source_target_pairs={{0,2},{2,0},{4,6},{6,4},{8,10},{10,8},{12,14},{14,12},{16,18},{18,... | collective-permute-start | bytes 491528 | tf_op jit(solution)/shard_map/ppermute | solution.py:373
  28.3 1.9 %collective-permute-start.10 = (bf16[64,640]{1,0:T(8,128)(2,1)S(1)}, bf16[64,640]{1,0:T(8,128)(2,1)S(1)}, u32[]{:S(2)}, u32[]{:S(2)}) collective-permute-start(bf16[64,640]{1,0:T(8,128)(2,1)S(1)} %get-tuple-element.60), channel_id=1, source_target_pairs={{0,2},{2,0},{4,6},{6,4},{8,10},{10,8},{12,14},{14,12},{16,18},{18,... | collective-permute-start | bytes 245768 | tf_op jit(solution)/shard_map/ppermute | solution.py:373
  29.6 4.3 %copy-start.1 = (bf16[128,2048]{1,0:T(8,128)(2,1)S(1)}, bf16[128,2048]{1,0:T(8,128)(2,1)}, u32[]{:S(2)}) copy-start(bf16[128,2048]{1,0:T(8,128)(2,1)} %tok_ref.1) | copy-start | bytes 1572868
  29.6 3.0 %collective-permute-start.9 = (bf16[64,640]{1,0:T(8,128)(2,1)S(1)}, bf16[64,640]{1,0:T(8,128)(2,1)S(1)}, u32[]{:S(2)}, u32[]{:S(2)}) collective-permute-start(bf16[64,640]{1,0:T(8,128)(2,1)S(1)} %get-tuple-element.57), channel_id=1, source_target_pairs={{0,2},{2,0},{4,6},{6,4},{8,10},{10,8},{12,14},{14,12},{16,18},{18,... | collective-permute-start | bytes 245768 | tf_op jit(solution)/shard_map/ppermute | solution.py:373
  31.0 8.3 %collective-permute-start.11 = (bf16[64,2048]{1,0:T(8,128)(2,1)S(1)}, bf16[64,2048]{1,0:T(8,128)(2,1)S(1)}, u32[]{:S(2)}, u32[]{:S(2)}) collective-permute-start(bf16[64,2048]{1,0:T(8,128)(2,1)S(1)} %leave.1), channel_id=1, source_target_pairs={{0,1},{1,0},{2,3},{3,2},{4,5},{5,4},{6,7},{7,6},{8,9},{9,8},{10,11... | collective-permute-start | bytes 786440 | tf_op jit(solution)/shard_map/ppermute | solution.py:512
  33.8 5.5 %collective-permute-start.12 = (bf16[8,2,32,256]{3,2,1,0:T(8,128)(2,1)S(1)}, bf16[8,2,32,256]{3,2,1,0:T(8,128)(2,1)S(1)}, u32[]{:S(2)}, u32[]{:S(2)}) collective-permute-start(bf16[8,2,32,256]{3,2,1,0:T(8,128)(2,1)S(1)} %get-tuple-element.71), channel_id=1, source_target_pairs={{0,2},{2,0},{4,6},{6,4},{8,10},{10,8},{12,14},{14,12},{16,18},{18,... | collective-permute-start | bytes 786440 | tf_op jit(solution)/shard_map/ppermute | solution.py:373

commit v11 on v10

--- a/solution.py
+++ b/solution.py
@@ -15,7 +15,7 @@
 EPS = 1e-05
 MASKED = -1e30
 FLOOR = -1e29
-WEIGHT_STEPS = 4
+WEIGHT_STEPS = 2
 MIB = 1024 * 1024
 SCALE = math.log2(math.e) / math.sqrt(HEAD)
 
@@ -76,33 +76,21 @@
     return u * cosine + pltpu.roll(u, HEAD // 2, 1) * signed_sine
 
 
-def weight_copies(refs, scratch, sems):
-    copies = []
+def weight_copies(source, scratch, sems):
     depth = scratch.shape[0] // WEIGHT_STEPS
-    for step in range(WEIGHT_STEPS):
-        group, column = [], 0
-        for i, ref in enumerate(refs):
-            rows, cols = pl.ds(step * depth, depth), pl.ds(column, ref.shape[1])
-            group.append(
-                pltpu.make_async_copy(ref.at[rows, :], scratch.at[rows, cols], sems.at[step, i])
-            )
-            column += ref.shape[1]
-        copies.append(group)
-    return copies
-
-
-def start_all(copies):
-    for group in copies:
-        for copy in group:
-            copy.start()
+    return [
+        pltpu.make_async_copy(
+            source.at[pl.ds(step * depth, depth), :], scratch.at[pl.ds(step * depth, depth), :], sems.at[step]
+        )
+        for step in range(WEIGHT_STEPS)
+    ]
 
 
 def stepped_dot(left, copies, scratch):
     depth = scratch.shape[0] // WEIGHT_STEPS
     total = None
-    for step in range(WEIGHT_STEPS):
-        for copy in copies[step]:
-            copy.wait()
+    for step, copy in enumerate(copies):
+        copy.wait()
         rows = slice(step * depth, (step + 1) * depth)
         part = jnp.dot(left[:, rows], scratch[rows, :], preferred_element_type=f32)
         total = part if total is None else total + part
@@ -111,74 +99,89 @@
 
 def project_kernel(
     block_hbm, len_hbm, freq_hbm, tok_hbm, gain_hbm, wk_hbm, wv_hbm, wq_hbm,
-    kv_ref, both_ref,
-    block_ref, len_ref, freq_ref, tok_ref, gain_ref, kv_weights, q_weights, small_sems, kv_sems, q_sems,
+    kv_hbm, both_hbm,
+    block_ref, len_ref, freq_ref, tok_ref, gain_ref, k_weights, v_weights, q_weights, both_ref,
+    small_sems, k_sems, v_sems, q_sems, out_sems,
 ):
     small = [
         pltpu.make_async_copy(source, target, small_sems.at[i])
         for i, (source, target) in enumerate(
             (
+                (tok_hbm, tok_ref),
                 (block_hbm, block_ref),
                 (len_hbm, len_ref),
                 (freq_hbm, freq_ref),
-                (tok_hbm, tok_ref),
                 (gain_hbm, gain_ref),
             )
         )
     ]
-    kv_copies = weight_copies((wk_hbm, wv_hbm), kv_weights, kv_sems)
-    q_copies = weight_copies((wq_hbm,), q_weights, q_sems)
-    for copy in small:
+    k_copies = weight_copies(wk_hbm, k_weights, k_sems)
+    v_copies = weight_copies(wv_hbm, v_weights, v_sems)
+    q_copies = weight_copies(wq_hbm, q_weights, q_sems)
+    for copy in small + k_copies + v_copies + q_copies:
         copy.start()
-    start_all(kv_copies)
-    start_all(q_copies)
     rows = tok_ref.shape[0]
-    for copy in small[:3]:
+    key_width = wk_hbm.shape[1]
+    kv_width = kv_hbm.shape[1]
+    for copy in small[1:4]:
         copy.wait()
     position = positions(blocks_of(block_ref, lax.axis_index("seq")), rows // 2, 0, (rows, HEAD))
     angle = (position - prompt_begin(position, len_ref)).astype(f32) * freq_ref[...]
     cosine, sine = jnp.cos(angle), jnp.sin(angle)
     lane = lax.broadcasted_iota(jnp.int32, (rows, HEAD), 1)
     sine = jnp.where(lane < HEAD // 2, -sine, sine)
-    for copy in small[3:]:
+    for copy in small[:1] + small[4:]:
         copy.wait()
     wide = tok_ref[...].astype(f32)
     scale = lax.rsqrt(jnp.mean(wide * wide, -1, keepdims=True) + EPS)
     normed = (wide * scale * gain_ref[...]).astype(bf16)
-    product = stepped_dot(normed, kv_copies, kv_weights)
-    key_width = wk_hbm.shape[1]
+    product = stepped_dot(normed, k_copies, k_weights)
     for h in range(key_width // HEAD):
         cols = slice(h * HEAD, (h + 1) * HEAD)
-        kv_ref[:, cols] = rotate(product[:, cols], cosine, sine).astype(bf16)
-    kv_ref[:, key_width:] = product[:, key_width:].astype(bf16)
-    both_ref[:, : kv_ref.shape[1]] = kv_ref[...]
+        both_ref[:, cols] = rotate(product[:, cols], cosine, sine).astype(bf16)
+    both_ref[:, key_width:kv_width] = stepped_dot(normed, v_copies, v_weights).astype(bf16)
+    kv_part = both_ref.at[:, pl.ds(0, kv_width)]
+    q_part = pl.ds(kv_width, wq_hbm.shape[1])
+    writes = [
+        pltpu.make_async_copy(kv_part, kv_hbm, out_sems.at[0]),
+        pltpu.make_async_copy(kv_part, both_hbm.at[:, pl.ds(0, kv_width)], out_sems.at[1]),
+    ]
+    for copy in writes:
+        copy.start()
     product = stepped_dot(normed, q_copies, q_weights)
     for h in range(wq_hbm.shape[1] // HEAD):
         cols = slice(h * HEAD, (h + 1) * HEAD)
         turned = rotate(product[:, cols], cosine, sine).astype(bf16)
-        both_ref[:, pl.ds(kv_ref.shape[1] + h * HEAD, HEAD)] = turned
-
-
-def attend_kernel(pieces, side, block_ref, len_ref, q_ref, far_ref, *refs):
+        both_ref[:, kv_width + h * HEAD : kv_width + (h + 1) * HEAD] = turned
+    writes.append(pltpu.make_async_copy(both_ref.at[:, q_part], both_hbm.at[:, q_part], out_sems.at[2]))
+    writes[2].start()
+    for copy in writes:
+        copy.wait()
+
+
+def attend_kernel(pieces, side, key_pos_ref, q_pos_ref, q_begin_ref, q_ref, far_ref, *refs):
     pieces, refs = with_refs(pieces, refs)
     shard = lax.axis_index("seq")
     rows, q_width = q_ref.shape
     key_width = pieces[0].arrays[0].shape[1] // 2
     kv_heads = key_width // HEAD
     group = q_width // key_width
-    shards = [shard, shard ^ 1]
     if side is None:
-        taken, span = rows, slice(None)
-        blocks = [block for s in shards for block in blocks_of(block_ref, s)]
+        taken, first = rows, 0
+        span = slice(None)
     else:
         part = lax.axis_index("req")
-        part = 1 - part if side else part
         taken = rows // 2
-        span = pl.ds(pl.multiple_of(part * taken, taken), taken)
-        blocks = [jnp.where(part == 0, *blocks_of(block_ref, s)) for s in shards]
+        first = pl.multiple_of((1 - part if side else part) * taken, taken)
+        span = pl.ds(first, taken)
     both = 2 * taken
-    q_pos = positions(blocks, rows // 2, 0, (both, 1))
-    q_begin = prompt_begin(q_pos, len_ref)
+
+    def of_both_cores(ref):
+        return jnp.concatenate(
+            [ref[pl.ds(pl.multiple_of(core * rows + first, taken), taken), :] for core in (0, 1)], 0
+        )
+
+    q_pos, q_begin = of_both_cores(q_pos_ref), of_both_cores(q_begin_ref)
     queries = [
         jnp.concatenate(
             [
@@ -192,10 +195,11 @@
     ]
 
     def absorb(state, blocks, sources):
-        width = rows * len(blocks)
-        held = [block for s in sources for block in blocks_of(block_ref, s)]
-        key_pos = positions(held, rows // 2, 1, (1, width))
-        bias = jnp.where((key_pos >= q_begin) & (key_pos <= q_pos), 0.0, MASKED)
+        bias = []
+        for source in sources:
+            key_pos = key_pos_ref[pl.ds(source, 1), :]
+            bias.append(jnp.where((key_pos >= q_begin) & (key_pos <= q_pos), 0.0, MASKED))
+        bias = jnp.concatenate(bias, 1)
         bias = jnp.concatenate([bias] * group, 0)
         out = []
         for g in range(kv_heads):
@@ -265,9 +269,21 @@
     packed_ref[:, q_width:] = parts.astype(bf16)
 
 
-def stage_kernel(both_ref, kv_out, q_out):
+def stage_kernel(block_ref, len_ref, both_ref, kv_out, q_out, key_pos_ref, q_pos_ref, q_begin_ref):
     kv_out[...] = both_ref[:, : kv_out.shape[1]]
     q_out[...] = both_ref[:, kv_out.shape[1] :]
+    shards, rows = key_pos_ref.shape
+    shard = lax.axis_index("seq")
+
+    def lay(s, carry):
+        key_pos_ref[pl.ds(s, 1), :] = positions(blocks_of(block_ref, s), rows // 2, 1, (1, rows))
+        return carry
+
+    lax.fori_loop(0, shards, lay, 0, unroll=shards <= 16)
+    blocks = [block for s in (shard, shard ^ 1) for block in blocks_of(block_ref, s)]
+    q_pos = positions(blocks, rows // 2, 0, q_pos_ref.shape)
+    q_pos_ref[...] = q_pos
+    q_begin_ref[...] = prompt_begin(q_pos, len_ref)
 
 
 def joined_rows(partials, first, half):
@@ -412,18 +428,22 @@
         project_kernel,
         out_shape=(struct((rows, kv_width), bf16), struct((rows, kv_width + q_width), bf16)),
         in_specs=in_hbm(8),
-        out_specs=tuple(in_vmem(2)),
+        out_specs=tuple(in_hbm(2)),
         scratch_shapes=[
             pltpu.SMEM(block_split.shape, jnp.int32),
             pltpu.SMEM(lengths.shape, jnp.int32),
             pltpu.VMEM((1, HEAD), f32),
             pltpu.VMEM((rows, width), bf16),
             pltpu.VMEM((1, width), f32),
-            pltpu.VMEM((width, kv_width), bf16),
+            pltpu.VMEM(key_projection.shape, bf16),
+            pltpu.VMEM(value_projection.shape, bf16),
             pltpu.VMEM((width, q_width), bf16),
+            pltpu.VMEM((rows, kv_width + q_width), bf16),
             pltpu.SemaphoreType.DMA((5,)),
-            pltpu.SemaphoreType.DMA((WEIGHT_STEPS, 2)),
-            pltpu.SemaphoreType.DMA((WEIGHT_STEPS, 1)),
+            pltpu.SemaphoreType.DMA((WEIGHT_STEPS,)),
+            pltpu.SemaphoreType.DMA((WEIGHT_STEPS,)),
+            pltpu.SemaphoreType.DMA((WEIGHT_STEPS,)),
+            pltpu.SemaphoreType.DMA((3,)),
         ],
         compiler_params=kernel_params(62),
         cost_estimate=cost(2 * rows * width * (kv_width + q_width), 2 * width * (kv_width + q_width)),
@@ -432,15 +452,21 @@
         block_split, lengths, inverse_frequencies(), tokens, norm_gain.reshape(1, width),
         key_projection, value_projection, w_query,
     )
-    staged, queries = pl.pallas_call(
+    staged, queries, *places = pl.pallas_call(
         stage_kernel,
-        out_shape=(struct((rows, kv_width), bf16), struct((rows, q_width), bf16)),
-        in_specs=in_vmem(1),
-        out_specs=tuple(in_vmem(2)),
+        out_shape=(
+            struct((rows, kv_width), bf16),
+            struct((rows, q_width), bf16),
+            struct((n, rows), jnp.int32),
+            struct((2 * rows, HEAD), jnp.int32),
+            struct((2 * rows, HEAD), jnp.int32),
+        ),
+        in_specs=in_smem(2) + in_vmem(1),
+        out_specs=tuple(in_vmem(5)),
         compiler_params=kernel_params(24),
         cost_estimate=cost(0, 0),
         name="stage",
-    )(both)
+    )(block_split, lengths, both)
     far_queries = swap(queries, n, 1)
 
     def attend(pieces, side=None):
@@ -453,13 +479,13 @@
                 struct((taken, HEAD), f32),
                 struct((taken, q_width + HEAD), bf16),
             ),
-            in_specs=in_smem(2) + in_vmem(2 + len(arrays)),
+            in_specs=in_vmem(5 + len(arrays)),
             out_specs=tuple(in_vmem(3)),
             compiler_params=kernel_params(32),
             cost_estimate=cost(0, 0),
             name="attend",
-        )(block_split, lengths, queries, far_queries, *arrays)
-        return [mine, stats, swap(packed, n, 1)]
+        )(*places, queries, far_queries, *arrays)
+        return [mine, stats, packed]
 
     def place_pages(pieces):
         arrays = operands(pieces)
@@ -488,6 +514,7 @@
         third = swapped(second, 4)
         (second, first_across, beside), _ = tied_all([second, first_across, beside], ())
         partials = attend([own, beside, first, second, first_across, third])
+        partials[2] = swap(partials[2], n, 1)
         queries, partials[1] = lax.optimization_barrier((queries, partials[1]))
         remaining = [swapped(second, 2), swapped(third, 2)]
         placed = [own, beside, first, second, first_across, third] + remaining
@@ -498,6 +525,7 @@
         partials, placed = [], remaining
     leaving = attend(remaining, 1)
     queries, leaving[1] = lax.optimization_barrier((queries, leaving[1]))
+    leaving[2] = swap(leaving[2], n, 1)
     staying = attend(remaining, 0)
     leaving[0], staying[1] = lax.optimization_barrier((leaving[0], staying[1]))
     sent = pl.pallas_call(
@@ -510,8 +538,8 @@
         name="leave",
     )(w_out, *partials, *leaving)
     received = lax.ppermute(sent, "req", [(i, (i + 1) % parts) for i in range(parts)])
-    placed, (staging, sent) = tied_all(placed, (staying[2], sent))
-    staying[2] = staging
+    staying[2] = swap(staying[2], n, 1)
+    placed, (staying[2], sent) = tied_all(placed, (staying[2], sent))
     cache, other = place_pages(placed)
     kept = pl.pallas_call(
         keep_kernel,

time: 40.3 us -> 39.2 us (0.973)
  Pallas kernels: 12.7 us -> 11.5 us
    pallas_call x3, Pallas kernels: 4.63 us -> 3 us  [attend(): pl.pallas_call(functools.partial(attend_kernel, pieces, side), out_shape=...]
    pallas_call x1, Pallas kernels: 0.02 us -> 0.61 us  [on_device(): pl.pallas_call(stage_kernel, out_shape=(struct((rows, kv_width), bf16), s...]
  transfers between devices with their start and end apart: 13 -> 13, of which waited for: 6 -> 5; matrix products, arithmetic and copies ran while one was open for 0% -> 0% of each run, Pallas kernels for 19% -> 16%
where the time goes in v11:
time: 39.2 us; the launch traced here: 39 us
  starting transfers between devices  14.7 us (38%)
  Pallas kernels  11.5 us (29%)
  waiting for transfers between devices  11 us (28%)
  local copies, waits for them, and re-layouts  0.98 us (2%)
  between operations  0.79 us (2%)
    ppermute x12, starting transfers between devices, swap(): return lax.ppermute(x, 'seq', [(i, i ^ bit) for i in range(n)])  13.1 us
    ppermute x12, waiting for transfers between devices, swap(): return lax.ppermute(x, 'seq', [(i, i ^ bit) for i in range(n)])  6.33 us
    ppermute x1, waiting for transfers between devices, on_device(): lax.ppermute(sent, 'req', [(i, (i + 1) % parts) for i in range(parts)])  4.71 us
    pallas_call x1, Pallas kernels, on_device(): pl.pallas_call(project_kernel, out_shape=(struct((rows, kv_width), bf16),...  4.21 us
    pallas_call x3, Pallas kernels, attend(): pl.pallas_call(functools.partial(attend_kernel, pieces, side), out_shape=...  3 us
    ppermute x1, starting transfers between devices, on_device(): lax.ppermute(sent, 'req', [(i, (i + 1) % parts) for i in range(parts)])  1.59 us
    pallas_call x1, Pallas kernels, place_pages(): pl.pallas_call(functools.partial(cache_kernel, pieces), out_shape=(struct...  1.21 us
    unnamed x12, local copies, waits for them, and re-layouts  0.98 us
  transfers between devices with their start and end apart: 13, of which 5 were waited for; matrix products, arithmetic and copies ran while one was open for 0% of the time, Pallas kernels for 16%

profile of v11, /device:TPU:0, one launch (start us, length us, event | category | flops | bytes accessed | tf_op | source)
XLA Modules:
  0.0 39.0 jit_solution(12653589233485402283)
XLA Ops:
  0.7 4.2 %project.1 = (bf16[128,512]{1,0:T(8,128)(2,1)}, bf16[128,1024]{1,0:T(8,128)(2,1)}) custom-call(s32[16]{0:T(128)} %block_ref.3, s32[4]{0:T(128)} %len_ref.1, f32[1,128]{1,0:T(1,128)} %constant.2.clone.freq_hbm, bf16[128,2048]{1,0:T(8,128)(2,1)} %tok_ref.1, f32[1,2048]{1,0:T(1,128)} %bitcast.1, bf16[2048,256]{1,0:T(8,128)(2,1)} %wk_hbm.1, ...), custom_call_target="tpu_custom_call" | custom-call | flops 536870912 | bytes 4194304 | tf_op jit(solution)/shard_map/project/pallas_call | solution.py:427
  4.9 3.1 %collective-permute-start.2 = (bf16[128,512]{1,0:T(8,128)(2,1)}, bf16[128,512]{1,0:T(8,128)(2,1)S(1)}, u32[]{:S(2)}, u32[]{:S(2)}) collective-permute-start(bf16[128,512]{1,0:T(8,128)(2,1)} %get-tuple-element.45), channel_id=1, source_target_pairs={{0,8},{2,10},{4,12},{6,14},{8,0},{10,2},{12,4},{14,6},{16,24},{18,... | collective-permute-start | bytes 393224 | tf_op jit(solution)/shard_map/ppermute | solution.py:389
  8.0 2.6 %collective-permute-start.1 = (bf16[128,512]{1,0:T(8,128)(2,1)}, bf16[128,512]{1,0:T(8,128)(2,1)S(1)}, u32[]{:S(2)}, u32[]{:S(2)}) collective-permute-start(bf16[128,512]{1,0:T(8,128)(2,1)} %get-tuple-element.45), channel_id=1, source_target_pairs={{0,16},{2,18},{4,20},{6,22},{8,24},{10,26},{12,28},{14,30},{16,0},... | collective-permute-start | bytes 393224 | tf_op jit(solution)/shard_map/ppermute | solution.py:389
  10.6 1.5 %collective-permute-start.4 = (bf16[128,512]{1,0:T(8,128)(2,1)}, bf16[128,512]{1,0:T(8,128)(2,1)S(1)}, u32[]{:S(2)}, u32[]{:S(2)}) collective-permute-start(bf16[128,512]{1,0:T(8,128)(2,1)} %get-tuple-element.45), channel_id=1, source_target_pairs={{0,4},{2,6},{4,0},{6,2},{8,12},{10,14},{12,8},{14,10},{16,20},{18,... | collective-permute-start | bytes 393224 | tf_op jit(solution)/shard_map/ppermute | solution.py:389
  12.1 0.9 %copy-done.2 = bf16[128,1024]{1,0:T(8,128)(2,1)S(1)} copy-done((bf16[128,1024]{1,0:T(8,128)(2,1)S(1)}, bf16[128,1024]{1,0:T(8,128)(2,1)}, u32[]{:S(2)}) %copy-start.2) | copy-done | bytes 262168
  13.0 0.6 %stage.1 = (bf16[128,512]{1,0:T(8,128)(2,1)S(1)}, bf16[128,512]{1,0:T(8,128)(2,1)S(1)}, s32[16,128]{1,0:T(8,128)S(1)}, s32[256,128]{1,0:T(8,128)S(1)}, s32[256,128]{1,0:T(8,128)S(1)}) custom-call(s32[16]{0:T(128)S(1)} %copy-done.3, s32[4]{0:T(128)S(1)} %copy-done.4, bf16[128,1024]{1,0:T(8,128)(2,1)S(1)} %copy-done.2), custom_call_target="tpu_custom_call" | custom-call | tf_op jit(solution)/shard_map/stage/pallas_call | solution.py:455
  13.6 1.7 %collective-permute-start.3 = (bf16[128,512]{1,0:T(8,128)(2,1)S(1)}, bf16[128,512]{1,0:T(8,128)(2,1)S(1)}, u32[]{:S(2)}, u32[]{:S(2)}) collective-permute-start(bf16[128,512]{1,0:T(8,128)(2,1)S(1)} %collective-permute-done.2.refs_2_), channel_id=1, source_target_pairs={{0,4},{2,6},{4,0},{6,2},{8,12},{10,14},{12,8},{14,10},{16,20},{18,... | collective-permute-start | bytes 393224 | tf_op jit(solution)/shard_map/ppermute | solution.py:389
  15.3 1.6 %collective-permute-done.1.refs_3_ = bf16[128,512]{1,0:T(8,128)(2,1)S(1)} collective-permute-done((bf16[128,512]{1,0:T(8,128)(2,1)}, bf16[128,512]{1,0:T(8,128)(2,1)S(1)}, u32[]{:S(2)}, u32[]{:S(2)}) %collective-permute-start.1) | collective-permute-done | bytes 131104 | tf_op jit(solution)/shard_map/ppermute | solution.py:389
  16.9 0.4 %collective-permute-start.5 = (bf16[128,512]{1,0:T(8,128)(2,1)S(1)}, bf16[128,512]{1,0:T(8,128)(2,1)S(1)}, u32[]{:S(2)}, u32[]{:S(2)}) collective-permute-start(bf16[128,512]{1,0:T(8,128)(2,1)S(1)} %collective-permute-done.1.refs_3_), channel_id=1, source_target_pairs={{0,8},{2,10},{4,12},{6,14},{8,0},{10,2},{12,4},{14,6},{16,24},{18,... | collective-permute-start | bytes 393224 | tf_op jit(solution)/shard_map/ppermute | solution.py:389
  17.4 1.3 %collective-permute-done.3.refs_4_ = bf16[128,512]{1,0:T(8,128)(2,1)S(1)} collective-permute-done((bf16[128,512]{1,0:T(8,128)(2,1)S(1)}, bf16[128,512]{1,0:T(8,128)(2,1)S(1)}, u32[]{:S(2)}, u32[]{:S(2)}) %collective-permute-start.3) | collective-permute-done | bytes 131104 | tf_op jit(solution)/shard_map/ppermute | solution.py:389
  18.7 1.6 %collective-permute-start.7 = (bf16[128,512]{1,0:T(8,128)(2,1)S(1)}, bf16[128,512]{1,0:T(8,128)(2,1)S(1)}, u32[]{:S(2)}, u32[]{:S(2)}) collective-permute-start(bf16[128,512]{1,0:T(8,128)(2,1)S(1)} %collective-permute-done.1.refs_3_), channel_id=1, source_target_pairs={{0,4},{2,6},{4,0},{6,2},{8,12},{10,14},{12,8},{14,10},{16,20},{18,... | collective-permute-start | bytes 393224 | tf_op jit(solution)/shard_map/ppermute | solution.py:389
  20.3 1.6 %collective-permute-done.5.refs_5_ = bf16[128,512]{1,0:T(8,128)(2,1)S(1)} collective-permute-done((bf16[128,512]{1,0:T(8,128)(2,1)S(1)}, bf16[128,512]{1,0:T(8,128)(2,1)S(1)}, u32[]{:S(2)}, u32[]{:S(2)}) %collective-permute-start.5) | collective-permute-done | bytes 131104 | tf_op jit(solution)/shard_map/ppermute | solution.py:389
  21.9 1.5 %collective-permute-start.8 = (bf16[128,512]{1,0:T(8,128)(2,1)S(1)}, bf16[128,512]{1,0:T(8,128)(2,1)S(1)}, u32[]{:S(2)}, u32[]{:S(2)}) collective-permute-start(bf16[128,512]{1,0:T(8,128)(2,1)S(1)} %collective-permute-done.5.refs_5_), channel_id=1, source_target_pairs={{0,4},{2,6},{4,0},{6,2},{8,12},{10,14},{12,8},{14,10},{16,20},{18,... | collective-permute-start | bytes 393224 | tf_op jit(solution)/shard_map/ppermute | solution.py:389
  23.4 1.6 %attend.3 = (f32[128,512]{1,0:T(8,128)S(1)}, f32[128,128]{1,0:T(8,128)S(1)}, bf16[128,640]{1,0:T(8,128)(2,1)S(1)}) custom-call(s32[16,128]{1,0:T(8,128)S(1)} %get-tuple-element.41.key_pos_ref, s32[256,128]{1,0:T(8,128)S(1)} %get-tuple-element.42.q_pos_ref, s32[256,128]{1,0:T(8,128)S(1)} %get-tuple-element.43.q_begin_ref, ...), custom_call_target="tpu_custom_call" | custom-call | tf_op jit(solution)/shard_map/attend/pallas_call | solution.py:475
  25.1 1.8 %collective-permute-done.8.refs_1_.refs_7_ = bf16[128,512]{1,0:T(8,128)(2,1)S(1)} collective-permute-done((bf16[128,512]{1,0:T(8,128)(2,1)S(1)}, bf16[128,512]{1,0:T(8,128)(2,1)S(1)}, u32[]{:S(2)}, u32[]{:S(2)}) %collective-permute-start.8) | collective-permute-done | bytes 131104 | tf_op jit(solution)/shard_map/ppermute | solution.py:389
  26.9 0.7 %attend.4 = (f32[64,512]{1,0:T(8,128)S(1)}, f32[64,128]{1,0:T(8,128)S(1)}, bf16[64,640]{1,0:T(8,128)(2,1)S(1)}) custom-call(s32[16,128]{1,0:T(8,128)S(1)} %get-tuple-element.41.key_pos_ref, s32[256,128]{1,0:T(8,128)S(1)} %get-tuple-element.42.q_pos_ref, s32[256,128]{1,0:T(8,128)S(1)} %get-tuple-element.43.q_begin_ref, ...), custom_call_target="tpu_custom_call" | custom-call | tf_op jit(solution)/shard_map/attend/pallas_call | solution.py:475
  27.6 0.7 %attend.5 = (f32[64,512]{1,0:T(8,128)S(1)}, f32[64,128]{1,0:T(8,128)S(1)}, bf16[64,640]{1,0:T(8,128)(2,1)S(1)}) custom-call(s32[16,128]{1,0:T(8,128)S(1)} %get-tuple-element.41.key_pos_ref, s32[256,128]{1,0:T(8,128)S(1)} %get-tuple-element.42.q_pos_ref, s32[256,128]{1,0:T(8,128)S(1)} %get-tuple-element.43.q_begin_ref, ...), custom_call_target="tpu_custom_call" | custom-call | tf_op jit(solution)/shard_map/attend/pallas_call | solution.py:475
  28.4 0.6 %collective-permute-start.9 = (bf16[64,640]{1,0:T(8,128)(2,1)S(1)}, bf16[64,640]{1,0:T(8,128)(2,1)S(1)}, u32[]{:S(2)}, u32[]{:S(2)}) collective-permute-start(bf16[64,640]{1,0:T(8,128)(2,1)S(1)} %get-tuple-element.63), channel_id=1, source_target_pairs={{0,2},{2,0},{4,6},{6,4},{8,10},{10,8},{12,14},{14,12},{16,18},{18,... | collective-permute-start | bytes 245768 | tf_op jit(solution)/shard_map/ppermute | solution.py:389
  28.9 0.8 %leave.1 = bf16[64,2048]{1,0:T(8,128)(2,1)S(1)} custom-call(bf16[512,2048]{1,0:T(8,128)(2,1)S(1)} %copy-done, f32[128,512]{1,0:T(8,128)S(1)} %get-tuple-element.52.refs_0_, f32[128,128]{1,0:T(8,128)S(1)} %get-tuple-element.54.refs_1_, bf16[128,640]{1,0:T(8,128)(2,1)S(1)} %collective-permute-done.6.refs_2_, f32[64,512]{1,0:T(8,128)S(1)} %get-tuple-element.64.refs_3_, ...), custom_call_target="tpu_custom_call" | custom-call | tf_op jit(solution)/shard_map/leave/pallas_call | solution.py:531
  29.7 1.6 %collective-permute-start.11 = (bf16[64,2048]{1,0:T(8,128)(2,1)S(1)}, bf16[64,2048]{1,0:T(8,128)(2,1)S(1)}, u32[]{:S(2)}, u32[]{:S(2)}) collective-permute-start(bf16[64,2048]{1,0:T(8,128)(2,1)S(1)} %leave.1), channel_id=1, source_target_pairs={{0,1},{1,0},{2,3},{3,2},{4,5},{5,4},{6,7},{7,6},{8,9},{9,8},{10,11... | collective-permute-start | bytes 786440 | tf_op jit(solution)/shard_map/ppermute | solution.py:540
  31.3 1.2 %cache.1 = (bf16[8,2,32,256]{3,2,1,0:T(8,128)(2,1)S(1)}, bf16[8,2,32,256]{3,2,1,0:T(8,128)(2,1)S(1)}) custom-call(s32[16]{0:T(128)S(1)} %copy-done.3, s32[64]{0:T(128)S(1)} %copy-done.5, bf16[128,512]{1,0:T(8,128)(2,1)S(1)} %get-tuple-element.68.refs_0_, bf16[128,512]{1,0:T(8,128)(2,1)S(1)} %collective-permute-done.4.refs_1_, ...), custom_call_target="tpu_custom_call" | custom-call | tf_op jit(solution)/shard_map/cache/pallas_call | solution.py:493
  32.6 0.8 %keep.1.kept_ref = f32[64,2048]{1,0:T(8,128)S(1)} custom-call(bf16[512,2048]{1,0:T(8,128)(2,1)S(1)} %copy-done, bf16[128,2048]{1,0:T(8,128)(2,1)S(1)} %copy-done.1, f32[128,512]{1,0:T(8,128)S(1)} %get-tuple-element.52.refs_0_, f32[128,128]{1,0:T(8,128)S(1)} %get-tuple-element.54.refs_1_, bf16[128,640]{1,0:T(8,128)(2,1)S(1)} %collective-permute-done.6.refs_2_, ...), custom_call_target="tpu_custom_call" | custom-call | tf_op jit(solution)/shard_map/keep/pallas_call | solution.py:544
  33.4 4.7 %collective-permute-done.11.received_ref = bf16[64,2048]{1,0:T(8,128)(2,1)S(1)} collective-permute-done((bf16[64,2048]{1,0:T(8,128)(2,1)S(1)}, bf16[64,2048]{1,0:T(8,128)(2,1)S(1)}, u32[]{:S(2)}, u32[]{:S(2)}) %collective-permute-start.11) | collective-permute-done | bytes 262176 | tf_op jit(solution)/shard_map/ppermute | solution.py:540
  38.2 0.9 %finish.1 = (bf16[64,2048]{1,0:T(8,128)(2,1)}, bf16[8,2,32,256]{3,2,1,0:T(8,128)(2,1)}) custom-call(f32[64,2048]{1,0:T(8,128)S(1)} %keep.1.kept_ref, bf16[64,2048]{1,0:T(8,128)(2,1)S(1)} %collective-permute-done.11.received_ref, bf16[8,2,32,256]{3,2,1,0:T(8,128)(2,1)S(1)} %get-tuple-element.76.mine_ref, ...), custom_call_target="tpu_custom_call" | custom-call | tf_op jit(solution)/shard_map/finish/pallas_call | solution.py:553
  (23 shorter events, 0.3 us)
Async XLA Ops:
  0.6 11.4 %copy-start.3 = (s32[16]{0:T(128)S(1)}, s32[16]{0:T(128)}, u32[]{:S(2)}) copy-start(s32[16]{0:T(128)} %block_ref.3) | copy-start | bytes 196
  0.6 11.4 %copy-start.4 = (s32[4]{0:T(128)S(1)}, s32[4]{0:T(128)}, u32[]{:S(2)}) copy-start(s32[4]{0:T(128)} %len_ref.1) | copy-start | bytes 52
  4.9 24.1 %copy-start = (bf16[512,2048]{1,0:T(8,128)(2,1)S(1)}, bf16[512,2048]{1,0:T(8,128)(2,1)}, u32[]{:S(2)}) copy-start(bf16[512,2048]{1,0:T(8,128)(2,1)} %wo_ref.3) | copy-start | bytes 6291460
  4.9 8.7 %collective-permute-start.2 = (bf16[128,512]{1,0:T(8,128)(2,1)}, bf16[128,512]{1,0:T(8,128)(2,1)S(1)}, u32[]{:S(2)}, u32[]{:S(2)}) collective-permute-start(bf16[128,512]{1,0:T(8,128)(2,1)} %get-tuple-element.45), channel_id=1, source_target_pairs={{0,8},{2,10},{4,12},{6,14},{8,0},{10,2},{12,4},{14,6},{16,24},{18,... | collective-permute-start | bytes 393224 | tf_op jit(solution)/shard_map/ppermute | solution.py:389
  8.0 8.9 %collective-permute-start.1 = (bf16[128,512]{1,0:T(8,128)(2,1)}, bf16[128,512]{1,0:T(8,128)(2,1)S(1)}, u32[]{:S(2)}, u32[]{:S(2)}) collective-permute-start(bf16[128,512]{1,0:T(8,128)(2,1)} %get-tuple-element.45), channel_id=1, source_target_pairs={{0,16},{2,18},{4,20},{6,22},{8,24},{10,26},{12,28},{14,30},{16,0},... | collective-permute-start | bytes 393224 | tf_op jit(solution)/shard_map/ppermute | solution.py:389
  10.6 6.8 %collective-permute-start.4 = (bf16[128,512]{1,0:T(8,128)(2,1)}, bf16[128,512]{1,0:T(8,128)(2,1)S(1)}, u32[]{:S(2)}, u32[]{:S(2)}) collective-permute-start(bf16[128,512]{1,0:T(8,128)(2,1)} %get-tuple-element.45), channel_id=1, source_target_pairs={{0,4},{2,6},{4,0},{6,2},{8,12},{10,14},{12,8},{14,10},{16,20},{18,... | collective-permute-start | bytes 393224 | tf_op jit(solution)/shard_map/ppermute | solution.py:389
  12.1 1.0 %copy-start.2 = (bf16[128,1024]{1,0:T(8,128)(2,1)S(1)}, bf16[128,1024]{1,0:T(8,128)(2,1)}, u32[]{:S(2)}) copy-start(bf16[128,1024]{1,0:T(8,128)(2,1)} %get-tuple-element.40.both_ref) | copy-start | bytes 786436
  13.6 5.0 %collective-permute-start.3 = (bf16[128,512]{1,0:T(8,128)(2,1)S(1)}, bf16[128,512]{1,0:T(8,128)(2,1)S(1)}, u32[]{:S(2)}, u32[]{:S(2)}) collective-permute-start(bf16[128,512]{1,0:T(8,128)(2,1)S(1)} %collective-permute-done.2.refs_2_), channel_id=1, source_target_pairs={{0,4},{2,6},{4,0},{6,2},{8,12},{10,14},{12,8},{14,10},{16,20},{18,... | collective-permute-start | bytes 393224 | tf_op jit(solution)/shard_map/ppermute | solution.py:389
  16.9 5.0 %collective-permute-start.5 = (bf16[128,512]{1,0:T(8,128)(2,1)S(1)}, bf16[128,512]{1,0:T(8,128)(2,1)S(1)}, u32[]{:S(2)}, u32[]{:S(2)}) collective-permute-start(bf16[128,512]{1,0:T(8,128)(2,1)S(1)} %collective-permute-done.1.refs_3_), channel_id=1, source_target_pairs={{0,8},{2,10},{4,12},{6,14},{8,0},{10,2},{12,4},{14,6},{16,24},{18,... | collective-permute-start | bytes 393224 | tf_op jit(solution)/shard_map/ppermute | solution.py:389
  17.4 6.0 %collective-permute-start = (bf16[128,512]{1,0:T(8,128)(2,1)S(1)}, bf16[128,512]{1,0:T(8,128)(2,1)S(1)}, u32[]{:S(2)}, u32[]{:S(2)}) collective-permute-start(bf16[128,512]{1,0:T(8,128)(2,1)S(1)} %get-tuple-element.58.q_ref), channel_id=1, source_target_pairs={{0,2},{2,0},{4,6},{6,4},{8,10},{10,8},{12,14},{14,12},{16,18},{18,... | collective-permute-start | bytes 393224 | tf_op jit(solution)/shard_map/ppermute | solution.py:389
  18.7 6.4 %collective-permute-start.7 = (bf16[128,512]{1,0:T(8,128)(2,1)S(1)}, bf16[128,512]{1,0:T(8,128)(2,1)S(1)}, u32[]{:S(2)}, u32[]{:S(2)}) collective-permute-start(bf16[128,512]{1,0:T(8,128)(2,1)S(1)} %collective-permute-done.1.refs_3_), channel_id=1, source_target_pairs={{0,4},{2,6},{4,0},{6,2},{8,12},{10,14},{12,8},{14,10},{16,20},{18,... | collective-permute-start | bytes 393224 | tf_op jit(solution)/shard_map/ppermute | solution.py:389
  21.9 5.0 %collective-permute-start.8 = (bf16[128,512]{1,0:T(8,128)(2,1)S(1)}, bf16[128,512]{1,0:T(8,128)(2,1)S(1)}, u32[]{:S(2)}, u32[]{:S(2)}) collective-permute-start(bf16[128,512]{1,0:T(8,128)(2,1)S(1)} %collective-permute-done.5.refs_5_), channel_id=1, source_target_pairs={{0,4},{2,6},{4,0},{6,2},{8,12},{10,14},{12,8},{14,10},{16,20},{18,... | collective-permute-start | bytes 393224 | tf_op jit(solution)/shard_map/ppermute | solution.py:389
  25.0 3.9 %collective-permute-start.6 = (bf16[128,640]{1,0:T(8,128)(2,1)S(1)}, bf16[128,640]{1,0:T(8,128)(2,1)S(1)}, u32[]{:S(2)}, u32[]{:S(2)}) collective-permute-start(bf16[128,640]{1,0:T(8,128)(2,1)S(1)} %get-tuple-element.55), channel_id=1, source_target_pairs={{0,2},{2,0},{4,6},{6,4},{8,10},{10,8},{12,14},{14,12},{16,18},{18,... | collective-permute-start | bytes 491528 | tf_op jit(solution)/shard_map/ppermute | solution.py:389
  27.6 3.8 %copy-start.5 = (s32[64]{0:T(128)S(1)}, s32[64]{0:T(128)}, u32[]{:S(2)}) copy-start(s32[64]{0:T(128)} %slot_ref.1) | copy-start | bytes 772
  27.6 1.4 %collective-permute-start.10 = (bf16[64,640]{1,0:T(8,128)(2,1)S(1)}, bf16[64,640]{1,0:T(8,128)(2,1)S(1)}, u32[]{:S(2)}, u32[]{:S(2)}) collective-permute-start(bf16[64,640]{1,0:T(8,128)(2,1)S(1)} %get-tuple-element.66), channel_id=1, source_target_pairs={{0,2},{2,0},{4,6},{6,4},{8,10},{10,8},{12,14},{14,12},{16,18},{18,... | collective-permute-start | bytes 245768 | tf_op jit(solution)/shard_map/ppermute | solution.py:389
  28.3 4.3 %copy-start.1 = (bf16[128,2048]{1,0:T(8,128)(2,1)S(1)}, bf16[128,2048]{1,0:T(8,128)(2,1)}, u32[]{:S(2)}) copy-start(bf16[128,2048]{1,0:T(8,128)(2,1)} %tok_ref.1) | copy-start | bytes 1572868
  28.4 3.0 %collective-permute-start.9 = (bf16[64,640]{1,0:T(8,128)(2,1)S(1)}, bf16[64,640]{1,0:T(8,128)(2,1)S(1)}, u32[]{:S(2)}, u32[]{:S(2)}) collective-permute-start(bf16[64,640]{1,0:T(8,128)(2,1)S(1)} %get-tuple-element.63), channel_id=1, source_target_pairs={{0,2},{2,0},{4,6},{6,4},{8,10},{10,8},{12,14},{14,12},{16,18},{18,... | collective-permute-start | bytes 245768 | tf_op jit(solution)/shard_map/ppermute | solution.py:389
  29.7 8.4 %collective-permute-start.11 = (bf16[64,2048]{1,0:T(8,128)(2,1)S(1)}, bf16[64,2048]{1,0:T(8,128)(2,1)S(1)}, u32[]{:S(2)}, u32[]{:S(2)}) collective-permute-start(bf16[64,2048]{1,0:T(8,128)(2,1)S(1)} %leave.1), channel_id=1, source_target_pairs={{0,1},{1,0},{2,3},{3,2},{4,5},{5,4},{6,7},{7,6},{8,9},{9,8},{10,11... | collective-permute-start | bytes 786440 | tf_op jit(solution)/shard_map/ppermute | solution.py:540
  32.5 5.6 %collective-permute-start.12 = (bf16[8,2,32,256]{3,2,1,0:T(8,128)(2,1)S(1)}, bf16[8,2,32,256]{3,2,1,0:T(8,128)(2,1)S(1)}, u32[]{:S(2)}, u32[]{:S(2)}) collective-permute-start(bf16[8,2,32,256]{3,2,1,0:T(8,128)(2,1)S(1)} %get-tuple-element.77), channel_id=1, source_target_pairs={{0,2},{2,0},{4,6},{6,4},{8,10},{10,8},{12,14},{14,12},{16,18},{18,... | collective-permute-start | bytes 786440 | tf_op jit(solution)/shard_map/ppermute | solution.py:389

commit v12 on v11

--- a/solution.py
+++ b/solution.py
@@ -44,10 +44,12 @@
     return pl.CostEstimate(flops=flops, bytes_accessed=moved, transcendentals=0)
 
 
-def inverse_frequencies():
+def rotary_constants(half):
     exponent = np.arange(HEAD // 2, dtype=np.float64) * (2.0 / HEAD)
-    freq = (THETA**-exponent).astype(np.float32)
-    return jnp.asarray(np.concatenate([freq, freq])[None, :])
+    freq = np.tile(THETA**-exponent, 2)[None, :]
+    angle = np.arange(half, dtype=np.float64)[:, None] * freq
+    rows = [np.cos(angle), np.sin(angle), np.broadcast_to(freq, (8, HEAD))]
+    return jnp.asarray(np.concatenate(rows).astype(np.float32))
 
 
 def blocks_of(block_ref, shard):
@@ -97,10 +99,41 @@
     return total
 
 
+def rotary_tables(block_ref, len_ref, turn_ref, half):
+    prompts = len_ref.shape[0]
+    blocks = blocks_of(block_ref, lax.axis_index("seq"))
+    starts = [jnp.int32(0)]
+    for r in range(prompts - 1):
+        starts.append(starts[-1] + len_ref[r])
+    count = 2 * prompts
+    index = lax.broadcasted_iota(jnp.int32, (count, HEAD), 0)
+    base = jnp.zeros((count, HEAD), jnp.int32)
+    for k, block in enumerate(blocks):
+        for p, start in enumerate(starts):
+            base = jnp.where(index == k * prompts + p, block * half - start, base)
+    angle = base.astype(f32) * turn_ref[2 * half : 2 * half + 1, :]
+    base_cos, base_sin = jnp.cos(angle), jnp.sin(angle)
+    row_cos, row_sin = turn_ref[:half, :], turn_ref[half : 2 * half, :]
+    row = lax.broadcasted_iota(jnp.int32, (half, HEAD), 0)
+    lane = lax.broadcasted_iota(jnp.int32, (half, HEAD), 1)
+    cosines, sines = [], []
+    for k, block in enumerate(blocks):
+        at = k * prompts
+        cos, sin = base_cos[at : at + 1], base_sin[at : at + 1]
+        for p in range(1, prompts):
+            inside = row >= starts[p] - block * half
+            cos = jnp.where(inside, base_cos[at + p : at + p + 1], cos)
+            sin = jnp.where(inside, base_sin[at + p : at + p + 1], sin)
+        cosines.append(row_cos * cos - row_sin * sin)
+        sine = row_sin * cos + row_cos * sin
+        sines.append(jnp.where(lane < HEAD // 2, -sine, sine))
+    return jnp.concatenate(cosines, 0), jnp.concatenate(sines, 0)
+
+
 def project_kernel(
-    block_hbm, len_hbm, freq_hbm, tok_hbm, gain_hbm, wk_hbm, wv_hbm, wq_hbm,
+    block_hbm, len_hbm, turn_hbm, tok_hbm, gain_hbm, wk_hbm, wv_hbm, wq_hbm,
     kv_hbm, both_hbm,
-    block_ref, len_ref, freq_ref, tok_ref, gain_ref, k_weights, v_weights, q_weights, both_ref,
+    block_ref, len_ref, turn_ref, tok_ref, gain_ref, k_weights, v_weights, q_weights, both_ref,
     small_sems, k_sems, v_sems, q_sems, out_sems,
 ):
     small = [
@@ -110,7 +143,7 @@
                 (tok_hbm, tok_ref),
                 (block_hbm, block_ref),
                 (len_hbm, len_ref),
-                (freq_hbm, freq_ref),
+                (turn_hbm, turn_ref),
                 (gain_hbm, gain_ref),
             )
         )
@@ -123,18 +156,12 @@
     rows = tok_ref.shape[0]
     key_width = wk_hbm.shape[1]
     kv_width = kv_hbm.shape[1]
-    for copy in small[1:4]:
-        copy.wait()
-    position = positions(blocks_of(block_ref, lax.axis_index("seq")), rows // 2, 0, (rows, HEAD))
-    angle = (position - prompt_begin(position, len_ref)).astype(f32) * freq_ref[...]
-    cosine, sine = jnp.cos(angle), jnp.sin(angle)
-    lane = lax.broadcasted_iota(jnp.int32, (rows, HEAD), 1)
-    sine = jnp.where(lane < HEAD // 2, -sine, sine)
-    for copy in small[:1] + small[4:]:
+    for copy in small:
         copy.wait()
     wide = tok_ref[...].astype(f32)
     scale = lax.rsqrt(jnp.mean(wide * wide, -1, keepdims=True) + EPS)
     normed = (wide * scale * gain_ref[...]).astype(bf16)
+    cosine, sine = rotary_tables(block_ref, len_ref, turn_ref, rows // 2)
     product = stepped_dot(normed, k_copies, k_weights)
     for h in range(key_width // HEAD):
         cols = slice(h * HEAD, (h + 1) * HEAD)
@@ -323,8 +350,12 @@
     sent_ref[...] = jnp.dot(context, wo_ref[...], preferred_element_type=f32).astype(bf16)
 
 
-def keep_kernel(wo_ref, tok_ref, *refs):
-    partials, out_ref = refs[:-1], refs[-1]
+def keep_kernel(wo_ref, tok_ref, mine_ref, *refs):
+    others, partials, (out_ref, cache_ref) = refs[:2], refs[2:-2], refs[-2:]
+    share = mine_ref.shape[0] // 2
+    for i, other_ref in enumerate(others):
+        part = slice(i * share, (i + 1) * share)
+        cache_ref[part] = mine_ref[part] + other_ref[...]
     half = out_ref.shape[0]
     first = lax.axis_index("req") * half
     context = joined_rows(partials, first, half)
@@ -332,20 +363,20 @@
     out_ref[...] = jnp.dot(context, wo_ref[...], preferred_element_type=f32) + residual
 
 
-def finish_kernel(kept_ref, received_ref, mine_ref, other_ref, hidden_ref, cache_ref):
+def finish_kernel(kept_ref, received_ref, hidden_ref):
     hidden_ref[...] = (kept_ref[...] + received_ref[...].astype(f32)).astype(bf16)
-    cache_ref[...] = mine_ref[...] + other_ref[...]
 
 
 def cache_kernel(pieces, block_ref, slot_ref, *refs):
-    pieces, (mine_ref, other_ref) = with_refs(pieces, refs)
+    pieces, (mine_ref, *other_refs) = with_refs(pieces, refs)
     shard = lax.axis_index("seq")
     slots = mine_ref.shape[0]
     key_width = mine_ref.shape[3]
     rows = slots * PAGE // 2
     pages = rows // 2 // PAGE
-    for target in (mine_ref, other_ref):
+    for target in (mine_ref, *other_refs):
         target[...] = jnp.zeros_like(target)
+    share = slots // len(other_refs)
 
     def place(ref, at, source):
         for k, block in enumerate(blocks_of(block_ref, source)):
@@ -356,12 +387,20 @@
                 offset = at + (k * pages + j) * PAGE
                 if not isinstance(offset, int):
                     offset = pl.multiple_of(offset, PAGE)
-                for target, owner in ((mine_ref, shard), (other_ref, shard ^ 1)):
-
-                    @pl.when(holder == owner)
+
+                def write(target, at_slot):
+                    target[at_slot, 0] = ref[pl.ds(offset, PAGE), :key_width]
+                    target[at_slot, 1] = ref[pl.ds(offset, PAGE), key_width:]
+
+                @pl.when(holder == shard)
+                def _():
+                    write(mine_ref, local)
+
+                for i, target in enumerate(other_refs):
+
+                    @pl.when((holder == shard ^ 1) & (local // share == i))
                     def _():
-                        target[local, 0] = ref[pl.ds(offset, PAGE), :key_width]
-                        target[local, 1] = ref[pl.ds(offset, PAGE), key_width:]
+                        write(target, local - i * share)
 
     for piece in pieces:
         if piece.count == 1:
@@ -432,7 +471,7 @@
         scratch_shapes=[
             pltpu.SMEM(block_split.shape, jnp.int32),
             pltpu.SMEM(lengths.shape, jnp.int32),
-            pltpu.VMEM((1, HEAD), f32),
+            pltpu.VMEM((2 * half + 8, HEAD), f32),
             pltpu.VMEM((rows, width), bf16),
             pltpu.VMEM((1, width), f32),
             pltpu.VMEM(key_projection.shape, bf16),
@@ -449,7 +488,7 @@
         cost_estimate=cost(2 * rows * width * (kv_width + q_width), 2 * width * (kv_width + q_width)),
         name="project",
     )(
-        block_split, lengths, inverse_frequencies(), tokens, norm_gain.reshape(1, width),
+        block_split, lengths, rotary_constants(half), tokens, norm_gain.reshape(1, width),
         key_projection, value_projection, w_query,
     )
     staged, queries, *places = pl.pallas_call(
@@ -492,9 +531,9 @@
         shape = (2 * rows // PAGE, 2, PAGE, kv_width // 2)
         return pl.pallas_call(
             functools.partial(cache_kernel, pieces),
-            out_shape=(struct(shape, bf16),) * 2,
+            out_shape=(struct(shape, bf16),) + (struct((shape[0] // 2,) + shape[1:], bf16),) * 2,
             in_specs=in_smem(2) + in_vmem(len(arrays)),
-            out_specs=tuple(in_vmem(2)),
+            out_specs=tuple(in_vmem(1 + 2)),
             compiler_params=kernel_params(32),
             cost_estimate=cost(0, 0),
             name="cache",
@@ -540,25 +579,26 @@
     received = lax.ppermute(sent, "req", [(i, (i + 1) % parts) for i in range(parts)])
     staying[2] = swap(staying[2], n, 1)
     placed, (staying[2], sent) = tied_all(placed, (staying[2], sent))
-    cache, other = place_pages(placed)
-    kept = pl.pallas_call(
+    cache, *other = place_pages(placed)
+    kept, cache = pl.pallas_call(
         keep_kernel,
-        out_shape=struct((half, width), f32),
-        in_specs=in_vmem(5 + len(partials)),
+        out_shape=(struct((half, width), f32), struct(cache.shape, bf16)),
+        in_specs=in_vmem(6 + 2 + len(partials)),
+        out_specs=tuple(in_vmem(2)),
+        compiler_params=kernel_params(24),
+        cost_estimate=cost(0, 0),
+        name="keep",
+    )(w_out, tokens, cache, *[swap(x, n, 1) for x in other], *partials, *staying)
+    hidden = pl.pallas_call(
+        finish_kernel,
+        out_shape=struct((half, width), bf16),
+        in_specs=in_vmem(2),
         out_specs=in_vmem(1)[0],
         compiler_params=kernel_params(24),
         cost_estimate=cost(0, 0),
-        name="keep",
-    )(w_out, tokens, *partials, *staying)
-    return pl.pallas_call(
-        finish_kernel,
-        out_shape=(struct((half, width), bf16), struct(cache.shape, bf16)),
-        in_specs=in_vmem(4),
-        out_specs=tuple(in_vmem(2)),
-        compiler_params=kernel_params(24),
-        cost_estimate=cost(0, 0),
         name="finish",
-    )(kept, received, cache, swap(other, n, 1))
+    )(kept, received)
+    return hidden, cache
 
 
 def solution(mesh):

time: 39.2 us -> 39.1 us (level)
  waiting for transfers between devices: 11 us -> 10 us
  Pallas kernels: 11.5 us -> 12.4 us
    ppermute x1, waiting for transfers between devices: 4.71 us -> 0.91 us  [on_device(): lax.ppermute(sent, 'req', [(i, (i + 1) % parts) for i in range(parts)])]
    ppermute x12 -> x13, waiting for transfers between devices: 6.33 us -> 9.11 us  [swap(): return lax.ppermute(x, 'seq', [(i, i ^ bit) for i in range(n)])]
    pallas_call x2, Pallas kernels: 1.67 us -> 2.2 us  [the longest x1 1.44 us: on_device(): pl.pallas_call(keep_kernel, out_shape=(struct((half, width), f32), struct...]
    ppermute x12 -> x13, starting transfers between devices: 13.1 us -> 13.1 us  [swap(): return lax.ppermute(x, 'seq', [(i, i ^ bit) for i in range(n)])]
  transfers between devices with their start and end apart: 13 -> 14, of which waited for: 5 -> 9; matrix products, arithmetic and copies ran while one was open for 0% -> 0% of each run, Pallas kernels for 16% -> 17%
where the time goes in v12:
time: 39.1 us; the launch traced here: 38.9 us
  starting transfers between devices  14.7 us (38%)
  Pallas kernels  12.4 us (32%)
  waiting for transfers between devices  10 us (26%)
  local copies, waits for them, and re-layouts  0.98 us (3%)
  between operations  0.77 us (2%)
    ppermute x13, starting transfers between devices, swap(): return lax.ppermute(x, 'seq', [(i, i ^ bit) for i in range(n)])  13.1 us
    ppermute x13, waiting for transfers between devices, swap(): return lax.ppermute(x, 'seq', [(i, i ^ bit) for i in range(n)])  9.11 us
    pallas_call x1, Pallas kernels, on_device(): pl.pallas_call(project_kernel, out_shape=(struct((rows, kv_width), bf16),...  4.22 us
    pallas_call x3, Pallas kernels, attend(): pl.pallas_call(functools.partial(attend_kernel, pieces, side), out_shape=...  3 us
    pallas_call x1, Pallas kernels, place_pages(): pl.pallas_call(functools.partial(cache_kernel, pieces), out_shape=(struct...  1.6 us
    ppermute x1, starting transfers between devices, on_device(): lax.ppermute(sent, 'req', [(i, (i + 1) % parts) for i in range(parts)])  1.59 us
    pallas_call x1, Pallas kernels, on_device(): pl.pallas_call(keep_kernel, out_shape=(struct((half, width), f32), struct...  1.44 us
    unnamed x12, local copies, waits for them, and re-layouts  0.98 us
  transfers between devices with their start and end apart: 14, of which 9 were waited for; matrix products, arithmetic and copies ran while one was open for 0% of the time, Pallas kernels for 17%

profile of v12, /device:TPU:0, one launch (start us, length us, event | category | flops | bytes accessed | tf_op | source)
XLA Modules:
  0.0 38.9 jit_solution(3933932976602955753)
XLA Ops:
  0.7 4.2 %project.1 = (bf16[128,512]{1,0:T(8,128)(2,1)}, bf16[128,1024]{1,0:T(8,128)(2,1)}) custom-call(s32[16]{0:T(128)} %block_ref.3, s32[4]{0:T(128)} %len_ref.1, f32[136,128]{1,0:T(8,128)} %constant.2.clone.turn_hbm, bf16[128,2048]{1,0:T(8,128)(2,1)} %tok_ref.1, f32[1,2048]{1,0:T(1,128)} %bitcast.1, bf16[2048,256]{1,0:T(8,128)(2,1)} %wk_hbm.1, ...), custom_call_target="tpu_custom_call" | custom-call | flops 536870912 | bytes 4194304 | tf_op jit(solution)/shard_map/project/pallas_call | solution.py:466
  4.9 3.1 %collective-permute-start.1 = (bf16[128,512]{1,0:T(8,128)(2,1)}, bf16[128,512]{1,0:T(8,128)(2,1)S(1)}, u32[]{:S(2)}, u32[]{:S(2)}) collective-permute-start(bf16[128,512]{1,0:T(8,128)(2,1)} %get-tuple-element.43), channel_id=1, source_target_pairs={{0,8},{2,10},{4,12},{6,14},{8,0},{10,2},{12,4},{14,6},{16,24},{18,... | collective-permute-start | bytes 393224 | tf_op jit(solution)/shard_map/ppermute | solution.py:428
  8.0 2.6 %collective-permute-start = (bf16[128,512]{1,0:T(8,128)(2,1)}, bf16[128,512]{1,0:T(8,128)(2,1)S(1)}, u32[]{:S(2)}, u32[]{:S(2)}) collective-permute-start(bf16[128,512]{1,0:T(8,128)(2,1)} %get-tuple-element.43), channel_id=1, source_target_pairs={{0,16},{2,18},{4,20},{6,22},{8,24},{10,26},{12,28},{14,30},{16,0},... | collective-permute-start | bytes 393224 | tf_op jit(solution)/shard_map/ppermute | solution.py:428
  10.6 1.5 %collective-permute-start.3 = (bf16[128,512]{1,0:T(8,128)(2,1)}, bf16[128,512]{1,0:T(8,128)(2,1)S(1)}, u32[]{:S(2)}, u32[]{:S(2)}) collective-permute-start(bf16[128,512]{1,0:T(8,128)(2,1)} %get-tuple-element.43), channel_id=1, source_target_pairs={{0,4},{2,6},{4,0},{6,2},{8,12},{10,14},{12,8},{14,10},{16,20},{18,... | collective-permute-start | bytes 393224 | tf_op jit(solution)/shard_map/ppermute | solution.py:428
  12.1 0.9 %copy-done.2 = bf16[128,1024]{1,0:T(8,128)(2,1)S(1)} copy-done((bf16[128,1024]{1,0:T(8,128)(2,1)S(1)}, bf16[128,1024]{1,0:T(8,128)(2,1)}, u32[]{:S(2)}) %copy-start.2) | copy-done | bytes 262168
  13.0 0.6 %stage.1 = (bf16[128,512]{1,0:T(8,128)(2,1)S(1)}, bf16[128,512]{1,0:T(8,128)(2,1)S(1)}, s32[16,128]{1,0:T(8,128)S(1)}, s32[256,128]{1,0:T(8,128)S(1)}, s32[256,128]{1,0:T(8,128)S(1)}) custom-call(s32[16]{0:T(128)S(1)} %copy-done.3, s32[4]{0:T(128)S(1)} %copy-done.4, bf16[128,1024]{1,0:T(8,128)(2,1)S(1)} %copy-done.2), custom_call_target="tpu_custom_call" | custom-call | tf_op jit(solution)/shard_map/stage/pallas_call | solution.py:494
  13.6 1.7 %collective-permute-start.2 = (bf16[128,512]{1,0:T(8,128)(2,1)S(1)}, bf16[128,512]{1,0:T(8,128)(2,1)S(1)}, u32[]{:S(2)}, u32[]{:S(2)}) collective-permute-start(bf16[128,512]{1,0:T(8,128)(2,1)S(1)} %collective-permute-done.1.refs_2_), channel_id=1, source_target_pairs={{0,4},{2,6},{4,0},{6,2},{8,12},{10,14},{12,8},{14,10},{16,20},{18,... | collective-permute-start | bytes 393224 | tf_op jit(solution)/shard_map/ppermute | solution.py:428
  15.3 1.6 %collective-permute-done.refs_3_ = bf16[128,512]{1,0:T(8,128)(2,1)S(1)} collective-permute-done((bf16[128,512]{1,0:T(8,128)(2,1)}, bf16[128,512]{1,0:T(8,128)(2,1)S(1)}, u32[]{:S(2)}, u32[]{:S(2)}) %collective-permute-start) | collective-permute-done | bytes 131104 | tf_op jit(solution)/shard_map/ppermute | solution.py:428
  17.4 1.3 %collective-permute-done.2.refs_4_ = bf16[128,512]{1,0:T(8,128)(2,1)S(1)} collective-permute-done((bf16[128,512]{1,0:T(8,128)(2,1)S(1)}, bf16[128,512]{1,0:T(8,128)(2,1)S(1)}, u32[]{:S(2)}, u32[]{:S(2)}) %collective-permute-start.2) | collective-permute-done | bytes 131104 | tf_op jit(solution)/shard_map/ppermute | solution.py:428
  18.7 1.6 %collective-permute-start.5 = (bf16[128,512]{1,0:T(8,128)(2,1)S(1)}, bf16[128,512]{1,0:T(8,128)(2,1)S(1)}, u32[]{:S(2)}, u32[]{:S(2)}) collective-permute-start(bf16[128,512]{1,0:T(8,128)(2,1)S(1)} %collective-permute-done.refs_3_), channel_id=1, source_target_pairs={{0,4},{2,6},{4,0},{6,2},{8,12},{10,14},{12,8},{14,10},{16,20},{18,... | collective-permute-start | bytes 393224 | tf_op jit(solution)/shard_map/ppermute | solution.py:428
  20.3 1.6 %collective-permute-done.4.refs_5_ = bf16[128,512]{1,0:T(8,128)(2,1)S(1)} collective-permute-done((bf16[128,512]{1,0:T(8,128)(2,1)S(1)}, bf16[128,512]{1,0:T(8,128)(2,1)S(1)}, u32[]{:S(2)}, u32[]{:S(2)}) %collective-permute-start.4) | collective-permute-done | bytes 131104 | tf_op jit(solution)/shard_map/ppermute | solution.py:428
  21.9 1.5 %collective-permute-start.6 = (bf16[128,512]{1,0:T(8,128)(2,1)S(1)}, bf16[128,512]{1,0:T(8,128)(2,1)S(1)}, u32[]{:S(2)}, u32[]{:S(2)}) collective-permute-start(bf16[128,512]{1,0:T(8,128)(2,1)S(1)} %collective-permute-done.4.refs_5_), channel_id=1, source_target_pairs={{0,4},{2,6},{4,0},{6,2},{8,12},{10,14},{12,8},{14,10},{16,20},{18,... | collective-permute-start | bytes 393224 | tf_op jit(solution)/shard_map/ppermute | solution.py:428
  23.4 1.6 %attend.3 = (f32[128,512]{1,0:T(8,128)S(1)}, f32[128,128]{1,0:T(8,128)S(1)}, bf16[128,640]{1,0:T(8,128)(2,1)S(1)}) custom-call(s32[16,128]{1,0:T(8,128)S(1)} %get-tuple-element.51.key_pos_ref, s32[256,128]{1,0:T(8,128)S(1)} %get-tuple-element.52.q_pos_ref, s32[256,128]{1,0:T(8,128)S(1)} %get-tuple-element.53.q_begin_ref, ...), custom_call_target="tpu_custom_call" | custom-call | tf_op jit(solution)/shard_map/attend/pallas_call | solution.py:514
  25.1 1.8 %collective-permute-done.6.refs_1_.refs_7_ = bf16[128,512]{1,0:T(8,128)(2,1)S(1)} collective-permute-done((bf16[128,512]{1,0:T(8,128)(2,1)S(1)}, bf16[128,512]{1,0:T(8,128)(2,1)S(1)}, u32[]{:S(2)}, u32[]{:S(2)}) %collective-permute-start.6) | collective-permute-done | bytes 131104 | tf_op jit(solution)/shard_map/ppermute | solution.py:428
  26.9 0.7 %attend.4 = (f32[64,512]{1,0:T(8,128)S(1)}, f32[64,128]{1,0:T(8,128)S(1)}, bf16[64,640]{1,0:T(8,128)(2,1)S(1)}) custom-call(s32[16,128]{1,0:T(8,128)S(1)} %get-tuple-element.51.key_pos_ref, s32[256,128]{1,0:T(8,128)S(1)} %get-tuple-element.52.q_pos_ref, s32[256,128]{1,0:T(8,128)S(1)} %get-tuple-element.53.q_begin_ref, ...), custom_call_target="tpu_custom_call" | custom-call | tf_op jit(solution)/shard_map/attend/pallas_call | solution.py:514
  27.6 0.7 %attend.5 = (f32[64,512]{1,0:T(8,128)S(1)}, f32[64,128]{1,0:T(8,128)S(1)}, bf16[64,640]{1,0:T(8,128)(2,1)S(1)}) custom-call(s32[16,128]{1,0:T(8,128)S(1)} %get-tuple-element.51.key_pos_ref, s32[256,128]{1,0:T(8,128)S(1)} %get-tuple-element.52.q_pos_ref, s32[256,128]{1,0:T(8,128)S(1)} %get-tuple-element.53.q_begin_ref, ...), custom_call_target="tpu_custom_call" | custom-call | tf_op jit(solution)/shard_map/attend/pallas_call | solution.py:514
  28.9 0.8 %leave.1 = bf16[64,2048]{1,0:T(8,128)(2,1)S(1)} custom-call(bf16[512,2048]{1,0:T(8,128)(2,1)S(1)} %copy-done, f32[128,512]{1,0:T(8,128)S(1)} %get-tuple-element.60.refs_0_.refs_2_, f32[128,128]{1,0:T(8,128)S(1)} %get-tuple-element.61.refs_1_.refs_3_, bf16[128,640]{1,0:T(8,128)(2,1)S(1)} %collective-permute-done.9.refs_2_.refs_4_, ...), custom_call_target="tpu_custom_call" | custom-call | tf_op jit(solution)/shard_map/leave/pallas_call | solution.py:570
  29.7 1.6 %collective-permute-start.13 = (bf16[64,2048]{1,0:T(8,128)(2,1)S(1)}, bf16[64,2048]{1,0:T(8,128)(2,1)S(1)}, u32[]{:S(2)}, u32[]{:S(2)}) collective-permute-start(bf16[64,2048]{1,0:T(8,128)(2,1)S(1)} %leave.1), channel_id=1, source_target_pairs={{0,1},{1,0},{2,3},{3,2},{4,5},{5,4},{6,7},{7,6},{8,9},{9,8},{10,11... | collective-permute-start | bytes 786440 | tf_op jit(solution)/shard_map/ppermute | solution.py:579
  31.3 1.3 %collective-permute-done.8.refs_7_ = bf16[64,640]{1,0:T(8,128)(2,1)S(1)} collective-permute-done((bf16[64,640]{1,0:T(8,128)(2,1)S(1)}, bf16[64,640]{1,0:T(8,128)(2,1)S(1)}, u32[]{:S(2)}, u32[]{:S(2)}) %collective-permute-start.8) | collective-permute-done | bytes 81952 | tf_op jit(solution)/shard_map/ppermute | solution.py:428
  32.6 1.6 %cache.1 = (bf16[8,2,32,256]{3,2,1,0:T(8,128)(2,1)S(1)}, bf16[4,2,32,256]{3,2,1,0:T(8,128)(2,1)S(1)}, bf16[4,2,32,256]{3,2,1,0:T(8,128)(2,1)S(1)}) custom-call(s32[16]{0:T(128)S(1)} %copy-done.3, s32[64]{0:T(128)S(1)} %copy-done.5, bf16[128,512]{1,0:T(8,128)(2,1)S(1)} %get-tuple-element.68.refs_0_, bf16[128,512]{1,0:T(8,128)(2,1)S(1)} %collective-permute-done.3.refs_1_, ...), custom_call_target="tpu_custom_call" | custom-call | tf_op jit(solution)/shard_map/cache/pallas_call | solution.py:532
  34.8 0.8 %collective-permute-done.11.refs_0_ = bf16[4,2,32,256]{3,2,1,0:T(8,128)(2,1)S(1)} collective-permute-done((bf16[4,2,32,256]{3,2,1,0:T(8,128)(2,1)S(1)}, bf16[4,2,32,256]{3,2,1,0:T(8,128)(2,1)S(1)}, u32[]{:S(2)}, u32[]{:S(2)}) %collective-permute-start.11) | collective-permute-done | bytes 131104 | tf_op jit(solution)/shard_map/ppermute | solution.py:428
  35.8 1.4 %keep.1 = (f32[64,2048]{1,0:T(8,128)S(1)}, bf16[8,2,32,256]{3,2,1,0:T(8,128)(2,1)}) custom-call(bf16[512,2048]{1,0:T(8,128)(2,1)S(1)} %copy-done, bf16[128,2048]{1,0:T(8,128)(2,1)S(1)} %copy-done.1, bf16[8,2,32,256]{3,2,1,0:T(8,128)(2,1)S(1)} %get-tuple-element.76.mine_ref, bf16[4,2,32,256]{3,2,1,0:T(8,128)(2,1)S(1)} %collective-permute-done.11.refs_0_, ...), custom_call_target="tpu_custom_call" | custom-call | tf_op jit(solution)/shard_map/keep/pallas_call | solution.py:583
  37.2 0.9 %collective-permute-done.13.received_ref = bf16[64,2048]{1,0:T(8,128)(2,1)S(1)} collective-permute-done((bf16[64,2048]{1,0:T(8,128)(2,1)S(1)}, bf16[64,2048]{1,0:T(8,128)(2,1)S(1)}, u32[]{:S(2)}, u32[]{:S(2)}) %collective-permute-start.13) | collective-permute-done | bytes 262176 | tf_op jit(solution)/shard_map/ppermute | solution.py:579
  38.1 0.8 %finish.1 = bf16[64,2048]{1,0:T(8,128)(2,1)} custom-call(f32[64,2048]{1,0:T(8,128)S(1)} %get-tuple-element.82.kept_ref, bf16[64,2048]{1,0:T(8,128)(2,1)S(1)} %collective-permute-done.13.received_ref), custom_call_target="tpu_custom_call" | custom-call | tf_op jit(solution)/shard_map/finish/pallas_call | solution.py:592
  (25 shorter events, 1.9 us)
Async XLA Ops:
  0.6 11.4 %copy-start.3 = (s32[16]{0:T(128)S(1)}, s32[16]{0:T(128)}, u32[]{:S(2)}) copy-start(s32[16]{0:T(128)} %block_ref.3) | copy-start | bytes 196
  0.6 11.4 %copy-start.4 = (s32[4]{0:T(128)S(1)}, s32[4]{0:T(128)}, u32[]{:S(2)}) copy-start(s32[4]{0:T(128)} %len_ref.1) | copy-start | bytes 52
  4.9 24.0 %copy-start = (bf16[512,2048]{1,0:T(8,128)(2,1)S(1)}, bf16[512,2048]{1,0:T(8,128)(2,1)}, u32[]{:S(2)}) copy-start(bf16[512,2048]{1,0:T(8,128)(2,1)} %wo_ref.3) | copy-start | bytes 6291460
  4.9 8.8 %collective-permute-start.1 = (bf16[128,512]{1,0:T(8,128)(2,1)}, bf16[128,512]{1,0:T(8,128)(2,1)S(1)}, u32[]{:S(2)}, u32[]{:S(2)}) collective-permute-start(bf16[128,512]{1,0:T(8,128)(2,1)} %get-tuple-element.43), channel_id=1, source_target_pairs={{0,8},{2,10},{4,12},{6,14},{8,0},{10,2},{12,4},{14,6},{16,24},{18,... | collective-permute-start | bytes 393224 | tf_op jit(solution)/shard_map/ppermute | solution.py:428
  8.0 8.9 %collective-permute-start = (bf16[128,512]{1,0:T(8,128)(2,1)}, bf16[128,512]{1,0:T(8,128)(2,1)S(1)}, u32[]{:S(2)}, u32[]{:S(2)}) collective-permute-start(bf16[128,512]{1,0:T(8,128)(2,1)} %get-tuple-element.43), channel_id=1, source_target_pairs={{0,16},{2,18},{4,20},{6,22},{8,24},{10,26},{12,28},{14,30},{16,0},... | collective-permute-start | bytes 393224 | tf_op jit(solution)/shard_map/ppermute | solution.py:428
  10.6 6.8 %collective-permute-start.3 = (bf16[128,512]{1,0:T(8,128)(2,1)}, bf16[128,512]{1,0:T(8,128)(2,1)S(1)}, u32[]{:S(2)}, u32[]{:S(2)}) collective-permute-start(bf16[128,512]{1,0:T(8,128)(2,1)} %get-tuple-element.43), channel_id=1, source_target_pairs={{0,4},{2,6},{4,0},{6,2},{8,12},{10,14},{12,8},{14,10},{16,20},{18,... | collective-permute-start | bytes 393224 | tf_op jit(solution)/shard_map/ppermute | solution.py:428
  12.1 1.0 %copy-start.2 = (bf16[128,1024]{1,0:T(8,128)(2,1)S(1)}, bf16[128,1024]{1,0:T(8,128)(2,1)}, u32[]{:S(2)}) copy-start(bf16[128,1024]{1,0:T(8,128)(2,1)} %get-tuple-element.44.both_ref) | copy-start | bytes 786436
  13.6 5.0 %collective-permute-start.2 = (bf16[128,512]{1,0:T(8,128)(2,1)S(1)}, bf16[128,512]{1,0:T(8,128)(2,1)S(1)}, u32[]{:S(2)}, u32[]{:S(2)}) collective-permute-start(bf16[128,512]{1,0:T(8,128)(2,1)S(1)} %collective-permute-done.1.refs_2_), channel_id=1, source_target_pairs={{0,4},{2,6},{4,0},{6,2},{8,12},{10,14},{12,8},{14,10},{16,20},{18,... | collective-permute-start | bytes 393224 | tf_op jit(solution)/shard_map/ppermute | solution.py:428
  16.9 5.0 %collective-permute-start.4 = (bf16[128,512]{1,0:T(8,128)(2,1)S(1)}, bf16[128,512]{1,0:T(8,128)(2,1)S(1)}, u32[]{:S(2)}, u32[]{:S(2)}) collective-permute-start(bf16[128,512]{1,0:T(8,128)(2,1)S(1)} %collective-permute-done.refs_3_), channel_id=1, source_target_pairs={{0,8},{2,10},{4,12},{6,14},{8,0},{10,2},{12,4},{14,6},{16,24},{18,... | collective-permute-start | bytes 393224 | tf_op jit(solution)/shard_map/ppermute | solution.py:428
  17.4 6.0 %collective-permute-start.7 = (bf16[128,512]{1,0:T(8,128)(2,1)S(1)}, bf16[128,512]{1,0:T(8,128)(2,1)S(1)}, u32[]{:S(2)}, u32[]{:S(2)}) collective-permute-start(bf16[128,512]{1,0:T(8,128)(2,1)S(1)} %get-tuple-element.58.q_ref), channel_id=1, source_target_pairs={{0,2},{2,0},{4,6},{6,4},{8,10},{10,8},{12,14},{14,12},{16,18},{18,... | collective-permute-start | bytes 393224 | tf_op jit(solution)/shard_map/ppermute | solution.py:428
  18.7 6.4 %collective-permute-start.5 = (bf16[128,512]{1,0:T(8,128)(2,1)S(1)}, bf16[128,512]{1,0:T(8,128)(2,1)S(1)}, u32[]{:S(2)}, u32[]{:S(2)}) collective-permute-start(bf16[128,512]{1,0:T(8,128)(2,1)S(1)} %collective-permute-done.refs_3_), channel_id=1, source_target_pairs={{0,4},{2,6},{4,0},{6,2},{8,12},{10,14},{12,8},{14,10},{16,20},{18,... | collective-permute-start | bytes 393224 | tf_op jit(solution)/shard_map/ppermute | solution.py:428
  21.9 5.0 %collective-permute-start.6 = (bf16[128,512]{1,0:T(8,128)(2,1)S(1)}, bf16[128,512]{1,0:T(8,128)(2,1)S(1)}, u32[]{:S(2)}, u32[]{:S(2)}) collective-permute-start(bf16[128,512]{1,0:T(8,128)(2,1)S(1)} %collective-permute-done.4.refs_5_), channel_id=1, source_target_pairs={{0,4},{2,6},{4,0},{6,2},{8,12},{10,14},{12,8},{14,10},{16,20},{18,... | collective-permute-start | bytes 393224 | tf_op jit(solution)/shard_map/ppermute | solution.py:428
  25.0 3.4 %collective-permute-start.9 = (bf16[128,640]{1,0:T(8,128)(2,1)S(1)}, bf16[128,640]{1,0:T(8,128)(2,1)S(1)}, u32[]{:S(2)}, u32[]{:S(2)}) collective-permute-start(bf16[128,640]{1,0:T(8,128)(2,1)S(1)} %get-tuple-element.62), channel_id=1, source_target_pairs={{0,2},{2,0},{4,6},{6,4},{8,10},{10,8},{12,14},{14,12},{16,18},{18,... | collective-permute-start | bytes 491528 | tf_op jit(solution)/shard_map/ppermute | solution.py:428
  27.5 5.0 %copy-start.5 = (s32[64]{0:T(128)S(1)}, s32[64]{0:T(128)}, u32[]{:S(2)}) copy-start(s32[64]{0:T(128)} %slot_ref.1) | copy-start | bytes 772
  27.6 1.3 %collective-permute-start.10 = (bf16[64,640]{1,0:T(8,128)(2,1)S(1)}, bf16[64,640]{1,0:T(8,128)(2,1)S(1)}, u32[]{:S(2)}, u32[]{:S(2)}) collective-permute-start(bf16[64,640]{1,0:T(8,128)(2,1)S(1)} %get-tuple-element.67), channel_id=1, source_target_pairs={{0,2},{2,0},{4,6},{6,4},{8,10},{10,8},{12,14},{14,12},{16,18},{18,... | collective-permute-start | bytes 245768 | tf_op jit(solution)/shard_map/ppermute | solution.py:428
  28.3 7.5 %copy-start.1 = (bf16[128,2048]{1,0:T(8,128)(2,1)S(1)}, bf16[128,2048]{1,0:T(8,128)(2,1)}, u32[]{:S(2)}) copy-start(bf16[128,2048]{1,0:T(8,128)(2,1)} %tok_ref.1) | copy-start | bytes 1572868
  29.7 8.4 %collective-permute-start.13 = (bf16[64,2048]{1,0:T(8,128)(2,1)S(1)}, bf16[64,2048]{1,0:T(8,128)(2,1)S(1)}, u32[]{:S(2)}, u32[]{:S(2)}) collective-permute-start(bf16[64,2048]{1,0:T(8,128)(2,1)S(1)} %leave.1), channel_id=1, source_target_pairs={{0,1},{1,0},{2,3},{3,2},{4,5},{5,4},{6,7},{7,6},{8,9},{9,8},{10,11... | collective-permute-start | bytes 786440 | tf_op jit(solution)/shard_map/ppermute | solution.py:579
  31.3 1.3 %collective-permute-start.8 = (bf16[64,640]{1,0:T(8,128)(2,1)S(1)}, bf16[64,640]{1,0:T(8,128)(2,1)S(1)}, u32[]{:S(2)}, u32[]{:S(2)}) collective-permute-start(bf16[64,640]{1,0:T(8,128)(2,1)S(1)} %get-tuple-element.59), channel_id=1, source_target_pairs={{0,2},{2,0},{4,6},{6,4},{8,10},{10,8},{12,14},{14,12},{16,18},{18,... | collective-permute-start | bytes 245768 | tf_op jit(solution)/shard_map/ppermute | solution.py:428
  34.2 1.4 %collective-permute-start.11 = (bf16[4,2,32,256]{3,2,1,0:T(8,128)(2,1)S(1)}, bf16[4,2,32,256]{3,2,1,0:T(8,128)(2,1)S(1)}, u32[]{:S(2)}, u32[]{:S(2)}) collective-permute-start(bf16[4,2,32,256]{3,2,1,0:T(8,128)(2,1)S(1)} %get-tuple-element.77), channel_id=1, source_target_pairs={{0,2},{2,0},{4,6},{6,4},{8,10},{10,8},{12,14},{14,12},{16,18},{18,... | collective-permute-start | bytes 393224 | tf_op jit(solution)/shard_map/ppermute | solution.py:428
  34.4 1.4 %collective-permute-start.12 = (bf16[4,2,32,256]{3,2,1,0:T(8,128)(2,1)S(1)}, bf16[4,2,32,256]{3,2,1,0:T(8,128)(2,1)S(1)}, u32[]{:S(2)}, u32[]{:S(2)}) collective-permute-start(bf16[4,2,32,256]{3,2,1,0:T(8,128)(2,1)S(1)} %get-tuple-element.78), channel_id=1, source_target_pairs={{0,2},{2,0},{4,6},{6,4},{8,10},{10,8},{12,14},{14,12},{16,18},{18,... | collective-permute-start | bytes 393224 | tf_op jit(solution)/shard_map/ppermute | solution.py:428

commit v13 on v12

--- a/solution.py
+++ b/solution.py
@@ -151,8 +151,10 @@
     k_copies = weight_copies(wk_hbm, k_weights, k_sems)
     v_copies = weight_copies(wv_hbm, v_weights, v_sems)
     q_copies = weight_copies(wq_hbm, q_weights, q_sems)
-    for copy in small + k_copies + v_copies + q_copies:
+    for copy in small:
         copy.start()
+    for i, copy in enumerate(k_copies + v_copies + q_copies):
+        copy.start(priority=1 - i % 2)
     rows = tok_ref.shape[0]
     key_width = wk_hbm.shape[1]
     kv_width = kv_hbm.shape[1]

time: 39.1 us -> 39.1 us (level)
  no operation moved by 1% of the time
where the time goes in v13:
time: 39.1 us; the launch traced here: 38.9 us
  starting transfers between devices  14.7 us (38%)
  Pallas kernels  12.5 us (32%)
  waiting for transfers between devices  10 us (26%)
  local copies, waits for them, and re-layouts  0.98 us (3%)
  between operations  0.77 us (2%)
    ppermute x13, starting transfers between devices, swap(): return lax.ppermute(x, 'seq', [(i, i ^ bit) for i in range(n)])  13.1 us
    ppermute x13, waiting for transfers between devices, swap(): return lax.ppermute(x, 'seq', [(i, i ^ bit) for i in range(n)])  9.12 us
    pallas_call x1, Pallas kernels, on_device(): pl.pallas_call(project_kernel, out_shape=(struct((rows, kv_width), bf16),...  4.25 us
    pallas_call x3, Pallas kernels, attend(): pl.pallas_call(functools.partial(attend_kernel, pieces, side), out_shape=...  3 us
    pallas_call x1, Pallas kernels, place_pages(): pl.pallas_call(functools.partial(cache_kernel, pieces), out_shape=(struct...  1.6 us
    ppermute x1, starting transfers between devices, on_device(): lax.ppermute(sent, 'req', [(i, (i + 1) % parts) for i in range(parts)])  1.59 us
    pallas_call x1, Pallas kernels, on_device(): pl.pallas_call(keep_kernel, out_shape=(struct((half, width), f32), struct...  1.44 us
    unnamed x12, local copies, waits for them, and re-layouts  0.98 us
  transfers between devices with their start and end apart: 14, of which 9 were waited for; matrix products, arithmetic and copies ran while one was open for 0% of the time, Pallas kernels for 17%

profile of v13, /device:TPU:0, one launch (start us, length us, event | category | flops | bytes accessed | tf_op | source)
XLA Modules:
  0.0 38.9 jit_solution(5676209232026522154)
XLA Ops:
  0.7 4.3 %project.1 = (bf16[128,512]{1,0:T(8,128)(2,1)}, bf16[128,1024]{1,0:T(8,128)(2,1)}) custom-call(s32[16]{0:T(128)} %block_ref.3, s32[4]{0:T(128)} %len_ref.1, f32[136,128]{1,0:T(8,128)} %constant.2.clone.turn_hbm, bf16[128,2048]{1,0:T(8,128)(2,1)} %tok_ref.1, f32[1,2048]{1,0:T(1,128)} %bitcast.1, bf16[2048,256]{1,0:T(8,128)(2,1)} %wk_hbm.1, ...), custom_call_target="tpu_custom_call" | custom-call | flops 536870912 | bytes 4194304 | tf_op jit(solution)/shard_map/project/pallas_call | solution.py:468
  4.9 3.1 %collective-permute-start.1 = (bf16[128,512]{1,0:T(8,128)(2,1)}, bf16[128,512]{1,0:T(8,128)(2,1)S(1)}, u32[]{:S(2)}, u32[]{:S(2)}) collective-permute-start(bf16[128,512]{1,0:T(8,128)(2,1)} %get-tuple-element.43), channel_id=1, source_target_pairs={{0,8},{2,10},{4,12},{6,14},{8,0},{10,2},{12,4},{14,6},{16,24},{18,... | collective-permute-start | bytes 393224 | tf_op jit(solution)/shard_map/ppermute | solution.py:430
  8.0 2.6 %collective-permute-start = (bf16[128,512]{1,0:T(8,128)(2,1)}, bf16[128,512]{1,0:T(8,128)(2,1)S(1)}, u32[]{:S(2)}, u32[]{:S(2)}) collective-permute-start(bf16[128,512]{1,0:T(8,128)(2,1)} %get-tuple-element.43), channel_id=1, source_target_pairs={{0,16},{2,18},{4,20},{6,22},{8,24},{10,26},{12,28},{14,30},{16,0},... | collective-permute-start | bytes 393224 | tf_op jit(solution)/shard_map/ppermute | solution.py:430
  10.6 1.5 %collective-permute-start.3 = (bf16[128,512]{1,0:T(8,128)(2,1)}, bf16[128,512]{1,0:T(8,128)(2,1)S(1)}, u32[]{:S(2)}, u32[]{:S(2)}) collective-permute-start(bf16[128,512]{1,0:T(8,128)(2,1)} %get-tuple-element.43), channel_id=1, source_target_pairs={{0,4},{2,6},{4,0},{6,2},{8,12},{10,14},{12,8},{14,10},{16,20},{18,... | collective-permute-start | bytes 393224 | tf_op jit(solution)/shard_map/ppermute | solution.py:430
  12.1 0.9 %copy-done.2 = bf16[128,1024]{1,0:T(8,128)(2,1)S(1)} copy-done((bf16[128,1024]{1,0:T(8,128)(2,1)S(1)}, bf16[128,1024]{1,0:T(8,128)(2,1)}, u32[]{:S(2)}) %copy-start.2) | copy-done | bytes 262168
  13.0 0.6 %stage.1 = (bf16[128,512]{1,0:T(8,128)(2,1)S(1)}, bf16[128,512]{1,0:T(8,128)(2,1)S(1)}, s32[16,128]{1,0:T(8,128)S(1)}, s32[256,128]{1,0:T(8,128)S(1)}, s32[256,128]{1,0:T(8,128)S(1)}) custom-call(s32[16]{0:T(128)S(1)} %copy-done.3, s32[4]{0:T(128)S(1)} %copy-done.4, bf16[128,1024]{1,0:T(8,128)(2,1)S(1)} %copy-done.2), custom_call_target="tpu_custom_call" | custom-call | tf_op jit(solution)/shard_map/stage/pallas_call | solution.py:496
  13.7 1.7 %collective-permute-start.2 = (bf16[128,512]{1,0:T(8,128)(2,1)S(1)}, bf16[128,512]{1,0:T(8,128)(2,1)S(1)}, u32[]{:S(2)}, u32[]{:S(2)}) collective-permute-start(bf16[128,512]{1,0:T(8,128)(2,1)S(1)} %collective-permute-done.1.refs_2_), channel_id=1, source_target_pairs={{0,4},{2,6},{4,0},{6,2},{8,12},{10,14},{12,8},{14,10},{16,20},{18,... | collective-permute-start | bytes 393224 | tf_op jit(solution)/shard_map/ppermute | solution.py:430
  15.4 1.6 %collective-permute-done.refs_3_ = bf16[128,512]{1,0:T(8,128)(2,1)S(1)} collective-permute-done((bf16[128,512]{1,0:T(8,128)(2,1)}, bf16[128,512]{1,0:T(8,128)(2,1)S(1)}, u32[]{:S(2)}, u32[]{:S(2)}) %collective-permute-start) | collective-permute-done | bytes 131104 | tf_op jit(solution)/shard_map/ppermute | solution.py:430
  17.4 1.3 %collective-permute-done.2.refs_4_ = bf16[128,512]{1,0:T(8,128)(2,1)S(1)} collective-permute-done((bf16[128,512]{1,0:T(8,128)(2,1)S(1)}, bf16[128,512]{1,0:T(8,128)(2,1)S(1)}, u32[]{:S(2)}, u32[]{:S(2)}) %collective-permute-start.2) | collective-permute-done | bytes 131104 | tf_op jit(solution)/shard_map/ppermute | solution.py:430
  18.7 1.6 %collective-permute-start.5 = (bf16[128,512]{1,0:T(8,128)(2,1)S(1)}, bf16[128,512]{1,0:T(8,128)(2,1)S(1)}, u32[]{:S(2)}, u32[]{:S(2)}) collective-permute-start(bf16[128,512]{1,0:T(8,128)(2,1)S(1)} %collective-permute-done.refs_3_), channel_id=1, source_target_pairs={{0,4},{2,6},{4,0},{6,2},{8,12},{10,14},{12,8},{14,10},{16,20},{18,... | collective-permute-start | bytes 393224 | tf_op jit(solution)/shard_map/ppermute | solution.py:430
  20.3 1.6 %collective-permute-done.4.refs_5_ = bf16[128,512]{1,0:T(8,128)(2,1)S(1)} collective-permute-done((bf16[128,512]{1,0:T(8,128)(2,1)S(1)}, bf16[128,512]{1,0:T(8,128)(2,1)S(1)}, u32[]{:S(2)}, u32[]{:S(2)}) %collective-permute-start.4) | collective-permute-done | bytes 131104 | tf_op jit(solution)/shard_map/ppermute | solution.py:430
  21.9 1.5 %collective-permute-start.6 = (bf16[128,512]{1,0:T(8,128)(2,1)S(1)}, bf16[128,512]{1,0:T(8,128)(2,1)S(1)}, u32[]{:S(2)}, u32[]{:S(2)}) collective-permute-start(bf16[128,512]{1,0:T(8,128)(2,1)S(1)} %collective-permute-done.4.refs_5_), channel_id=1, source_target_pairs={{0,4},{2,6},{4,0},{6,2},{8,12},{10,14},{12,8},{14,10},{16,20},{18,... | collective-permute-start | bytes 393224 | tf_op jit(solution)/shard_map/ppermute | solution.py:430
  23.4 1.6 %attend.3 = (f32[128,512]{1,0:T(8,128)S(1)}, f32[128,128]{1,0:T(8,128)S(1)}, bf16[128,640]{1,0:T(8,128)(2,1)S(1)}) custom-call(s32[16,128]{1,0:T(8,128)S(1)} %get-tuple-element.51.key_pos_ref, s32[256,128]{1,0:T(8,128)S(1)} %get-tuple-element.52.q_pos_ref, s32[256,128]{1,0:T(8,128)S(1)} %get-tuple-element.53.q_begin_ref, ...), custom_call_target="tpu_custom_call" | custom-call | tf_op jit(solution)/shard_map/attend/pallas_call | solution.py:516
  25.1 1.8 %collective-permute-done.6.refs_1_.refs_7_ = bf16[128,512]{1,0:T(8,128)(2,1)S(1)} collective-permute-done((bf16[128,512]{1,0:T(8,128)(2,1)S(1)}, bf16[128,512]{1,0:T(8,128)(2,1)S(1)}, u32[]{:S(2)}, u32[]{:S(2)}) %collective-permute-start.6) | collective-permute-done | bytes 131104 | tf_op jit(solution)/shard_map/ppermute | solution.py:430
  26.9 0.7 %attend.4 = (f32[64,512]{1,0:T(8,128)S(1)}, f32[64,128]{1,0:T(8,128)S(1)}, bf16[64,640]{1,0:T(8,128)(2,1)S(1)}) custom-call(s32[16,128]{1,0:T(8,128)S(1)} %get-tuple-element.51.key_pos_ref, s32[256,128]{1,0:T(8,128)S(1)} %get-tuple-element.52.q_pos_ref, s32[256,128]{1,0:T(8,128)S(1)} %get-tuple-element.53.q_begin_ref, ...), custom_call_target="tpu_custom_call" | custom-call | tf_op jit(solution)/shard_map/attend/pallas_call | solution.py:516
  27.7 0.7 %attend.5 = (f32[64,512]{1,0:T(8,128)S(1)}, f32[64,128]{1,0:T(8,128)S(1)}, bf16[64,640]{1,0:T(8,128)(2,1)S(1)}) custom-call(s32[16,128]{1,0:T(8,128)S(1)} %get-tuple-element.51.key_pos_ref, s32[256,128]{1,0:T(8,128)S(1)} %get-tuple-element.52.q_pos_ref, s32[256,128]{1,0:T(8,128)S(1)} %get-tuple-element.53.q_begin_ref, ...), custom_call_target="tpu_custom_call" | custom-call | tf_op jit(solution)/shard_map/attend/pallas_call | solution.py:516
  28.9 0.8 %leave.1 = bf16[64,2048]{1,0:T(8,128)(2,1)S(1)} custom-call(bf16[512,2048]{1,0:T(8,128)(2,1)S(1)} %copy-done, f32[128,512]{1,0:T(8,128)S(1)} %get-tuple-element.60.refs_0_.refs_2_, f32[128,128]{1,0:T(8,128)S(1)} %get-tuple-element.61.refs_1_.refs_3_, bf16[128,640]{1,0:T(8,128)(2,1)S(1)} %collective-permute-done.9.refs_2_.refs_4_, ...), custom_call_target="tpu_custom_call" | custom-call | tf_op jit(solution)/shard_map/leave/pallas_call | solution.py:572
  29.7 1.6 %collective-permute-start.13 = (bf16[64,2048]{1,0:T(8,128)(2,1)S(1)}, bf16[64,2048]{1,0:T(8,128)(2,1)S(1)}, u32[]{:S(2)}, u32[]{:S(2)}) collective-permute-start(bf16[64,2048]{1,0:T(8,128)(2,1)S(1)} %leave.1), channel_id=1, source_target_pairs={{0,1},{1,0},{2,3},{3,2},{4,5},{5,4},{6,7},{7,6},{8,9},{9,8},{10,11... | collective-permute-start | bytes 786440 | tf_op jit(solution)/shard_map/ppermute | solution.py:581
  31.3 1.3 %collective-permute-done.8.refs_7_ = bf16[64,640]{1,0:T(8,128)(2,1)S(1)} collective-permute-done((bf16[64,640]{1,0:T(8,128)(2,1)S(1)}, bf16[64,640]{1,0:T(8,128)(2,1)S(1)}, u32[]{:S(2)}, u32[]{:S(2)}) %collective-permute-start.8) | collective-permute-done | bytes 81952 | tf_op jit(solution)/shard_map/ppermute | solution.py:430
  32.6 1.6 %cache.1 = (bf16[8,2,32,256]{3,2,1,0:T(8,128)(2,1)S(1)}, bf16[4,2,32,256]{3,2,1,0:T(8,128)(2,1)S(1)}, bf16[4,2,32,256]{3,2,1,0:T(8,128)(2,1)S(1)}) custom-call(s32[16]{0:T(128)S(1)} %copy-done.3, s32[64]{0:T(128)S(1)} %copy-done.5, bf16[128,512]{1,0:T(8,128)(2,1)S(1)} %get-tuple-element.68.refs_0_, bf16[128,512]{1,0:T(8,128)(2,1)S(1)} %collective-permute-done.3.refs_1_, ...), custom_call_target="tpu_custom_call" | custom-call | tf_op jit(solution)/shard_map/cache/pallas_call | solution.py:534
  34.8 0.8 %collective-permute-done.11.refs_0_ = bf16[4,2,32,256]{3,2,1,0:T(8,128)(2,1)S(1)} collective-permute-done((bf16[4,2,32,256]{3,2,1,0:T(8,128)(2,1)S(1)}, bf16[4,2,32,256]{3,2,1,0:T(8,128)(2,1)S(1)}, u32[]{:S(2)}, u32[]{:S(2)}) %collective-permute-start.11) | collective-permute-done | bytes 131104 | tf_op jit(solution)/shard_map/ppermute | solution.py:430
  35.8 1.4 %keep.1 = (f32[64,2048]{1,0:T(8,128)S(1)}, bf16[8,2,32,256]{3,2,1,0:T(8,128)(2,1)}) custom-call(bf16[512,2048]{1,0:T(8,128)(2,1)S(1)} %copy-done, bf16[128,2048]{1,0:T(8,128)(2,1)S(1)} %copy-done.1, bf16[8,2,32,256]{3,2,1,0:T(8,128)(2,1)S(1)} %get-tuple-element.76.mine_ref, bf16[4,2,32,256]{3,2,1,0:T(8,128)(2,1)S(1)} %collective-permute-done.11.refs_0_, ...), custom_call_target="tpu_custom_call" | custom-call | tf_op jit(solution)/shard_map/keep/pallas_call | solution.py:585
  37.3 0.9 %collective-permute-done.13.received_ref = bf16[64,2048]{1,0:T(8,128)(2,1)S(1)} collective-permute-done((bf16[64,2048]{1,0:T(8,128)(2,1)S(1)}, bf16[64,2048]{1,0:T(8,128)(2,1)S(1)}, u32[]{:S(2)}, u32[]{:S(2)}) %collective-permute-start.13) | collective-permute-done | bytes 262176 | tf_op jit(solution)/shard_map/ppermute | solution.py:581
  38.2 0.8 %finish.1 = bf16[64,2048]{1,0:T(8,128)(2,1)} custom-call(f32[64,2048]{1,0:T(8,128)S(1)} %get-tuple-element.82.kept_ref, bf16[64,2048]{1,0:T(8,128)(2,1)S(1)} %collective-permute-done.13.received_ref), custom_call_target="tpu_custom_call" | custom-call | tf_op jit(solution)/shard_map/finish/pallas_call | solution.py:594
  (25 shorter events, 1.9 us)
Async XLA Ops:
  0.6 11.5 %copy-start.3 = (s32[16]{0:T(128)S(1)}, s32[16]{0:T(128)}, u32[]{:S(2)}) copy-start(s32[16]{0:T(128)} %block_ref.3) | copy-start | bytes 196
  0.6 11.5 %copy-start.4 = (s32[4]{0:T(128)S(1)}, s32[4]{0:T(128)}, u32[]{:S(2)}) copy-start(s32[4]{0:T(128)} %len_ref.1) | copy-start | bytes 52
  4.9 24.0 %copy-start = (bf16[512,2048]{1,0:T(8,128)(2,1)S(1)}, bf16[512,2048]{1,0:T(8,128)(2,1)}, u32[]{:S(2)}) copy-start(bf16[512,2048]{1,0:T(8,128)(2,1)} %wo_ref.3) | copy-start | bytes 6291460
  4.9 8.7 %collective-permute-start.1 = (bf16[128,512]{1,0:T(8,128)(2,1)}, bf16[128,512]{1,0:T(8,128)(2,1)S(1)}, u32[]{:S(2)}, u32[]{:S(2)}) collective-permute-start(bf16[128,512]{1,0:T(8,128)(2,1)} %get-tuple-element.43), channel_id=1, source_target_pairs={{0,8},{2,10},{4,12},{6,14},{8,0},{10,2},{12,4},{14,6},{16,24},{18,... | collective-permute-start | bytes 393224 | tf_op jit(solution)/shard_map/ppermute | solution.py:430
  8.0 8.9 %collective-permute-start = (bf16[128,512]{1,0:T(8,128)(2,1)}, bf16[128,512]{1,0:T(8,128)(2,1)S(1)}, u32[]{:S(2)}, u32[]{:S(2)}) collective-permute-start(bf16[128,512]{1,0:T(8,128)(2,1)} %get-tuple-element.43), channel_id=1, source_target_pairs={{0,16},{2,18},{4,20},{6,22},{8,24},{10,26},{12,28},{14,30},{16,0},... | collective-permute-start | bytes 393224 | tf_op jit(solution)/shard_map/ppermute | solution.py:430
  10.6 6.8 %collective-permute-start.3 = (bf16[128,512]{1,0:T(8,128)(2,1)}, bf16[128,512]{1,0:T(8,128)(2,1)S(1)}, u32[]{:S(2)}, u32[]{:S(2)}) collective-permute-start(bf16[128,512]{1,0:T(8,128)(2,1)} %get-tuple-element.43), channel_id=1, source_target_pairs={{0,4},{2,6},{4,0},{6,2},{8,12},{10,14},{12,8},{14,10},{16,20},{18,... | collective-permute-start | bytes 393224 | tf_op jit(solution)/shard_map/ppermute | solution.py:430
  12.1 1.0 %copy-start.2 = (bf16[128,1024]{1,0:T(8,128)(2,1)S(1)}, bf16[128,1024]{1,0:T(8,128)(2,1)}, u32[]{:S(2)}) copy-start(bf16[128,1024]{1,0:T(8,128)(2,1)} %get-tuple-element.44.both_ref) | copy-start | bytes 786436
  13.7 5.0 %collective-permute-start.2 = (bf16[128,512]{1,0:T(8,128)(2,1)S(1)}, bf16[128,512]{1,0:T(8,128)(2,1)S(1)}, u32[]{:S(2)}, u32[]{:S(2)}) collective-permute-start(bf16[128,512]{1,0:T(8,128)(2,1)S(1)} %collective-permute-done.1.refs_2_), channel_id=1, source_target_pairs={{0,4},{2,6},{4,0},{6,2},{8,12},{10,14},{12,8},{14,10},{16,20},{18,... | collective-permute-start | bytes 393224 | tf_op jit(solution)/shard_map/ppermute | solution.py:430
  16.9 5.0 %collective-permute-start.4 = (bf16[128,512]{1,0:T(8,128)(2,1)S(1)}, bf16[128,512]{1,0:T(8,128)(2,1)S(1)}, u32[]{:S(2)}, u32[]{:S(2)}) collective-permute-start(bf16[128,512]{1,0:T(8,128)(2,1)S(1)} %collective-permute-done.refs_3_), channel_id=1, source_target_pairs={{0,8},{2,10},{4,12},{6,14},{8,0},{10,2},{12,4},{14,6},{16,24},{18,... | collective-permute-start | bytes 393224 | tf_op jit(solution)/shard_map/ppermute | solution.py:430
  17.4 6.0 %collective-permute-start.7 = (bf16[128,512]{1,0:T(8,128)(2,1)S(1)}, bf16[128,512]{1,0:T(8,128)(2,1)S(1)}, u32[]{:S(2)}, u32[]{:S(2)}) collective-permute-start(bf16[128,512]{1,0:T(8,128)(2,1)S(1)} %get-tuple-element.58.q_ref), channel_id=1, source_target_pairs={{0,2},{2,0},{4,6},{6,4},{8,10},{10,8},{12,14},{14,12},{16,18},{18,... | collective-permute-start | bytes 393224 | tf_op jit(solution)/shard_map/ppermute | solution.py:430
  18.7 6.4 %collective-permute-start.5 = (bf16[128,512]{1,0:T(8,128)(2,1)S(1)}, bf16[128,512]{1,0:T(8,128)(2,1)S(1)}, u32[]{:S(2)}, u32[]{:S(2)}) collective-permute-start(bf16[128,512]{1,0:T(8,128)(2,1)S(1)} %collective-permute-done.refs_3_), channel_id=1, source_target_pairs={{0,4},{2,6},{4,0},{6,2},{8,12},{10,14},{12,8},{14,10},{16,20},{18,... | collective-permute-start | bytes 393224 | tf_op jit(solution)/shard_map/ppermute | solution.py:430
  21.9 5.0 %collective-permute-start.6 = (bf16[128,512]{1,0:T(8,128)(2,1)S(1)}, bf16[128,512]{1,0:T(8,128)(2,1)S(1)}, u32[]{:S(2)}, u32[]{:S(2)}) collective-permute-start(bf16[128,512]{1,0:T(8,128)(2,1)S(1)} %collective-permute-done.4.refs_5_), channel_id=1, source_target_pairs={{0,4},{2,6},{4,0},{6,2},{8,12},{10,14},{12,8},{14,10},{16,20},{18,... | collective-permute-start | bytes 393224 | tf_op jit(solution)/shard_map/ppermute | solution.py:430
  25.0 3.4 %collective-permute-start.9 = (bf16[128,640]{1,0:T(8,128)(2,1)S(1)}, bf16[128,640]{1,0:T(8,128)(2,1)S(1)}, u32[]{:S(2)}, u32[]{:S(2)}) collective-permute-start(bf16[128,640]{1,0:T(8,128)(2,1)S(1)} %get-tuple-element.62), channel_id=1, source_target_pairs={{0,2},{2,0},{4,6},{6,4},{8,10},{10,8},{12,14},{14,12},{16,18},{18,... | collective-permute-start | bytes 491528 | tf_op jit(solution)/shard_map/ppermute | solution.py:430
  27.6 5.0 %copy-start.5 = (s32[64]{0:T(128)S(1)}, s32[64]{0:T(128)}, u32[]{:S(2)}) copy-start(s32[64]{0:T(128)} %slot_ref.1) | copy-start | bytes 772
  27.6 1.3 %collective-permute-start.10 = (bf16[64,640]{1,0:T(8,128)(2,1)S(1)}, bf16[64,640]{1,0:T(8,128)(2,1)S(1)}, u32[]{:S(2)}, u32[]{:S(2)}) collective-permute-start(bf16[64,640]{1,0:T(8,128)(2,1)S(1)} %get-tuple-element.67), channel_id=1, source_target_pairs={{0,2},{2,0},{4,6},{6,4},{8,10},{10,8},{12,14},{14,12},{16,18},{18,... | collective-permute-start | bytes 245768 | tf_op jit(solution)/shard_map/ppermute | solution.py:430
  28.4 7.5 %copy-start.1 = (bf16[128,2048]{1,0:T(8,128)(2,1)S(1)}, bf16[128,2048]{1,0:T(8,128)(2,1)}, u32[]{:S(2)}) copy-start(bf16[128,2048]{1,0:T(8,128)(2,1)} %tok_ref.1) | copy-start | bytes 1572868
  29.7 8.4 %collective-permute-start.13 = (bf16[64,2048]{1,0:T(8,128)(2,1)S(1)}, bf16[64,2048]{1,0:T(8,128)(2,1)S(1)}, u32[]{:S(2)}, u32[]{:S(2)}) collective-permute-start(bf16[64,2048]{1,0:T(8,128)(2,1)S(1)} %leave.1), channel_id=1, source_target_pairs={{0,1},{1,0},{2,3},{3,2},{4,5},{5,4},{6,7},{7,6},{8,9},{9,8},{10,11... | collective-permute-start | bytes 786440 | tf_op jit(solution)/shard_map/ppermute | solution.py:581
  31.3 1.3 %collective-permute-start.8 = (bf16[64,640]{1,0:T(8,128)(2,1)S(1)}, bf16[64,640]{1,0:T(8,128)(2,1)S(1)}, u32[]{:S(2)}, u32[]{:S(2)}) collective-permute-start(bf16[64,640]{1,0:T(8,128)(2,1)S(1)} %get-tuple-element.59), channel_id=1, source_target_pairs={{0,2},{2,0},{4,6},{6,4},{8,10},{10,8},{12,14},{14,12},{16,18},{18,... | collective-permute-start | bytes 245768 | tf_op jit(solution)/shard_map/ppermute | solution.py:430
  34.2 1.4 %collective-permute-start.11 = (bf16[4,2,32,256]{3,2,1,0:T(8,128)(2,1)S(1)}, bf16[4,2,32,256]{3,2,1,0:T(8,128)(2,1)S(1)}, u32[]{:S(2)}, u32[]{:S(2)}) collective-permute-start(bf16[4,2,32,256]{3,2,1,0:T(8,128)(2,1)S(1)} %get-tuple-element.77), channel_id=1, source_target_pairs={{0,2},{2,0},{4,6},{6,4},{8,10},{10,8},{12,14},{14,12},{16,18},{18,... | collective-permute-start | bytes 393224 | tf_op jit(solution)/shard_map/ppermute | solution.py:430
  34.4 1.4 %collective-permute-start.12 = (bf16[4,2,32,256]{3,2,1,0:T(8,128)(2,1)S(1)}, bf16[4,2,32,256]{3,2,1,0:T(8,128)(2,1)S(1)}, u32[]{:S(2)}, u32[]{:S(2)}) collective-permute-start(bf16[4,2,32,256]{3,2,1,0:T(8,128)(2,1)S(1)} %get-tuple-element.78), channel_id=1, source_target_pairs={{0,2},{2,0},{4,6},{6,4},{8,10},{10,8},{12,14},{14,12},{16,18},{18,... | collective-permute-start | bytes 393224 | tf_op jit(solution)/shard_map/ppermute | solution.py:430

commit v14 on v13

--- a/solution.py
+++ b/solution.py
@@ -55,15 +55,6 @@
 def blocks_of(block_ref, shard):
     first = block_ref[shard]
     return first, 2 * block_ref.shape[0] - 1 - first
-
-
-def prompt_begin(position, len_ref):
-    begin = jnp.zeros_like(position)
-    start = jnp.int32(0)
-    for r in range(len_ref.shape[0] - 1):
-        start = start + len_ref[r]
-        begin = jnp.where(position >= start, start, begin)
-    return begin
 
 
 def positions(blocks, half, dim, shape):
@@ -302,17 +293,33 @@
     kv_out[...] = both_ref[:, : kv_out.shape[1]]
     q_out[...] = both_ref[:, kv_out.shape[1] :]
     shards, rows = key_pos_ref.shape
+    half = rows // 2
     shard = lax.axis_index("seq")
 
-    def lay(s, carry):
-        key_pos_ref[pl.ds(s, 1), :] = positions(blocks_of(block_ref, s), rows // 2, 1, (1, rows))
-        return carry
-
-    lax.fori_loop(0, shards, lay, 0, unroll=shards <= 16)
-    blocks = [block for s in (shard, shard ^ 1) for block in blocks_of(block_ref, s)]
-    q_pos = positions(blocks, rows // 2, 0, q_pos_ref.shape)
+    def picked(values, mask):
+        return jnp.sum(jnp.where(mask, values, 0.0), -1, keepdims=True).astype(jnp.int32)
+
+    def lanes(shape):
+        return lax.broadcasted_iota(jnp.int32, shape, 1)
+
+    blocks = block_ref[...].astype(f32)
+    square = (shards, shards)
+    first = picked(blocks, lanes(square) == lax.broadcasted_iota(jnp.int32, square, 0))
+    index = lanes((shards, rows))
+    key_pos_ref[...] = index + jnp.where(index < half, first, 2 * shards - 2 - first) * half
+
+    held = []
+    for s in (shard, shard ^ 1):
+        first = picked(blocks, lanes(block_ref.shape) == s)
+        held += [first, 2 * shards - 1 - first]
+    q_pos = positions(held, half, 0, q_pos_ref.shape)
     q_pos_ref[...] = q_pos
-    q_begin_ref[...] = prompt_begin(q_pos, len_ref)
+    lengths = len_ref[...].astype(f32)
+    begin = jnp.zeros_like(q_pos)
+    for r in range(1, len_ref.shape[1]):
+        start = picked(lengths, lanes(len_ref.shape) < r)
+        begin = jnp.where(q_pos >= start, start, begin)
+    q_begin_ref[...] = begin
 
 
 def joined_rows(partials, first, half):
@@ -502,12 +509,12 @@
             struct((2 * rows, HEAD), jnp.int32),
             struct((2 * rows, HEAD), jnp.int32),
         ),
-        in_specs=in_smem(2) + in_vmem(1),
+        in_specs=in_vmem(3),
         out_specs=tuple(in_vmem(5)),
         compiler_params=kernel_params(24),
         cost_estimate=cost(0, 0),
         name="stage",
-    )(block_split, lengths, both)
+    )(block_split.reshape(1, n), lengths.reshape(1, -1), both)
     far_queries = swap(queries, n, 1)
 
     def attend(pieces, side=None):
@@ -554,11 +561,12 @@
         own = own.moved([staged])
         third = swapped(second, 4)
         (second, first_across, beside), _ = tied_all([second, first_across, beside], ())
-        partials = attend([own, beside, first, second, first_across, third])
+        second_across = swapped(second, 2)
+        partials = attend([own, beside, first, second, first_across, third, second_across])
         partials[2] = swap(partials[2], n, 1)
         queries, partials[1] = lax.optimization_barrier((queries, partials[1]))
-        remaining = [swapped(second, 2), swapped(third, 2)]
-        placed = [own, beside, first, second, first_across, third] + remaining
+        remaining = [swapped(third, 2)]
+        placed = [own, beside, first, second, first_across, third, second_across] + remaining
     else:
         same = [list(range(c, n, 2)) for c in range(2)]
         gathered = lax.all_gather(kv, "seq", axis=0, tiled=True, axis_index_groups=same)

time: 39.1 us -> 39.1 us (level)
  starting transfers between devices: 14.7 us -> 15.3 us
  Pallas kernels: 12.5 us -> 12.1 us
    ppermute x13, starting transfers between devices: 13.1 us -> 13.8 us  [swap(): return lax.ppermute(x, 'seq', [(i, i ^ bit) for i in range(n)])]
    pallas_call x1, Pallas kernels: 0.61 us -> 0.13 us  [on_device(): pl.pallas_call(stage_kernel, out_shape=(struct((rows, kv_width), bf16), s...]
  transfers between devices with their start and end apart: 14 -> 14, of which waited for: 9 -> 11; matrix products, arithmetic and copies ran while one was open for 0% -> 0% of each run, Pallas kernels for 17% -> 16%
where the time goes in v14:
time: 39.1 us; the launch traced here: 39 us
  starting transfers between devices  15.3 us (39%)
  Pallas kernels  12.1 us (31%)
  waiting for transfers between devices  9.84 us (25%)
  local copies, waits for them, and re-layouts  0.98 us (3%)
  between operations  0.73 us (2%)
    ppermute x13, starting transfers between devices, swap(): return lax.ppermute(x, 'seq', [(i, i ^ bit) for i in range(n)])  13.8 us
    ppermute x13, waiting for transfers between devices, swap(): return lax.ppermute(x, 'seq', [(i, i ^ bit) for i in range(n)])  8.8 us
    pallas_call x1, Pallas kernels, on_device(): pl.pallas_call(project_kernel, out_shape=(struct((rows, kv_width), bf16),...  4.25 us
    pallas_call x3, Pallas kernels, attend(): pl.pallas_call(functools.partial(attend_kernel, pieces, side), out_shape=...  3.11 us
    pallas_call x1, Pallas kernels, place_pages(): pl.pallas_call(functools.partial(cache_kernel, pieces), out_shape=(struct...  1.6 us
    ppermute x1, starting transfers between devices, on_device(): lax.ppermute(sent, 'req', [(i, (i + 1) % parts) for i in range(parts)])  1.59 us
    pallas_call x1, Pallas kernels, on_device(): pl.pallas_call(keep_kernel, out_shape=(struct((half, width), f32), struct...  1.44 us
    ppermute x1, waiting for transfers between devices, on_device(): lax.ppermute(sent, 'req', [(i, (i + 1) % parts) for i in range(parts)])  1.03 us
  transfers between devices with their start and end apart: 14, of which 11 were waited for; matrix products, arithmetic and copies ran while one was open for 0% of the time, Pallas kernels for 16%

profile of v14, /device:TPU:0, one launch (start us, length us, event | category | flops | bytes accessed | tf_op | source)
XLA Modules:
  0.0 39.0 jit_solution(10569224335165054167)
XLA Ops:
  0.7 4.3 %project.1 = (bf16[128,512]{1,0:T(8,128)(2,1)}, bf16[128,1024]{1,0:T(8,128)(2,1)}) custom-call(s32[16]{0:T(128)} %block_ref.1, s32[4]{0:T(128)} %len_hbm.1, f32[136,128]{1,0:T(8,128)} %constant.2.clone.turn_hbm, bf16[128,2048]{1,0:T(8,128)(2,1)} %tok_ref.1, f32[1,2048]{1,0:T(1,128)} %bitcast.5, bf16[2048,256]{1,0:T(8,128)(2,1)} %wk_hbm.1, ...), custom_call_target="tpu_custom_call" | custom-call | flops 536870912 | bytes 4194304 | tf_op jit(solution)/shard_map/project/pallas_call | solution.py:475
  4.9 3.1 %collective-permute-start.1 = (bf16[128,512]{1,0:T(8,128)(2,1)}, bf16[128,512]{1,0:T(8,128)(2,1)S(1)}, u32[]{:S(2)}, u32[]{:S(2)}) collective-permute-start(bf16[128,512]{1,0:T(8,128)(2,1)} %get-tuple-element.43), channel_id=1, source_target_pairs={{0,8},{2,10},{4,12},{6,14},{8,0},{10,2},{12,4},{14,6},{16,24},{18,... | collective-permute-start | bytes 393224 | tf_op jit(solution)/shard_map/ppermute | solution.py:437
  8.0 2.6 %collective-permute-start = (bf16[128,512]{1,0:T(8,128)(2,1)}, bf16[128,512]{1,0:T(8,128)(2,1)S(1)}, u32[]{:S(2)}, u32[]{:S(2)}) collective-permute-start(bf16[128,512]{1,0:T(8,128)(2,1)} %get-tuple-element.43), channel_id=1, source_target_pairs={{0,16},{2,18},{4,20},{6,22},{8,24},{10,26},{12,28},{14,30},{16,0},... | collective-permute-start | bytes 393224 | tf_op jit(solution)/shard_map/ppermute | solution.py:437
  10.6 1.5 %collective-permute-start.3 = (bf16[128,512]{1,0:T(8,128)(2,1)}, bf16[128,512]{1,0:T(8,128)(2,1)S(1)}, u32[]{:S(2)}, u32[]{:S(2)}) collective-permute-start(bf16[128,512]{1,0:T(8,128)(2,1)} %get-tuple-element.43), channel_id=1, source_target_pairs={{0,4},{2,6},{4,0},{6,2},{8,12},{10,14},{12,8},{14,10},{16,20},{18,... | collective-permute-start | bytes 393224 | tf_op jit(solution)/shard_map/ppermute | solution.py:437
  12.1 1.4 %collective-permute-done.1.refs_2_ = bf16[128,512]{1,0:T(8,128)(2,1)S(1)} collective-permute-done((bf16[128,512]{1,0:T(8,128)(2,1)}, bf16[128,512]{1,0:T(8,128)(2,1)S(1)}, u32[]{:S(2)}, u32[]{:S(2)}) %collective-permute-start.1) | collective-permute-done | bytes 131104 | tf_op jit(solution)/shard_map/ppermute | solution.py:437
  13.5 1.8 %collective-permute-start.2 = (bf16[128,512]{1,0:T(8,128)(2,1)S(1)}, bf16[128,512]{1,0:T(8,128)(2,1)S(1)}, u32[]{:S(2)}, u32[]{:S(2)}) collective-permute-start(bf16[128,512]{1,0:T(8,128)(2,1)S(1)} %collective-permute-done.1.refs_2_), channel_id=1, source_target_pairs={{0,4},{2,6},{4,0},{6,2},{8,12},{10,14},{12,8},{14,10},{16,20},{18,... | collective-permute-start | bytes 393224 | tf_op jit(solution)/shard_map/ppermute | solution.py:437
  15.4 0.9 %copy-done.2 = bf16[128,1024]{1,0:T(8,128)(2,1)S(1)} copy-done((bf16[128,1024]{1,0:T(8,128)(2,1)S(1)}, bf16[128,1024]{1,0:T(8,128)(2,1)}, u32[]{:S(2)}) %copy-start.2) | copy-done | bytes 262168
  16.4 0.5 %collective-permute-done.refs_3_ = bf16[128,512]{1,0:T(8,128)(2,1)S(1)} collective-permute-done((bf16[128,512]{1,0:T(8,128)(2,1)}, bf16[128,512]{1,0:T(8,128)(2,1)S(1)}, u32[]{:S(2)}, u32[]{:S(2)}) %collective-permute-start) | collective-permute-done | bytes 131104 | tf_op jit(solution)/shard_map/ppermute | solution.py:437
  17.4 1.1 %collective-permute-done.2.refs_4_ = bf16[128,512]{1,0:T(8,128)(2,1)S(1)} collective-permute-done((bf16[128,512]{1,0:T(8,128)(2,1)S(1)}, bf16[128,512]{1,0:T(8,128)(2,1)S(1)}, u32[]{:S(2)}, u32[]{:S(2)}) %collective-permute-start.2) | collective-permute-done | bytes 131104 | tf_op jit(solution)/shard_map/ppermute | solution.py:437
  18.5 1.8 %collective-permute-start.5 = (bf16[128,512]{1,0:T(8,128)(2,1)S(1)}, bf16[128,512]{1,0:T(8,128)(2,1)S(1)}, u32[]{:S(2)}, u32[]{:S(2)}) collective-permute-start(bf16[128,512]{1,0:T(8,128)(2,1)S(1)} %collective-permute-done.refs_3_), channel_id=1, source_target_pairs={{0,4},{2,6},{4,0},{6,2},{8,12},{10,14},{12,8},{14,10},{16,20},{18,... | collective-permute-start | bytes 393224 | tf_op jit(solution)/shard_map/ppermute | solution.py:437
  20.3 1.6 %collective-permute-done.4.refs_5_ = bf16[128,512]{1,0:T(8,128)(2,1)S(1)} collective-permute-done((bf16[128,512]{1,0:T(8,128)(2,1)S(1)}, bf16[128,512]{1,0:T(8,128)(2,1)S(1)}, u32[]{:S(2)}, u32[]{:S(2)}) %collective-permute-start.4) | collective-permute-done | bytes 131104 | tf_op jit(solution)/shard_map/ppermute | solution.py:437
  21.9 1.5 %collective-permute-start.6 = (bf16[128,512]{1,0:T(8,128)(2,1)S(1)}, bf16[128,512]{1,0:T(8,128)(2,1)S(1)}, u32[]{:S(2)}, u32[]{:S(2)}) collective-permute-start(bf16[128,512]{1,0:T(8,128)(2,1)S(1)} %collective-permute-done.4.refs_5_), channel_id=1, source_target_pairs={{0,4},{2,6},{4,0},{6,2},{8,12},{10,14},{12,8},{14,10},{16,20},{18,... | collective-permute-start | bytes 393224 | tf_op jit(solution)/shard_map/ppermute | solution.py:437
  23.4 1.3 %collective-permute-done.5.refs_6_ = bf16[128,512]{1,0:T(8,128)(2,1)S(1)} collective-permute-done((bf16[128,512]{1,0:T(8,128)(2,1)S(1)}, bf16[128,512]{1,0:T(8,128)(2,1)S(1)}, u32[]{:S(2)}, u32[]{:S(2)}) %collective-permute-start.5) | collective-permute-done | bytes 131104 | tf_op jit(solution)/shard_map/ppermute | solution.py:437
  24.7 1.9 %attend.3 = (f32[128,512]{1,0:T(8,128)S(1)}, f32[128,128]{1,0:T(8,128)S(1)}, bf16[128,640]{1,0:T(8,128)(2,1)S(1)}) custom-call(s32[16,128]{1,0:T(8,128)S(1)} %get-tuple-element.51.key_pos_ref, s32[256,128]{1,0:T(8,128)S(1)} %get-tuple-element.52.q_pos_ref, s32[256,128]{1,0:T(8,128)S(1)} %get-tuple-element.53.q_begin_ref, ...), custom_call_target="tpu_custom_call" | custom-call | tf_op jit(solution)/shard_map/attend/pallas_call | solution.py:523
  26.9 0.6 %attend.4 = (f32[64,512]{1,0:T(8,128)S(1)}, f32[64,128]{1,0:T(8,128)S(1)}, bf16[64,640]{1,0:T(8,128)(2,1)S(1)}) custom-call(s32[16,128]{1,0:T(8,128)S(1)} %get-tuple-element.51.key_pos_ref, s32[256,128]{1,0:T(8,128)S(1)} %get-tuple-element.52.q_pos_ref, s32[256,128]{1,0:T(8,128)S(1)} %get-tuple-element.53.q_begin_ref, ...), custom_call_target="tpu_custom_call" | custom-call | tf_op jit(solution)/shard_map/attend/pallas_call | solution.py:523
  27.9 0.6 %attend.5 = (f32[64,512]{1,0:T(8,128)S(1)}, f32[64,128]{1,0:T(8,128)S(1)}, bf16[64,640]{1,0:T(8,128)(2,1)S(1)}) custom-call(s32[16,128]{1,0:T(8,128)S(1)} %get-tuple-element.51.key_pos_ref, s32[256,128]{1,0:T(8,128)S(1)} %get-tuple-element.52.q_pos_ref, s32[256,128]{1,0:T(8,128)S(1)} %get-tuple-element.53.q_begin_ref, ...), custom_call_target="tpu_custom_call" | custom-call | tf_op jit(solution)/shard_map/attend/pallas_call | solution.py:523
  28.9 0.8 %leave.1 = bf16[64,2048]{1,0:T(8,128)(2,1)S(1)} custom-call(bf16[512,2048]{1,0:T(8,128)(2,1)S(1)} %copy-done, f32[128,512]{1,0:T(8,128)S(1)} %get-tuple-element.60.refs_0_.refs_2_, f32[128,128]{1,0:T(8,128)S(1)} %get-tuple-element.61.refs_1_.refs_3_, bf16[128,640]{1,0:T(8,128)(2,1)S(1)} %collective-permute-done.9.refs_2_.refs_4_, ...), custom_call_target="tpu_custom_call" | custom-call | tf_op jit(solution)/shard_map/leave/pallas_call | solution.py:580
  29.7 1.6 %collective-permute-start.13 = (bf16[64,2048]{1,0:T(8,128)(2,1)S(1)}, bf16[64,2048]{1,0:T(8,128)(2,1)S(1)}, u32[]{:S(2)}, u32[]{:S(2)}) collective-permute-start(bf16[64,2048]{1,0:T(8,128)(2,1)S(1)} %leave.1), channel_id=1, source_target_pairs={{0,1},{1,0},{2,3},{3,2},{4,5},{5,4},{6,7},{7,6},{8,9},{9,8},{10,11... | collective-permute-start | bytes 786440 | tf_op jit(solution)/shard_map/ppermute | solution.py:589
  31.3 1.3 %collective-permute-done.8.refs_7_ = bf16[64,640]{1,0:T(8,128)(2,1)S(1)} collective-permute-done((bf16[64,640]{1,0:T(8,128)(2,1)S(1)}, bf16[64,640]{1,0:T(8,128)(2,1)S(1)}, u32[]{:S(2)}, u32[]{:S(2)}) %collective-permute-start.8) | collective-permute-done | bytes 81952 | tf_op jit(solution)/shard_map/ppermute | solution.py:437
  32.5 1.6 %cache.1 = (bf16[8,2,32,256]{3,2,1,0:T(8,128)(2,1)S(1)}, bf16[4,2,32,256]{3,2,1,0:T(8,128)(2,1)S(1)}, bf16[4,2,32,256]{3,2,1,0:T(8,128)(2,1)S(1)}) custom-call(s32[16]{0:T(128)S(1)} %copy-done.3, s32[64]{0:T(128)S(1)} %copy-done.5, bf16[128,512]{1,0:T(8,128)(2,1)S(1)} %get-tuple-element.68.refs_0_, bf16[128,512]{1,0:T(8,128)(2,1)S(1)} %collective-permute-done.3.refs_1_, ...), custom_call_target="tpu_custom_call" | custom-call | tf_op jit(solution)/shard_map/cache/pallas_call | solution.py:541
  34.7 0.8 %collective-permute-done.11.refs_0_ = bf16[4,2,32,256]{3,2,1,0:T(8,128)(2,1)S(1)} collective-permute-done((bf16[4,2,32,256]{3,2,1,0:T(8,128)(2,1)S(1)}, bf16[4,2,32,256]{3,2,1,0:T(8,128)(2,1)S(1)}, u32[]{:S(2)}, u32[]{:S(2)}) %collective-permute-start.11) | collective-permute-done | bytes 131104 | tf_op jit(solution)/shard_map/ppermute | solution.py:437
  35.7 1.4 %keep.1 = (f32[64,2048]{1,0:T(8,128)S(1)}, bf16[8,2,32,256]{3,2,1,0:T(8,128)(2,1)}) custom-call(bf16[512,2048]{1,0:T(8,128)(2,1)S(1)} %copy-done, bf16[128,2048]{1,0:T(8,128)(2,1)S(1)} %copy-done.1, bf16[8,2,32,256]{3,2,1,0:T(8,128)(2,1)S(1)} %get-tuple-element.76.mine_ref, bf16[4,2,32,256]{3,2,1,0:T(8,128)(2,1)S(1)} %collective-permute-done.11.refs_0_, ...), custom_call_target="tpu_custom_call" | custom-call | tf_op jit(solution)/shard_map/keep/pallas_call | solution.py:593
  37.2 1.0 %collective-permute-done.13.received_ref = bf16[64,2048]{1,0:T(8,128)(2,1)S(1)} collective-permute-done((bf16[64,2048]{1,0:T(8,128)(2,1)S(1)}, bf16[64,2048]{1,0:T(8,128)(2,1)S(1)}, u32[]{:S(2)}, u32[]{:S(2)}) %collective-permute-start.13) | collective-permute-done | bytes 262176 | tf_op jit(solution)/shard_map/ppermute | solution.py:589
  38.2 0.8 %finish.1 = bf16[64,2048]{1,0:T(8,128)(2,1)} custom-call(f32[64,2048]{1,0:T(8,128)S(1)} %get-tuple-element.82.kept_ref, bf16[64,2048]{1,0:T(8,128)(2,1)S(1)} %collective-permute-done.13.received_ref), custom_call_target="tpu_custom_call" | custom-call | tf_op jit(solution)/shard_map/finish/pallas_call | solution.py:602
  (25 shorter events, 2.4 us)
Async XLA Ops:
  0.6 14.7 %copy-start.3 = (s32[16]{0:T(128)S(1)}, s32[16]{0:T(128)}, u32[]{:S(2)}) copy-start(s32[16]{0:T(128)} %block_ref.1) | copy-start | bytes 196
  0.6 14.7 %copy-start.4 = (s32[4]{0:T(128)S(1)}, s32[4]{0:T(128)}, u32[]{:S(2)}) copy-start(s32[4]{0:T(128)} %len_hbm.1) | copy-start | bytes 52
  4.9 23.9 %copy-start = (bf16[512,2048]{1,0:T(8,128)(2,1)S(1)}, bf16[512,2048]{1,0:T(8,128)(2,1)}, u32[]{:S(2)}) copy-start(bf16[512,2048]{1,0:T(8,128)(2,1)} %wo_ref.3) | copy-start | bytes 6291460
  4.9 8.6 %collective-permute-start.1 = (bf16[128,512]{1,0:T(8,128)(2,1)}, bf16[128,512]{1,0:T(8,128)(2,1)S(1)}, u32[]{:S(2)}, u32[]{:S(2)}) collective-permute-start(bf16[128,512]{1,0:T(8,128)(2,1)} %get-tuple-element.43), channel_id=1, source_target_pairs={{0,8},{2,10},{4,12},{6,14},{8,0},{10,2},{12,4},{14,6},{16,24},{18,... | collective-permute-start | bytes 393224 | tf_op jit(solution)/shard_map/ppermute | solution.py:437
  8.0 8.9 %collective-permute-start = (bf16[128,512]{1,0:T(8,128)(2,1)}, bf16[128,512]{1,0:T(8,128)(2,1)S(1)}, u32[]{:S(2)}, u32[]{:S(2)}) collective-permute-start(bf16[128,512]{1,0:T(8,128)(2,1)} %get-tuple-element.43), channel_id=1, source_target_pairs={{0,16},{2,18},{4,20},{6,22},{8,24},{10,26},{12,28},{14,30},{16,0},... | collective-permute-start | bytes 393224 | tf_op jit(solution)/shard_map/ppermute | solution.py:437
  10.6 6.8 %collective-permute-start.3 = (bf16[128,512]{1,0:T(8,128)(2,1)}, bf16[128,512]{1,0:T(8,128)(2,1)S(1)}, u32[]{:S(2)}, u32[]{:S(2)}) collective-permute-start(bf16[128,512]{1,0:T(8,128)(2,1)} %get-tuple-element.43), channel_id=1, source_target_pairs={{0,4},{2,6},{4,0},{6,2},{8,12},{10,14},{12,8},{14,10},{16,20},{18,... | collective-permute-start | bytes 393224 | tf_op jit(solution)/shard_map/ppermute | solution.py:437
  13.5 5.0 %collective-permute-start.2 = (bf16[128,512]{1,0:T(8,128)(2,1)S(1)}, bf16[128,512]{1,0:T(8,128)(2,1)S(1)}, u32[]{:S(2)}, u32[]{:S(2)}) collective-permute-start(bf16[128,512]{1,0:T(8,128)(2,1)S(1)} %collective-permute-done.1.refs_2_), channel_id=1, source_target_pairs={{0,4},{2,6},{4,0},{6,2},{8,12},{10,14},{12,8},{14,10},{16,20},{18,... | collective-permute-start | bytes 393224 | tf_op jit(solution)/shard_map/ppermute | solution.py:437
  15.4 1.0 %copy-start.2 = (bf16[128,1024]{1,0:T(8,128)(2,1)S(1)}, bf16[128,1024]{1,0:T(8,128)(2,1)}, u32[]{:S(2)}) copy-start(bf16[128,1024]{1,0:T(8,128)(2,1)} %get-tuple-element.44.both_ref) | copy-start | bytes 786436
  16.9 5.0 %collective-permute-start.4 = (bf16[128,512]{1,0:T(8,128)(2,1)S(1)}, bf16[128,512]{1,0:T(8,128)(2,1)S(1)}, u32[]{:S(2)}, u32[]{:S(2)}) collective-permute-start(bf16[128,512]{1,0:T(8,128)(2,1)S(1)} %collective-permute-done.refs_3_), channel_id=1, source_target_pairs={{0,8},{2,10},{4,12},{6,14},{8,0},{10,2},{12,4},{14,6},{16,24},{18,... | collective-permute-start | bytes 393224 | tf_op jit(solution)/shard_map/ppermute | solution.py:437
  17.4 6.0 %collective-permute-start.7 = (bf16[128,512]{1,0:T(8,128)(2,1)S(1)}, bf16[128,512]{1,0:T(8,128)(2,1)S(1)}, u32[]{:S(2)}, u32[]{:S(2)}) collective-permute-start(bf16[128,512]{1,0:T(8,128)(2,1)S(1)} %get-tuple-element.58.q_ref), channel_id=1, source_target_pairs={{0,2},{2,0},{4,6},{6,4},{8,10},{10,8},{12,14},{14,12},{16,18},{18,... | collective-permute-start | bytes 393224 | tf_op jit(solution)/shard_map/ppermute | solution.py:437
  18.5 6.2 %collective-permute-start.5 = (bf16[128,512]{1,0:T(8,128)(2,1)S(1)}, bf16[128,512]{1,0:T(8,128)(2,1)S(1)}, u32[]{:S(2)}, u32[]{:S(2)}) collective-permute-start(bf16[128,512]{1,0:T(8,128)(2,1)S(1)} %collective-permute-done.refs_3_), channel_id=1, source_target_pairs={{0,4},{2,6},{4,0},{6,2},{8,12},{10,14},{12,8},{14,10},{16,20},{18,... | collective-permute-start | bytes 393224 | tf_op jit(solution)/shard_map/ppermute | solution.py:437
  21.9 5.0 %collective-permute-start.6 = (bf16[128,512]{1,0:T(8,128)(2,1)S(1)}, bf16[128,512]{1,0:T(8,128)(2,1)S(1)}, u32[]{:S(2)}, u32[]{:S(2)}) collective-permute-start(bf16[128,512]{1,0:T(8,128)(2,1)S(1)} %collective-permute-done.4.refs_5_), channel_id=1, source_target_pairs={{0,4},{2,6},{4,0},{6,2},{8,12},{10,14},{12,8},{14,10},{16,20},{18,... | collective-permute-start | bytes 393224 | tf_op jit(solution)/shard_map/ppermute | solution.py:437
  26.6 2.3 %collective-permute-start.9 = (bf16[128,640]{1,0:T(8,128)(2,1)S(1)}, bf16[128,640]{1,0:T(8,128)(2,1)S(1)}, u32[]{:S(2)}, u32[]{:S(2)}) collective-permute-start(bf16[128,640]{1,0:T(8,128)(2,1)S(1)} %get-tuple-element.62), channel_id=1, source_target_pairs={{0,2},{2,0},{4,6},{6,4},{8,10},{10,8},{12,14},{14,12},{16,18},{18,... | collective-permute-start | bytes 491528 | tf_op jit(solution)/shard_map/ppermute | solution.py:437
  26.7 5.9 %copy-start.5 = (s32[64]{0:T(128)S(1)}, s32[64]{0:T(128)}, u32[]{:S(2)}) copy-start(s32[64]{0:T(128)} %slot_ref.1) | copy-start | bytes 772
  27.5 1.3 %collective-permute-start.10 = (bf16[64,640]{1,0:T(8,128)(2,1)S(1)}, bf16[64,640]{1,0:T(8,128)(2,1)S(1)}, u32[]{:S(2)}, u32[]{:S(2)}) collective-permute-start(bf16[64,640]{1,0:T(8,128)(2,1)S(1)} %get-tuple-element.67), channel_id=1, source_target_pairs={{0,2},{2,0},{4,6},{6,4},{8,10},{10,8},{12,14},{14,12},{16,18},{18,... | collective-permute-start | bytes 245768 | tf_op jit(solution)/shard_map/ppermute | solution.py:437
  28.5 7.3 %copy-start.1 = (bf16[128,2048]{1,0:T(8,128)(2,1)S(1)}, bf16[128,2048]{1,0:T(8,128)(2,1)}, u32[]{:S(2)}) copy-start(bf16[128,2048]{1,0:T(8,128)(2,1)} %tok_ref.1) | copy-start | bytes 1572868
  29.7 8.6 %collective-permute-start.13 = (bf16[64,2048]{1,0:T(8,128)(2,1)S(1)}, bf16[64,2048]{1,0:T(8,128)(2,1)S(1)}, u32[]{:S(2)}, u32[]{:S(2)}) collective-permute-start(bf16[64,2048]{1,0:T(8,128)(2,1)S(1)} %leave.1), channel_id=1, source_target_pairs={{0,1},{1,0},{2,3},{3,2},{4,5},{5,4},{6,7},{7,6},{8,9},{9,8},{10,11... | collective-permute-start | bytes 786440 | tf_op jit(solution)/shard_map/ppermute | solution.py:589
  31.3 1.3 %collective-permute-start.8 = (bf16[64,640]{1,0:T(8,128)(2,1)S(1)}, bf16[64,640]{1,0:T(8,128)(2,1)S(1)}, u32[]{:S(2)}, u32[]{:S(2)}) collective-permute-start(bf16[64,640]{1,0:T(8,128)(2,1)S(1)} %get-tuple-element.59), channel_id=1, source_target_pairs={{0,2},{2,0},{4,6},{6,4},{8,10},{10,8},{12,14},{14,12},{16,18},{18,... | collective-permute-start | bytes 245768 | tf_op jit(solution)/shard_map/ppermute | solution.py:437
  34.1 1.4 %collective-permute-start.11 = (bf16[4,2,32,256]{3,2,1,0:T(8,128)(2,1)S(1)}, bf16[4,2,32,256]{3,2,1,0:T(8,128)(2,1)S(1)}, u32[]{:S(2)}, u32[]{:S(2)}) collective-permute-start(bf16[4,2,32,256]{3,2,1,0:T(8,128)(2,1)S(1)} %get-tuple-element.77), channel_id=1, source_target_pairs={{0,2},{2,0},{4,6},{6,4},{8,10},{10,8},{12,14},{14,12},{16,18},{18,... | collective-permute-start | bytes 393224 | tf_op jit(solution)/shard_map/ppermute | solution.py:437
  34.4 1.4 %collective-permute-start.12 = (bf16[4,2,32,256]{3,2,1,0:T(8,128)(2,1)S(1)}, bf16[4,2,32,256]{3,2,1,0:T(8,128)(2,1)S(1)}, u32[]{:S(2)}, u32[]{:S(2)}) collective-permute-start(bf16[4,2,32,256]{3,2,1,0:T(8,128)(2,1)S(1)} %get-tuple-element.78), channel_id=1, source_target_pairs={{0,2},{2,0},{4,6},{6,4},{8,10},{10,8},{12,14},{14,12},{16,18},{18,... | collective-permute-start | bytes 393224 | tf_op jit(solution)/shard_map/ppermute | solution.py:437

commit v15 on v14

--- a/solution.py
+++ b/solution.py
@@ -122,10 +122,10 @@
 
 
 def project_kernel(
-    block_hbm, len_hbm, turn_hbm, tok_hbm, gain_hbm, wk_hbm, wv_hbm, wq_hbm,
-    kv_hbm, both_hbm,
-    block_ref, len_ref, turn_ref, tok_ref, gain_ref, k_weights, v_weights, q_weights, both_ref,
-    small_sems, k_sems, v_sems, q_sems, out_sems,
+    block_hbm, len_hbm, turn_hbm, tok_hbm, gain_hbm, wk_hbm, wv_hbm,
+    kv_hbm, normed_hbm, turned_hbm,
+    block_ref, len_ref, turn_ref, tok_ref, gain_ref, k_weights, v_weights, kv_ref, normed_ref, turned_ref,
+    small_sems, k_sems, v_sems, out_sems,
 ):
     small = [
         pltpu.make_async_copy(source, target, small_sems.at[i])
@@ -141,42 +141,43 @@
     ]
     k_copies = weight_copies(wk_hbm, k_weights, k_sems)
     v_copies = weight_copies(wv_hbm, v_weights, v_sems)
-    q_copies = weight_copies(wq_hbm, q_weights, q_sems)
-    for copy in small:
+    for copy in small + k_copies + v_copies:
         copy.start()
-    for i, copy in enumerate(k_copies + v_copies + q_copies):
-        copy.start(priority=1 - i % 2)
     rows = tok_ref.shape[0]
     key_width = wk_hbm.shape[1]
-    kv_width = kv_hbm.shape[1]
     for copy in small:
         copy.wait()
     wide = tok_ref[...].astype(f32)
     scale = lax.rsqrt(jnp.mean(wide * wide, -1, keepdims=True) + EPS)
     normed = (wide * scale * gain_ref[...]).astype(bf16)
+    normed_ref[...] = normed
+    writes = [
+        pltpu.make_async_copy(source, target, out_sems.at[i])
+        for i, (source, target) in enumerate(
+            ((normed_ref, normed_hbm), (turned_ref, turned_hbm), (kv_ref, kv_hbm))
+        )
+    ]
+    writes[0].start()
     cosine, sine = rotary_tables(block_ref, len_ref, turn_ref, rows // 2)
+    turned_ref[:, :HEAD] = cosine
+    turned_ref[:, HEAD:] = sine
+    writes[1].start()
     product = stepped_dot(normed, k_copies, k_weights)
     for h in range(key_width // HEAD):
         cols = slice(h * HEAD, (h + 1) * HEAD)
-        both_ref[:, cols] = rotate(product[:, cols], cosine, sine).astype(bf16)
-    both_ref[:, key_width:kv_width] = stepped_dot(normed, v_copies, v_weights).astype(bf16)
-    kv_part = both_ref.at[:, pl.ds(0, kv_width)]
-    q_part = pl.ds(kv_width, wq_hbm.shape[1])
-    writes = [
-        pltpu.make_async_copy(kv_part, kv_hbm, out_sems.at[0]),
-        pltpu.make_async_copy(kv_part, both_hbm.at[:, pl.ds(0, kv_width)], out_sems.at[1]),
-    ]
-    for copy in writes:
-        copy.start()
-    product = stepped_dot(normed, q_copies, q_weights)
-    for h in range(wq_hbm.shape[1] // HEAD):
-        cols = slice(h * HEAD, (h + 1) * HEAD)
-        turned = rotate(product[:, cols], cosine, sine).astype(bf16)
-        both_ref[:, kv_width + h * HEAD : kv_width + (h + 1) * HEAD] = turned
-    writes.append(pltpu.make_async_copy(both_ref.at[:, q_part], both_hbm.at[:, q_part], out_sems.at[2]))
+        kv_ref[:, cols] = rotate(product[:, cols], cosine, sine).astype(bf16)
+    kv_ref[:, key_width:] = stepped_dot(normed, v_copies, v_weights).astype(bf16)
     writes[2].start()
     for copy in writes:
         copy.wait()
+
+
+def query_kernel(normed_ref, turned_ref, wq_ref, q_ref):
+    product = jnp.dot(normed_ref[...], wq_ref[...], preferred_element_type=f32)
+    cosine, sine = turned_ref[:, :HEAD], turned_ref[:, HEAD:]
+    for h in range(q_ref.shape[1] // HEAD):
+        cols = slice(h * HEAD, (h + 1) * HEAD)
+        q_ref[:, cols] = rotate(product[:, cols], cosine, sine).astype(bf16)
 
 
 def attend_kernel(pieces, side, key_pos_ref, q_pos_ref, q_begin_ref, q_ref, far_ref, *refs):
@@ -289,9 +290,8 @@
     packed_ref[:, q_width:] = parts.astype(bf16)
 
 
-def stage_kernel(block_ref, len_ref, both_ref, kv_out, q_out, key_pos_ref, q_pos_ref, q_begin_ref):
-    kv_out[...] = both_ref[:, : kv_out.shape[1]]
-    q_out[...] = both_ref[:, kv_out.shape[1] :]
+def stage_kernel(block_ref, len_ref, kv_ref, kv_out, key_pos_ref, q_pos_ref, q_begin_ref):
+    kv_out[...] = kv_ref[...]
     shards, rows = key_pos_ref.shape
     half = rows // 2
     shard = lax.axis_index("seq")
@@ -472,11 +472,15 @@
     half = rows // 2
     q_width = w_query.shape[1]
     kv_width = key_projection.shape[1] + value_projection.shape[1]
-    kv, both = pl.pallas_call(
+    kv, normed, turned = pl.pallas_call(
         project_kernel,
-        out_shape=(struct((rows, kv_width), bf16), struct((rows, kv_width + q_width), bf16)),
-        in_specs=in_hbm(8),
-        out_specs=tuple(in_hbm(2)),
+        out_shape=(
+            struct((rows, kv_width), bf16),
+            struct((rows, width), bf16),
+            struct((rows, 2 * HEAD), f32),
+        ),
+        in_specs=in_hbm(7),
+        out_specs=tuple(in_hbm(3)),
         scratch_shapes=[
             pltpu.SMEM(block_split.shape, jnp.int32),
             pltpu.SMEM(lengths.shape, jnp.int32),
@@ -485,39 +489,49 @@
             pltpu.VMEM((1, width), f32),
             pltpu.VMEM(key_projection.shape, bf16),
             pltpu.VMEM(value_projection.shape, bf16),
-            pltpu.VMEM((width, q_width), bf16),
-            pltpu.VMEM((rows, kv_width + q_width), bf16),
+            pltpu.VMEM((rows, kv_width), bf16),
+            pltpu.VMEM((rows, width), bf16),
+            pltpu.VMEM((rows, 2 * HEAD), f32),
             pltpu.SemaphoreType.DMA((5,)),
-            pltpu.SemaphoreType.DMA((WEIGHT_STEPS,)),
             pltpu.SemaphoreType.DMA((WEIGHT_STEPS,)),
             pltpu.SemaphoreType.DMA((WEIGHT_STEPS,)),
             pltpu.SemaphoreType.DMA((3,)),
         ],
         compiler_params=kernel_params(62),
-        cost_estimate=cost(2 * rows * width * (kv_width + q_width), 2 * width * (kv_width + q_width)),
+        cost_estimate=cost(0, 0),
         name="project",
     )(
         block_split, lengths, rotary_constants(half), tokens, norm_gain.reshape(1, width),
-        key_projection, value_projection, w_query,
+        key_projection, value_projection,
     )
-    staged, queries, *places = pl.pallas_call(
+    staged, *places = pl.pallas_call(
         stage_kernel,
         out_shape=(
             struct((rows, kv_width), bf16),
-            struct((rows, q_width), bf16),
             struct((n, rows), jnp.int32),
             struct((2 * rows, HEAD), jnp.int32),
             struct((2 * rows, HEAD), jnp.int32),
         ),
         in_specs=in_vmem(3),
-        out_specs=tuple(in_vmem(5)),
+        out_specs=tuple(in_vmem(4)),
         compiler_params=kernel_params(24),
-        cost_estimate=cost(0, 0),
+        cost_estimate=cost(10**9, 10**7),
         name="stage",
-    )(block_split.reshape(1, n), lengths.reshape(1, -1), both)
-    far_queries = swap(queries, n, 1)
-
-    def attend(pieces, side=None):
+    )(block_split.reshape(1, n), lengths.reshape(1, -1), kv)
+
+    def project_queries(normed):
+        queries = pl.pallas_call(
+            query_kernel,
+            out_shape=struct((rows, q_width), bf16),
+            in_specs=in_vmem(3),
+            out_specs=in_vmem(1)[0],
+            compiler_params=kernel_params(24),
+            cost_estimate=cost(0, 0),
+            name="query",
+        )(normed, turned, w_query)
+        return queries, swap(queries, n, 1)
+
+    def attend(queries, far_queries, pieces, side=None):
         arrays = operands(pieces)
         taken = rows if side is None else half
         mine, stats, packed = pl.pallas_call(
@@ -560,22 +574,26 @@
         second, staged = tied(second, staged)
         own = own.moved([staged])
         third = swapped(second, 4)
+        second, normed = tied(second, normed)
         (second, first_across, beside), _ = tied_all([second, first_across, beside], ())
-        second_across = swapped(second, 2)
-        partials = attend([own, beside, first, second, first_across, third, second_across])
+        queries, far_queries = project_queries(normed)
+        third, queries = tied(third, queries)
+        early = [own, beside, first, second, first_across, third]
+        partials = attend(queries, far_queries, early)
         partials[2] = swap(partials[2], n, 1)
         queries, partials[1] = lax.optimization_barrier((queries, partials[1]))
-        remaining = [swapped(third, 2)]
-        placed = [own, beside, first, second, first_across, third, second_across] + remaining
+        remaining = [swapped(second, 2), swapped(third, 2)]
+        placed = early + remaining
     else:
         same = [list(range(c, n, 2)) for c in range(2)]
         gathered = lax.all_gather(kv, "seq", axis=0, tiled=True, axis_index_groups=same)
         remaining = [Piece([gathered], lambda shard, i: 2 * i + shard % 2, n // 2)]
         partials, placed = [], remaining
-    leaving = attend(remaining, 1)
+        queries, far_queries = project_queries(normed)
+    leaving = attend(queries, far_queries, remaining, 1)
     queries, leaving[1] = lax.optimization_barrier((queries, leaving[1]))
     leaving[2] = swap(leaving[2], n, 1)
-    staying = attend(remaining, 0)
+    staying = attend(queries, far_queries, remaining, 0)
     leaving[0], staying[1] = lax.optimization_barrier((leaving[0], staying[1]))
     sent = pl.pallas_call(
         leave_kernel,

time: 39.1 us -> 38.2 us (0.977)
  Pallas kernels: 12.1 us -> 11.6 us
    pallas_call x1, Pallas kernels: 4.25 us -> 3.32 us  [on_device(): pl.pallas_call(project_kernel, out_shape=(struct((rows, kv_width), bf16),...]
    pallas_call x0 -> x1, Pallas kernels: none -> 0.55 us  [project_queries(): pl.pallas_call(query_kernel, out_shape=struct((rows, q_width), bf16), in_...]
    unnamed x12 -> x18, local copies, waits for them, and re-layouts: 0.98 us -> 0.98 us
  transfers between devices with their start and end apart: 14 -> 14, of which waited for: 11 -> 10; matrix products, arithmetic and copies ran while one was open for 0% -> 0% of each run, Pallas kernels for 16% -> 18%
where the time goes in v15:
time: 38.2 us; the launch traced here: 38 us
  starting transfers between devices  15 us (39%)
  Pallas kernels  11.6 us (30%)
  waiting for transfers between devices  9.63 us (25%)
  local copies, waits for them, and re-layouts  0.98 us (3%)
  between operations  0.81 us (2%)
    ppermute x13, starting transfers between devices, swap(): return lax.ppermute(x, 'seq', [(i, i ^ bit) for i in range(n)])  13.4 us
    ppermute x13, waiting for transfers between devices, swap(): return lax.ppermute(x, 'seq', [(i, i ^ bit) for i in range(n)])  8.71 us
    pallas_call x1, Pallas kernels, on_device(): pl.pallas_call(project_kernel, out_shape=(struct((rows, kv_width), bf16),...  3.32 us
    pallas_call x3, Pallas kernels, attend(): pl.pallas_call(functools.partial(attend_kernel, pieces, side), out_shape=...  3 us
    pallas_call x1, Pallas kernels, place_pages(): pl.pallas_call(functools.partial(cache_kernel, pieces), out_shape=(struct...  1.6 us
    ppermute x1, starting transfers between devices, on_device(): lax.ppermute(sent, 'req', [(i, (i + 1) % parts) for i in range(parts)])  1.58 us
    pallas_call x1, Pallas kernels, on_device(): pl.pallas_call(keep_kernel, out_shape=(struct((half, width), f32), struct...  1.44 us
    unnamed x18, local copies, waits for them, and re-layouts  0.98 us
  transfers between devices with their start and end apart: 14, of which 10 were waited for; matrix products, arithmetic and copies ran while one was open for 0% of the time, Pallas kernels for 18%

profile of v15, /device:TPU:0, one launch (start us, length us, event | category | flops | bytes accessed | tf_op | source)
XLA Modules:
  0.0 38.0 jit_solution(15223165408550779019)
XLA Ops:
  0.7 3.3 %project.1 = (bf16[128,512]{1,0:T(8,128)(2,1)}, bf16[128,2048]{1,0:T(8,128)(2,1)}, f32[128,256]{1,0:T(8,128)}) custom-call(s32[16]{0:T(128)} %block_ref.1, s32[4]{0:T(128)} %len_hbm.1, f32[136,128]{1,0:T(8,128)} %constant.2.clone.turn_hbm, bf16[128,2048]{1,0:T(8,128)(2,1)} %tok_ref.1, f32[1,2048]{1,0:T(1,128)} %bitcast.5, bf16[2048,256]{1,0:T(8,128)(2,1)} %wk_hbm.1, ...), custom_call_target="tpu_custom_call" | custom-call | tf_op jit(solution)/shard_map/project/pallas_call | solution.py:475
  4.0 3.1 %collective-permute-start.1 = (bf16[128,512]{1,0:T(8,128)(2,1)}, bf16[128,512]{1,0:T(8,128)(2,1)S(1)}, u32[]{:S(2)}, u32[]{:S(2)}) collective-permute-start(bf16[128,512]{1,0:T(8,128)(2,1)} %get-tuple-element.47.kv_ref), channel_id=1, source_target_pairs={{0,8},{2,10},{4,12},{6,14},{8,0},{10,2},{12,4},{14,6},{16,24},{18,... | collective-permute-start | bytes 393224 | tf_op jit(solution)/shard_map/ppermute | solution.py:437
  7.1 2.6 %collective-permute-start = (bf16[128,512]{1,0:T(8,128)(2,1)}, bf16[128,512]{1,0:T(8,128)(2,1)S(1)}, u32[]{:S(2)}, u32[]{:S(2)}) collective-permute-start(bf16[128,512]{1,0:T(8,128)(2,1)} %get-tuple-element.47.kv_ref), channel_id=1, source_target_pairs={{0,16},{2,18},{4,20},{6,22},{8,24},{10,26},{12,28},{14,30},{16,0},... | collective-permute-start | bytes 393224 | tf_op jit(solution)/shard_map/ppermute | solution.py:437
  9.7 1.5 %collective-permute-start.3 = (bf16[128,512]{1,0:T(8,128)(2,1)}, bf16[128,512]{1,0:T(8,128)(2,1)S(1)}, u32[]{:S(2)}, u32[]{:S(2)}) collective-permute-start(bf16[128,512]{1,0:T(8,128)(2,1)} %get-tuple-element.47.kv_ref), channel_id=1, source_target_pairs={{0,4},{2,6},{4,0},{6,2},{8,12},{10,14},{12,8},{14,10},{16,20},{18,... | collective-permute-start | bytes 393224 | tf_op jit(solution)/shard_map/ppermute | solution.py:437
  11.2 0.9 %copy-done.8 = bf16[128,512]{1,0:T(8,128)(2,1)S(1)} copy-done((bf16[128,512]{1,0:T(8,128)(2,1)S(1)}, bf16[128,512]{1,0:T(8,128)(2,1)}, u32[]{:S(2)}) %copy-start.8) | copy-done | bytes 131096
  12.6 1.8 %collective-permute-start.2 = (bf16[128,512]{1,0:T(8,128)(2,1)S(1)}, bf16[128,512]{1,0:T(8,128)(2,1)S(1)}, u32[]{:S(2)}, u32[]{:S(2)}) collective-permute-start(bf16[128,512]{1,0:T(8,128)(2,1)S(1)} %collective-permute-done.1.refs_2_), channel_id=1, source_target_pairs={{0,4},{2,6},{4,0},{6,2},{8,12},{10,14},{12,8},{14,10},{16,20},{18,... | collective-permute-start | bytes 393224 | tf_op jit(solution)/shard_map/ppermute | solution.py:437
  14.4 1.6 %collective-permute-done.refs_3_ = bf16[128,512]{1,0:T(8,128)(2,1)S(1)} collective-permute-done((bf16[128,512]{1,0:T(8,128)(2,1)}, bf16[128,512]{1,0:T(8,128)(2,1)S(1)}, u32[]{:S(2)}, u32[]{:S(2)}) %collective-permute-start) | collective-permute-done | bytes 131104 | tf_op jit(solution)/shard_map/ppermute | solution.py:437
  16.5 0.6 %query.1.q_ref = bf16[128,512]{1,0:T(8,128)(2,1)S(1)} custom-call(bf16[128,2048]{1,0:T(8,128)(2,1)S(1)} %copy-done.3, f32[128,256]{1,0:T(8,128)S(1)} %copy-done.4, bf16[2048,512]{1,0:T(8,128)(2,1)S(1)} %copy-done.1), custom_call_target="tpu_custom_call" | custom-call | tf_op jit(solution)/shard_map/query/pallas_call | solution.py:523
  17.7 1.7 %collective-permute-start.5 = (bf16[128,512]{1,0:T(8,128)(2,1)S(1)}, bf16[128,512]{1,0:T(8,128)(2,1)S(1)}, u32[]{:S(2)}, u32[]{:S(2)}) collective-permute-start(bf16[128,512]{1,0:T(8,128)(2,1)S(1)} %collective-permute-done.refs_3_), channel_id=1, source_target_pairs={{0,4},{2,6},{4,0},{6,2},{8,12},{10,14},{12,8},{14,10},{16,20},{18,... | collective-permute-start | bytes 393224 | tf_op jit(solution)/shard_map/ppermute | solution.py:437
  19.4 1.6 %collective-permute-done.4.refs_5_ = bf16[128,512]{1,0:T(8,128)(2,1)S(1)} collective-permute-done((bf16[128,512]{1,0:T(8,128)(2,1)S(1)}, bf16[128,512]{1,0:T(8,128)(2,1)S(1)}, u32[]{:S(2)}, u32[]{:S(2)}) %collective-permute-start.4) | collective-permute-done | bytes 131104 | tf_op jit(solution)/shard_map/ppermute | solution.py:437
  21.0 1.5 %collective-permute-start.6 = (bf16[128,512]{1,0:T(8,128)(2,1)S(1)}, bf16[128,512]{1,0:T(8,128)(2,1)S(1)}, u32[]{:S(2)}, u32[]{:S(2)}) collective-permute-start(bf16[128,512]{1,0:T(8,128)(2,1)S(1)} %collective-permute-done.4.refs_5_), channel_id=1, source_target_pairs={{0,4},{2,6},{4,0},{6,2},{8,12},{10,14},{12,8},{14,10},{16,20},{18,... | collective-permute-start | bytes 393224 | tf_op jit(solution)/shard_map/ppermute | solution.py:437
  22.5 1.6 %attend.3 = (f32[128,512]{1,0:T(8,128)S(1)}, f32[128,128]{1,0:T(8,128)S(1)}, bf16[128,640]{1,0:T(8,128)(2,1)S(1)}) custom-call(s32[16,128]{1,0:T(8,128)S(1)} %get-tuple-element.59.key_pos_ref, s32[256,128]{1,0:T(8,128)S(1)} %get-tuple-element.60.q_pos_ref, s32[256,128]{1,0:T(8,128)S(1)} %get-tuple-element.61.q_begin_ref, bf16[128,512]{1,0:T(8,128)(2,1)S(1)} %query.1.q_ref, ...), custom_call_target="tpu_custom_call" | custom-call | tf_op jit(solution)/shard_map/attend/pallas_call | solution.py:537
  24.2 1.8 %collective-permute-done.6.refs_1_.refs_7_ = bf16[128,512]{1,0:T(8,128)(2,1)S(1)} collective-permute-done((bf16[128,512]{1,0:T(8,128)(2,1)S(1)}, bf16[128,512]{1,0:T(8,128)(2,1)S(1)}, u32[]{:S(2)}, u32[]{:S(2)}) %collective-permute-start.6) | collective-permute-done | bytes 131104 | tf_op jit(solution)/shard_map/ppermute | solution.py:437
  26.0 0.7 %attend.4 = (f32[64,512]{1,0:T(8,128)S(1)}, f32[64,128]{1,0:T(8,128)S(1)}, bf16[64,640]{1,0:T(8,128)(2,1)S(1)}) custom-call(s32[16,128]{1,0:T(8,128)S(1)} %get-tuple-element.59.key_pos_ref, s32[256,128]{1,0:T(8,128)S(1)} %get-tuple-element.60.q_pos_ref, s32[256,128]{1,0:T(8,128)S(1)} %get-tuple-element.61.q_begin_ref, bf16[128,512]{1,0:T(8,128)(2,1)S(1)} %query.1.q_ref, ...), custom_call_target="tpu_custom_call" | custom-call | tf_op jit(solution)/shard_map/attend/pallas_call | solution.py:537
  26.8 0.7 %attend.5 = (f32[64,512]{1,0:T(8,128)S(1)}, f32[64,128]{1,0:T(8,128)S(1)}, bf16[64,640]{1,0:T(8,128)(2,1)S(1)}) custom-call(s32[16,128]{1,0:T(8,128)S(1)} %get-tuple-element.59.key_pos_ref, s32[256,128]{1,0:T(8,128)S(1)} %get-tuple-element.60.q_pos_ref, s32[256,128]{1,0:T(8,128)S(1)} %get-tuple-element.61.q_begin_ref, bf16[128,512]{1,0:T(8,128)(2,1)S(1)} %query.1.q_ref, ...), custom_call_target="tpu_custom_call" | custom-call | tf_op jit(solution)/shard_map/attend/pallas_call | solution.py:537
  27.5 0.5 %collective-permute-done.10.refs_5_ = bf16[64,640]{1,0:T(8,128)(2,1)S(1)} collective-permute-done((bf16[64,640]{1,0:T(8,128)(2,1)S(1)}, bf16[64,640]{1,0:T(8,128)(2,1)S(1)}, u32[]{:S(2)}, u32[]{:S(2)}) %collective-permute-start.10) | collective-permute-done | bytes 81952 | tf_op jit(solution)/shard_map/ppermute | solution.py:437
  28.0 0.8 %leave.1 = bf16[64,2048]{1,0:T(8,128)(2,1)S(1)} custom-call(bf16[512,2048]{1,0:T(8,128)(2,1)S(1)} %copy-done, f32[128,512]{1,0:T(8,128)S(1)} %get-tuple-element.68.refs_0_.refs_2_, f32[128,128]{1,0:T(8,128)S(1)} %get-tuple-element.69.refs_1_.refs_3_, bf16[128,640]{1,0:T(8,128)(2,1)S(1)} %collective-permute-done.9.refs_2_.refs_4_, ...), custom_call_target="tpu_custom_call" | custom-call | tf_op jit(solution)/shard_map/leave/pallas_call | solution.py:598
  28.8 1.6 %collective-permute-start.13 = (bf16[64,2048]{1,0:T(8,128)(2,1)S(1)}, bf16[64,2048]{1,0:T(8,128)(2,1)S(1)}, u32[]{:S(2)}, u32[]{:S(2)}) collective-permute-start(bf16[64,2048]{1,0:T(8,128)(2,1)S(1)} %leave.1), channel_id=1, source_target_pairs={{0,1},{1,0},{2,3},{3,2},{4,5},{5,4},{6,7},{7,6},{8,9},{9,8},{10,11... | collective-permute-start | bytes 786440 | tf_op jit(solution)/shard_map/ppermute | solution.py:607
  30.4 1.3 %collective-permute-done.8.refs_7_ = bf16[64,640]{1,0:T(8,128)(2,1)S(1)} collective-permute-done((bf16[64,640]{1,0:T(8,128)(2,1)S(1)}, bf16[64,640]{1,0:T(8,128)(2,1)S(1)}, u32[]{:S(2)}, u32[]{:S(2)}) %collective-permute-start.8) | collective-permute-done | bytes 81952 | tf_op jit(solution)/shard_map/ppermute | solution.py:437
  31.7 1.6 %cache.1 = (bf16[8,2,32,256]{3,2,1,0:T(8,128)(2,1)S(1)}, bf16[4,2,32,256]{3,2,1,0:T(8,128)(2,1)S(1)}, bf16[4,2,32,256]{3,2,1,0:T(8,128)(2,1)S(1)}) custom-call(s32[16]{0:T(128)S(1)} %copy-done.5, s32[64]{0:T(128)S(1)} %copy-done.6, bf16[128,512]{1,0:T(8,128)(2,1)S(1)} %get-tuple-element.76.refs_0_, bf16[128,512]{1,0:T(8,128)(2,1)S(1)} %collective-permute-done.3.refs_1_, ...), custom_call_target="tpu_custom_call" | custom-call | tf_op jit(solution)/shard_map/cache/pallas_call | solution.py:555
  33.9 0.8 %collective-permute-done.11.refs_0_ = bf16[4,2,32,256]{3,2,1,0:T(8,128)(2,1)S(1)} collective-permute-done((bf16[4,2,32,256]{3,2,1,0:T(8,128)(2,1)S(1)}, bf16[4,2,32,256]{3,2,1,0:T(8,128)(2,1)S(1)}, u32[]{:S(2)}, u32[]{:S(2)}) %collective-permute-start.11) | collective-permute-done | bytes 131104 | tf_op jit(solution)/shard_map/ppermute | solution.py:437
  34.9 1.4 %keep.1 = (f32[64,2048]{1,0:T(8,128)S(1)}, bf16[8,2,32,256]{3,2,1,0:T(8,128)(2,1)}) custom-call(bf16[512,2048]{1,0:T(8,128)(2,1)S(1)} %copy-done, bf16[128,2048]{1,0:T(8,128)(2,1)S(1)} %copy-done.2, bf16[8,2,32,256]{3,2,1,0:T(8,128)(2,1)S(1)} %get-tuple-element.84.mine_ref, bf16[4,2,32,256]{3,2,1,0:T(8,128)(2,1)S(1)} %collective-permute-done.11.refs_0_, ...), custom_call_target="tpu_custom_call" | custom-call | tf_op jit(solution)/shard_map/keep/pallas_call | solution.py:611
  36.4 0.9 %collective-permute-done.13.received_ref = bf16[64,2048]{1,0:T(8,128)(2,1)S(1)} collective-permute-done((bf16[64,2048]{1,0:T(8,128)(2,1)S(1)}, bf16[64,2048]{1,0:T(8,128)(2,1)S(1)}, u32[]{:S(2)}, u32[]{:S(2)}) %collective-permute-start.13) | collective-permute-done | bytes 262176 | tf_op jit(solution)/shard_map/ppermute | solution.py:607
  37.3 0.8 %finish.1 = bf16[64,2048]{1,0:T(8,128)(2,1)} custom-call(f32[64,2048]{1,0:T(8,128)S(1)} %get-tuple-element.90.kept_ref, bf16[64,2048]{1,0:T(8,128)(2,1)S(1)} %collective-permute-done.13.received_ref), custom_call_target="tpu_custom_call" | custom-call | tf_op jit(solution)/shard_map/finish/pallas_call | solution.py:620
  (32 shorter events, 2.5 us)
Async XLA Ops:
  0.6 10.6 %copy-start.5 = (s32[16]{0:T(128)S(1)}, s32[16]{0:T(128)}, u32[]{:S(2)}) copy-start(s32[16]{0:T(128)} %block_ref.1) | copy-start | bytes 196
  0.6 10.5 %copy-start.7 = (s32[4]{0:T(128)S(1)}, s32[4]{0:T(128)}, u32[]{:S(2)}) copy-start(s32[4]{0:T(128)} %len_hbm.1) | copy-start | bytes 52
  4.0 12.5 %copy-start.1 = (bf16[2048,512]{1,0:T(8,128)(2,1)S(1)}, bf16[2048,512]{1,0:T(8,128)(2,1)}, u32[]{:S(2)}) copy-start(bf16[2048,512]{1,0:T(8,128)(2,1)} %wq_ref.1) | copy-start | bytes 6291460
  4.0 12.5 %copy-start.3 = (bf16[128,2048]{1,0:T(8,128)(2,1)S(1)}, bf16[128,2048]{1,0:T(8,128)(2,1)}, u32[]{:S(2)}) copy-start(bf16[128,2048]{1,0:T(8,128)(2,1)} %get-tuple-element.56.normed_ref) | copy-start | bytes 1572868
  4.0 12.5 %copy-start.4 = (f32[128,256]{1,0:T(8,128)S(1)}, f32[128,256]{1,0:T(8,128)}, u32[]{:S(2)}) copy-start(f32[128,256]{1,0:T(8,128)} %get-tuple-element.57.turned_ref) | copy-start | bytes 393220
  4.0 8.6 %collective-permute-start.1 = (bf16[128,512]{1,0:T(8,128)(2,1)}, bf16[128,512]{1,0:T(8,128)(2,1)S(1)}, u32[]{:S(2)}, u32[]{:S(2)}) collective-permute-start(bf16[128,512]{1,0:T(8,128)(2,1)} %get-tuple-element.47.kv_ref), channel_id=1, source_target_pairs={{0,8},{2,10},{4,12},{6,14},{8,0},{10,2},{12,4},{14,6},{16,24},{18,... | collective-permute-start | bytes 393224 | tf_op jit(solution)/shard_map/ppermute | solution.py:437
  7.1 8.9 %collective-permute-start = (bf16[128,512]{1,0:T(8,128)(2,1)}, bf16[128,512]{1,0:T(8,128)(2,1)S(1)}, u32[]{:S(2)}, u32[]{:S(2)}) collective-permute-start(bf16[128,512]{1,0:T(8,128)(2,1)} %get-tuple-element.47.kv_ref), channel_id=1, source_target_pairs={{0,16},{2,18},{4,20},{6,22},{8,24},{10,26},{12,28},{14,30},{16,0},... | collective-permute-start | bytes 393224 | tf_op jit(solution)/shard_map/ppermute | solution.py:437
  9.7 7.4 %collective-permute-start.3 = (bf16[128,512]{1,0:T(8,128)(2,1)}, bf16[128,512]{1,0:T(8,128)(2,1)S(1)}, u32[]{:S(2)}, u32[]{:S(2)}) collective-permute-start(bf16[128,512]{1,0:T(8,128)(2,1)} %get-tuple-element.47.kv_ref), channel_id=1, source_target_pairs={{0,4},{2,6},{4,0},{6,2},{8,12},{10,14},{12,8},{14,10},{16,20},{18,... | collective-permute-start | bytes 393224 | tf_op jit(solution)/shard_map/ppermute | solution.py:437
  11.2 0.9 %copy-start.8 = (bf16[128,512]{1,0:T(8,128)(2,1)S(1)}, bf16[128,512]{1,0:T(8,128)(2,1)}, u32[]{:S(2)}) copy-start(bf16[128,512]{1,0:T(8,128)(2,1)} %get-tuple-element.47.kv_ref) | copy-start | bytes 393220
  12.6 5.1 %collective-permute-start.2 = (bf16[128,512]{1,0:T(8,128)(2,1)S(1)}, bf16[128,512]{1,0:T(8,128)(2,1)S(1)}, u32[]{:S(2)}, u32[]{:S(2)}) collective-permute-start(bf16[128,512]{1,0:T(8,128)(2,1)S(1)} %collective-permute-done.1.refs_2_), channel_id=1, source_target_pairs={{0,4},{2,6},{4,0},{6,2},{8,12},{10,14},{12,8},{14,10},{16,20},{18,... | collective-permute-start | bytes 393224 | tf_op jit(solution)/shard_map/ppermute | solution.py:437
  16.0 5.0 %collective-permute-start.4 = (bf16[128,512]{1,0:T(8,128)(2,1)S(1)}, bf16[128,512]{1,0:T(8,128)(2,1)S(1)}, u32[]{:S(2)}, u32[]{:S(2)}) collective-permute-start(bf16[128,512]{1,0:T(8,128)(2,1)S(1)} %collective-permute-done.refs_3_), channel_id=1, source_target_pairs={{0,8},{2,10},{4,12},{6,14},{8,0},{10,2},{12,4},{14,6},{16,24},{18,... | collective-permute-start | bytes 393224 | tf_op jit(solution)/shard_map/ppermute | solution.py:437
  17.0 11.0 %copy-start = (bf16[512,2048]{1,0:T(8,128)(2,1)S(1)}, bf16[512,2048]{1,0:T(8,128)(2,1)}, u32[]{:S(2)}) copy-start(bf16[512,2048]{1,0:T(8,128)(2,1)} %wo_ref.3) | copy-start | bytes 6291460
  17.1 5.4 %collective-permute-start.7 = (bf16[128,512]{1,0:T(8,128)(2,1)S(1)}, bf16[128,512]{1,0:T(8,128)(2,1)S(1)}, u32[]{:S(2)}, u32[]{:S(2)}) collective-permute-start(bf16[128,512]{1,0:T(8,128)(2,1)S(1)} %query.1.q_ref), channel_id=1, source_target_pairs={{0,2},{2,0},{4,6},{6,4},{8,10},{10,8},{12,14},{14,12},{16,18},{18,... | collective-permute-start | bytes 393224 | tf_op jit(solution)/shard_map/ppermute | solution.py:437
  17.7 6.5 %collective-permute-start.5 = (bf16[128,512]{1,0:T(8,128)(2,1)S(1)}, bf16[128,512]{1,0:T(8,128)(2,1)S(1)}, u32[]{:S(2)}, u32[]{:S(2)}) collective-permute-start(bf16[128,512]{1,0:T(8,128)(2,1)S(1)} %collective-permute-done.refs_3_), channel_id=1, source_target_pairs={{0,4},{2,6},{4,0},{6,2},{8,12},{10,14},{12,8},{14,10},{16,20},{18,... | collective-permute-start | bytes 393224 | tf_op jit(solution)/shard_map/ppermute | solution.py:437
  21.0 5.0 %collective-permute-start.6 = (bf16[128,512]{1,0:T(8,128)(2,1)S(1)}, bf16[128,512]{1,0:T(8,128)(2,1)S(1)}, u32[]{:S(2)}, u32[]{:S(2)}) collective-permute-start(bf16[128,512]{1,0:T(8,128)(2,1)S(1)} %collective-permute-done.4.refs_5_), channel_id=1, source_target_pairs={{0,4},{2,6},{4,0},{6,2},{8,12},{10,14},{12,8},{14,10},{16,20},{18,... | collective-permute-start | bytes 393224 | tf_op jit(solution)/shard_map/ppermute | solution.py:437
  24.1 3.4 %collective-permute-start.9 = (bf16[128,640]{1,0:T(8,128)(2,1)S(1)}, bf16[128,640]{1,0:T(8,128)(2,1)S(1)}, u32[]{:S(2)}, u32[]{:S(2)}) collective-permute-start(bf16[128,640]{1,0:T(8,128)(2,1)S(1)} %get-tuple-element.70), channel_id=1, source_target_pairs={{0,2},{2,0},{4,6},{6,4},{8,10},{10,8},{12,14},{14,12},{16,18},{18,... | collective-permute-start | bytes 491528 | tf_op jit(solution)/shard_map/ppermute | solution.py:437
  26.7 5.0 %copy-start.6 = (s32[64]{0:T(128)S(1)}, s32[64]{0:T(128)}, u32[]{:S(2)}) copy-start(s32[64]{0:T(128)} %slot_ref.1) | copy-start | bytes 772
  26.7 1.3 %collective-permute-start.10 = (bf16[64,640]{1,0:T(8,128)(2,1)S(1)}, bf16[64,640]{1,0:T(8,128)(2,1)S(1)}, u32[]{:S(2)}, u32[]{:S(2)}) collective-permute-start(bf16[64,640]{1,0:T(8,128)(2,1)S(1)} %get-tuple-element.75), channel_id=1, source_target_pairs={{0,2},{2,0},{4,6},{6,4},{8,10},{10,8},{12,14},{14,12},{16,18},{18,... | collective-permute-start | bytes 245768 | tf_op jit(solution)/shard_map/ppermute | solution.py:437
  27.5 7.4 %copy-start.2 = (bf16[128,2048]{1,0:T(8,128)(2,1)S(1)}, bf16[128,2048]{1,0:T(8,128)(2,1)}, u32[]{:S(2)}) copy-start(bf16[128,2048]{1,0:T(8,128)(2,1)} %tok_ref.1) | copy-start | bytes 1572868
  28.8 8.4 %collective-permute-start.13 = (bf16[64,2048]{1,0:T(8,128)(2,1)S(1)}, bf16[64,2048]{1,0:T(8,128)(2,1)S(1)}, u32[]{:S(2)}, u32[]{:S(2)}) collective-permute-start(bf16[64,2048]{1,0:T(8,128)(2,1)S(1)} %leave.1), channel_id=1, source_target_pairs={{0,1},{1,0},{2,3},{3,2},{4,5},{5,4},{6,7},{7,6},{8,9},{9,8},{10,11... | collective-permute-start | bytes 786440 | tf_op jit(solution)/shard_map/ppermute | solution.py:607
  30.4 1.3 %collective-permute-start.8 = (bf16[64,640]{1,0:T(8,128)(2,1)S(1)}, bf16[64,640]{1,0:T(8,128)(2,1)S(1)}, u32[]{:S(2)}, u32[]{:S(2)}) collective-permute-start(bf16[64,640]{1,0:T(8,128)(2,1)S(1)} %get-tuple-element.67), channel_id=1, source_target_pairs={{0,2},{2,0},{4,6},{6,4},{8,10},{10,8},{12,14},{14,12},{16,18},{18,... | collective-permute-start | bytes 245768 | tf_op jit(solution)/shard_map/ppermute | solution.py:437
  33.3 1.4 %collective-permute-start.11 = (bf16[4,2,32,256]{3,2,1,0:T(8,128)(2,1)S(1)}, bf16[4,2,32,256]{3,2,1,0:T(8,128)(2,1)S(1)}, u32[]{:S(2)}, u32[]{:S(2)}) collective-permute-start(bf16[4,2,32,256]{3,2,1,0:T(8,128)(2,1)S(1)} %get-tuple-element.85), channel_id=1, source_target_pairs={{0,2},{2,0},{4,6},{6,4},{8,10},{10,8},{12,14},{14,12},{16,18},{18,... | collective-permute-start | bytes 393224 | tf_op jit(solution)/shard_map/ppermute | solution.py:437
  33.5 1.4 %collective-permute-start.12 = (bf16[4,2,32,256]{3,2,1,0:T(8,128)(2,1)S(1)}, bf16[4,2,32,256]{3,2,1,0:T(8,128)(2,1)S(1)}, u32[]{:S(2)}, u32[]{:S(2)}) collective-permute-start(bf16[4,2,32,256]{3,2,1,0:T(8,128)(2,1)S(1)} %get-tuple-element.86), channel_id=1, source_target_pairs={{0,2},{2,0},{4,6},{6,4},{8,10},{10,8},{12,14},{14,12},{16,18},{18,... | collective-permute-start | bytes 393224 | tf_op jit(solution)/shard_map/ppermute | solution.py:437

commit v16 on v15

--- a/solution.py
+++ b/solution.py
@@ -574,15 +574,15 @@
         second, staged = tied(second, staged)
         own = own.moved([staged])
         third = swapped(second, 4)
+        last = swapped(second, 6)
         second, normed = tied(second, normed)
         (second, first_across, beside), _ = tied_all([second, first_across, beside], ())
         queries, far_queries = project_queries(normed)
-        third, queries = tied(third, queries)
-        early = [own, beside, first, second, first_across, third]
+        early = [own, beside, first, second, first_across, last]
         partials = attend(queries, far_queries, early)
         partials[2] = swap(partials[2], n, 1)
         queries, partials[1] = lax.optimization_barrier((queries, partials[1]))
-        remaining = [swapped(second, 2), swapped(third, 2)]
+        remaining = [third, swapped(second, 2)]
         placed = early + remaining
     else:
         same = [list(range(c, n, 2)) for c in range(2)]

time: 38.2 us -> 38.6 us (1.010)
  waiting for transfers between devices: 9.63 us -> 10.2 us
    ppermute x13, waiting for transfers between devices: 8.71 us -> 9.26 us  [swap(): return lax.ppermute(x, 'seq', [(i, i ^ bit) for i in range(n)])]
  transfers between devices with their start and end apart: 14 -> 14, of which waited for: 10 -> 9; matrix products, arithmetic and copies ran while one was open for 0% -> 0% of each run, Pallas kernels for 18% -> 17%
where the time goes in v16:
time: 38.6 us; the launch traced here: 38.5 us
  starting transfers between devices  14.9 us (39%)
  Pallas kernels  11.6 us (30%)
  waiting for transfers between devices  10.2 us (26%)
  local copies, waits for them, and re-layouts  0.95 us (2%)
  between operations  0.8 us (2%)
    ppermute x13, starting transfers between devices, swap(): return lax.ppermute(x, 'seq', [(i, i ^ bit) for i in range(n)])  13.3 us
    ppermute x13, waiting for transfers between devices, swap(): return lax.ppermute(x, 'seq', [(i, i ^ bit) for i in range(n)])  9.26 us
    pallas_call x1, Pallas kernels, on_device(): pl.pallas_call(project_kernel, out_shape=(struct((rows, kv_width), bf16),...  3.32 us
    pallas_call x3, Pallas kernels, attend(): pl.pallas_call(functools.partial(attend_kernel, pieces, side), out_shape=...  3 us
    pallas_call x1, Pallas kernels, place_pages(): pl.pallas_call(functools.partial(cache_kernel, pieces), out_shape=(struct...  1.6 us
    ppermute x1, starting transfers between devices, on_device(): lax.ppermute(sent, 'req', [(i, (i + 1) % parts) for i in range(parts)])  1.58 us
    pallas_call x1, Pallas kernels, on_device(): pl.pallas_call(keep_kernel, out_shape=(struct((half, width), f32), struct...  1.44 us
    unnamed x18, local copies, waits for them, and re-layouts  0.95 us
  transfers between devices with their start and end apart: 14, of which 9 were waited for; matrix products, arithmetic and copies ran while one was open for 0% of the time, Pallas kernels for 17%

profile of v16, /device:TPU:0, one launch (start us, length us, event | category | flops | bytes accessed | tf_op | source)
XLA Modules:
  0.0 38.5 jit_solution(4133142692627246086)
XLA Ops:
  0.7 3.3 %project.1 = (bf16[128,512]{1,0:T(8,128)(2,1)}, bf16[128,2048]{1,0:T(8,128)(2,1)}, f32[128,256]{1,0:T(8,128)}) custom-call(s32[16]{0:T(128)} %block_ref.1, s32[4]{0:T(128)} %len_hbm.1, f32[136,128]{1,0:T(8,128)} %constant.2.clone.turn_hbm, bf16[128,2048]{1,0:T(8,128)(2,1)} %tok_ref.1, f32[1,2048]{1,0:T(1,128)} %bitcast.5, bf16[2048,256]{1,0:T(8,128)(2,1)} %wk_hbm.1, ...), custom_call_target="tpu_custom_call" | custom-call | tf_op jit(solution)/shard_map/project/pallas_call | solution.py:475
  4.0 3.1 %collective-permute-start.1 = (bf16[128,512]{1,0:T(8,128)(2,1)}, bf16[128,512]{1,0:T(8,128)(2,1)S(1)}, u32[]{:S(2)}, u32[]{:S(2)}) collective-permute-start(bf16[128,512]{1,0:T(8,128)(2,1)} %get-tuple-element.45.kv_ref), channel_id=1, source_target_pairs={{0,8},{2,10},{4,12},{6,14},{8,0},{10,2},{12,4},{14,6},{16,24},{18,... | collective-permute-start | bytes 393224 | tf_op jit(solution)/shard_map/ppermute | solution.py:437
  7.1 2.6 %collective-permute-start = (bf16[128,512]{1,0:T(8,128)(2,1)}, bf16[128,512]{1,0:T(8,128)(2,1)S(1)}, u32[]{:S(2)}, u32[]{:S(2)}) collective-permute-start(bf16[128,512]{1,0:T(8,128)(2,1)} %get-tuple-element.45.kv_ref), channel_id=1, source_target_pairs={{0,16},{2,18},{4,20},{6,22},{8,24},{10,26},{12,28},{14,30},{16,0},... | collective-permute-start | bytes 393224 | tf_op jit(solution)/shard_map/ppermute | solution.py:437
  9.7 1.5 %collective-permute-start.3 = (bf16[128,512]{1,0:T(8,128)(2,1)}, bf16[128,512]{1,0:T(8,128)(2,1)S(1)}, u32[]{:S(2)}, u32[]{:S(2)}) collective-permute-start(bf16[128,512]{1,0:T(8,128)(2,1)} %get-tuple-element.45.kv_ref), channel_id=1, source_target_pairs={{0,4},{2,6},{4,0},{6,2},{8,12},{10,14},{12,8},{14,10},{16,20},{18,... | collective-permute-start | bytes 393224 | tf_op jit(solution)/shard_map/ppermute | solution.py:437
  11.2 1.4 %collective-permute-done.1.refs_2_ = bf16[128,512]{1,0:T(8,128)(2,1)S(1)} collective-permute-done((bf16[128,512]{1,0:T(8,128)(2,1)}, bf16[128,512]{1,0:T(8,128)(2,1)S(1)}, u32[]{:S(2)}, u32[]{:S(2)}) %collective-permute-start.1) | collective-permute-done | bytes 131104 | tf_op jit(solution)/shard_map/ppermute | solution.py:437
  12.6 1.8 %collective-permute-start.2 = (bf16[128,512]{1,0:T(8,128)(2,1)S(1)}, bf16[128,512]{1,0:T(8,128)(2,1)S(1)}, u32[]{:S(2)}, u32[]{:S(2)}) collective-permute-start(bf16[128,512]{1,0:T(8,128)(2,1)S(1)} %collective-permute-done.1.refs_2_), channel_id=1, source_target_pairs={{0,4},{2,6},{4,0},{6,2},{8,12},{10,14},{12,8},{14,10},{16,20},{18,... | collective-permute-start | bytes 393224 | tf_op jit(solution)/shard_map/ppermute | solution.py:437
  14.4 0.9 %copy-done.8 = bf16[128,512]{1,0:T(8,128)(2,1)S(1)} copy-done((bf16[128,512]{1,0:T(8,128)(2,1)S(1)}, bf16[128,512]{1,0:T(8,128)(2,1)}, u32[]{:S(2)}) %copy-start.8) | copy-done | bytes 131096
  15.5 0.6 %collective-permute-done.refs_3_ = bf16[128,512]{1,0:T(8,128)(2,1)S(1)} collective-permute-done((bf16[128,512]{1,0:T(8,128)(2,1)}, bf16[128,512]{1,0:T(8,128)(2,1)S(1)}, u32[]{:S(2)}, u32[]{:S(2)}) %collective-permute-start) | collective-permute-done | bytes 131104 | tf_op jit(solution)/shard_map/ppermute | solution.py:437
  16.1 0.6 %query.1.q_ref = bf16[128,512]{1,0:T(8,128)(2,1)S(1)} custom-call(bf16[128,2048]{1,0:T(8,128)(2,1)S(1)} %copy-done.3, f32[128,256]{1,0:T(8,128)S(1)} %copy-done.4, bf16[2048,512]{1,0:T(8,128)(2,1)S(1)} %copy-done.1), custom_call_target="tpu_custom_call" | custom-call | tf_op jit(solution)/shard_map/query/pallas_call | solution.py:523
  16.7 1.4 %collective-permute-start.4 = (bf16[128,512]{1,0:T(8,128)(2,1)S(1)}, bf16[128,512]{1,0:T(8,128)(2,1)S(1)}, u32[]{:S(2)}, u32[]{:S(2)}) collective-permute-start(bf16[128,512]{1,0:T(8,128)(2,1)S(1)} %collective-permute-done.refs_3_), channel_id=1, source_target_pairs={{0,12},{2,14},{4,8},{6,10},{8,4},{10,6},{12,0},{14,2},{16,28},{18,... | collective-permute-start | bytes 393224 | tf_op jit(solution)/shard_map/ppermute | solution.py:437
  18.1 1.6 %collective-permute-start.5 = (bf16[128,512]{1,0:T(8,128)(2,1)S(1)}, bf16[128,512]{1,0:T(8,128)(2,1)S(1)}, u32[]{:S(2)}, u32[]{:S(2)}) collective-permute-start(bf16[128,512]{1,0:T(8,128)(2,1)S(1)} %collective-permute-done.refs_3_), channel_id=1, source_target_pairs={{0,8},{2,10},{4,12},{6,14},{8,0},{10,2},{12,4},{14,6},{16,24},{18,... | collective-permute-start | bytes 393224 | tf_op jit(solution)/shard_map/ppermute | solution.py:437
  20.3 3.7 %collective-permute-done.4.refs_5_ = bf16[128,512]{1,0:T(8,128)(2,1)S(1)} collective-permute-done((bf16[128,512]{1,0:T(8,128)(2,1)S(1)}, bf16[128,512]{1,0:T(8,128)(2,1)S(1)}, u32[]{:S(2)}, u32[]{:S(2)}) %collective-permute-start.4) | collective-permute-done | bytes 131104 | tf_op jit(solution)/shard_map/ppermute | solution.py:437
  24.0 1.6 %attend.3 = (f32[128,512]{1,0:T(8,128)S(1)}, f32[128,128]{1,0:T(8,128)S(1)}, bf16[128,640]{1,0:T(8,128)(2,1)S(1)}) custom-call(s32[16,128]{1,0:T(8,128)S(1)} %get-tuple-element.54.key_pos_ref, s32[256,128]{1,0:T(8,128)S(1)} %get-tuple-element.55.q_pos_ref, s32[256,128]{1,0:T(8,128)S(1)} %get-tuple-element.56.q_begin_ref, bf16[128,512]{1,0:T(8,128)(2,1)S(1)} %query.1.q_ref, ...), custom_call_target="tpu_custom_call" | custom-call | tf_op jit(solution)/shard_map/attend/pallas_call | solution.py:537
  25.7 0.7 %collective-permute-done.5.refs_0_.refs_6_ = bf16[128,512]{1,0:T(8,128)(2,1)S(1)} collective-permute-done((bf16[128,512]{1,0:T(8,128)(2,1)S(1)}, bf16[128,512]{1,0:T(8,128)(2,1)S(1)}, u32[]{:S(2)}, u32[]{:S(2)}) %collective-permute-start.5) | collective-permute-done | bytes 131104 | tf_op jit(solution)/shard_map/ppermute | solution.py:437
  26.4 0.7 %attend.4 = (f32[64,512]{1,0:T(8,128)S(1)}, f32[64,128]{1,0:T(8,128)S(1)}, bf16[64,640]{1,0:T(8,128)(2,1)S(1)}) custom-call(s32[16,128]{1,0:T(8,128)S(1)} %get-tuple-element.54.key_pos_ref, s32[256,128]{1,0:T(8,128)S(1)} %get-tuple-element.55.q_pos_ref, s32[256,128]{1,0:T(8,128)S(1)} %get-tuple-element.56.q_begin_ref, bf16[128,512]{1,0:T(8,128)(2,1)S(1)} %query.1.q_ref, ...), custom_call_target="tpu_custom_call" | custom-call | tf_op jit(solution)/shard_map/attend/pallas_call | solution.py:537
  27.2 0.7 %attend.5 = (f32[64,512]{1,0:T(8,128)S(1)}, f32[64,128]{1,0:T(8,128)S(1)}, bf16[64,640]{1,0:T(8,128)(2,1)S(1)}) custom-call(s32[16,128]{1,0:T(8,128)S(1)} %get-tuple-element.54.key_pos_ref, s32[256,128]{1,0:T(8,128)S(1)} %get-tuple-element.55.q_pos_ref, s32[256,128]{1,0:T(8,128)S(1)} %get-tuple-element.56.q_begin_ref, bf16[128,512]{1,0:T(8,128)(2,1)S(1)} %query.1.q_ref, ...), custom_call_target="tpu_custom_call" | custom-call | tf_op jit(solution)/shard_map/attend/pallas_call | solution.py:537
  28.5 0.8 %leave.1 = bf16[64,2048]{1,0:T(8,128)(2,1)S(1)} custom-call(bf16[512,2048]{1,0:T(8,128)(2,1)S(1)} %copy-done, f32[128,512]{1,0:T(8,128)S(1)} %get-tuple-element.64.refs_0_.refs_2_, f32[128,128]{1,0:T(8,128)S(1)} %get-tuple-element.65.refs_1_.refs_3_, bf16[128,640]{1,0:T(8,128)(2,1)S(1)} %collective-permute-done.9.refs_2_.refs_4_, ...), custom_call_target="tpu_custom_call" | custom-call | tf_op jit(solution)/shard_map/leave/pallas_call | solution.py:598
  29.3 1.6 %collective-permute-start.13 = (bf16[64,2048]{1,0:T(8,128)(2,1)S(1)}, bf16[64,2048]{1,0:T(8,128)(2,1)S(1)}, u32[]{:S(2)}, u32[]{:S(2)}) collective-permute-start(bf16[64,2048]{1,0:T(8,128)(2,1)S(1)} %leave.1), channel_id=1, source_target_pairs={{0,1},{1,0},{2,3},{3,2},{4,5},{5,4},{6,7},{7,6},{8,9},{9,8},{10,11... | collective-permute-start | bytes 786440 | tf_op jit(solution)/shard_map/ppermute | solution.py:607
  30.8 1.3 %collective-permute-done.8.refs_7_ = bf16[64,640]{1,0:T(8,128)(2,1)S(1)} collective-permute-done((bf16[64,640]{1,0:T(8,128)(2,1)S(1)}, bf16[64,640]{1,0:T(8,128)(2,1)S(1)}, u32[]{:S(2)}, u32[]{:S(2)}) %collective-permute-start.8) | collective-permute-done | bytes 81952 | tf_op jit(solution)/shard_map/ppermute | solution.py:437
  32.1 1.6 %cache.1 = (bf16[8,2,32,256]{3,2,1,0:T(8,128)(2,1)S(1)}, bf16[4,2,32,256]{3,2,1,0:T(8,128)(2,1)S(1)}, bf16[4,2,32,256]{3,2,1,0:T(8,128)(2,1)S(1)}) custom-call(s32[16]{0:T(128)S(1)} %copy-done.5, s32[64]{0:T(128)S(1)} %copy-done.6, bf16[128,512]{1,0:T(8,128)(2,1)S(1)} %get-tuple-element.72.refs_0_, bf16[128,512]{1,0:T(8,128)(2,1)S(1)} %collective-permute-done.3.refs_1_, ...), custom_call_target="tpu_custom_call" | custom-call | tf_op jit(solution)/shard_map/cache/pallas_call | solution.py:555
  34.3 0.8 %collective-permute-done.11.refs_0_ = bf16[4,2,32,256]{3,2,1,0:T(8,128)(2,1)S(1)} collective-permute-done((bf16[4,2,32,256]{3,2,1,0:T(8,128)(2,1)S(1)}, bf16[4,2,32,256]{3,2,1,0:T(8,128)(2,1)S(1)}, u32[]{:S(2)}, u32[]{:S(2)}) %collective-permute-start.11) | collective-permute-done | bytes 131104 | tf_op jit(solution)/shard_map/ppermute | solution.py:437
  35.3 1.4 %keep.1 = (f32[64,2048]{1,0:T(8,128)S(1)}, bf16[8,2,32,256]{3,2,1,0:T(8,128)(2,1)}) custom-call(bf16[512,2048]{1,0:T(8,128)(2,1)S(1)} %copy-done, bf16[128,2048]{1,0:T(8,128)(2,1)S(1)} %copy-done.2, bf16[8,2,32,256]{3,2,1,0:T(8,128)(2,1)S(1)} %get-tuple-element.80.mine_ref, bf16[4,2,32,256]{3,2,1,0:T(8,128)(2,1)S(1)} %collective-permute-done.11.refs_0_, ...), custom_call_target="tpu_custom_call" | custom-call | tf_op jit(solution)/shard_map/keep/pallas_call | solution.py:611
  36.8 0.9 %collective-permute-done.13.received_ref = bf16[64,2048]{1,0:T(8,128)(2,1)S(1)} collective-permute-done((bf16[64,2048]{1,0:T(8,128)(2,1)S(1)}, bf16[64,2048]{1,0:T(8,128)(2,1)S(1)}, u32[]{:S(2)}, u32[]{:S(2)}) %collective-permute-start.13) | collective-permute-done | bytes 262176 | tf_op jit(solution)/shard_map/ppermute | solution.py:607
  37.7 0.8 %finish.1 = bf16[64,2048]{1,0:T(8,128)(2,1)} custom-call(f32[64,2048]{1,0:T(8,128)S(1)} %get-tuple-element.86.kept_ref, bf16[64,2048]{1,0:T(8,128)(2,1)S(1)} %collective-permute-done.13.received_ref), custom_call_target="tpu_custom_call" | custom-call | tf_op jit(solution)/shard_map/finish/pallas_call | solution.py:620
  (32 shorter events, 2.2 us)
Async XLA Ops:
  0.6 13.8 %copy-start.5 = (s32[16]{0:T(128)S(1)}, s32[16]{0:T(128)}, u32[]{:S(2)}) copy-start(s32[16]{0:T(128)} %block_ref.1) | copy-start | bytes 196
  0.6 13.8 %copy-start.7 = (s32[4]{0:T(128)S(1)}, s32[4]{0:T(128)}, u32[]{:S(2)}) copy-start(s32[4]{0:T(128)} %len_hbm.1) | copy-start | bytes 52
  4.0 12.1 %copy-start.1 = (bf16[2048,512]{1,0:T(8,128)(2,1)S(1)}, bf16[2048,512]{1,0:T(8,128)(2,1)}, u32[]{:S(2)}) copy-start(bf16[2048,512]{1,0:T(8,128)(2,1)} %wq_ref.1) | copy-start | bytes 6291460
  4.0 12.1 %copy-start.3 = (bf16[128,2048]{1,0:T(8,128)(2,1)S(1)}, bf16[128,2048]{1,0:T(8,128)(2,1)}, u32[]{:S(2)}) copy-start(bf16[128,2048]{1,0:T(8,128)(2,1)} %get-tuple-element.57.normed_ref) | copy-start | bytes 1572868
  4.0 12.0 %copy-start.4 = (f32[128,256]{1,0:T(8,128)S(1)}, f32[128,256]{1,0:T(8,128)}, u32[]{:S(2)}) copy-start(f32[128,256]{1,0:T(8,128)} %get-tuple-element.58.turned_ref) | copy-start | bytes 393220
  4.0 8.6 %collective-permute-start.1 = (bf16[128,512]{1,0:T(8,128)(2,1)}, bf16[128,512]{1,0:T(8,128)(2,1)S(1)}, u32[]{:S(2)}, u32[]{:S(2)}) collective-permute-start(bf16[128,512]{1,0:T(8,128)(2,1)} %get-tuple-element.45.kv_ref), channel_id=1, source_target_pairs={{0,8},{2,10},{4,12},{6,14},{8,0},{10,2},{12,4},{14,6},{16,24},{18,... | collective-permute-start | bytes 393224 | tf_op jit(solution)/shard_map/ppermute | solution.py:437
  7.1 8.9 %collective-permute-start = (bf16[128,512]{1,0:T(8,128)(2,1)}, bf16[128,512]{1,0:T(8,128)(2,1)S(1)}, u32[]{:S(2)}, u32[]{:S(2)}) collective-permute-start(bf16[128,512]{1,0:T(8,128)(2,1)} %get-tuple-element.45.kv_ref), channel_id=1, source_target_pairs={{0,16},{2,18},{4,20},{6,22},{8,24},{10,26},{12,28},{14,30},{16,0},... | collective-permute-start | bytes 393224 | tf_op jit(solution)/shard_map/ppermute | solution.py:437
  9.7 10.0 %collective-permute-start.3 = (bf16[128,512]{1,0:T(8,128)(2,1)}, bf16[128,512]{1,0:T(8,128)(2,1)S(1)}, u32[]{:S(2)}, u32[]{:S(2)}) collective-permute-start(bf16[128,512]{1,0:T(8,128)(2,1)} %get-tuple-element.45.kv_ref), channel_id=1, source_target_pairs={{0,4},{2,6},{4,0},{6,2},{8,12},{10,14},{12,8},{14,10},{16,20},{18,... | collective-permute-start | bytes 393224 | tf_op jit(solution)/shard_map/ppermute | solution.py:437
  12.6 7.1 %collective-permute-start.2 = (bf16[128,512]{1,0:T(8,128)(2,1)S(1)}, bf16[128,512]{1,0:T(8,128)(2,1)S(1)}, u32[]{:S(2)}, u32[]{:S(2)}) collective-permute-start(bf16[128,512]{1,0:T(8,128)(2,1)S(1)} %collective-permute-done.1.refs_2_), channel_id=1, source_target_pairs={{0,4},{2,6},{4,0},{6,2},{8,12},{10,14},{12,8},{14,10},{16,20},{18,... | collective-permute-start | bytes 393224 | tf_op jit(solution)/shard_map/ppermute | solution.py:437
  14.4 0.9 %copy-start.8 = (bf16[128,512]{1,0:T(8,128)(2,1)S(1)}, bf16[128,512]{1,0:T(8,128)(2,1)}, u32[]{:S(2)}) copy-start(bf16[128,512]{1,0:T(8,128)(2,1)} %get-tuple-element.45.kv_ref) | copy-start | bytes 393220
  16.6 11.8 %copy-start = (bf16[512,2048]{1,0:T(8,128)(2,1)S(1)}, bf16[512,2048]{1,0:T(8,128)(2,1)}, u32[]{:S(2)}) copy-start(bf16[512,2048]{1,0:T(8,128)(2,1)} %wo_ref.3) | copy-start | bytes 6291460
  16.6 3.6 %collective-permute-start.7 = (bf16[128,512]{1,0:T(8,128)(2,1)S(1)}, bf16[128,512]{1,0:T(8,128)(2,1)S(1)}, u32[]{:S(2)}, u32[]{:S(2)}) collective-permute-start(bf16[128,512]{1,0:T(8,128)(2,1)S(1)} %query.1.q_ref), channel_id=1, source_target_pairs={{0,2},{2,0},{4,6},{6,4},{8,10},{10,8},{12,14},{14,12},{16,18},{18,... | collective-permute-start | bytes 393224 | tf_op jit(solution)/shard_map/ppermute | solution.py:437
  16.7 7.3 %collective-permute-start.4 = (bf16[128,512]{1,0:T(8,128)(2,1)S(1)}, bf16[128,512]{1,0:T(8,128)(2,1)S(1)}, u32[]{:S(2)}, u32[]{:S(2)}) collective-permute-start(bf16[128,512]{1,0:T(8,128)(2,1)S(1)} %collective-permute-done.refs_3_), channel_id=1, source_target_pairs={{0,12},{2,14},{4,8},{6,10},{8,4},{10,6},{12,0},{14,2},{16,28},{18,... | collective-permute-start | bytes 393224 | tf_op jit(solution)/shard_map/ppermute | solution.py:437
  18.1 8.3 %collective-permute-start.5 = (bf16[128,512]{1,0:T(8,128)(2,1)S(1)}, bf16[128,512]{1,0:T(8,128)(2,1)S(1)}, u32[]{:S(2)}, u32[]{:S(2)}) collective-permute-start(bf16[128,512]{1,0:T(8,128)(2,1)S(1)} %collective-permute-done.refs_3_), channel_id=1, source_target_pairs={{0,8},{2,10},{4,12},{6,14},{8,0},{10,2},{12,4},{14,6},{16,24},{18,... | collective-permute-start | bytes 393224 | tf_op jit(solution)/shard_map/ppermute | solution.py:437
  19.7 6.7 %collective-permute-start.6 = (bf16[128,512]{1,0:T(8,128)(2,1)S(1)}, bf16[128,512]{1,0:T(8,128)(2,1)S(1)}, u32[]{:S(2)}, u32[]{:S(2)}) collective-permute-start(bf16[128,512]{1,0:T(8,128)(2,1)S(1)} %collective-permute-done.refs_3_), channel_id=1, source_target_pairs={{0,4},{2,6},{4,0},{6,2},{8,12},{10,14},{12,8},{14,10},{16,20},{18,... | collective-permute-start | bytes 393224 | tf_op jit(solution)/shard_map/ppermute | solution.py:437
  25.6 2.3 %collective-permute-start.9 = (bf16[128,640]{1,0:T(8,128)(2,1)S(1)}, bf16[128,640]{1,0:T(8,128)(2,1)S(1)}, u32[]{:S(2)}, u32[]{:S(2)}) collective-permute-start(bf16[128,640]{1,0:T(8,128)(2,1)S(1)} %get-tuple-element.66), channel_id=1, source_target_pairs={{0,2},{2,0},{4,6},{6,4},{8,10},{10,8},{12,14},{14,12},{16,18},{18,... | collective-permute-start | bytes 491528 | tf_op jit(solution)/shard_map/ppermute | solution.py:437
  27.1 5.0 %copy-start.6 = (s32[64]{0:T(128)S(1)}, s32[64]{0:T(128)}, u32[]{:S(2)}) copy-start(s32[64]{0:T(128)} %slot_ref.1) | copy-start | bytes 772
  27.1 1.3 %collective-permute-start.10 = (bf16[64,640]{1,0:T(8,128)(2,1)S(1)}, bf16[64,640]{1,0:T(8,128)(2,1)S(1)}, u32[]{:S(2)}, u32[]{:S(2)}) collective-permute-start(bf16[64,640]{1,0:T(8,128)(2,1)S(1)} %get-tuple-element.71), channel_id=1, source_target_pairs={{0,2},{2,0},{4,6},{6,4},{8,10},{10,8},{12,14},{14,12},{16,18},{18,... | collective-permute-start | bytes 245768 | tf_op jit(solution)/shard_map/ppermute | solution.py:437
  27.9 7.4 %copy-start.2 = (bf16[128,2048]{1,0:T(8,128)(2,1)S(1)}, bf16[128,2048]{1,0:T(8,128)(2,1)}, u32[]{:S(2)}) copy-start(bf16[128,2048]{1,0:T(8,128)(2,1)} %tok_ref.1) | copy-start | bytes 1572868
  29.3 8.4 %collective-permute-start.13 = (bf16[64,2048]{1,0:T(8,128)(2,1)S(1)}, bf16[64,2048]{1,0:T(8,128)(2,1)S(1)}, u32[]{:S(2)}, u32[]{:S(2)}) collective-permute-start(bf16[64,2048]{1,0:T(8,128)(2,1)S(1)} %leave.1), channel_id=1, source_target_pairs={{0,1},{1,0},{2,3},{3,2},{4,5},{5,4},{6,7},{7,6},{8,9},{9,8},{10,11... | collective-permute-start | bytes 786440 | tf_op jit(solution)/shard_map/ppermute | solution.py:607
  30.8 1.3 %collective-permute-start.8 = (bf16[64,640]{1,0:T(8,128)(2,1)S(1)}, bf16[64,640]{1,0:T(8,128)(2,1)S(1)}, u32[]{:S(2)}, u32[]{:S(2)}) collective-permute-start(bf16[64,640]{1,0:T(8,128)(2,1)S(1)} %get-tuple-element.63), channel_id=1, source_target_pairs={{0,2},{2,0},{4,6},{6,4},{8,10},{10,8},{12,14},{14,12},{16,18},{18,... | collective-permute-start | bytes 245768 | tf_op jit(solution)/shard_map/ppermute | solution.py:437
  33.7 1.4 %collective-permute-start.11 = (bf16[4,2,32,256]{3,2,1,0:T(8,128)(2,1)S(1)}, bf16[4,2,32,256]{3,2,1,0:T(8,128)(2,1)S(1)}, u32[]{:S(2)}, u32[]{:S(2)}) collective-permute-start(bf16[4,2,32,256]{3,2,1,0:T(8,128)(2,1)S(1)} %get-tuple-element.81), channel_id=1, source_target_pairs={{0,2},{2,0},{4,6},{6,4},{8,10},{10,8},{12,14},{14,12},{16,18},{18,... | collective-permute-start | bytes 393224 | tf_op jit(solution)/shard_map/ppermute | solution.py:437
  34.0 1.4 %collective-permute-start.12 = (bf16[4,2,32,256]{3,2,1,0:T(8,128)(2,1)S(1)}, bf16[4,2,32,256]{3,2,1,0:T(8,128)(2,1)S(1)}, u32[]{:S(2)}, u32[]{:S(2)}) collective-permute-start(bf16[4,2,32,256]{3,2,1,0:T(8,128)(2,1)S(1)} %get-tuple-element.82), channel_id=1, source_target_pairs={{0,2},{2,0},{4,6},{6,4},{8,10},{10,8},{12,14},{14,12},{16,18},{18,... | collective-permute-start | bytes 393224 | tf_op jit(solution)/shard_map/ppermute | solution.py:437

commit v17 on v16

--- a/solution.py
+++ b/solution.py
@@ -571,13 +571,13 @@
         own = Piece([kv], at_distance(0))
         second, first, beside = swapped(own, 8), swapped(own, 4), swapped(own, 2)
         first_across = swapped(first, 2)
-        second, staged = tied(second, staged)
+        first, normed = tied(first, normed)
+        queries, far_queries = project_queries(normed)
+        second, (staged, queries) = tied(second, (staged, queries))
         own = own.moved([staged])
         third = swapped(second, 4)
         last = swapped(second, 6)
-        second, normed = tied(second, normed)
         (second, first_across, beside), _ = tied_all([second, first_across, beside], ())
-        queries, far_queries = project_queries(normed)
         early = [own, beside, first, second, first_across, last]
         partials = attend(queries, far_queries, early)
         partials[2] = swap(partials[2], n, 1)

time: 38.6 us -> 38 us (0.984)
  waiting for transfers between devices: 10.2 us -> 9.53 us
    ppermute x13, waiting for transfers between devices: 9.26 us -> 8.62 us  [swap(): return lax.ppermute(x, 'seq', [(i, i ^ bit) for i in range(n)])]
  transfers between devices with their start and end apart: 14 -> 14, of which waited for: 9 -> 8; matrix products, arithmetic and copies ran while one was open for 0% -> 0% of each run, Pallas kernels for 17% -> 18%
where the time goes in v17:
time: 38 us; the launch traced here: 37.8 us
  starting transfers between devices  14.9 us (39%)
  Pallas kernels  11.6 us (31%)
  waiting for transfers between devices  9.53 us (25%)
  local copies, waits for them, and re-layouts  0.95 us (2%)
  between operations  0.83 us (2%)
    ppermute x13, starting transfers between devices, swap(): return lax.ppermute(x, 'seq', [(i, i ^ bit) for i in range(n)])  13.4 us
    ppermute x13, waiting for transfers between devices, swap(): return lax.ppermute(x, 'seq', [(i, i ^ bit) for i in range(n)])  8.62 us
    pallas_call x1, Pallas kernels, on_device(): pl.pallas_call(project_kernel, out_shape=(struct((rows, kv_width), bf16),...  3.32 us
    pallas_call x3, Pallas kernels, attend(): pl.pallas_call(functools.partial(attend_kernel, pieces, side), out_shape=...  3 us
    pallas_call x1, Pallas kernels, place_pages(): pl.pallas_call(functools.partial(cache_kernel, pieces), out_shape=(struct...  1.6 us
    ppermute x1, starting transfers between devices, on_device(): lax.ppermute(sent, 'req', [(i, (i + 1) % parts) for i in range(parts)])  1.59 us
    pallas_call x1, Pallas kernels, on_device(): pl.pallas_call(keep_kernel, out_shape=(struct((half, width), f32), struct...  1.44 us
    unnamed x18, local copies, waits for them, and re-layouts  0.95 us
  transfers between devices with their start and end apart: 14, of which 8 were waited for; matrix products, arithmetic and copies ran while one was open for 0% of the time, Pallas kernels for 18%

profile of v17, /device:TPU:0, one launch (start us, length us, event | category | flops | bytes accessed | tf_op | source)
XLA Modules:
  0.0 37.8 jit_solution(12886683507756693474)
XLA Ops:
  0.7 3.3 %project.1 = (bf16[128,512]{1,0:T(8,128)(2,1)}, bf16[128,2048]{1,0:T(8,128)(2,1)}, f32[128,256]{1,0:T(8,128)}) custom-call(s32[16]{0:T(128)} %block_ref.1, s32[4]{0:T(128)} %len_hbm.1, f32[136,128]{1,0:T(8,128)} %constant.2.clone.turn_hbm, bf16[128,2048]{1,0:T(8,128)(2,1)} %tok_ref.1, f32[1,2048]{1,0:T(1,128)} %bitcast.5, bf16[2048,256]{1,0:T(8,128)(2,1)} %wk_hbm.1, ...), custom_call_target="tpu_custom_call" | custom-call | tf_op jit(solution)/shard_map/project/pallas_call | solution.py:475
  4.0 3.1 %collective-permute-start.1 = (bf16[128,512]{1,0:T(8,128)(2,1)}, bf16[128,512]{1,0:T(8,128)(2,1)S(1)}, u32[]{:S(2)}, u32[]{:S(2)}) collective-permute-start(bf16[128,512]{1,0:T(8,128)(2,1)} %get-tuple-element.46.kv_ref), channel_id=1, source_target_pairs={{0,8},{2,10},{4,12},{6,14},{8,0},{10,2},{12,4},{14,6},{16,24},{18,... | collective-permute-start | bytes 393224 | tf_op jit(solution)/shard_map/ppermute | solution.py:437
  7.1 2.6 %collective-permute-start = (bf16[128,512]{1,0:T(8,128)(2,1)}, bf16[128,512]{1,0:T(8,128)(2,1)S(1)}, u32[]{:S(2)}, u32[]{:S(2)}) collective-permute-start(bf16[128,512]{1,0:T(8,128)(2,1)} %get-tuple-element.46.kv_ref), channel_id=1, source_target_pairs={{0,16},{2,18},{4,20},{6,22},{8,24},{10,26},{12,28},{14,30},{16,0},... | collective-permute-start | bytes 393224 | tf_op jit(solution)/shard_map/ppermute | solution.py:437
  9.7 1.5 %collective-permute-start.3 = (bf16[128,512]{1,0:T(8,128)(2,1)}, bf16[128,512]{1,0:T(8,128)(2,1)S(1)}, u32[]{:S(2)}, u32[]{:S(2)}) collective-permute-start(bf16[128,512]{1,0:T(8,128)(2,1)} %get-tuple-element.46.kv_ref), channel_id=1, source_target_pairs={{0,4},{2,6},{4,0},{6,2},{8,12},{10,14},{12,8},{14,10},{16,20},{18,... | collective-permute-start | bytes 393224 | tf_op jit(solution)/shard_map/ppermute | solution.py:437
  11.2 1.4 %collective-permute-done.1.refs_2_ = bf16[128,512]{1,0:T(8,128)(2,1)S(1)} collective-permute-done((bf16[128,512]{1,0:T(8,128)(2,1)}, bf16[128,512]{1,0:T(8,128)(2,1)S(1)}, u32[]{:S(2)}, u32[]{:S(2)}) %collective-permute-start.1) | collective-permute-done | bytes 131104 | tf_op jit(solution)/shard_map/ppermute | solution.py:437
  12.6 1.8 %collective-permute-start.2 = (bf16[128,512]{1,0:T(8,128)(2,1)S(1)}, bf16[128,512]{1,0:T(8,128)(2,1)S(1)}, u32[]{:S(2)}, u32[]{:S(2)}) collective-permute-start(bf16[128,512]{1,0:T(8,128)(2,1)S(1)} %collective-permute-done.1.refs_2_), channel_id=1, source_target_pairs={{0,4},{2,6},{4,0},{6,2},{8,12},{10,14},{12,8},{14,10},{16,20},{18,... | collective-permute-start | bytes 393224 | tf_op jit(solution)/shard_map/ppermute | solution.py:437
  14.4 0.9 %copy-done.8 = bf16[128,512]{1,0:T(8,128)(2,1)S(1)} copy-done((bf16[128,512]{1,0:T(8,128)(2,1)S(1)}, bf16[128,512]{1,0:T(8,128)(2,1)}, u32[]{:S(2)}) %copy-start.8) | copy-done | bytes 131096
  15.5 0.6 %query.1.q_ref = bf16[128,512]{1,0:T(8,128)(2,1)S(1)} custom-call(bf16[128,2048]{1,0:T(8,128)(2,1)S(1)} %copy-done.3, f32[128,256]{1,0:T(8,128)S(1)} %copy-done.4, bf16[2048,512]{1,0:T(8,128)(2,1)S(1)} %copy-done.1), custom_call_target="tpu_custom_call" | custom-call | tf_op jit(solution)/shard_map/query/pallas_call | solution.py:523
  16.2 1.2 %collective-permute-start.4 = (bf16[128,512]{1,0:T(8,128)(2,1)S(1)}, bf16[128,512]{1,0:T(8,128)(2,1)S(1)}, u32[]{:S(2)}, u32[]{:S(2)}) collective-permute-start(bf16[128,512]{1,0:T(8,128)(2,1)S(1)} %collective-permute-done.refs_3_), channel_id=1, source_target_pairs={{0,12},{2,14},{4,8},{6,10},{8,4},{10,6},{12,0},{14,2},{16,28},{18,... | collective-permute-start | bytes 393224 | tf_op jit(solution)/shard_map/ppermute | solution.py:437
  17.4 1.6 %collective-permute-start.5 = (bf16[128,512]{1,0:T(8,128)(2,1)S(1)}, bf16[128,512]{1,0:T(8,128)(2,1)S(1)}, u32[]{:S(2)}, u32[]{:S(2)}) collective-permute-start(bf16[128,512]{1,0:T(8,128)(2,1)S(1)} %collective-permute-done.refs_3_), channel_id=1, source_target_pairs={{0,8},{2,10},{4,12},{6,14},{8,0},{10,2},{12,4},{14,6},{16,24},{18,... | collective-permute-start | bytes 393224 | tf_op jit(solution)/shard_map/ppermute | solution.py:437
  19.0 0.7 %collective-permute-start.6 = (bf16[128,512]{1,0:T(8,128)(2,1)S(1)}, bf16[128,512]{1,0:T(8,128)(2,1)S(1)}, u32[]{:S(2)}, u32[]{:S(2)}) collective-permute-start(bf16[128,512]{1,0:T(8,128)(2,1)S(1)} %collective-permute-done.refs_3_), channel_id=1, source_target_pairs={{0,4},{2,6},{4,0},{6,2},{8,12},{10,14},{12,8},{14,10},{16,20},{18,... | collective-permute-start | bytes 393224 | tf_op jit(solution)/shard_map/ppermute | solution.py:437
  19.7 3.7 %collective-permute-done.4.refs_5_ = bf16[128,512]{1,0:T(8,128)(2,1)S(1)} collective-permute-done((bf16[128,512]{1,0:T(8,128)(2,1)S(1)}, bf16[128,512]{1,0:T(8,128)(2,1)S(1)}, u32[]{:S(2)}, u32[]{:S(2)}) %collective-permute-start.4) | collective-permute-done | bytes 131104 | tf_op jit(solution)/shard_map/ppermute | solution.py:437
  23.5 1.6 %attend.3 = (f32[128,512]{1,0:T(8,128)S(1)}, f32[128,128]{1,0:T(8,128)S(1)}, bf16[128,640]{1,0:T(8,128)(2,1)S(1)}) custom-call(s32[16,128]{1,0:T(8,128)S(1)} %get-tuple-element.57.key_pos_ref, s32[256,128]{1,0:T(8,128)S(1)} %get-tuple-element.58.q_pos_ref, s32[256,128]{1,0:T(8,128)S(1)} %get-tuple-element.59.q_begin_ref, bf16[128,512]{1,0:T(8,128)(2,1)S(1)} %query.1.q_ref, ...), custom_call_target="tpu_custom_call" | custom-call | tf_op jit(solution)/shard_map/attend/pallas_call | solution.py:537
  25.2 0.6 %collective-permute-done.6.refs_1_.refs_7_ = bf16[128,512]{1,0:T(8,128)(2,1)S(1)} collective-permute-done((bf16[128,512]{1,0:T(8,128)(2,1)S(1)}, bf16[128,512]{1,0:T(8,128)(2,1)S(1)}, u32[]{:S(2)}, u32[]{:S(2)}) %collective-permute-start.6) | collective-permute-done | bytes 131104 | tf_op jit(solution)/shard_map/ppermute | solution.py:437
  25.8 0.7 %attend.4 = (f32[64,512]{1,0:T(8,128)S(1)}, f32[64,128]{1,0:T(8,128)S(1)}, bf16[64,640]{1,0:T(8,128)(2,1)S(1)}) custom-call(s32[16,128]{1,0:T(8,128)S(1)} %get-tuple-element.57.key_pos_ref, s32[256,128]{1,0:T(8,128)S(1)} %get-tuple-element.58.q_pos_ref, s32[256,128]{1,0:T(8,128)S(1)} %get-tuple-element.59.q_begin_ref, bf16[128,512]{1,0:T(8,128)(2,1)S(1)} %query.1.q_ref, ...), custom_call_target="tpu_custom_call" | custom-call | tf_op jit(solution)/shard_map/attend/pallas_call | solution.py:537
  26.6 0.7 %attend.5 = (f32[64,512]{1,0:T(8,128)S(1)}, f32[64,128]{1,0:T(8,128)S(1)}, bf16[64,640]{1,0:T(8,128)(2,1)S(1)}) custom-call(s32[16,128]{1,0:T(8,128)S(1)} %get-tuple-element.57.key_pos_ref, s32[256,128]{1,0:T(8,128)S(1)} %get-tuple-element.58.q_pos_ref, s32[256,128]{1,0:T(8,128)S(1)} %get-tuple-element.59.q_begin_ref, bf16[128,512]{1,0:T(8,128)(2,1)S(1)} %query.1.q_ref, ...), custom_call_target="tpu_custom_call" | custom-call | tf_op jit(solution)/shard_map/attend/pallas_call | solution.py:537
  27.8 0.8 %leave.1 = bf16[64,2048]{1,0:T(8,128)(2,1)S(1)} custom-call(bf16[512,2048]{1,0:T(8,128)(2,1)S(1)} %copy-done, f32[128,512]{1,0:T(8,128)S(1)} %get-tuple-element.66.refs_0_.refs_2_, f32[128,128]{1,0:T(8,128)S(1)} %get-tuple-element.67.refs_1_.refs_3_, bf16[128,640]{1,0:T(8,128)(2,1)S(1)} %collective-permute-done.9.refs_2_.refs_4_, ...), custom_call_target="tpu_custom_call" | custom-call | tf_op jit(solution)/shard_map/leave/pallas_call | solution.py:598
  28.7 1.6 %collective-permute-start.13 = (bf16[64,2048]{1,0:T(8,128)(2,1)S(1)}, bf16[64,2048]{1,0:T(8,128)(2,1)S(1)}, u32[]{:S(2)}, u32[]{:S(2)}) collective-permute-start(bf16[64,2048]{1,0:T(8,128)(2,1)S(1)} %leave.1), channel_id=1, source_target_pairs={{0,1},{1,0},{2,3},{3,2},{4,5},{5,4},{6,7},{7,6},{8,9},{9,8},{10,11... | collective-permute-start | bytes 786440 | tf_op jit(solution)/shard_map/ppermute | solution.py:607
  30.2 1.3 %collective-permute-done.8.refs_7_ = bf16[64,640]{1,0:T(8,128)(2,1)S(1)} collective-permute-done((bf16[64,640]{1,0:T(8,128)(2,1)S(1)}, bf16[64,640]{1,0:T(8,128)(2,1)S(1)}, u32[]{:S(2)}, u32[]{:S(2)}) %collective-permute-start.8) | collective-permute-done | bytes 81952 | tf_op jit(solution)/shard_map/ppermute | solution.py:437
  31.5 1.6 %cache.1 = (bf16[8,2,32,256]{3,2,1,0:T(8,128)(2,1)S(1)}, bf16[4,2,32,256]{3,2,1,0:T(8,128)(2,1)S(1)}, bf16[4,2,32,256]{3,2,1,0:T(8,128)(2,1)S(1)}) custom-call(s32[16]{0:T(128)S(1)} %copy-done.5, s32[64]{0:T(128)S(1)} %copy-done.6, bf16[128,512]{1,0:T(8,128)(2,1)S(1)} %get-tuple-element.74.refs_0_, bf16[128,512]{1,0:T(8,128)(2,1)S(1)} %collective-permute-done.3.refs_1_, ...), custom_call_target="tpu_custom_call" | custom-call | tf_op jit(solution)/shard_map/cache/pallas_call | solution.py:555
  33.7 0.8 %collective-permute-done.11.refs_0_ = bf16[4,2,32,256]{3,2,1,0:T(8,128)(2,1)S(1)} collective-permute-done((bf16[4,2,32,256]{3,2,1,0:T(8,128)(2,1)S(1)}, bf16[4,2,32,256]{3,2,1,0:T(8,128)(2,1)S(1)}, u32[]{:S(2)}, u32[]{:S(2)}) %collective-permute-start.11) | collective-permute-done | bytes 131104 | tf_op jit(solution)/shard_map/ppermute | solution.py:437
  34.7 1.4 %keep.1 = (f32[64,2048]{1,0:T(8,128)S(1)}, bf16[8,2,32,256]{3,2,1,0:T(8,128)(2,1)}) custom-call(bf16[512,2048]{1,0:T(8,128)(2,1)S(1)} %copy-done, bf16[128,2048]{1,0:T(8,128)(2,1)S(1)} %copy-done.2, bf16[8,2,32,256]{3,2,1,0:T(8,128)(2,1)S(1)} %get-tuple-element.82.mine_ref, bf16[4,2,32,256]{3,2,1,0:T(8,128)(2,1)S(1)} %collective-permute-done.11.refs_0_, ...), custom_call_target="tpu_custom_call" | custom-call | tf_op jit(solution)/shard_map/keep/pallas_call | solution.py:611
  36.2 0.9 %collective-permute-done.13.received_ref = bf16[64,2048]{1,0:T(8,128)(2,1)S(1)} collective-permute-done((bf16[64,2048]{1,0:T(8,128)(2,1)S(1)}, bf16[64,2048]{1,0:T(8,128)(2,1)S(1)}, u32[]{:S(2)}, u32[]{:S(2)}) %collective-permute-start.13) | collective-permute-done | bytes 262176 | tf_op jit(solution)/shard_map/ppermute | solution.py:607
  37.1 0.8 %finish.1 = bf16[64,2048]{1,0:T(8,128)(2,1)} custom-call(f32[64,2048]{1,0:T(8,128)S(1)} %get-tuple-element.88.kept_ref, bf16[64,2048]{1,0:T(8,128)(2,1)S(1)} %collective-permute-done.13.received_ref), custom_call_target="tpu_custom_call" | custom-call | tf_op jit(solution)/shard_map/finish/pallas_call | solution.py:620
  (32 shorter events, 1.7 us)
Async XLA Ops:
  0.6 13.8 %copy-start.5 = (s32[16]{0:T(128)S(1)}, s32[16]{0:T(128)}, u32[]{:S(2)}) copy-start(s32[16]{0:T(128)} %block_ref.1) | copy-start | bytes 196
  0.6 13.8 %copy-start.7 = (s32[4]{0:T(128)S(1)}, s32[4]{0:T(128)}, u32[]{:S(2)}) copy-start(s32[4]{0:T(128)} %len_hbm.1) | copy-start | bytes 52
  4.0 11.5 %copy-start.1 = (bf16[2048,512]{1,0:T(8,128)(2,1)S(1)}, bf16[2048,512]{1,0:T(8,128)(2,1)}, u32[]{:S(2)}) copy-start(bf16[2048,512]{1,0:T(8,128)(2,1)} %wq_ref.1) | copy-start | bytes 6291460
  4.0 11.5 %copy-start.3 = (bf16[128,2048]{1,0:T(8,128)(2,1)S(1)}, bf16[128,2048]{1,0:T(8,128)(2,1)}, u32[]{:S(2)}) copy-start(bf16[128,2048]{1,0:T(8,128)(2,1)} %get-tuple-element.49.normed_ref) | copy-start | bytes 1572868
  4.0 11.5 %copy-start.4 = (f32[128,256]{1,0:T(8,128)S(1)}, f32[128,256]{1,0:T(8,128)}, u32[]{:S(2)}) copy-start(f32[128,256]{1,0:T(8,128)} %get-tuple-element.50.turned_ref) | copy-start | bytes 393220
  4.0 8.6 %collective-permute-start.1 = (bf16[128,512]{1,0:T(8,128)(2,1)}, bf16[128,512]{1,0:T(8,128)(2,1)S(1)}, u32[]{:S(2)}, u32[]{:S(2)}) collective-permute-start(bf16[128,512]{1,0:T(8,128)(2,1)} %get-tuple-element.46.kv_ref), channel_id=1, source_target_pairs={{0,8},{2,10},{4,12},{6,14},{8,0},{10,2},{12,4},{14,6},{16,24},{18,... | collective-permute-start | bytes 393224 | tf_op jit(solution)/shard_map/ppermute | solution.py:437
  7.1 9.1 %collective-permute-start = (bf16[128,512]{1,0:T(8,128)(2,1)}, bf16[128,512]{1,0:T(8,128)(2,1)S(1)}, u32[]{:S(2)}, u32[]{:S(2)}) collective-permute-start(bf16[128,512]{1,0:T(8,128)(2,1)} %get-tuple-element.46.kv_ref), channel_id=1, source_target_pairs={{0,16},{2,18},{4,20},{6,22},{8,24},{10,26},{12,28},{14,30},{16,0},... | collective-permute-start | bytes 393224 | tf_op jit(solution)/shard_map/ppermute | solution.py:437
  9.7 9.3 %collective-permute-start.3 = (bf16[128,512]{1,0:T(8,128)(2,1)}, bf16[128,512]{1,0:T(8,128)(2,1)S(1)}, u32[]{:S(2)}, u32[]{:S(2)}) collective-permute-start(bf16[128,512]{1,0:T(8,128)(2,1)} %get-tuple-element.46.kv_ref), channel_id=1, source_target_pairs={{0,4},{2,6},{4,0},{6,2},{8,12},{10,14},{12,8},{14,10},{16,20},{18,... | collective-permute-start | bytes 393224 | tf_op jit(solution)/shard_map/ppermute | solution.py:437
  12.6 6.4 %collective-permute-start.2 = (bf16[128,512]{1,0:T(8,128)(2,1)S(1)}, bf16[128,512]{1,0:T(8,128)(2,1)S(1)}, u32[]{:S(2)}, u32[]{:S(2)}) collective-permute-start(bf16[128,512]{1,0:T(8,128)(2,1)S(1)} %collective-permute-done.1.refs_2_), channel_id=1, source_target_pairs={{0,4},{2,6},{4,0},{6,2},{8,12},{10,14},{12,8},{14,10},{16,20},{18,... | collective-permute-start | bytes 393224 | tf_op jit(solution)/shard_map/ppermute | solution.py:437
  14.4 0.9 %copy-start.8 = (bf16[128,512]{1,0:T(8,128)(2,1)S(1)}, bf16[128,512]{1,0:T(8,128)(2,1)}, u32[]{:S(2)}) copy-start(bf16[128,512]{1,0:T(8,128)(2,1)} %get-tuple-element.46.kv_ref) | copy-start | bytes 393220
  16.1 11.8 %copy-start = (bf16[512,2048]{1,0:T(8,128)(2,1)S(1)}, bf16[512,2048]{1,0:T(8,128)(2,1)}, u32[]{:S(2)}) copy-start(bf16[512,2048]{1,0:T(8,128)(2,1)} %wo_ref.3) | copy-start | bytes 6291460
  16.1 3.7 %collective-permute-start.7 = (bf16[128,512]{1,0:T(8,128)(2,1)S(1)}, bf16[128,512]{1,0:T(8,128)(2,1)S(1)}, u32[]{:S(2)}, u32[]{:S(2)}) collective-permute-start(bf16[128,512]{1,0:T(8,128)(2,1)S(1)} %query.1.q_ref), channel_id=1, source_target_pairs={{0,2},{2,0},{4,6},{6,4},{8,10},{10,8},{12,14},{14,12},{16,18},{18,... | collective-permute-start | bytes 393224 | tf_op jit(solution)/shard_map/ppermute | solution.py:437
  16.2 7.3 %collective-permute-start.4 = (bf16[128,512]{1,0:T(8,128)(2,1)S(1)}, bf16[128,512]{1,0:T(8,128)(2,1)S(1)}, u32[]{:S(2)}, u32[]{:S(2)}) collective-permute-start(bf16[128,512]{1,0:T(8,128)(2,1)S(1)} %collective-permute-done.refs_3_), channel_id=1, source_target_pairs={{0,12},{2,14},{4,8},{6,10},{8,4},{10,6},{12,0},{14,2},{16,28},{18,... | collective-permute-start | bytes 393224 | tf_op jit(solution)/shard_map/ppermute | solution.py:437
  17.4 7.8 %collective-permute-start.5 = (bf16[128,512]{1,0:T(8,128)(2,1)S(1)}, bf16[128,512]{1,0:T(8,128)(2,1)S(1)}, u32[]{:S(2)}, u32[]{:S(2)}) collective-permute-start(bf16[128,512]{1,0:T(8,128)(2,1)S(1)} %collective-permute-done.refs_3_), channel_id=1, source_target_pairs={{0,8},{2,10},{4,12},{6,14},{8,0},{10,2},{12,4},{14,6},{16,24},{18,... | collective-permute-start | bytes 393224 | tf_op jit(solution)/shard_map/ppermute | solution.py:437
  19.0 6.8 %collective-permute-start.6 = (bf16[128,512]{1,0:T(8,128)(2,1)S(1)}, bf16[128,512]{1,0:T(8,128)(2,1)S(1)}, u32[]{:S(2)}, u32[]{:S(2)}) collective-permute-start(bf16[128,512]{1,0:T(8,128)(2,1)S(1)} %collective-permute-done.refs_3_), channel_id=1, source_target_pairs={{0,4},{2,6},{4,0},{6,2},{8,12},{10,14},{12,8},{14,10},{16,20},{18,... | collective-permute-start | bytes 393224 | tf_op jit(solution)/shard_map/ppermute | solution.py:437
  25.1 2.2 %collective-permute-start.9 = (bf16[128,640]{1,0:T(8,128)(2,1)S(1)}, bf16[128,640]{1,0:T(8,128)(2,1)S(1)}, u32[]{:S(2)}, u32[]{:S(2)}) collective-permute-start(bf16[128,640]{1,0:T(8,128)(2,1)S(1)} %get-tuple-element.68), channel_id=1, source_target_pairs={{0,2},{2,0},{4,6},{6,4},{8,10},{10,8},{12,14},{14,12},{16,18},{18,... | collective-permute-start | bytes 491528 | tf_op jit(solution)/shard_map/ppermute | solution.py:437
  26.5 5.0 %copy-start.6 = (s32[64]{0:T(128)S(1)}, s32[64]{0:T(128)}, u32[]{:S(2)}) copy-start(s32[64]{0:T(128)} %slot_ref.1) | copy-start | bytes 772
  26.5 1.3 %collective-permute-start.10 = (bf16[64,640]{1,0:T(8,128)(2,1)S(1)}, bf16[64,640]{1,0:T(8,128)(2,1)S(1)}, u32[]{:S(2)}, u32[]{:S(2)}) collective-permute-start(bf16[64,640]{1,0:T(8,128)(2,1)S(1)} %get-tuple-element.73), channel_id=1, source_target_pairs={{0,2},{2,0},{4,6},{6,4},{8,10},{10,8},{12,14},{14,12},{16,18},{18,... | collective-permute-start | bytes 245768 | tf_op jit(solution)/shard_map/ppermute | solution.py:437
  27.3 7.5 %copy-start.2 = (bf16[128,2048]{1,0:T(8,128)(2,1)S(1)}, bf16[128,2048]{1,0:T(8,128)(2,1)}, u32[]{:S(2)}) copy-start(bf16[128,2048]{1,0:T(8,128)(2,1)} %tok_ref.1) | copy-start | bytes 1572868
  28.7 8.4 %collective-permute-start.13 = (bf16[64,2048]{1,0:T(8,128)(2,1)S(1)}, bf16[64,2048]{1,0:T(8,128)(2,1)S(1)}, u32[]{:S(2)}, u32[]{:S(2)}) collective-permute-start(bf16[64,2048]{1,0:T(8,128)(2,1)S(1)} %leave.1), channel_id=1, source_target_pairs={{0,1},{1,0},{2,3},{3,2},{4,5},{5,4},{6,7},{7,6},{8,9},{9,8},{10,11... | collective-permute-start | bytes 786440 | tf_op jit(solution)/shard_map/ppermute | solution.py:607
  30.2 1.3 %collective-permute-start.8 = (bf16[64,640]{1,0:T(8,128)(2,1)S(1)}, bf16[64,640]{1,0:T(8,128)(2,1)S(1)}, u32[]{:S(2)}, u32[]{:S(2)}) collective-permute-start(bf16[64,640]{1,0:T(8,128)(2,1)S(1)} %get-tuple-element.65), channel_id=1, source_target_pairs={{0,2},{2,0},{4,6},{6,4},{8,10},{10,8},{12,14},{14,12},{16,18},{18,... | collective-permute-start | bytes 245768 | tf_op jit(solution)/shard_map/ppermute | solution.py:437
  33.1 1.4 %collective-permute-start.11 = (bf16[4,2,32,256]{3,2,1,0:T(8,128)(2,1)S(1)}, bf16[4,2,32,256]{3,2,1,0:T(8,128)(2,1)S(1)}, u32[]{:S(2)}, u32[]{:S(2)}) collective-permute-start(bf16[4,2,32,256]{3,2,1,0:T(8,128)(2,1)S(1)} %get-tuple-element.83), channel_id=1, source_target_pairs={{0,2},{2,0},{4,6},{6,4},{8,10},{10,8},{12,14},{14,12},{16,18},{18,... | collective-permute-start | bytes 393224 | tf_op jit(solution)/shard_map/ppermute | solution.py:437
  33.3 1.4 %collective-permute-start.12 = (bf16[4,2,32,256]{3,2,1,0:T(8,128)(2,1)S(1)}, bf16[4,2,32,256]{3,2,1,0:T(8,128)(2,1)S(1)}, u32[]{:S(2)}, u32[]{:S(2)}) collective-permute-start(bf16[4,2,32,256]{3,2,1,0:T(8,128)(2,1)S(1)} %get-tuple-element.84), channel_id=1, source_target_pairs={{0,2},{2,0},{4,6},{6,4},{8,10},{10,8},{12,14},{14,12},{16,18},{18,... | collective-permute-start | bytes 393224 | tf_op jit(solution)/shard_map/ppermute | solution.py:437

commit v18 on v17

--- a/solution.py
+++ b/solution.py
@@ -571,18 +571,18 @@
         own = Piece([kv], at_distance(0))
         second, first, beside = swapped(own, 8), swapped(own, 4), swapped(own, 2)
         first_across = swapped(first, 2)
-        first, normed = tied(first, normed)
+        first, (normed, staged) = tied(first, (normed, staged))
         queries, far_queries = project_queries(normed)
         second, (staged, queries) = tied(second, (staged, queries))
         own = own.moved([staged])
         third = swapped(second, 4)
         last = swapped(second, 6)
         (second, first_across, beside), _ = tied_all([second, first_across, beside], ())
-        early = [own, beside, first, second, first_across, last]
+        early = [own, beside, first, second, first_across]
         partials = attend(queries, far_queries, early)
         partials[2] = swap(partials[2], n, 1)
         queries, partials[1] = lax.optimization_barrier((queries, partials[1]))
-        remaining = [third, swapped(second, 2)]
+        remaining = [third, last, swapped(second, 2)]
         placed = early + remaining
     else:
         same = [list(range(c, n, 2)) for c in range(2)]

time: 38 us -> 37.7 us (level)
  waiting for transfers between devices: 9.53 us -> 8.39 us
  starting transfers between devices: 14.9 us -> 15.8 us
    ppermute x13, waiting for transfers between devices: 8.62 us -> 7.48 us  [swap(): return lax.ppermute(x, 'seq', [(i, i ^ bit) for i in range(n)])]
    ppermute x13, starting transfers between devices: 13.4 us -> 14.2 us  [swap(): return lax.ppermute(x, 'seq', [(i, i ^ bit) for i in range(n)])]
where the time goes in v18:
time: 37.7 us; the launch traced here: 37.6 us
  starting transfers between devices  15.8 us (42%)
  Pallas kernels  11.6 us (31%)
  waiting for transfers between devices  8.39 us (22%)
  local copies, waits for them, and re-layouts  0.95 us (3%)
  between operations  0.83 us (2%)
    ppermute x13, starting transfers between devices, swap(): return lax.ppermute(x, 'seq', [(i, i ^ bit) for i in range(n)])  14.2 us
    ppermute x13, waiting for transfers between devices, swap(): return lax.ppermute(x, 'seq', [(i, i ^ bit) for i in range(n)])  7.48 us
    pallas_call x1, Pallas kernels, on_device(): pl.pallas_call(project_kernel, out_shape=(struct((rows, kv_width), bf16),...  3.32 us
    pallas_call x3, Pallas kernels, attend(): pl.pallas_call(functools.partial(attend_kernel, pieces, side), out_shape=...  3.01 us
    pallas_call x1, Pallas kernels, place_pages(): pl.pallas_call(functools.partial(cache_kernel, pieces), out_shape=(struct...  1.6 us
    ppermute x1, starting transfers between devices, on_device(): lax.ppermute(sent, 'req', [(i, (i + 1) % parts) for i in range(parts)])  1.59 us
    pallas_call x1, Pallas kernels, on_device(): pl.pallas_call(keep_kernel, out_shape=(struct((half, width), f32), struct...  1.44 us
    unnamed x18, local copies, waits for them, and re-layouts  0.95 us
  transfers between devices with their start and end apart: 14, of which 8 were waited for; matrix products, arithmetic and copies ran while one was open for 0% of the time, Pallas kernels for 18%

profile of v18, /device:TPU:0, one launch (start us, length us, event | category | flops | bytes accessed | tf_op | source)
XLA Modules:
  0.0 37.6 jit_solution(9634000109133228825)
XLA Ops:
  0.7 3.3 %project.1 = (bf16[128,512]{1,0:T(8,128)(2,1)}, bf16[128,2048]{1,0:T(8,128)(2,1)}, f32[128,256]{1,0:T(8,128)}) custom-call(s32[16]{0:T(128)} %block_ref.1, s32[4]{0:T(128)} %len_hbm.1, f32[136,128]{1,0:T(8,128)} %constant.2.clone.turn_hbm, bf16[128,2048]{1,0:T(8,128)(2,1)} %tok_ref.1, f32[1,2048]{1,0:T(1,128)} %bitcast.5, bf16[2048,256]{1,0:T(8,128)(2,1)} %wk_hbm.1, ...), custom_call_target="tpu_custom_call" | custom-call | tf_op jit(solution)/shard_map/project/pallas_call | solution.py:475
  4.0 3.1 %collective-permute-start.1 = (bf16[128,512]{1,0:T(8,128)(2,1)}, bf16[128,512]{1,0:T(8,128)(2,1)S(1)}, u32[]{:S(2)}, u32[]{:S(2)}) collective-permute-start(bf16[128,512]{1,0:T(8,128)(2,1)} %get-tuple-element.47.kv_ref), channel_id=1, source_target_pairs={{0,8},{2,10},{4,12},{6,14},{8,0},{10,2},{12,4},{14,6},{16,24},{18,... | collective-permute-start | bytes 393224 | tf_op jit(solution)/shard_map/ppermute | solution.py:437
  7.1 1.5 %collective-permute-start.3 = (bf16[128,512]{1,0:T(8,128)(2,1)}, bf16[128,512]{1,0:T(8,128)(2,1)S(1)}, u32[]{:S(2)}, u32[]{:S(2)}) collective-permute-start(bf16[128,512]{1,0:T(8,128)(2,1)} %get-tuple-element.47.kv_ref), channel_id=1, source_target_pairs={{0,4},{2,6},{4,0},{6,2},{8,12},{10,14},{12,8},{14,10},{16,20},{18,... | collective-permute-start | bytes 393224 | tf_op jit(solution)/shard_map/ppermute | solution.py:437
  8.6 2.6 %collective-permute-start = (bf16[128,512]{1,0:T(8,128)(2,1)}, bf16[128,512]{1,0:T(8,128)(2,1)S(1)}, u32[]{:S(2)}, u32[]{:S(2)}) collective-permute-start(bf16[128,512]{1,0:T(8,128)(2,1)} %get-tuple-element.47.kv_ref), channel_id=1, source_target_pairs={{0,16},{2,18},{4,20},{6,22},{8,24},{10,26},{12,28},{14,30},{16,0},... | collective-permute-start | bytes 393224 | tf_op jit(solution)/shard_map/ppermute | solution.py:437
  11.2 2.7 %collective-permute-start.2 = (bf16[128,512]{1,0:T(8,128)(2,1)S(1)}, bf16[128,512]{1,0:T(8,128)(2,1)S(1)}, u32[]{:S(2)}, u32[]{:S(2)}) collective-permute-start(bf16[128,512]{1,0:T(8,128)(2,1)S(1)} %collective-permute-done.1.refs_2_), channel_id=1, source_target_pairs={{0,4},{2,6},{4,0},{6,2},{8,12},{10,14},{12,8},{14,10},{16,20},{18,... | collective-permute-start | bytes 393224 | tf_op jit(solution)/shard_map/ppermute | solution.py:437
  13.9 0.9 %copy-done.8 = bf16[128,512]{1,0:T(8,128)(2,1)S(1)} copy-done((bf16[128,512]{1,0:T(8,128)(2,1)S(1)}, bf16[128,512]{1,0:T(8,128)(2,1)}, u32[]{:S(2)}) %copy-start.8) | copy-done | bytes 131096
  15.0 0.6 %query.1.q_ref = bf16[128,512]{1,0:T(8,128)(2,1)S(1)} custom-call(bf16[128,2048]{1,0:T(8,128)(2,1)S(1)} %copy-done.3, f32[128,256]{1,0:T(8,128)S(1)} %copy-done.4, bf16[2048,512]{1,0:T(8,128)(2,1)S(1)} %copy-done.1), custom_call_target="tpu_custom_call" | custom-call | tf_op jit(solution)/shard_map/query/pallas_call | solution.py:523
  15.7 1.5 %collective-permute-done.refs_3_ = bf16[128,512]{1,0:T(8,128)(2,1)S(1)} collective-permute-done((bf16[128,512]{1,0:T(8,128)(2,1)}, bf16[128,512]{1,0:T(8,128)(2,1)S(1)}, u32[]{:S(2)}, u32[]{:S(2)}) %collective-permute-start) | collective-permute-done | bytes 131104 | tf_op jit(solution)/shard_map/ppermute | solution.py:437
  17.4 1.8 %collective-permute-start.4 = (bf16[128,512]{1,0:T(8,128)(2,1)S(1)}, bf16[128,512]{1,0:T(8,128)(2,1)S(1)}, u32[]{:S(2)}, u32[]{:S(2)}) collective-permute-start(bf16[128,512]{1,0:T(8,128)(2,1)S(1)} %collective-permute-done.refs_3_), channel_id=1, source_target_pairs={{0,8},{2,10},{4,12},{6,14},{8,0},{10,2},{12,4},{14,6},{16,24},{18,... | collective-permute-start | bytes 393224 | tf_op jit(solution)/shard_map/ppermute | solution.py:437
  19.3 1.4 %collective-permute-start.6 = (bf16[128,512]{1,0:T(8,128)(2,1)S(1)}, bf16[128,512]{1,0:T(8,128)(2,1)S(1)}, u32[]{:S(2)}, u32[]{:S(2)}) collective-permute-start(bf16[128,512]{1,0:T(8,128)(2,1)S(1)} %collective-permute-done.refs_3_), channel_id=1, source_target_pairs={{0,4},{2,6},{4,0},{6,2},{8,12},{10,14},{12,8},{14,10},{16,20},{18,... | collective-permute-start | bytes 393224 | tf_op jit(solution)/shard_map/ppermute | solution.py:437
  20.7 1.4 %attend.3 = (f32[128,512]{1,0:T(8,128)S(1)}, f32[128,128]{1,0:T(8,128)S(1)}, bf16[128,640]{1,0:T(8,128)(2,1)S(1)}) custom-call(s32[16,128]{1,0:T(8,128)S(1)} %get-tuple-element.59.key_pos_ref, s32[256,128]{1,0:T(8,128)S(1)} %get-tuple-element.60.q_pos_ref, s32[256,128]{1,0:T(8,128)S(1)} %get-tuple-element.61.q_begin_ref, bf16[128,512]{1,0:T(8,128)(2,1)S(1)} %query.1.q_ref, ...), custom_call_target="tpu_custom_call" | custom-call | tf_op jit(solution)/shard_map/attend/pallas_call | solution.py:537
  22.2 1.9 %collective-permute-done.5.refs_1_.refs_6_ = bf16[128,512]{1,0:T(8,128)(2,1)S(1)} collective-permute-done((bf16[128,512]{1,0:T(8,128)(2,1)S(1)}, bf16[128,512]{1,0:T(8,128)(2,1)S(1)}, u32[]{:S(2)}, u32[]{:S(2)}) %collective-permute-start.5) | collective-permute-done | bytes 131104 | tf_op jit(solution)/shard_map/ppermute | solution.py:437
  24.1 1.3 %collective-permute-done.6.refs_2_.refs_7_ = bf16[128,512]{1,0:T(8,128)(2,1)S(1)} collective-permute-done((bf16[128,512]{1,0:T(8,128)(2,1)S(1)}, bf16[128,512]{1,0:T(8,128)(2,1)S(1)}, u32[]{:S(2)}, u32[]{:S(2)}) %collective-permute-start.6) | collective-permute-done | bytes 131104 | tf_op jit(solution)/shard_map/ppermute | solution.py:437
  25.4 0.8 %attend.4 = (f32[64,512]{1,0:T(8,128)S(1)}, f32[64,128]{1,0:T(8,128)S(1)}, bf16[64,640]{1,0:T(8,128)(2,1)S(1)}) custom-call(s32[16,128]{1,0:T(8,128)S(1)} %get-tuple-element.59.key_pos_ref, s32[256,128]{1,0:T(8,128)S(1)} %get-tuple-element.60.q_pos_ref, s32[256,128]{1,0:T(8,128)S(1)} %get-tuple-element.61.q_begin_ref, bf16[128,512]{1,0:T(8,128)(2,1)S(1)} %query.1.q_ref, ...), custom_call_target="tpu_custom_call" | custom-call | tf_op jit(solution)/shard_map/attend/pallas_call | solution.py:537
  26.3 0.8 %attend.5 = (f32[64,512]{1,0:T(8,128)S(1)}, f32[64,128]{1,0:T(8,128)S(1)}, bf16[64,640]{1,0:T(8,128)(2,1)S(1)}) custom-call(s32[16,128]{1,0:T(8,128)S(1)} %get-tuple-element.59.key_pos_ref, s32[256,128]{1,0:T(8,128)S(1)} %get-tuple-element.60.q_pos_ref, s32[256,128]{1,0:T(8,128)S(1)} %get-tuple-element.61.q_begin_ref, bf16[128,512]{1,0:T(8,128)(2,1)S(1)} %query.1.q_ref, ...), custom_call_target="tpu_custom_call" | custom-call | tf_op jit(solution)/shard_map/attend/pallas_call | solution.py:537
  27.1 0.4 %collective-permute-done.10.refs_5_ = bf16[64,640]{1,0:T(8,128)(2,1)S(1)} collective-permute-done((bf16[64,640]{1,0:T(8,128)(2,1)S(1)}, bf16[64,640]{1,0:T(8,128)(2,1)S(1)}, u32[]{:S(2)}, u32[]{:S(2)}) %collective-permute-start.10) | collective-permute-done | bytes 81952 | tf_op jit(solution)/shard_map/ppermute | solution.py:437
  27.6 0.8 %leave.1 = bf16[64,2048]{1,0:T(8,128)(2,1)S(1)} custom-call(bf16[512,2048]{1,0:T(8,128)(2,1)S(1)} %copy-done, f32[128,512]{1,0:T(8,128)S(1)} %get-tuple-element.68.refs_0_.refs_2_, f32[128,128]{1,0:T(8,128)S(1)} %get-tuple-element.69.refs_1_.refs_3_, bf16[128,640]{1,0:T(8,128)(2,1)S(1)} %collective-permute-done.9.refs_2_.refs_4_, ...), custom_call_target="tpu_custom_call" | custom-call | tf_op jit(solution)/shard_map/leave/pallas_call | solution.py:598
  28.4 1.6 %collective-permute-start.13 = (bf16[64,2048]{1,0:T(8,128)(2,1)S(1)}, bf16[64,2048]{1,0:T(8,128)(2,1)S(1)}, u32[]{:S(2)}, u32[]{:S(2)}) collective-permute-start(bf16[64,2048]{1,0:T(8,128)(2,1)S(1)} %leave.1), channel_id=1, source_target_pairs={{0,1},{1,0},{2,3},{3,2},{4,5},{5,4},{6,7},{7,6},{8,9},{9,8},{10,11... | collective-permute-start | bytes 786440 | tf_op jit(solution)/shard_map/ppermute | solution.py:607
  30.0 1.3 %collective-permute-done.8.refs_7_ = bf16[64,640]{1,0:T(8,128)(2,1)S(1)} collective-permute-done((bf16[64,640]{1,0:T(8,128)(2,1)S(1)}, bf16[64,640]{1,0:T(8,128)(2,1)S(1)}, u32[]{:S(2)}, u32[]{:S(2)}) %collective-permute-start.8) | collective-permute-done | bytes 81952 | tf_op jit(solution)/shard_map/ppermute | solution.py:437
  31.2 1.6 %cache.1 = (bf16[8,2,32,256]{3,2,1,0:T(8,128)(2,1)S(1)}, bf16[4,2,32,256]{3,2,1,0:T(8,128)(2,1)S(1)}, bf16[4,2,32,256]{3,2,1,0:T(8,128)(2,1)S(1)}) custom-call(s32[16]{0:T(128)S(1)} %copy-done.5, s32[64]{0:T(128)S(1)} %copy-done.6, bf16[128,512]{1,0:T(8,128)(2,1)S(1)} %get-tuple-element.76.refs_0_, bf16[128,512]{1,0:T(8,128)(2,1)S(1)} %collective-permute-done.3.refs_1_, ...), custom_call_target="tpu_custom_call" | custom-call | tf_op jit(solution)/shard_map/cache/pallas_call | solution.py:555
  33.4 0.8 %collective-permute-done.11.refs_0_ = bf16[4,2,32,256]{3,2,1,0:T(8,128)(2,1)S(1)} collective-permute-done((bf16[4,2,32,256]{3,2,1,0:T(8,128)(2,1)S(1)}, bf16[4,2,32,256]{3,2,1,0:T(8,128)(2,1)S(1)}, u32[]{:S(2)}, u32[]{:S(2)}) %collective-permute-start.11) | collective-permute-done | bytes 131104 | tf_op jit(solution)/shard_map/ppermute | solution.py:437
  34.5 1.4 %keep.1 = (f32[64,2048]{1,0:T(8,128)S(1)}, bf16[8,2,32,256]{3,2,1,0:T(8,128)(2,1)}) custom-call(bf16[512,2048]{1,0:T(8,128)(2,1)S(1)} %copy-done, bf16[128,2048]{1,0:T(8,128)(2,1)S(1)} %copy-done.2, bf16[8,2,32,256]{3,2,1,0:T(8,128)(2,1)S(1)} %get-tuple-element.84.mine_ref, bf16[4,2,32,256]{3,2,1,0:T(8,128)(2,1)S(1)} %collective-permute-done.11.refs_0_, ...), custom_call_target="tpu_custom_call" | custom-call | tf_op jit(solution)/shard_map/keep/pallas_call | solution.py:611
  35.9 0.9 %collective-permute-done.13.received_ref = bf16[64,2048]{1,0:T(8,128)(2,1)S(1)} collective-permute-done((bf16[64,2048]{1,0:T(8,128)(2,1)S(1)}, bf16[64,2048]{1,0:T(8,128)(2,1)S(1)}, u32[]{:S(2)}, u32[]{:S(2)}) %collective-permute-start.13) | collective-permute-done | bytes 262176 | tf_op jit(solution)/shard_map/ppermute | solution.py:607
  36.8 0.8 %finish.1 = bf16[64,2048]{1,0:T(8,128)(2,1)} custom-call(f32[64,2048]{1,0:T(8,128)S(1)} %get-tuple-element.90.kept_ref, bf16[64,2048]{1,0:T(8,128)(2,1)S(1)} %collective-permute-done.13.received_ref), custom_call_target="tpu_custom_call" | custom-call | tf_op jit(solution)/shard_map/finish/pallas_call | solution.py:620
  (32 shorter events, 1.4 us)
Async XLA Ops:
  0.6 13.3 %copy-start.5 = (s32[16]{0:T(128)S(1)}, s32[16]{0:T(128)}, u32[]{:S(2)}) copy-start(s32[16]{0:T(128)} %block_ref.1) | copy-start | bytes 196
  0.6 13.3 %copy-start.7 = (s32[4]{0:T(128)S(1)}, s32[4]{0:T(128)}, u32[]{:S(2)}) copy-start(s32[4]{0:T(128)} %len_hbm.1) | copy-start | bytes 52
  4.0 11.0 %copy-start.1 = (bf16[2048,512]{1,0:T(8,128)(2,1)S(1)}, bf16[2048,512]{1,0:T(8,128)(2,1)}, u32[]{:S(2)}) copy-start(bf16[2048,512]{1,0:T(8,128)(2,1)} %wq_ref.1) | copy-start | bytes 6291460
  4.0 11.0 %copy-start.3 = (bf16[128,2048]{1,0:T(8,128)(2,1)S(1)}, bf16[128,2048]{1,0:T(8,128)(2,1)}, u32[]{:S(2)}) copy-start(bf16[128,2048]{1,0:T(8,128)(2,1)} %get-tuple-element.51.normed_ref) | copy-start | bytes 1572868
  4.0 11.0 %copy-start.4 = (f32[128,256]{1,0:T(8,128)S(1)}, f32[128,256]{1,0:T(8,128)}, u32[]{:S(2)}) copy-start(f32[128,256]{1,0:T(8,128)} %get-tuple-element.52.turned_ref) | copy-start | bytes 393220
  4.0 7.2 %collective-permute-start.1 = (bf16[128,512]{1,0:T(8,128)(2,1)}, bf16[128,512]{1,0:T(8,128)(2,1)S(1)}, u32[]{:S(2)}, u32[]{:S(2)}) collective-permute-start(bf16[128,512]{1,0:T(8,128)(2,1)} %get-tuple-element.47.kv_ref), channel_id=1, source_target_pairs={{0,8},{2,10},{4,12},{6,14},{8,0},{10,2},{12,4},{14,6},{16,24},{18,... | collective-permute-start | bytes 393224 | tf_op jit(solution)/shard_map/ppermute | solution.py:437
  7.1 12.1 %collective-permute-start.3 = (bf16[128,512]{1,0:T(8,128)(2,1)}, bf16[128,512]{1,0:T(8,128)(2,1)S(1)}, u32[]{:S(2)}, u32[]{:S(2)}) collective-permute-start(bf16[128,512]{1,0:T(8,128)(2,1)} %get-tuple-element.47.kv_ref), channel_id=1, source_target_pairs={{0,4},{2,6},{4,0},{6,2},{8,12},{10,14},{12,8},{14,10},{16,20},{18,... | collective-permute-start | bytes 393224 | tf_op jit(solution)/shard_map/ppermute | solution.py:437
  8.6 8.6 %collective-permute-start = (bf16[128,512]{1,0:T(8,128)(2,1)}, bf16[128,512]{1,0:T(8,128)(2,1)S(1)}, u32[]{:S(2)}, u32[]{:S(2)}) collective-permute-start(bf16[128,512]{1,0:T(8,128)(2,1)} %get-tuple-element.47.kv_ref), channel_id=1, source_target_pairs={{0,16},{2,18},{4,20},{6,22},{8,24},{10,26},{12,28},{14,30},{16,0},... | collective-permute-start | bytes 393224 | tf_op jit(solution)/shard_map/ppermute | solution.py:437
  11.2 8.1 %collective-permute-start.2 = (bf16[128,512]{1,0:T(8,128)(2,1)S(1)}, bf16[128,512]{1,0:T(8,128)(2,1)S(1)}, u32[]{:S(2)}, u32[]{:S(2)}) collective-permute-start(bf16[128,512]{1,0:T(8,128)(2,1)S(1)} %collective-permute-done.1.refs_2_), channel_id=1, source_target_pairs={{0,4},{2,6},{4,0},{6,2},{8,12},{10,14},{12,8},{14,10},{16,20},{18,... | collective-permute-start | bytes 393224 | tf_op jit(solution)/shard_map/ppermute | solution.py:437
  13.9 0.9 %copy-start.8 = (bf16[128,512]{1,0:T(8,128)(2,1)S(1)}, bf16[128,512]{1,0:T(8,128)(2,1)}, u32[]{:S(2)}) copy-start(bf16[128,512]{1,0:T(8,128)(2,1)} %get-tuple-element.47.kv_ref) | copy-start | bytes 393220
  15.6 12.0 %copy-start = (bf16[512,2048]{1,0:T(8,128)(2,1)S(1)}, bf16[512,2048]{1,0:T(8,128)(2,1)}, u32[]{:S(2)}) copy-start(bf16[512,2048]{1,0:T(8,128)(2,1)} %wo_ref.3) | copy-start | bytes 6291460
  15.6 5.1 %collective-permute-start.7 = (bf16[128,512]{1,0:T(8,128)(2,1)S(1)}, bf16[128,512]{1,0:T(8,128)(2,1)S(1)}, u32[]{:S(2)}, u32[]{:S(2)}) collective-permute-start(bf16[128,512]{1,0:T(8,128)(2,1)S(1)} %query.1.q_ref), channel_id=1, source_target_pairs={{0,2},{2,0},{4,6},{6,4},{8,10},{10,8},{12,14},{14,12},{16,18},{18,... | collective-permute-start | bytes 393224 | tf_op jit(solution)/shard_map/ppermute | solution.py:437
  17.2 6.9 %collective-permute-start.5 = (bf16[128,512]{1,0:T(8,128)(2,1)S(1)}, bf16[128,512]{1,0:T(8,128)(2,1)S(1)}, u32[]{:S(2)}, u32[]{:S(2)}) collective-permute-start(bf16[128,512]{1,0:T(8,128)(2,1)S(1)} %collective-permute-done.refs_3_), channel_id=1, source_target_pairs={{0,12},{2,14},{4,8},{6,10},{8,4},{10,6},{12,0},{14,2},{16,28},{18,... | collective-permute-start | bytes 393224 | tf_op jit(solution)/shard_map/ppermute | solution.py:437
  17.4 6.7 %collective-permute-start.4 = (bf16[128,512]{1,0:T(8,128)(2,1)S(1)}, bf16[128,512]{1,0:T(8,128)(2,1)S(1)}, u32[]{:S(2)}, u32[]{:S(2)}) collective-permute-start(bf16[128,512]{1,0:T(8,128)(2,1)S(1)} %collective-permute-done.refs_3_), channel_id=1, source_target_pairs={{0,8},{2,10},{4,12},{6,14},{8,0},{10,2},{12,4},{14,6},{16,24},{18,... | collective-permute-start | bytes 393224 | tf_op jit(solution)/shard_map/ppermute | solution.py:437
  19.3 6.1 %collective-permute-start.6 = (bf16[128,512]{1,0:T(8,128)(2,1)S(1)}, bf16[128,512]{1,0:T(8,128)(2,1)S(1)}, u32[]{:S(2)}, u32[]{:S(2)}) collective-permute-start(bf16[128,512]{1,0:T(8,128)(2,1)S(1)} %collective-permute-done.refs_3_), channel_id=1, source_target_pairs={{0,4},{2,6},{4,0},{6,2},{8,12},{10,14},{12,8},{14,10},{16,20},{18,... | collective-permute-start | bytes 393224 | tf_op jit(solution)/shard_map/ppermute | solution.py:437
  22.1 5.0 %collective-permute-start.9 = (bf16[128,640]{1,0:T(8,128)(2,1)S(1)}, bf16[128,640]{1,0:T(8,128)(2,1)S(1)}, u32[]{:S(2)}, u32[]{:S(2)}) collective-permute-start(bf16[128,640]{1,0:T(8,128)(2,1)S(1)} %get-tuple-element.70), channel_id=1, source_target_pairs={{0,2},{2,0},{4,6},{6,4},{8,10},{10,8},{12,14},{14,12},{16,18},{18,... | collective-permute-start | bytes 491528 | tf_op jit(solution)/shard_map/ppermute | solution.py:437
  26.2 5.0 %copy-start.6 = (s32[64]{0:T(128)S(1)}, s32[64]{0:T(128)}, u32[]{:S(2)}) copy-start(s32[64]{0:T(128)} %slot_ref.1) | copy-start | bytes 772
  26.2 1.3 %collective-permute-start.10 = (bf16[64,640]{1,0:T(8,128)(2,1)S(1)}, bf16[64,640]{1,0:T(8,128)(2,1)S(1)}, u32[]{:S(2)}, u32[]{:S(2)}) collective-permute-start(bf16[64,640]{1,0:T(8,128)(2,1)S(1)} %get-tuple-element.75), channel_id=1, source_target_pairs={{0,2},{2,0},{4,6},{6,4},{8,10},{10,8},{12,14},{14,12},{16,18},{18,... | collective-permute-start | bytes 245768 | tf_op jit(solution)/shard_map/ppermute | solution.py:437
  27.1 7.3 %copy-start.2 = (bf16[128,2048]{1,0:T(8,128)(2,1)S(1)}, bf16[128,2048]{1,0:T(8,128)(2,1)}, u32[]{:S(2)}) copy-start(bf16[128,2048]{1,0:T(8,128)(2,1)} %tok_ref.1) | copy-start | bytes 1572868
  28.4 8.4 %collective-permute-start.13 = (bf16[64,2048]{1,0:T(8,128)(2,1)S(1)}, bf16[64,2048]{1,0:T(8,128)(2,1)S(1)}, u32[]{:S(2)}, u32[]{:S(2)}) collective-permute-start(bf16[64,2048]{1,0:T(8,128)(2,1)S(1)} %leave.1), channel_id=1, source_target_pairs={{0,1},{1,0},{2,3},{3,2},{4,5},{5,4},{6,7},{7,6},{8,9},{9,8},{10,11... | collective-permute-start | bytes 786440 | tf_op jit(solution)/shard_map/ppermute | solution.py:607
  30.0 1.3 %collective-permute-start.8 = (bf16[64,640]{1,0:T(8,128)(2,1)S(1)}, bf16[64,640]{1,0:T(8,128)(2,1)S(1)}, u32[]{:S(2)}, u32[]{:S(2)}) collective-permute-start(bf16[64,640]{1,0:T(8,128)(2,1)S(1)} %get-tuple-element.67), channel_id=1, source_target_pairs={{0,2},{2,0},{4,6},{6,4},{8,10},{10,8},{12,14},{14,12},{16,18},{18,... | collective-permute-start | bytes 245768 | tf_op jit(solution)/shard_map/ppermute | solution.py:437
  32.8 1.4 %collective-permute-start.11 = (bf16[4,2,32,256]{3,2,1,0:T(8,128)(2,1)S(1)}, bf16[4,2,32,256]{3,2,1,0:T(8,128)(2,1)S(1)}, u32[]{:S(2)}, u32[]{:S(2)}) collective-permute-start(bf16[4,2,32,256]{3,2,1,0:T(8,128)(2,1)S(1)} %get-tuple-element.85), channel_id=1, source_target_pairs={{0,2},{2,0},{4,6},{6,4},{8,10},{10,8},{12,14},{14,12},{16,18},{18,... | collective-permute-start | bytes 393224 | tf_op jit(solution)/shard_map/ppermute | solution.py:437
  33.1 1.4 %collective-permute-start.12 = (bf16[4,2,32,256]{3,2,1,0:T(8,128)(2,1)S(1)}, bf16[4,2,32,256]{3,2,1,0:T(8,128)(2,1)S(1)}, u32[]{:S(2)}, u32[]{:S(2)}) collective-permute-start(bf16[4,2,32,256]{3,2,1,0:T(8,128)(2,1)S(1)} %get-tuple-element.86), channel_id=1, source_target_pairs={{0,2},{2,0},{4,6},{6,4},{8,10},{10,8},{12,14},{14,12},{16,18},{18,... | collective-permute-start | bytes 393224 | tf_op jit(solution)/shard_map/ppermute | solution.py:437

commit v19 on v18

--- a/solution.py
+++ b/solution.py
@@ -570,8 +570,8 @@
 
         own = Piece([kv], at_distance(0))
         second, first, beside = swapped(own, 8), swapped(own, 4), swapped(own, 2)
+        first, (normed, staged) = tied(first, (normed, staged))
         first_across = swapped(first, 2)
-        first, (normed, staged) = tied(first, (normed, staged))
         queries, far_queries = project_queries(normed)
         second, (staged, queries) = tied(second, (staged, queries))
         own = own.moved([staged])

time: 37.7 us -> 37.7 us (level)
  starting transfers between devices: 15.8 us -> 14.7 us
  waiting for transfers between devices: 8.39 us -> 9.45 us
    ppermute x13, starting transfers between devices: 14.2 us -> 13.1 us  [swap(): return lax.ppermute(x, 'seq', [(i, i ^ bit) for i in range(n)])]
    ppermute x13, waiting for transfers between devices: 7.48 us -> 8.55 us  [swap(): return lax.ppermute(x, 'seq', [(i, i ^ bit) for i in range(n)])]
where the time goes in v19:
time: 37.7 us; the launch traced here: 37.6 us
  starting transfers between devices  14.7 us (39%)
  Pallas kernels  11.6 us (31%)
  waiting for transfers between devices  9.45 us (25%)
  local copies, waits for them, and re-layouts  0.98 us (3%)
  between operations  0.81 us (2%)
    ppermute x13, starting transfers between devices, swap(): return lax.ppermute(x, 'seq', [(i, i ^ bit) for i in range(n)])  13.1 us
    ppermute x13, waiting for transfers between devices, swap(): return lax.ppermute(x, 'seq', [(i, i ^ bit) for i in range(n)])  8.55 us
    pallas_call x1, Pallas kernels, on_device(): pl.pallas_call(project_kernel, out_shape=(struct((rows, kv_width), bf16),...  3.32 us
    pallas_call x3, Pallas kernels, attend(): pl.pallas_call(functools.partial(attend_kernel, pieces, side), out_shape=...  3.01 us
    pallas_call x1, Pallas kernels, place_pages(): pl.pallas_call(functools.partial(cache_kernel, pieces), out_shape=(struct...  1.6 us
    ppermute x1, starting transfers between devices, on_device(): lax.ppermute(sent, 'req', [(i, (i + 1) % parts) for i in range(parts)])  1.59 us
    pallas_call x1, Pallas kernels, on_device(): pl.pallas_call(keep_kernel, out_shape=(struct((half, width), f32), struct...  1.44 us
    unnamed x18, local copies, waits for them, and re-layouts  0.98 us
  transfers between devices with their start and end apart: 14, of which 8 were waited for; matrix products, arithmetic and copies ran while one was open for 0% of the time, Pallas kernels for 18%

profile of v19, /device:TPU:0, one launch (start us, length us, event | category | flops | bytes accessed | tf_op | source)
XLA Modules:
  0.0 37.6 jit_solution(4982999126185689435)
XLA Ops:
  0.7 3.3 %project.1 = (bf16[128,512]{1,0:T(8,128)(2,1)}, bf16[128,2048]{1,0:T(8,128)(2,1)}, f32[128,256]{1,0:T(8,128)}) custom-call(s32[16]{0:T(128)} %block_ref.1, s32[4]{0:T(128)} %len_hbm.1, f32[136,128]{1,0:T(8,128)} %constant.2.clone.turn_hbm, bf16[128,2048]{1,0:T(8,128)(2,1)} %tok_ref.1, f32[1,2048]{1,0:T(1,128)} %bitcast.5, bf16[2048,256]{1,0:T(8,128)(2,1)} %wk_hbm.1, ...), custom_call_target="tpu_custom_call" | custom-call | tf_op jit(solution)/shard_map/project/pallas_call | solution.py:475
  4.0 3.1 %collective-permute-start.1 = (bf16[128,512]{1,0:T(8,128)(2,1)}, bf16[128,512]{1,0:T(8,128)(2,1)S(1)}, u32[]{:S(2)}, u32[]{:S(2)}) collective-permute-start(bf16[128,512]{1,0:T(8,128)(2,1)} %get-tuple-element.47.kv_ref), channel_id=1, source_target_pairs={{0,8},{2,10},{4,12},{6,14},{8,0},{10,2},{12,4},{14,6},{16,24},{18,... | collective-permute-start | bytes 393224 | tf_op jit(solution)/shard_map/ppermute | solution.py:437
  7.1 1.5 %collective-permute-start.3 = (bf16[128,512]{1,0:T(8,128)(2,1)}, bf16[128,512]{1,0:T(8,128)(2,1)S(1)}, u32[]{:S(2)}, u32[]{:S(2)}) collective-permute-start(bf16[128,512]{1,0:T(8,128)(2,1)} %get-tuple-element.47.kv_ref), channel_id=1, source_target_pairs={{0,4},{2,6},{4,0},{6,2},{8,12},{10,14},{12,8},{14,10},{16,20},{18,... | collective-permute-start | bytes 393224 | tf_op jit(solution)/shard_map/ppermute | solution.py:437
  8.6 2.6 %collective-permute-start = (bf16[128,512]{1,0:T(8,128)(2,1)}, bf16[128,512]{1,0:T(8,128)(2,1)S(1)}, u32[]{:S(2)}, u32[]{:S(2)}) collective-permute-start(bf16[128,512]{1,0:T(8,128)(2,1)} %get-tuple-element.47.kv_ref), channel_id=1, source_target_pairs={{0,16},{2,18},{4,20},{6,22},{8,24},{10,26},{12,28},{14,30},{16,0},... | collective-permute-start | bytes 393224 | tf_op jit(solution)/shard_map/ppermute | solution.py:437
  11.2 0.9 %copy-done.8 = bf16[128,512]{1,0:T(8,128)(2,1)S(1)} copy-done((bf16[128,512]{1,0:T(8,128)(2,1)S(1)}, bf16[128,512]{1,0:T(8,128)(2,1)}, u32[]{:S(2)}) %copy-start.8) | copy-done | bytes 131096
  12.3 1.7 %collective-permute-start.2 = (bf16[128,512]{1,0:T(8,128)(2,1)S(1)}, bf16[128,512]{1,0:T(8,128)(2,1)S(1)}, u32[]{:S(2)}, u32[]{:S(2)}) collective-permute-start(bf16[128,512]{1,0:T(8,128)(2,1)S(1)} %collective-permute-done.1.refs_2_), channel_id=1, source_target_pairs={{0,4},{2,6},{4,0},{6,2},{8,12},{10,14},{12,8},{14,10},{16,20},{18,... | collective-permute-start | bytes 393224 | tf_op jit(solution)/shard_map/ppermute | solution.py:437
  13.9 0.6 %query.1.q_ref = bf16[128,512]{1,0:T(8,128)(2,1)S(1)} custom-call(bf16[128,2048]{1,0:T(8,128)(2,1)S(1)} %copy-done.3, f32[128,256]{1,0:T(8,128)S(1)} %copy-done.4, bf16[2048,512]{1,0:T(8,128)(2,1)S(1)} %copy-done.1), custom_call_target="tpu_custom_call" | custom-call | tf_op jit(solution)/shard_map/query/pallas_call | solution.py:523
  14.6 2.6 %collective-permute-done.refs_3_ = bf16[128,512]{1,0:T(8,128)(2,1)S(1)} collective-permute-done((bf16[128,512]{1,0:T(8,128)(2,1)}, bf16[128,512]{1,0:T(8,128)(2,1)S(1)}, u32[]{:S(2)}, u32[]{:S(2)}) %collective-permute-start) | collective-permute-done | bytes 131104 | tf_op jit(solution)/shard_map/ppermute | solution.py:437
  17.4 1.8 %collective-permute-start.4 = (bf16[128,512]{1,0:T(8,128)(2,1)S(1)}, bf16[128,512]{1,0:T(8,128)(2,1)S(1)}, u32[]{:S(2)}, u32[]{:S(2)}) collective-permute-start(bf16[128,512]{1,0:T(8,128)(2,1)S(1)} %collective-permute-done.refs_3_), channel_id=1, source_target_pairs={{0,8},{2,10},{4,12},{6,14},{8,0},{10,2},{12,4},{14,6},{16,24},{18,... | collective-permute-start | bytes 393224 | tf_op jit(solution)/shard_map/ppermute | solution.py:437
  19.3 1.4 %collective-permute-start.6 = (bf16[128,512]{1,0:T(8,128)(2,1)S(1)}, bf16[128,512]{1,0:T(8,128)(2,1)S(1)}, u32[]{:S(2)}, u32[]{:S(2)}) collective-permute-start(bf16[128,512]{1,0:T(8,128)(2,1)S(1)} %collective-permute-done.refs_3_), channel_id=1, source_target_pairs={{0,4},{2,6},{4,0},{6,2},{8,12},{10,14},{12,8},{14,10},{16,20},{18,... | collective-permute-start | bytes 393224 | tf_op jit(solution)/shard_map/ppermute | solution.py:437
  20.7 1.4 %attend.3 = (f32[128,512]{1,0:T(8,128)S(1)}, f32[128,128]{1,0:T(8,128)S(1)}, bf16[128,640]{1,0:T(8,128)(2,1)S(1)}) custom-call(s32[16,128]{1,0:T(8,128)S(1)} %get-tuple-element.59.key_pos_ref, s32[256,128]{1,0:T(8,128)S(1)} %get-tuple-element.60.q_pos_ref, s32[256,128]{1,0:T(8,128)S(1)} %get-tuple-element.61.q_begin_ref, bf16[128,512]{1,0:T(8,128)(2,1)S(1)} %query.1.q_ref, ...), custom_call_target="tpu_custom_call" | custom-call | tf_op jit(solution)/shard_map/attend/pallas_call | solution.py:537
  22.2 1.9 %collective-permute-done.5.refs_1_.refs_6_ = bf16[128,512]{1,0:T(8,128)(2,1)S(1)} collective-permute-done((bf16[128,512]{1,0:T(8,128)(2,1)S(1)}, bf16[128,512]{1,0:T(8,128)(2,1)S(1)}, u32[]{:S(2)}, u32[]{:S(2)}) %collective-permute-start.5) | collective-permute-done | bytes 131104 | tf_op jit(solution)/shard_map/ppermute | solution.py:437
  24.1 1.3 %collective-permute-done.6.refs_2_.refs_7_ = bf16[128,512]{1,0:T(8,128)(2,1)S(1)} collective-permute-done((bf16[128,512]{1,0:T(8,128)(2,1)S(1)}, bf16[128,512]{1,0:T(8,128)(2,1)S(1)}, u32[]{:S(2)}, u32[]{:S(2)}) %collective-permute-start.6) | collective-permute-done | bytes 131104 | tf_op jit(solution)/shard_map/ppermute | solution.py:437
  25.4 0.8 %attend.4 = (f32[64,512]{1,0:T(8,128)S(1)}, f32[64,128]{1,0:T(8,128)S(1)}, bf16[64,640]{1,0:T(8,128)(2,1)S(1)}) custom-call(s32[16,128]{1,0:T(8,128)S(1)} %get-tuple-element.59.key_pos_ref, s32[256,128]{1,0:T(8,128)S(1)} %get-tuple-element.60.q_pos_ref, s32[256,128]{1,0:T(8,128)S(1)} %get-tuple-element.61.q_begin_ref, bf16[128,512]{1,0:T(8,128)(2,1)S(1)} %query.1.q_ref, ...), custom_call_target="tpu_custom_call" | custom-call | tf_op jit(solution)/shard_map/attend/pallas_call | solution.py:537
  26.3 0.8 %attend.5 = (f32[64,512]{1,0:T(8,128)S(1)}, f32[64,128]{1,0:T(8,128)S(1)}, bf16[64,640]{1,0:T(8,128)(2,1)S(1)}) custom-call(s32[16,128]{1,0:T(8,128)S(1)} %get-tuple-element.59.key_pos_ref, s32[256,128]{1,0:T(8,128)S(1)} %get-tuple-element.60.q_pos_ref, s32[256,128]{1,0:T(8,128)S(1)} %get-tuple-element.61.q_begin_ref, bf16[128,512]{1,0:T(8,128)(2,1)S(1)} %query.1.q_ref, ...), custom_call_target="tpu_custom_call" | custom-call | tf_op jit(solution)/shard_map/attend/pallas_call | solution.py:537
  27.1 0.4 %collective-permute-done.10.refs_5_ = bf16[64,640]{1,0:T(8,128)(2,1)S(1)} collective-permute-done((bf16[64,640]{1,0:T(8,128)(2,1)S(1)}, bf16[64,640]{1,0:T(8,128)(2,1)S(1)}, u32[]{:S(2)}, u32[]{:S(2)}) %collective-permute-start.10) | collective-permute-done | bytes 81952 | tf_op jit(solution)/shard_map/ppermute | solution.py:437
  27.6 0.8 %leave.1 = bf16[64,2048]{1,0:T(8,128)(2,1)S(1)} custom-call(bf16[512,2048]{1,0:T(8,128)(2,1)S(1)} %copy-done, f32[128,512]{1,0:T(8,128)S(1)} %get-tuple-element.68.refs_0_.refs_2_, f32[128,128]{1,0:T(8,128)S(1)} %get-tuple-element.69.refs_1_.refs_3_, bf16[128,640]{1,0:T(8,128)(2,1)S(1)} %collective-permute-done.9.refs_2_.refs_4_, ...), custom_call_target="tpu_custom_call" | custom-call | tf_op jit(solution)/shard_map/leave/pallas_call | solution.py:598
  28.4 1.6 %collective-permute-start.13 = (bf16[64,2048]{1,0:T(8,128)(2,1)S(1)}, bf16[64,2048]{1,0:T(8,128)(2,1)S(1)}, u32[]{:S(2)}, u32[]{:S(2)}) collective-permute-start(bf16[64,2048]{1,0:T(8,128)(2,1)S(1)} %leave.1), channel_id=1, source_target_pairs={{0,1},{1,0},{2,3},{3,2},{4,5},{5,4},{6,7},{7,6},{8,9},{9,8},{10,11... | collective-permute-start | bytes 786440 | tf_op jit(solution)/shard_map/ppermute | solution.py:607
  30.0 1.3 %collective-permute-done.8.refs_7_ = bf16[64,640]{1,0:T(8,128)(2,1)S(1)} collective-permute-done((bf16[64,640]{1,0:T(8,128)(2,1)S(1)}, bf16[64,640]{1,0:T(8,128)(2,1)S(1)}, u32[]{:S(2)}, u32[]{:S(2)}) %collective-permute-start.8) | collective-permute-done | bytes 81952 | tf_op jit(solution)/shard_map/ppermute | solution.py:437
  31.2 1.6 %cache.1 = (bf16[8,2,32,256]{3,2,1,0:T(8,128)(2,1)S(1)}, bf16[4,2,32,256]{3,2,1,0:T(8,128)(2,1)S(1)}, bf16[4,2,32,256]{3,2,1,0:T(8,128)(2,1)S(1)}) custom-call(s32[16]{0:T(128)S(1)} %copy-done.5, s32[64]{0:T(128)S(1)} %copy-done.6, bf16[128,512]{1,0:T(8,128)(2,1)S(1)} %get-tuple-element.76.refs_0_, bf16[128,512]{1,0:T(8,128)(2,1)S(1)} %collective-permute-done.3.refs_1_, ...), custom_call_target="tpu_custom_call" | custom-call | tf_op jit(solution)/shard_map/cache/pallas_call | solution.py:555
  33.4 0.8 %collective-permute-done.11.refs_0_ = bf16[4,2,32,256]{3,2,1,0:T(8,128)(2,1)S(1)} collective-permute-done((bf16[4,2,32,256]{3,2,1,0:T(8,128)(2,1)S(1)}, bf16[4,2,32,256]{3,2,1,0:T(8,128)(2,1)S(1)}, u32[]{:S(2)}, u32[]{:S(2)}) %collective-permute-start.11) | collective-permute-done | bytes 131104 | tf_op jit(solution)/shard_map/ppermute | solution.py:437
  34.5 1.4 %keep.1 = (f32[64,2048]{1,0:T(8,128)S(1)}, bf16[8,2,32,256]{3,2,1,0:T(8,128)(2,1)}) custom-call(bf16[512,2048]{1,0:T(8,128)(2,1)S(1)} %copy-done, bf16[128,2048]{1,0:T(8,128)(2,1)S(1)} %copy-done.2, bf16[8,2,32,256]{3,2,1,0:T(8,128)(2,1)S(1)} %get-tuple-element.84.mine_ref, bf16[4,2,32,256]{3,2,1,0:T(8,128)(2,1)S(1)} %collective-permute-done.11.refs_0_, ...), custom_call_target="tpu_custom_call" | custom-call | tf_op jit(solution)/shard_map/keep/pallas_call | solution.py:611
  35.9 0.9 %collective-permute-done.13.received_ref = bf16[64,2048]{1,0:T(8,128)(2,1)S(1)} collective-permute-done((bf16[64,2048]{1,0:T(8,128)(2,1)S(1)}, bf16[64,2048]{1,0:T(8,128)(2,1)S(1)}, u32[]{:S(2)}, u32[]{:S(2)}) %collective-permute-start.13) | collective-permute-done | bytes 262176 | tf_op jit(solution)/shard_map/ppermute | solution.py:607
  36.8 0.8 %finish.1 = bf16[64,2048]{1,0:T(8,128)(2,1)} custom-call(f32[64,2048]{1,0:T(8,128)S(1)} %get-tuple-element.90.kept_ref, bf16[64,2048]{1,0:T(8,128)(2,1)S(1)} %collective-permute-done.13.received_ref), custom_call_target="tpu_custom_call" | custom-call | tf_op jit(solution)/shard_map/finish/pallas_call | solution.py:620
  (32 shorter events, 1.4 us)
Async XLA Ops:
  0.6 10.6 %copy-start.5 = (s32[16]{0:T(128)S(1)}, s32[16]{0:T(128)}, u32[]{:S(2)}) copy-start(s32[16]{0:T(128)} %block_ref.1) | copy-start | bytes 196
  0.6 10.5 %copy-start.7 = (s32[4]{0:T(128)S(1)}, s32[4]{0:T(128)}, u32[]{:S(2)}) copy-start(s32[4]{0:T(128)} %len_hbm.1) | copy-start | bytes 52
  4.0 10.0 %copy-start.1 = (bf16[2048,512]{1,0:T(8,128)(2,1)S(1)}, bf16[2048,512]{1,0:T(8,128)(2,1)}, u32[]{:S(2)}) copy-start(bf16[2048,512]{1,0:T(8,128)(2,1)} %wq_ref.1) | copy-start | bytes 6291460
  4.0 9.9 %copy-start.3 = (bf16[128,2048]{1,0:T(8,128)(2,1)S(1)}, bf16[128,2048]{1,0:T(8,128)(2,1)}, u32[]{:S(2)}) copy-start(bf16[128,2048]{1,0:T(8,128)(2,1)} %get-tuple-element.51.normed_ref) | copy-start | bytes 1572868
  4.0 9.9 %copy-start.4 = (f32[128,256]{1,0:T(8,128)S(1)}, f32[128,256]{1,0:T(8,128)}, u32[]{:S(2)}) copy-start(f32[128,256]{1,0:T(8,128)} %get-tuple-element.52.turned_ref) | copy-start | bytes 393220
  4.0 8.2 %collective-permute-start.1 = (bf16[128,512]{1,0:T(8,128)(2,1)}, bf16[128,512]{1,0:T(8,128)(2,1)S(1)}, u32[]{:S(2)}, u32[]{:S(2)}) collective-permute-start(bf16[128,512]{1,0:T(8,128)(2,1)} %get-tuple-element.47.kv_ref), channel_id=1, source_target_pairs={{0,8},{2,10},{4,12},{6,14},{8,0},{10,2},{12,4},{14,6},{16,24},{18,... | collective-permute-start | bytes 393224 | tf_op jit(solution)/shard_map/ppermute | solution.py:437
  7.1 12.1 %collective-permute-start.3 = (bf16[128,512]{1,0:T(8,128)(2,1)}, bf16[128,512]{1,0:T(8,128)(2,1)S(1)}, u32[]{:S(2)}, u32[]{:S(2)}) collective-permute-start(bf16[128,512]{1,0:T(8,128)(2,1)} %get-tuple-element.47.kv_ref), channel_id=1, source_target_pairs={{0,4},{2,6},{4,0},{6,2},{8,12},{10,14},{12,8},{14,10},{16,20},{18,... | collective-permute-start | bytes 393224 | tf_op jit(solution)/shard_map/ppermute | solution.py:437
  8.6 8.6 %collective-permute-start = (bf16[128,512]{1,0:T(8,128)(2,1)}, bf16[128,512]{1,0:T(8,128)(2,1)S(1)}, u32[]{:S(2)}, u32[]{:S(2)}) collective-permute-start(bf16[128,512]{1,0:T(8,128)(2,1)} %get-tuple-element.47.kv_ref), channel_id=1, source_target_pairs={{0,16},{2,18},{4,20},{6,22},{8,24},{10,26},{12,28},{14,30},{16,0},... | collective-permute-start | bytes 393224 | tf_op jit(solution)/shard_map/ppermute | solution.py:437
  11.2 0.9 %copy-start.8 = (bf16[128,512]{1,0:T(8,128)(2,1)S(1)}, bf16[128,512]{1,0:T(8,128)(2,1)}, u32[]{:S(2)}) copy-start(bf16[128,512]{1,0:T(8,128)(2,1)} %get-tuple-element.47.kv_ref) | copy-start | bytes 393220
  12.3 7.0 %collective-permute-start.2 = (bf16[128,512]{1,0:T(8,128)(2,1)S(1)}, bf16[128,512]{1,0:T(8,128)(2,1)S(1)}, u32[]{:S(2)}, u32[]{:S(2)}) collective-permute-start(bf16[128,512]{1,0:T(8,128)(2,1)S(1)} %collective-permute-done.1.refs_2_), channel_id=1, source_target_pairs={{0,4},{2,6},{4,0},{6,2},{8,12},{10,14},{12,8},{14,10},{16,20},{18,... | collective-permute-start | bytes 393224 | tf_op jit(solution)/shard_map/ppermute | solution.py:437
  14.5 13.1 %copy-start = (bf16[512,2048]{1,0:T(8,128)(2,1)S(1)}, bf16[512,2048]{1,0:T(8,128)(2,1)}, u32[]{:S(2)}) copy-start(bf16[512,2048]{1,0:T(8,128)(2,1)} %wo_ref.3) | copy-start | bytes 6291460
  14.5 6.2 %collective-permute-start.7 = (bf16[128,512]{1,0:T(8,128)(2,1)S(1)}, bf16[128,512]{1,0:T(8,128)(2,1)S(1)}, u32[]{:S(2)}, u32[]{:S(2)}) collective-permute-start(bf16[128,512]{1,0:T(8,128)(2,1)S(1)} %query.1.q_ref), channel_id=1, source_target_pairs={{0,2},{2,0},{4,6},{6,4},{8,10},{10,8},{12,14},{14,12},{16,18},{18,... | collective-permute-start | bytes 393224 | tf_op jit(solution)/shard_map/ppermute | solution.py:437
  17.2 6.9 %collective-permute-start.5 = (bf16[128,512]{1,0:T(8,128)(2,1)S(1)}, bf16[128,512]{1,0:T(8,128)(2,1)S(1)}, u32[]{:S(2)}, u32[]{:S(2)}) collective-permute-start(bf16[128,512]{1,0:T(8,128)(2,1)S(1)} %collective-permute-done.refs_3_), channel_id=1, source_target_pairs={{0,12},{2,14},{4,8},{6,10},{8,4},{10,6},{12,0},{14,2},{16,28},{18,... | collective-permute-start | bytes 393224 | tf_op jit(solution)/shard_map/ppermute | solution.py:437
  17.4 6.7 %collective-permute-start.4 = (bf16[128,512]{1,0:T(8,128)(2,1)S(1)}, bf16[128,512]{1,0:T(8,128)(2,1)S(1)}, u32[]{:S(2)}, u32[]{:S(2)}) collective-permute-start(bf16[128,512]{1,0:T(8,128)(2,1)S(1)} %collective-permute-done.refs_3_), channel_id=1, source_target_pairs={{0,8},{2,10},{4,12},{6,14},{8,0},{10,2},{12,4},{14,6},{16,24},{18,... | collective-permute-start | bytes 393224 | tf_op jit(solution)/shard_map/ppermute | solution.py:437
  19.3 6.1 %collective-permute-start.6 = (bf16[128,512]{1,0:T(8,128)(2,1)S(1)}, bf16[128,512]{1,0:T(8,128)(2,1)S(1)}, u32[]{:S(2)}, u32[]{:S(2)}) collective-permute-start(bf16[128,512]{1,0:T(8,128)(2,1)S(1)} %collective-permute-done.refs_3_), channel_id=1, source_target_pairs={{0,4},{2,6},{4,0},{6,2},{8,12},{10,14},{12,8},{14,10},{16,20},{18,... | collective-permute-start | bytes 393224 | tf_op jit(solution)/shard_map/ppermute | solution.py:437
  22.1 5.0 %collective-permute-start.9 = (bf16[128,640]{1,0:T(8,128)(2,1)S(1)}, bf16[128,640]{1,0:T(8,128)(2,1)S(1)}, u32[]{:S(2)}, u32[]{:S(2)}) collective-permute-start(bf16[128,640]{1,0:T(8,128)(2,1)S(1)} %get-tuple-element.70), channel_id=1, source_target_pairs={{0,2},{2,0},{4,6},{6,4},{8,10},{10,8},{12,14},{14,12},{16,18},{18,... | collective-permute-start | bytes 491528 | tf_op jit(solution)/shard_map/ppermute | solution.py:437
  26.2 5.0 %copy-start.6 = (s32[64]{0:T(128)S(1)}, s32[64]{0:T(128)}, u32[]{:S(2)}) copy-start(s32[64]{0:T(128)} %slot_ref.1) | copy-start | bytes 772
  26.2 1.3 %collective-permute-start.10 = (bf16[64,640]{1,0:T(8,128)(2,1)S(1)}, bf16[64,640]{1,0:T(8,128)(2,1)S(1)}, u32[]{:S(2)}, u32[]{:S(2)}) collective-permute-start(bf16[64,640]{1,0:T(8,128)(2,1)S(1)} %get-tuple-element.75), channel_id=1, source_target_pairs={{0,2},{2,0},{4,6},{6,4},{8,10},{10,8},{12,14},{14,12},{16,18},{18,... | collective-permute-start | bytes 245768 | tf_op jit(solution)/shard_map/ppermute | solution.py:437
  27.1 7.3 %copy-start.2 = (bf16[128,2048]{1,0:T(8,128)(2,1)S(1)}, bf16[128,2048]{1,0:T(8,128)(2,1)}, u32[]{:S(2)}) copy-start(bf16[128,2048]{1,0:T(8,128)(2,1)} %tok_ref.1) | copy-start | bytes 1572868
  28.4 8.4 %collective-permute-start.13 = (bf16[64,2048]{1,0:T(8,128)(2,1)S(1)}, bf16[64,2048]{1,0:T(8,128)(2,1)S(1)}, u32[]{:S(2)}, u32[]{:S(2)}) collective-permute-start(bf16[64,2048]{1,0:T(8,128)(2,1)S(1)} %leave.1), channel_id=1, source_target_pairs={{0,1},{1,0},{2,3},{3,2},{4,5},{5,4},{6,7},{7,6},{8,9},{9,8},{10,11... | collective-permute-start | bytes 786440 | tf_op jit(solution)/shard_map/ppermute | solution.py:607
  30.0 1.3 %collective-permute-start.8 = (bf16[64,640]{1,0:T(8,128)(2,1)S(1)}, bf16[64,640]{1,0:T(8,128)(2,1)S(1)}, u32[]{:S(2)}, u32[]{:S(2)}) collective-permute-start(bf16[64,640]{1,0:T(8,128)(2,1)S(1)} %get-tuple-element.67), channel_id=1, source_target_pairs={{0,2},{2,0},{4,6},{6,4},{8,10},{10,8},{12,14},{14,12},{16,18},{18,... | collective-permute-start | bytes 245768 | tf_op jit(solution)/shard_map/ppermute | solution.py:437
  32.9 1.4 %collective-permute-start.11 = (bf16[4,2,32,256]{3,2,1,0:T(8,128)(2,1)S(1)}, bf16[4,2,32,256]{3,2,1,0:T(8,128)(2,1)S(1)}, u32[]{:S(2)}, u32[]{:S(2)}) collective-permute-start(bf16[4,2,32,256]{3,2,1,0:T(8,128)(2,1)S(1)} %get-tuple-element.85), channel_id=1, source_target_pairs={{0,2},{2,0},{4,6},{6,4},{8,10},{10,8},{12,14},{14,12},{16,18},{18,... | collective-permute-start | bytes 393224 | tf_op jit(solution)/shard_map/ppermute | solution.py:437
  33.1 1.4 %collective-permute-start.12 = (bf16[4,2,32,256]{3,2,1,0:T(8,128)(2,1)S(1)}, bf16[4,2,32,256]{3,2,1,0:T(8,128)(2,1)S(1)}, u32[]{:S(2)}, u32[]{:S(2)}) collective-permute-start(bf16[4,2,32,256]{3,2,1,0:T(8,128)(2,1)S(1)} %get-tuple-element.86), channel_id=1, source_target_pairs={{0,2},{2,0},{4,6},{6,4},{8,10},{10,8},{12,14},{14,12},{16,18},{18,... | collective-permute-start | bytes 393224 | tf_op jit(solution)/shard_map/ppermute | solution.py:437

commit v20 on v19

--- a/solution.py
+++ b/solution.py
@@ -575,9 +575,9 @@
         queries, far_queries = project_queries(normed)
         second, (staged, queries) = tied(second, (staged, queries))
         own = own.moved([staged])
-        third = swapped(second, 4)
         last = swapped(second, 6)
         (second, first_across, beside), _ = tied_all([second, first_across, beside], ())
+        third = swapped(second, 4)
         early = [own, beside, first, second, first_across]
         partials = attend(queries, far_queries, early)
         partials[2] = swap(partials[2], n, 1)

time: 37.7 us -> 36.9 us (0.979)
  waiting for transfers between devices: 9.45 us -> 8.64 us
    ppermute x13, waiting for transfers between devices: 8.55 us -> 7.73 us  [swap(): return lax.ppermute(x, 'seq', [(i, i ^ bit) for i in range(n)])]
where the time goes in v20:
time: 36.9 us; the launch traced here: 36.8 us
  starting transfers between devices  14.7 us (40%)
  Pallas kernels  11.6 us (31%)
  waiting for transfers between devices  8.64 us (23%)
  local copies, waits for them, and re-layouts  0.98 us (3%)
  between operations  0.81 us (2%)
    ppermute x13, starting transfers between devices, swap(): return lax.ppermute(x, 'seq', [(i, i ^ bit) for i in range(n)])  13.1 us
    ppermute x13, waiting for transfers between devices, swap(): return lax.ppermute(x, 'seq', [(i, i ^ bit) for i in range(n)])  7.73 us
    pallas_call x1, Pallas kernels, on_device(): pl.pallas_call(project_kernel, out_shape=(struct((rows, kv_width), bf16),...  3.32 us
    pallas_call x3, Pallas kernels, attend(): pl.pallas_call(functools.partial(attend_kernel, pieces, side), out_shape=...  3.01 us
    pallas_call x1, Pallas kernels, place_pages(): pl.pallas_call(functools.partial(cache_kernel, pieces), out_shape=(struct...  1.6 us
    ppermute x1, starting transfers between devices, on_device(): lax.ppermute(sent, 'req', [(i, (i + 1) % parts) for i in range(parts)])  1.59 us
    pallas_call x1, Pallas kernels, on_device(): pl.pallas_call(keep_kernel, out_shape=(struct((half, width), f32), struct...  1.44 us
    unnamed x18, local copies, waits for them, and re-layouts  0.98 us
  transfers between devices with their start and end apart: 14, of which 8 were waited for; matrix products, arithmetic and copies ran while one was open for 0% of the time, Pallas kernels for 18%

profile of v20, /device:TPU:0, one launch (start us, length us, event | category | flops | bytes accessed | tf_op | source)
XLA Modules:
  0.0 36.8 jit_solution(16799004736413142593)
XLA Ops:
  0.7 3.3 %project.1 = (bf16[128,512]{1,0:T(8,128)(2,1)}, bf16[128,2048]{1,0:T(8,128)(2,1)}, f32[128,256]{1,0:T(8,128)}) custom-call(s32[16]{0:T(128)} %block_ref.1, s32[4]{0:T(128)} %len_hbm.1, f32[136,128]{1,0:T(8,128)} %constant.2.clone.turn_hbm, bf16[128,2048]{1,0:T(8,128)(2,1)} %tok_ref.1, f32[1,2048]{1,0:T(1,128)} %bitcast.5, bf16[2048,256]{1,0:T(8,128)(2,1)} %wk_hbm.1, ...), custom_call_target="tpu_custom_call" | custom-call | tf_op jit(solution)/shard_map/project/pallas_call | solution.py:475
  4.0 3.1 %collective-permute-start.1 = (bf16[128,512]{1,0:T(8,128)(2,1)}, bf16[128,512]{1,0:T(8,128)(2,1)S(1)}, u32[]{:S(2)}, u32[]{:S(2)}) collective-permute-start(bf16[128,512]{1,0:T(8,128)(2,1)} %get-tuple-element.47.kv_ref), channel_id=1, source_target_pairs={{0,8},{2,10},{4,12},{6,14},{8,0},{10,2},{12,4},{14,6},{16,24},{18,... | collective-permute-start | bytes 393224 | tf_op jit(solution)/shard_map/ppermute | solution.py:437
  7.1 1.5 %collective-permute-start.3 = (bf16[128,512]{1,0:T(8,128)(2,1)}, bf16[128,512]{1,0:T(8,128)(2,1)S(1)}, u32[]{:S(2)}, u32[]{:S(2)}) collective-permute-start(bf16[128,512]{1,0:T(8,128)(2,1)} %get-tuple-element.47.kv_ref), channel_id=1, source_target_pairs={{0,4},{2,6},{4,0},{6,2},{8,12},{10,14},{12,8},{14,10},{16,20},{18,... | collective-permute-start | bytes 393224 | tf_op jit(solution)/shard_map/ppermute | solution.py:437
  8.6 2.6 %collective-permute-start = (bf16[128,512]{1,0:T(8,128)(2,1)}, bf16[128,512]{1,0:T(8,128)(2,1)S(1)}, u32[]{:S(2)}, u32[]{:S(2)}) collective-permute-start(bf16[128,512]{1,0:T(8,128)(2,1)} %get-tuple-element.47.kv_ref), channel_id=1, source_target_pairs={{0,16},{2,18},{4,20},{6,22},{8,24},{10,26},{12,28},{14,30},{16,0},... | collective-permute-start | bytes 393224 | tf_op jit(solution)/shard_map/ppermute | solution.py:437
  11.2 0.9 %copy-done.8 = bf16[128,512]{1,0:T(8,128)(2,1)S(1)} copy-done((bf16[128,512]{1,0:T(8,128)(2,1)S(1)}, bf16[128,512]{1,0:T(8,128)(2,1)}, u32[]{:S(2)}) %copy-start.8) | copy-done | bytes 131096
  12.3 1.7 %collective-permute-start.2 = (bf16[128,512]{1,0:T(8,128)(2,1)S(1)}, bf16[128,512]{1,0:T(8,128)(2,1)S(1)}, u32[]{:S(2)}, u32[]{:S(2)}) collective-permute-start(bf16[128,512]{1,0:T(8,128)(2,1)S(1)} %collective-permute-done.1.refs_2_), channel_id=1, source_target_pairs={{0,4},{2,6},{4,0},{6,2},{8,12},{10,14},{12,8},{14,10},{16,20},{18,... | collective-permute-start | bytes 393224 | tf_op jit(solution)/shard_map/ppermute | solution.py:437
  13.9 0.6 %query.1.q_ref = bf16[128,512]{1,0:T(8,128)(2,1)S(1)} custom-call(bf16[128,2048]{1,0:T(8,128)(2,1)S(1)} %copy-done.3, f32[128,256]{1,0:T(8,128)S(1)} %copy-done.4, bf16[2048,512]{1,0:T(8,128)(2,1)S(1)} %copy-done.1), custom_call_target="tpu_custom_call" | custom-call | tf_op jit(solution)/shard_map/query/pallas_call | solution.py:523
  14.6 2.6 %collective-permute-done.refs_3_ = bf16[128,512]{1,0:T(8,128)(2,1)S(1)} collective-permute-done((bf16[128,512]{1,0:T(8,128)(2,1)}, bf16[128,512]{1,0:T(8,128)(2,1)S(1)}, u32[]{:S(2)}, u32[]{:S(2)}) %collective-permute-start) | collective-permute-done | bytes 131104 | tf_op jit(solution)/shard_map/ppermute | solution.py:437
  17.4 1.5 %collective-permute-start.6 = (bf16[128,512]{1,0:T(8,128)(2,1)S(1)}, bf16[128,512]{1,0:T(8,128)(2,1)S(1)}, u32[]{:S(2)}, u32[]{:S(2)}) collective-permute-start(bf16[128,512]{1,0:T(8,128)(2,1)S(1)} %collective-permute-done.refs_3_), channel_id=1, source_target_pairs={{0,4},{2,6},{4,0},{6,2},{8,12},{10,14},{12,8},{14,10},{16,20},{18,... | collective-permute-start | bytes 393224 | tf_op jit(solution)/shard_map/ppermute | solution.py:437
  18.9 1.8 %collective-permute-start.4 = (bf16[128,512]{1,0:T(8,128)(2,1)S(1)}, bf16[128,512]{1,0:T(8,128)(2,1)S(1)}, u32[]{:S(2)}, u32[]{:S(2)}) collective-permute-start(bf16[128,512]{1,0:T(8,128)(2,1)S(1)} %collective-permute-done.refs_3_), channel_id=1, source_target_pairs={{0,8},{2,10},{4,12},{6,14},{8,0},{10,2},{12,4},{14,6},{16,24},{18,... | collective-permute-start | bytes 393224 | tf_op jit(solution)/shard_map/ppermute | solution.py:437
  20.7 1.4 %attend.3 = (f32[128,512]{1,0:T(8,128)S(1)}, f32[128,128]{1,0:T(8,128)S(1)}, bf16[128,640]{1,0:T(8,128)(2,1)S(1)}) custom-call(s32[16,128]{1,0:T(8,128)S(1)} %get-tuple-element.59.key_pos_ref, s32[256,128]{1,0:T(8,128)S(1)} %get-tuple-element.60.q_pos_ref, s32[256,128]{1,0:T(8,128)S(1)} %get-tuple-element.61.q_begin_ref, bf16[128,512]{1,0:T(8,128)(2,1)S(1)} %query.1.q_ref, ...), custom_call_target="tpu_custom_call" | custom-call | tf_op jit(solution)/shard_map/attend/pallas_call | solution.py:537
  22.2 1.9 %collective-permute-done.5.refs_1_.refs_6_ = bf16[128,512]{1,0:T(8,128)(2,1)S(1)} collective-permute-done((bf16[128,512]{1,0:T(8,128)(2,1)S(1)}, bf16[128,512]{1,0:T(8,128)(2,1)S(1)}, u32[]{:S(2)}, u32[]{:S(2)}) %collective-permute-start.5) | collective-permute-done | bytes 131104 | tf_op jit(solution)/shard_map/ppermute | solution.py:437
  24.1 0.5 %collective-permute-done.6.refs_2_.refs_7_ = bf16[128,512]{1,0:T(8,128)(2,1)S(1)} collective-permute-done((bf16[128,512]{1,0:T(8,128)(2,1)S(1)}, bf16[128,512]{1,0:T(8,128)(2,1)S(1)}, u32[]{:S(2)}, u32[]{:S(2)}) %collective-permute-start.6) | collective-permute-done | bytes 131104 | tf_op jit(solution)/shard_map/ppermute | solution.py:437
  24.6 0.8 %attend.4 = (f32[64,512]{1,0:T(8,128)S(1)}, f32[64,128]{1,0:T(8,128)S(1)}, bf16[64,640]{1,0:T(8,128)(2,1)S(1)}) custom-call(s32[16,128]{1,0:T(8,128)S(1)} %get-tuple-element.59.key_pos_ref, s32[256,128]{1,0:T(8,128)S(1)} %get-tuple-element.60.q_pos_ref, s32[256,128]{1,0:T(8,128)S(1)} %get-tuple-element.61.q_begin_ref, bf16[128,512]{1,0:T(8,128)(2,1)S(1)} %query.1.q_ref, ...), custom_call_target="tpu_custom_call" | custom-call | tf_op jit(solution)/shard_map/attend/pallas_call | solution.py:537
  25.5 0.8 %attend.5 = (f32[64,512]{1,0:T(8,128)S(1)}, f32[64,128]{1,0:T(8,128)S(1)}, bf16[64,640]{1,0:T(8,128)(2,1)S(1)}) custom-call(s32[16,128]{1,0:T(8,128)S(1)} %get-tuple-element.59.key_pos_ref, s32[256,128]{1,0:T(8,128)S(1)} %get-tuple-element.60.q_pos_ref, s32[256,128]{1,0:T(8,128)S(1)} %get-tuple-element.61.q_begin_ref, bf16[128,512]{1,0:T(8,128)(2,1)S(1)} %query.1.q_ref, ...), custom_call_target="tpu_custom_call" | custom-call | tf_op jit(solution)/shard_map/attend/pallas_call | solution.py:537
  26.3 0.4 %collective-permute-done.10.refs_5_ = bf16[64,640]{1,0:T(8,128)(2,1)S(1)} collective-permute-done((bf16[64,640]{1,0:T(8,128)(2,1)S(1)}, bf16[64,640]{1,0:T(8,128)(2,1)S(1)}, u32[]{:S(2)}, u32[]{:S(2)}) %collective-permute-start.10) | collective-permute-done | bytes 81952 | tf_op jit(solution)/shard_map/ppermute | solution.py:437
  26.8 0.8 %leave.1 = bf16[64,2048]{1,0:T(8,128)(2,1)S(1)} custom-call(bf16[512,2048]{1,0:T(8,128)(2,1)S(1)} %copy-done, f32[128,512]{1,0:T(8,128)S(1)} %get-tuple-element.68.refs_0_.refs_2_, f32[128,128]{1,0:T(8,128)S(1)} %get-tuple-element.69.refs_1_.refs_3_, bf16[128,640]{1,0:T(8,128)(2,1)S(1)} %collective-permute-done.9.refs_2_.refs_4_, ...), custom_call_target="tpu_custom_call" | custom-call | tf_op jit(solution)/shard_map/leave/pallas_call | solution.py:598
  27.6 1.6 %collective-permute-start.13 = (bf16[64,2048]{1,0:T(8,128)(2,1)S(1)}, bf16[64,2048]{1,0:T(8,128)(2,1)S(1)}, u32[]{:S(2)}, u32[]{:S(2)}) collective-permute-start(bf16[64,2048]{1,0:T(8,128)(2,1)S(1)} %leave.1), channel_id=1, source_target_pairs={{0,1},{1,0},{2,3},{3,2},{4,5},{5,4},{6,7},{7,6},{8,9},{9,8},{10,11... | collective-permute-start | bytes 786440 | tf_op jit(solution)/shard_map/ppermute | solution.py:607
  29.1 1.3 %collective-permute-done.8.refs_7_ = bf16[64,640]{1,0:T(8,128)(2,1)S(1)} collective-permute-done((bf16[64,640]{1,0:T(8,128)(2,1)S(1)}, bf16[64,640]{1,0:T(8,128)(2,1)S(1)}, u32[]{:S(2)}, u32[]{:S(2)}) %collective-permute-start.8) | collective-permute-done | bytes 81952 | tf_op jit(solution)/shard_map/ppermute | solution.py:437
  30.4 1.6 %cache.1 = (bf16[8,2,32,256]{3,2,1,0:T(8,128)(2,1)S(1)}, bf16[4,2,32,256]{3,2,1,0:T(8,128)(2,1)S(1)}, bf16[4,2,32,256]{3,2,1,0:T(8,128)(2,1)S(1)}) custom-call(s32[16]{0:T(128)S(1)} %copy-done.5, s32[64]{0:T(128)S(1)} %copy-done.6, bf16[128,512]{1,0:T(8,128)(2,1)S(1)} %get-tuple-element.76.refs_0_, bf16[128,512]{1,0:T(8,128)(2,1)S(1)} %collective-permute-done.3.refs_1_, ...), custom_call_target="tpu_custom_call" | custom-call | tf_op jit(solution)/shard_map/cache/pallas_call | solution.py:555
  32.6 0.8 %collective-permute-done.11.refs_0_ = bf16[4,2,32,256]{3,2,1,0:T(8,128)(2,1)S(1)} collective-permute-done((bf16[4,2,32,256]{3,2,1,0:T(8,128)(2,1)S(1)}, bf16[4,2,32,256]{3,2,1,0:T(8,128)(2,1)S(1)}, u32[]{:S(2)}, u32[]{:S(2)}) %collective-permute-start.11) | collective-permute-done | bytes 131104 | tf_op jit(solution)/shard_map/ppermute | solution.py:437
  33.6 1.4 %keep.1 = (f32[64,2048]{1,0:T(8,128)S(1)}, bf16[8,2,32,256]{3,2,1,0:T(8,128)(2,1)}) custom-call(bf16[512,2048]{1,0:T(8,128)(2,1)S(1)} %copy-done, bf16[128,2048]{1,0:T(8,128)(2,1)S(1)} %copy-done.2, bf16[8,2,32,256]{3,2,1,0:T(8,128)(2,1)S(1)} %get-tuple-element.84.mine_ref, bf16[4,2,32,256]{3,2,1,0:T(8,128)(2,1)S(1)} %collective-permute-done.11.refs_0_, ...), custom_call_target="tpu_custom_call" | custom-call | tf_op jit(solution)/shard_map/keep/pallas_call | solution.py:611
  35.1 0.9 %collective-permute-done.13.received_ref = bf16[64,2048]{1,0:T(8,128)(2,1)S(1)} collective-permute-done((bf16[64,2048]{1,0:T(8,128)(2,1)S(1)}, bf16[64,2048]{1,0:T(8,128)(2,1)S(1)}, u32[]{:S(2)}, u32[]{:S(2)}) %collective-permute-start.13) | collective-permute-done | bytes 262176 | tf_op jit(solution)/shard_map/ppermute | solution.py:607
  36.0 0.8 %finish.1 = bf16[64,2048]{1,0:T(8,128)(2,1)} custom-call(f32[64,2048]{1,0:T(8,128)S(1)} %get-tuple-element.90.kept_ref, bf16[64,2048]{1,0:T(8,128)(2,1)S(1)} %collective-permute-done.13.received_ref), custom_call_target="tpu_custom_call" | custom-call | tf_op jit(solution)/shard_map/finish/pallas_call | solution.py:620
  (32 shorter events, 1.4 us)
Async XLA Ops:
  0.6 10.6 %copy-start.5 = (s32[16]{0:T(128)S(1)}, s32[16]{0:T(128)}, u32[]{:S(2)}) copy-start(s32[16]{0:T(128)} %block_ref.1) | copy-start | bytes 196
  0.6 10.5 %copy-start.7 = (s32[4]{0:T(128)S(1)}, s32[4]{0:T(128)}, u32[]{:S(2)}) copy-start(s32[4]{0:T(128)} %len_hbm.1) | copy-start | bytes 52
  4.0 10.0 %copy-start.1 = (bf16[2048,512]{1,0:T(8,128)(2,1)S(1)}, bf16[2048,512]{1,0:T(8,128)(2,1)}, u32[]{:S(2)}) copy-start(bf16[2048,512]{1,0:T(8,128)(2,1)} %wq_ref.1) | copy-start | bytes 6291460
  4.0 9.9 %copy-start.3 = (bf16[128,2048]{1,0:T(8,128)(2,1)S(1)}, bf16[128,2048]{1,0:T(8,128)(2,1)}, u32[]{:S(2)}) copy-start(bf16[128,2048]{1,0:T(8,128)(2,1)} %get-tuple-element.51.normed_ref) | copy-start | bytes 1572868
  4.0 9.9 %copy-start.4 = (f32[128,256]{1,0:T(8,128)S(1)}, f32[128,256]{1,0:T(8,128)}, u32[]{:S(2)}) copy-start(f32[128,256]{1,0:T(8,128)} %get-tuple-element.52.turned_ref) | copy-start | bytes 393220
  4.0 8.2 %collective-permute-start.1 = (bf16[128,512]{1,0:T(8,128)(2,1)}, bf16[128,512]{1,0:T(8,128)(2,1)S(1)}, u32[]{:S(2)}, u32[]{:S(2)}) collective-permute-start(bf16[128,512]{1,0:T(8,128)(2,1)} %get-tuple-element.47.kv_ref), channel_id=1, source_target_pairs={{0,8},{2,10},{4,12},{6,14},{8,0},{10,2},{12,4},{14,6},{16,24},{18,... | collective-permute-start | bytes 393224 | tf_op jit(solution)/shard_map/ppermute | solution.py:437
  7.1 10.3 %collective-permute-start.3 = (bf16[128,512]{1,0:T(8,128)(2,1)}, bf16[128,512]{1,0:T(8,128)(2,1)S(1)}, u32[]{:S(2)}, u32[]{:S(2)}) collective-permute-start(bf16[128,512]{1,0:T(8,128)(2,1)} %get-tuple-element.47.kv_ref), channel_id=1, source_target_pairs={{0,4},{2,6},{4,0},{6,2},{8,12},{10,14},{12,8},{14,10},{16,20},{18,... | collective-permute-start | bytes 393224 | tf_op jit(solution)/shard_map/ppermute | solution.py:437
  8.6 8.6 %collective-permute-start = (bf16[128,512]{1,0:T(8,128)(2,1)}, bf16[128,512]{1,0:T(8,128)(2,1)S(1)}, u32[]{:S(2)}, u32[]{:S(2)}) collective-permute-start(bf16[128,512]{1,0:T(8,128)(2,1)} %get-tuple-element.47.kv_ref), channel_id=1, source_target_pairs={{0,16},{2,18},{4,20},{6,22},{8,24},{10,26},{12,28},{14,30},{16,0},... | collective-permute-start | bytes 393224 | tf_op jit(solution)/shard_map/ppermute | solution.py:437
  11.2 0.9 %copy-start.8 = (bf16[128,512]{1,0:T(8,128)(2,1)S(1)}, bf16[128,512]{1,0:T(8,128)(2,1)}, u32[]{:S(2)}) copy-start(bf16[128,512]{1,0:T(8,128)(2,1)} %get-tuple-element.47.kv_ref) | copy-start | bytes 393220
  12.3 5.1 %collective-permute-start.2 = (bf16[128,512]{1,0:T(8,128)(2,1)S(1)}, bf16[128,512]{1,0:T(8,128)(2,1)S(1)}, u32[]{:S(2)}, u32[]{:S(2)}) collective-permute-start(bf16[128,512]{1,0:T(8,128)(2,1)S(1)} %collective-permute-done.1.refs_2_), channel_id=1, source_target_pairs={{0,4},{2,6},{4,0},{6,2},{8,12},{10,14},{12,8},{14,10},{16,20},{18,... | collective-permute-start | bytes 393224 | tf_op jit(solution)/shard_map/ppermute | solution.py:437
  14.5 12.2 %copy-start = (bf16[512,2048]{1,0:T(8,128)(2,1)S(1)}, bf16[512,2048]{1,0:T(8,128)(2,1)}, u32[]{:S(2)}) copy-start(bf16[512,2048]{1,0:T(8,128)(2,1)} %wo_ref.3) | copy-start | bytes 6291460
  14.5 6.2 %collective-permute-start.7 = (bf16[128,512]{1,0:T(8,128)(2,1)S(1)}, bf16[128,512]{1,0:T(8,128)(2,1)S(1)}, u32[]{:S(2)}, u32[]{:S(2)}) collective-permute-start(bf16[128,512]{1,0:T(8,128)(2,1)S(1)} %query.1.q_ref), channel_id=1, source_target_pairs={{0,2},{2,0},{4,6},{6,4},{8,10},{10,8},{12,14},{14,12},{16,18},{18,... | collective-permute-start | bytes 393224 | tf_op jit(solution)/shard_map/ppermute | solution.py:437
  17.2 6.9 %collective-permute-start.5 = (bf16[128,512]{1,0:T(8,128)(2,1)S(1)}, bf16[128,512]{1,0:T(8,128)(2,1)S(1)}, u32[]{:S(2)}, u32[]{:S(2)}) collective-permute-start(bf16[128,512]{1,0:T(8,128)(2,1)S(1)} %collective-permute-done.refs_3_), channel_id=1, source_target_pairs={{0,12},{2,14},{4,8},{6,10},{8,4},{10,6},{12,0},{14,2},{16,28},{18,... | collective-permute-start | bytes 393224 | tf_op jit(solution)/shard_map/ppermute | solution.py:437
  17.4 7.2 %collective-permute-start.6 = (bf16[128,512]{1,0:T(8,128)(2,1)S(1)}, bf16[128,512]{1,0:T(8,128)(2,1)S(1)}, u32[]{:S(2)}, u32[]{:S(2)}) collective-permute-start(bf16[128,512]{1,0:T(8,128)(2,1)S(1)} %collective-permute-done.refs_3_), channel_id=1, source_target_pairs={{0,4},{2,6},{4,0},{6,2},{8,12},{10,14},{12,8},{14,10},{16,20},{18,... | collective-permute-start | bytes 393224 | tf_op jit(solution)/shard_map/ppermute | solution.py:437
  18.9 5.7 %collective-permute-start.4 = (bf16[128,512]{1,0:T(8,128)(2,1)S(1)}, bf16[128,512]{1,0:T(8,128)(2,1)S(1)}, u32[]{:S(2)}, u32[]{:S(2)}) collective-permute-start(bf16[128,512]{1,0:T(8,128)(2,1)S(1)} %collective-permute-done.refs_3_), channel_id=1, source_target_pairs={{0,8},{2,10},{4,12},{6,14},{8,0},{10,2},{12,4},{14,6},{16,24},{18,... | collective-permute-start | bytes 393224 | tf_op jit(solution)/shard_map/ppermute | solution.py:437
  22.1 4.2 %collective-permute-start.9 = (bf16[128,640]{1,0:T(8,128)(2,1)S(1)}, bf16[128,640]{1,0:T(8,128)(2,1)S(1)}, u32[]{:S(2)}, u32[]{:S(2)}) collective-permute-start(bf16[128,640]{1,0:T(8,128)(2,1)S(1)} %get-tuple-element.70), channel_id=1, source_target_pairs={{0,2},{2,0},{4,6},{6,4},{8,10},{10,8},{12,14},{14,12},{16,18},{18,... | collective-permute-start | bytes 491528 | tf_op jit(solution)/shard_map/ppermute | solution.py:437
  25.4 5.0 %copy-start.6 = (s32[64]{0:T(128)S(1)}, s32[64]{0:T(128)}, u32[]{:S(2)}) copy-start(s32[64]{0:T(128)} %slot_ref.1) | copy-start | bytes 772
  25.4 1.3 %collective-permute-start.10 = (bf16[64,640]{1,0:T(8,128)(2,1)S(1)}, bf16[64,640]{1,0:T(8,128)(2,1)S(1)}, u32[]{:S(2)}, u32[]{:S(2)}) collective-permute-start(bf16[64,640]{1,0:T(8,128)(2,1)S(1)} %get-tuple-element.75), channel_id=1, source_target_pairs={{0,2},{2,0},{4,6},{6,4},{8,10},{10,8},{12,14},{14,12},{16,18},{18,... | collective-permute-start | bytes 245768 | tf_op jit(solution)/shard_map/ppermute | solution.py:437
  26.3 7.3 %copy-start.2 = (bf16[128,2048]{1,0:T(8,128)(2,1)S(1)}, bf16[128,2048]{1,0:T(8,128)(2,1)}, u32[]{:S(2)}) copy-start(bf16[128,2048]{1,0:T(8,128)(2,1)} %tok_ref.1) | copy-start | bytes 1572868
  27.6 8.4 %collective-permute-start.13 = (bf16[64,2048]{1,0:T(8,128)(2,1)S(1)}, bf16[64,2048]{1,0:T(8,128)(2,1)S(1)}, u32[]{:S(2)}, u32[]{:S(2)}) collective-permute-start(bf16[64,2048]{1,0:T(8,128)(2,1)S(1)} %leave.1), channel_id=1, source_target_pairs={{0,1},{1,0},{2,3},{3,2},{4,5},{5,4},{6,7},{7,6},{8,9},{9,8},{10,11... | collective-permute-start | bytes 786440 | tf_op jit(solution)/shard_map/ppermute | solution.py:607
  29.1 1.3 %collective-permute-start.8 = (bf16[64,640]{1,0:T(8,128)(2,1)S(1)}, bf16[64,640]{1,0:T(8,128)(2,1)S(1)}, u32[]{:S(2)}, u32[]{:S(2)}) collective-permute-start(bf16[64,640]{1,0:T(8,128)(2,1)S(1)} %get-tuple-element.67), channel_id=1, source_target_pairs={{0,2},{2,0},{4,6},{6,4},{8,10},{10,8},{12,14},{14,12},{16,18},{18,... | collective-permute-start | bytes 245768 | tf_op jit(solution)/shard_map/ppermute | solution.py:437
  32.0 1.4 %collective-permute-start.11 = (bf16[4,2,32,256]{3,2,1,0:T(8,128)(2,1)S(1)}, bf16[4,2,32,256]{3,2,1,0:T(8,128)(2,1)S(1)}, u32[]{:S(2)}, u32[]{:S(2)}) collective-permute-start(bf16[4,2,32,256]{3,2,1,0:T(8,128)(2,1)S(1)} %get-tuple-element.85), channel_id=1, source_target_pairs={{0,2},{2,0},{4,6},{6,4},{8,10},{10,8},{12,14},{14,12},{16,18},{18,... | collective-permute-start | bytes 393224 | tf_op jit(solution)/shard_map/ppermute | solution.py:437
  32.3 1.4 %collective-permute-start.12 = (bf16[4,2,32,256]{3,2,1,0:T(8,128)(2,1)S(1)}, bf16[4,2,32,256]{3,2,1,0:T(8,128)(2,1)S(1)}, u32[]{:S(2)}, u32[]{:S(2)}) collective-permute-start(bf16[4,2,32,256]{3,2,1,0:T(8,128)(2,1)S(1)} %get-tuple-element.86), channel_id=1, source_target_pairs={{0,2},{2,0},{4,6},{6,4},{8,10},{10,8},{12,14},{14,12},{16,18},{18,... | collective-permute-start | bytes 393224 | tf_op jit(solution)/shard_map/ppermute | solution.py:437

commit v21 on v20

--- a/solution.py
+++ b/solution.py
@@ -575,14 +575,14 @@
         queries, far_queries = project_queries(normed)
         second, (staged, queries) = tied(second, (staged, queries))
         own = own.moved([staged])
-        last = swapped(second, 6)
         (second, first_across, beside), _ = tied_all([second, first_across, beside], ())
         third = swapped(second, 4)
+        last = swapped(second, 6)
         early = [own, beside, first, second, first_across]
         partials = attend(queries, far_queries, early)
         partials[2] = swap(partials[2], n, 1)
         queries, partials[1] = lax.optimization_barrier((queries, partials[1]))
-        remaining = [third, last, swapped(second, 2)]
+        remaining = [third, swapped(second, 2), last]
         placed = early + remaining
     else:
         same = [list(range(c, n, 2)) for c in range(2)]

time: 36.9 us -> 37.2 us (level)
  transfers between devices with their start and end apart: 14 -> 14, of which waited for: 8 -> 9; matrix products, arithmetic and copies ran while one was open for 0% -> 0% of each run, Pallas kernels for 18% -> 18%
where the time goes in v21:
time: 37.2 us; the launch traced here: 37 us
  starting transfers between devices  14.7 us (40%)
  Pallas kernels  11.6 us (31%)
  waiting for transfers between devices  8.88 us (24%)
  local copies, waits for them, and re-layouts  0.98 us (3%)
  between operations  0.81 us (2%)
    ppermute x13, starting transfers between devices, swap(): return lax.ppermute(x, 'seq', [(i, i ^ bit) for i in range(n)])  13.1 us
    ppermute x13, waiting for transfers between devices, swap(): return lax.ppermute(x, 'seq', [(i, i ^ bit) for i in range(n)])  7.97 us
    pallas_call x1, Pallas kernels, on_device(): pl.pallas_call(project_kernel, out_shape=(struct((rows, kv_width), bf16),...  3.32 us
    pallas_call x3, Pallas kernels, attend(): pl.pallas_call(functools.partial(attend_kernel, pieces, side), out_shape=...  3.01 us
    pallas_call x1, Pallas kernels, place_pages(): pl.pallas_call(functools.partial(cache_kernel, pieces), out_shape=(struct...  1.6 us
    ppermute x1, starting transfers between devices, on_device(): lax.ppermute(sent, 'req', [(i, (i + 1) % parts) for i in range(parts)])  1.58 us
    pallas_call x1, Pallas kernels, on_device(): pl.pallas_call(keep_kernel, out_shape=(struct((half, width), f32), struct...  1.44 us
    unnamed x18, local copies, waits for them, and re-layouts  0.98 us
  transfers between devices with their start and end apart: 14, of which 9 were waited for; matrix products, arithmetic and copies ran while one was open for 0% of the time, Pallas kernels for 18%

profile of v21, /device:TPU:0, one launch (start us, length us, event | category | flops | bytes accessed | tf_op | source)
XLA Modules:
  0.0 37.0 jit_solution(6946335888169469705)
XLA Ops:
  0.7 3.3 %project.1 = (bf16[128,512]{1,0:T(8,128)(2,1)}, bf16[128,2048]{1,0:T(8,128)(2,1)}, f32[128,256]{1,0:T(8,128)}) custom-call(s32[16]{0:T(128)} %block_ref.1, s32[4]{0:T(128)} %len_hbm.1, f32[136,128]{1,0:T(8,128)} %constant.2.clone.turn_hbm, bf16[128,2048]{1,0:T(8,128)(2,1)} %tok_ref.1, f32[1,2048]{1,0:T(1,128)} %bitcast.5, bf16[2048,256]{1,0:T(8,128)(2,1)} %wk_hbm.1, ...), custom_call_target="tpu_custom_call" | custom-call | tf_op jit(solution)/shard_map/project/pallas_call | solution.py:475
  4.0 3.1 %collective-permute-start.1 = (bf16[128,512]{1,0:T(8,128)(2,1)}, bf16[128,512]{1,0:T(8,128)(2,1)S(1)}, u32[]{:S(2)}, u32[]{:S(2)}) collective-permute-start(bf16[128,512]{1,0:T(8,128)(2,1)} %get-tuple-element.47.kv_ref), channel_id=1, source_target_pairs={{0,8},{2,10},{4,12},{6,14},{8,0},{10,2},{12,4},{14,6},{16,24},{18,... | collective-permute-start | bytes 393224 | tf_op jit(solution)/shard_map/ppermute | solution.py:437
  7.1 1.5 %collective-permute-start.3 = (bf16[128,512]{1,0:T(8,128)(2,1)}, bf16[128,512]{1,0:T(8,128)(2,1)S(1)}, u32[]{:S(2)}, u32[]{:S(2)}) collective-permute-start(bf16[128,512]{1,0:T(8,128)(2,1)} %get-tuple-element.47.kv_ref), channel_id=1, source_target_pairs={{0,4},{2,6},{4,0},{6,2},{8,12},{10,14},{12,8},{14,10},{16,20},{18,... | collective-permute-start | bytes 393224 | tf_op jit(solution)/shard_map/ppermute | solution.py:437
  8.6 2.6 %collective-permute-start = (bf16[128,512]{1,0:T(8,128)(2,1)}, bf16[128,512]{1,0:T(8,128)(2,1)S(1)}, u32[]{:S(2)}, u32[]{:S(2)}) collective-permute-start(bf16[128,512]{1,0:T(8,128)(2,1)} %get-tuple-element.47.kv_ref), channel_id=1, source_target_pairs={{0,16},{2,18},{4,20},{6,22},{8,24},{10,26},{12,28},{14,30},{16,0},... | collective-permute-start | bytes 393224 | tf_op jit(solution)/shard_map/ppermute | solution.py:437
  11.2 0.9 %copy-done.8 = bf16[128,512]{1,0:T(8,128)(2,1)S(1)} copy-done((bf16[128,512]{1,0:T(8,128)(2,1)S(1)}, bf16[128,512]{1,0:T(8,128)(2,1)}, u32[]{:S(2)}) %copy-start.8) | copy-done | bytes 131096
  12.3 1.7 %collective-permute-start.2 = (bf16[128,512]{1,0:T(8,128)(2,1)S(1)}, bf16[128,512]{1,0:T(8,128)(2,1)S(1)}, u32[]{:S(2)}, u32[]{:S(2)}) collective-permute-start(bf16[128,512]{1,0:T(8,128)(2,1)S(1)} %collective-permute-done.1.refs_2_), channel_id=1, source_target_pairs={{0,4},{2,6},{4,0},{6,2},{8,12},{10,14},{12,8},{14,10},{16,20},{18,... | collective-permute-start | bytes 393224 | tf_op jit(solution)/shard_map/ppermute | solution.py:437
  13.9 0.6 %query.1.q_ref = bf16[128,512]{1,0:T(8,128)(2,1)S(1)} custom-call(bf16[128,2048]{1,0:T(8,128)(2,1)S(1)} %copy-done.3, f32[128,256]{1,0:T(8,128)S(1)} %copy-done.4, bf16[2048,512]{1,0:T(8,128)(2,1)S(1)} %copy-done.1), custom_call_target="tpu_custom_call" | custom-call | tf_op jit(solution)/shard_map/query/pallas_call | solution.py:523
  14.6 2.6 %collective-permute-done.refs_3_ = bf16[128,512]{1,0:T(8,128)(2,1)S(1)} collective-permute-done((bf16[128,512]{1,0:T(8,128)(2,1)}, bf16[128,512]{1,0:T(8,128)(2,1)S(1)}, u32[]{:S(2)}, u32[]{:S(2)}) %collective-permute-start) | collective-permute-done | bytes 131104 | tf_op jit(solution)/shard_map/ppermute | solution.py:437
  17.3 1.3 %collective-permute-start.6 = (bf16[128,512]{1,0:T(8,128)(2,1)S(1)}, bf16[128,512]{1,0:T(8,128)(2,1)S(1)}, u32[]{:S(2)}, u32[]{:S(2)}) collective-permute-start(bf16[128,512]{1,0:T(8,128)(2,1)S(1)} %collective-permute-done.refs_3_), channel_id=1, source_target_pairs={{0,12},{2,14},{4,8},{6,10},{8,4},{10,6},{12,0},{14,2},{16,28},{18,... | collective-permute-start | bytes 393224 | tf_op jit(solution)/shard_map/ppermute | solution.py:437
  18.6 0.6 %collective-permute-start.5 = (bf16[128,512]{1,0:T(8,128)(2,1)S(1)}, bf16[128,512]{1,0:T(8,128)(2,1)S(1)}, u32[]{:S(2)}, u32[]{:S(2)}) collective-permute-start(bf16[128,512]{1,0:T(8,128)(2,1)S(1)} %collective-permute-done.refs_3_), channel_id=1, source_target_pairs={{0,4},{2,6},{4,0},{6,2},{8,12},{10,14},{12,8},{14,10},{16,20},{18,... | collective-permute-start | bytes 393224 | tf_op jit(solution)/shard_map/ppermute | solution.py:437
  19.2 1.6 %collective-permute-start.4 = (bf16[128,512]{1,0:T(8,128)(2,1)S(1)}, bf16[128,512]{1,0:T(8,128)(2,1)S(1)}, u32[]{:S(2)}, u32[]{:S(2)}) collective-permute-start(bf16[128,512]{1,0:T(8,128)(2,1)S(1)} %collective-permute-done.refs_3_), channel_id=1, source_target_pairs={{0,8},{2,10},{4,12},{6,14},{8,0},{10,2},{12,4},{14,6},{16,24},{18,... | collective-permute-start | bytes 393224 | tf_op jit(solution)/shard_map/ppermute | solution.py:437
  20.8 1.4 %attend.3 = (f32[128,512]{1,0:T(8,128)S(1)}, f32[128,128]{1,0:T(8,128)S(1)}, bf16[128,640]{1,0:T(8,128)(2,1)S(1)}) custom-call(s32[16,128]{1,0:T(8,128)S(1)} %get-tuple-element.59.key_pos_ref, s32[256,128]{1,0:T(8,128)S(1)} %get-tuple-element.60.q_pos_ref, s32[256,128]{1,0:T(8,128)S(1)} %get-tuple-element.61.q_begin_ref, bf16[128,512]{1,0:T(8,128)(2,1)S(1)} %query.1.q_ref, ...), custom_call_target="tpu_custom_call" | custom-call | tf_op jit(solution)/shard_map/attend/pallas_call | solution.py:537
  22.3 1.9 %collective-permute-done.6.refs_2_.refs_7_ = bf16[128,512]{1,0:T(8,128)(2,1)S(1)} collective-permute-done((bf16[128,512]{1,0:T(8,128)(2,1)S(1)}, bf16[128,512]{1,0:T(8,128)(2,1)S(1)}, u32[]{:S(2)}, u32[]{:S(2)}) %collective-permute-start.6) | collective-permute-done | bytes 131104 | tf_op jit(solution)/shard_map/ppermute | solution.py:437
  24.2 0.7 %collective-permute-done.5.refs_1_.refs_6_ = bf16[128,512]{1,0:T(8,128)(2,1)S(1)} collective-permute-done((bf16[128,512]{1,0:T(8,128)(2,1)S(1)}, bf16[128,512]{1,0:T(8,128)(2,1)S(1)}, u32[]{:S(2)}, u32[]{:S(2)}) %collective-permute-start.5) | collective-permute-done | bytes 131104 | tf_op jit(solution)/shard_map/ppermute | solution.py:437
  24.8 0.8 %attend.4 = (f32[64,512]{1,0:T(8,128)S(1)}, f32[64,128]{1,0:T(8,128)S(1)}, bf16[64,640]{1,0:T(8,128)(2,1)S(1)}) custom-call(s32[16,128]{1,0:T(8,128)S(1)} %get-tuple-element.59.key_pos_ref, s32[256,128]{1,0:T(8,128)S(1)} %get-tuple-element.60.q_pos_ref, s32[256,128]{1,0:T(8,128)S(1)} %get-tuple-element.61.q_begin_ref, bf16[128,512]{1,0:T(8,128)(2,1)S(1)} %query.1.q_ref, ...), custom_call_target="tpu_custom_call" | custom-call | tf_op jit(solution)/shard_map/attend/pallas_call | solution.py:537
  25.7 0.8 %attend.5 = (f32[64,512]{1,0:T(8,128)S(1)}, f32[64,128]{1,0:T(8,128)S(1)}, bf16[64,640]{1,0:T(8,128)(2,1)S(1)}) custom-call(s32[16,128]{1,0:T(8,128)S(1)} %get-tuple-element.59.key_pos_ref, s32[256,128]{1,0:T(8,128)S(1)} %get-tuple-element.60.q_pos_ref, s32[256,128]{1,0:T(8,128)S(1)} %get-tuple-element.61.q_begin_ref, bf16[128,512]{1,0:T(8,128)(2,1)S(1)} %query.1.q_ref, ...), custom_call_target="tpu_custom_call" | custom-call | tf_op jit(solution)/shard_map/attend/pallas_call | solution.py:537
  27.0 0.8 %leave.1 = bf16[64,2048]{1,0:T(8,128)(2,1)S(1)} custom-call(bf16[512,2048]{1,0:T(8,128)(2,1)S(1)} %copy-done, f32[128,512]{1,0:T(8,128)S(1)} %get-tuple-element.68.refs_0_.refs_2_, f32[128,128]{1,0:T(8,128)S(1)} %get-tuple-element.69.refs_1_.refs_3_, bf16[128,640]{1,0:T(8,128)(2,1)S(1)} %collective-permute-done.9.refs_2_.refs_4_, ...), custom_call_target="tpu_custom_call" | custom-call | tf_op jit(solution)/shard_map/leave/pallas_call | solution.py:598
  27.8 1.6 %collective-permute-start.13 = (bf16[64,2048]{1,0:T(8,128)(2,1)S(1)}, bf16[64,2048]{1,0:T(8,128)(2,1)S(1)}, u32[]{:S(2)}, u32[]{:S(2)}) collective-permute-start(bf16[64,2048]{1,0:T(8,128)(2,1)S(1)} %leave.1), channel_id=1, source_target_pairs={{0,1},{1,0},{2,3},{3,2},{4,5},{5,4},{6,7},{7,6},{8,9},{9,8},{10,11... | collective-permute-start | bytes 786440 | tf_op jit(solution)/shard_map/ppermute | solution.py:607
  29.4 1.3 %collective-permute-done.8.refs_7_ = bf16[64,640]{1,0:T(8,128)(2,1)S(1)} collective-permute-done((bf16[64,640]{1,0:T(8,128)(2,1)S(1)}, bf16[64,640]{1,0:T(8,128)(2,1)S(1)}, u32[]{:S(2)}, u32[]{:S(2)}) %collective-permute-start.8) | collective-permute-done | bytes 81952 | tf_op jit(solution)/shard_map/ppermute | solution.py:437
  30.7 1.6 %cache.1 = (bf16[8,2,32,256]{3,2,1,0:T(8,128)(2,1)S(1)}, bf16[4,2,32,256]{3,2,1,0:T(8,128)(2,1)S(1)}, bf16[4,2,32,256]{3,2,1,0:T(8,128)(2,1)S(1)}) custom-call(s32[16]{0:T(128)S(1)} %copy-done.5, s32[64]{0:T(128)S(1)} %copy-done.6, bf16[128,512]{1,0:T(8,128)(2,1)S(1)} %get-tuple-element.76.refs_0_, bf16[128,512]{1,0:T(8,128)(2,1)S(1)} %collective-permute-done.3.refs_1_, ...), custom_call_target="tpu_custom_call" | custom-call | tf_op jit(solution)/shard_map/cache/pallas_call | solution.py:555
  32.8 0.8 %collective-permute-done.11.refs_0_ = bf16[4,2,32,256]{3,2,1,0:T(8,128)(2,1)S(1)} collective-permute-done((bf16[4,2,32,256]{3,2,1,0:T(8,128)(2,1)S(1)}, bf16[4,2,32,256]{3,2,1,0:T(8,128)(2,1)S(1)}, u32[]{:S(2)}, u32[]{:S(2)}) %collective-permute-start.11) | collective-permute-done | bytes 131104 | tf_op jit(solution)/shard_map/ppermute | solution.py:437
  33.9 1.4 %keep.1 = (f32[64,2048]{1,0:T(8,128)S(1)}, bf16[8,2,32,256]{3,2,1,0:T(8,128)(2,1)}) custom-call(bf16[512,2048]{1,0:T(8,128)(2,1)S(1)} %copy-done, bf16[128,2048]{1,0:T(8,128)(2,1)S(1)} %copy-done.2, bf16[8,2,32,256]{3,2,1,0:T(8,128)(2,1)S(1)} %get-tuple-element.84.mine_ref, bf16[4,2,32,256]{3,2,1,0:T(8,128)(2,1)S(1)} %collective-permute-done.11.refs_0_, ...), custom_call_target="tpu_custom_call" | custom-call | tf_op jit(solution)/shard_map/keep/pallas_call | solution.py:611
  35.3 0.9 %collective-permute-done.13.received_ref = bf16[64,2048]{1,0:T(8,128)(2,1)S(1)} collective-permute-done((bf16[64,2048]{1,0:T(8,128)(2,1)S(1)}, bf16[64,2048]{1,0:T(8,128)(2,1)S(1)}, u32[]{:S(2)}, u32[]{:S(2)}) %collective-permute-start.13) | collective-permute-done | bytes 262176 | tf_op jit(solution)/shard_map/ppermute | solution.py:607
  36.2 0.8 %finish.1 = bf16[64,2048]{1,0:T(8,128)(2,1)} custom-call(f32[64,2048]{1,0:T(8,128)S(1)} %get-tuple-element.90.kept_ref, bf16[64,2048]{1,0:T(8,128)(2,1)S(1)} %collective-permute-done.13.received_ref), custom_call_target="tpu_custom_call" | custom-call | tf_op jit(solution)/shard_map/finish/pallas_call | solution.py:620
  (32 shorter events, 1.7 us)
Async XLA Ops:
  0.6 10.6 %copy-start.5 = (s32[16]{0:T(128)S(1)}, s32[16]{0:T(128)}, u32[]{:S(2)}) copy-start(s32[16]{0:T(128)} %block_ref.1) | copy-start | bytes 196
  0.6 10.5 %copy-start.7 = (s32[4]{0:T(128)S(1)}, s32[4]{0:T(128)}, u32[]{:S(2)}) copy-start(s32[4]{0:T(128)} %len_hbm.1) | copy-start | bytes 52
  4.0 10.0 %copy-start.1 = (bf16[2048,512]{1,0:T(8,128)(2,1)S(1)}, bf16[2048,512]{1,0:T(8,128)(2,1)}, u32[]{:S(2)}) copy-start(bf16[2048,512]{1,0:T(8,128)(2,1)} %wq_ref.1) | copy-start | bytes 6291460
  4.0 9.9 %copy-start.3 = (bf16[128,2048]{1,0:T(8,128)(2,1)S(1)}, bf16[128,2048]{1,0:T(8,128)(2,1)}, u32[]{:S(2)}) copy-start(bf16[128,2048]{1,0:T(8,128)(2,1)} %get-tuple-element.51.normed_ref) | copy-start | bytes 1572868
  4.0 9.9 %copy-start.4 = (f32[128,256]{1,0:T(8,128)S(1)}, f32[128,256]{1,0:T(8,128)}, u32[]{:S(2)}) copy-start(f32[128,256]{1,0:T(8,128)} %get-tuple-element.52.turned_ref) | copy-start | bytes 393220
  4.0 8.2 %collective-permute-start.1 = (bf16[128,512]{1,0:T(8,128)(2,1)}, bf16[128,512]{1,0:T(8,128)(2,1)S(1)}, u32[]{:S(2)}, u32[]{:S(2)}) collective-permute-start(bf16[128,512]{1,0:T(8,128)(2,1)} %get-tuple-element.47.kv_ref), channel_id=1, source_target_pairs={{0,8},{2,10},{4,12},{6,14},{8,0},{10,2},{12,4},{14,6},{16,24},{18,... | collective-permute-start | bytes 393224 | tf_op jit(solution)/shard_map/ppermute | solution.py:437
  7.1 10.1 %collective-permute-start.3 = (bf16[128,512]{1,0:T(8,128)(2,1)}, bf16[128,512]{1,0:T(8,128)(2,1)S(1)}, u32[]{:S(2)}, u32[]{:S(2)}) collective-permute-start(bf16[128,512]{1,0:T(8,128)(2,1)} %get-tuple-element.47.kv_ref), channel_id=1, source_target_pairs={{0,4},{2,6},{4,0},{6,2},{8,12},{10,14},{12,8},{14,10},{16,20},{18,... | collective-permute-start | bytes 393224 | tf_op jit(solution)/shard_map/ppermute | solution.py:437
  8.6 8.6 %collective-permute-start = (bf16[128,512]{1,0:T(8,128)(2,1)}, bf16[128,512]{1,0:T(8,128)(2,1)S(1)}, u32[]{:S(2)}, u32[]{:S(2)}) collective-permute-start(bf16[128,512]{1,0:T(8,128)(2,1)} %get-tuple-element.47.kv_ref), channel_id=1, source_target_pairs={{0,16},{2,18},{4,20},{6,22},{8,24},{10,26},{12,28},{14,30},{16,0},... | collective-permute-start | bytes 393224 | tf_op jit(solution)/shard_map/ppermute | solution.py:437
  11.2 0.9 %copy-start.8 = (bf16[128,512]{1,0:T(8,128)(2,1)S(1)}, bf16[128,512]{1,0:T(8,128)(2,1)}, u32[]{:S(2)}) copy-start(bf16[128,512]{1,0:T(8,128)(2,1)} %get-tuple-element.47.kv_ref) | copy-start | bytes 393220
  12.3 5.0 %collective-permute-start.2 = (bf16[128,512]{1,0:T(8,128)(2,1)S(1)}, bf16[128,512]{1,0:T(8,128)(2,1)S(1)}, u32[]{:S(2)}, u32[]{:S(2)}) collective-permute-start(bf16[128,512]{1,0:T(8,128)(2,1)S(1)} %collective-permute-done.1.refs_2_), channel_id=1, source_target_pairs={{0,4},{2,6},{4,0},{6,2},{8,12},{10,14},{12,8},{14,10},{16,20},{18,... | collective-permute-start | bytes 393224 | tf_op jit(solution)/shard_map/ppermute | solution.py:437
  14.5 12.5 %copy-start = (bf16[512,2048]{1,0:T(8,128)(2,1)S(1)}, bf16[512,2048]{1,0:T(8,128)(2,1)}, u32[]{:S(2)}) copy-start(bf16[512,2048]{1,0:T(8,128)(2,1)} %wo_ref.3) | copy-start | bytes 6291460
  14.5 6.3 %collective-permute-start.7 = (bf16[128,512]{1,0:T(8,128)(2,1)S(1)}, bf16[128,512]{1,0:T(8,128)(2,1)S(1)}, u32[]{:S(2)}, u32[]{:S(2)}) collective-permute-start(bf16[128,512]{1,0:T(8,128)(2,1)S(1)} %query.1.q_ref), channel_id=1, source_target_pairs={{0,2},{2,0},{4,6},{6,4},{8,10},{10,8},{12,14},{14,12},{16,18},{18,... | collective-permute-start | bytes 393224 | tf_op jit(solution)/shard_map/ppermute | solution.py:437
  17.3 6.9 %collective-permute-start.6 = (bf16[128,512]{1,0:T(8,128)(2,1)S(1)}, bf16[128,512]{1,0:T(8,128)(2,1)S(1)}, u32[]{:S(2)}, u32[]{:S(2)}) collective-permute-start(bf16[128,512]{1,0:T(8,128)(2,1)S(1)} %collective-permute-done.refs_3_), channel_id=1, source_target_pairs={{0,12},{2,14},{4,8},{6,10},{8,4},{10,6},{12,0},{14,2},{16,28},{18,... | collective-permute-start | bytes 393224 | tf_op jit(solution)/shard_map/ppermute | solution.py:437
  18.6 6.2 %collective-permute-start.5 = (bf16[128,512]{1,0:T(8,128)(2,1)S(1)}, bf16[128,512]{1,0:T(8,128)(2,1)S(1)}, u32[]{:S(2)}, u32[]{:S(2)}) collective-permute-start(bf16[128,512]{1,0:T(8,128)(2,1)S(1)} %collective-permute-done.refs_3_), channel_id=1, source_target_pairs={{0,4},{2,6},{4,0},{6,2},{8,12},{10,14},{12,8},{14,10},{16,20},{18,... | collective-permute-start | bytes 393224 | tf_op jit(solution)/shard_map/ppermute | solution.py:437
  19.2 5.6 %collective-permute-start.4 = (bf16[128,512]{1,0:T(8,128)(2,1)S(1)}, bf16[128,512]{1,0:T(8,128)(2,1)S(1)}, u32[]{:S(2)}, u32[]{:S(2)}) collective-permute-start(bf16[128,512]{1,0:T(8,128)(2,1)S(1)} %collective-permute-done.refs_3_), channel_id=1, source_target_pairs={{0,8},{2,10},{4,12},{6,14},{8,0},{10,2},{12,4},{14,6},{16,24},{18,... | collective-permute-start | bytes 393224 | tf_op jit(solution)/shard_map/ppermute | solution.py:437
  22.2 4.3 %collective-permute-start.9 = (bf16[128,640]{1,0:T(8,128)(2,1)S(1)}, bf16[128,640]{1,0:T(8,128)(2,1)S(1)}, u32[]{:S(2)}, u32[]{:S(2)}) collective-permute-start(bf16[128,640]{1,0:T(8,128)(2,1)S(1)} %get-tuple-element.70), channel_id=1, source_target_pairs={{0,2},{2,0},{4,6},{6,4},{8,10},{10,8},{12,14},{14,12},{16,18},{18,... | collective-permute-start | bytes 491528 | tf_op jit(solution)/shard_map/ppermute | solution.py:437
  25.6 5.0 %copy-start.6 = (s32[64]{0:T(128)S(1)}, s32[64]{0:T(128)}, u32[]{:S(2)}) copy-start(s32[64]{0:T(128)} %slot_ref.1) | copy-start | bytes 772
  25.6 1.3 %collective-permute-start.10 = (bf16[64,640]{1,0:T(8,128)(2,1)S(1)}, bf16[64,640]{1,0:T(8,128)(2,1)S(1)}, u32[]{:S(2)}, u32[]{:S(2)}) collective-permute-start(bf16[64,640]{1,0:T(8,128)(2,1)S(1)} %get-tuple-element.75), channel_id=1, source_target_pairs={{0,2},{2,0},{4,6},{6,4},{8,10},{10,8},{12,14},{14,12},{16,18},{18,... | collective-permute-start | bytes 245768 | tf_op jit(solution)/shard_map/ppermute | solution.py:437
  26.5 7.3 %copy-start.2 = (bf16[128,2048]{1,0:T(8,128)(2,1)S(1)}, bf16[128,2048]{1,0:T(8,128)(2,1)}, u32[]{:S(2)}) copy-start(bf16[128,2048]{1,0:T(8,128)(2,1)} %tok_ref.1) | copy-start | bytes 1572868
  27.8 8.4 %collective-permute-start.13 = (bf16[64,2048]{1,0:T(8,128)(2,1)S(1)}, bf16[64,2048]{1,0:T(8,128)(2,1)S(1)}, u32[]{:S(2)}, u32[]{:S(2)}) collective-permute-start(bf16[64,2048]{1,0:T(8,128)(2,1)S(1)} %leave.1), channel_id=1, source_target_pairs={{0,1},{1,0},{2,3},{3,2},{4,5},{5,4},{6,7},{7,6},{8,9},{9,8},{10,11... | collective-permute-start | bytes 786440 | tf_op jit(solution)/shard_map/ppermute | solution.py:607
  29.4 1.3 %collective-permute-start.8 = (bf16[64,640]{1,0:T(8,128)(2,1)S(1)}, bf16[64,640]{1,0:T(8,128)(2,1)S(1)}, u32[]{:S(2)}, u32[]{:S(2)}) collective-permute-start(bf16[64,640]{1,0:T(8,128)(2,1)S(1)} %get-tuple-element.67), channel_id=1, source_target_pairs={{0,2},{2,0},{4,6},{6,4},{8,10},{10,8},{12,14},{14,12},{16,18},{18,... | collective-permute-start | bytes 245768 | tf_op jit(solution)/shard_map/ppermute | solution.py:437
  32.3 1.4 %collective-permute-start.11 = (bf16[4,2,32,256]{3,2,1,0:T(8,128)(2,1)S(1)}, bf16[4,2,32,256]{3,2,1,0:T(8,128)(2,1)S(1)}, u32[]{:S(2)}, u32[]{:S(2)}) collective-permute-start(bf16[4,2,32,256]{3,2,1,0:T(8,128)(2,1)S(1)} %get-tuple-element.85), channel_id=1, source_target_pairs={{0,2},{2,0},{4,6},{6,4},{8,10},{10,8},{12,14},{14,12},{16,18},{18,... | collective-permute-start | bytes 393224 | tf_op jit(solution)/shard_map/ppermute | solution.py:437
  32.5 1.4 %collective-permute-start.12 = (bf16[4,2,32,256]{3,2,1,0:T(8,128)(2,1)S(1)}, bf16[4,2,32,256]{3,2,1,0:T(8,128)(2,1)S(1)}, u32[]{:S(2)}, u32[]{:S(2)}) collective-permute-start(bf16[4,2,32,256]{3,2,1,0:T(8,128)(2,1)S(1)} %get-tuple-element.86), channel_id=1, source_target_pairs={{0,2},{2,0},{4,6},{6,4},{8,10},{10,8},{12,14},{14,12},{16,18},{18,... | collective-permute-start | bytes 393224 | tf_op jit(solution)/shard_map/ppermute | solution.py:437
